TPU v7x, 128 devices: a whole 4x4x4 slice. The times are simulated.
128 devices in a mesh: lon: 32 (over y_hi, x, z), lat: 4 (over y_lo, core).
Axes of the slice: x: 4, y: 4 (y_hi: 2, y_lo: 2; y = y_hi * 2 + y_lo), z: 4, core: 2. Of those that a mesh axis runs over, the one named last changes fastest.
Arguments:
- features: bfloat16 [96, 384, 1536], P('lat', 'lon'), may hold values from -6 to 6
- upstream: bfloat16 [96, 384, 1536], P('lat', 'lon'), may hold values from -6 to 6
- region_ids: int32 [96, 384], P('lat', 'lon'), may hold values from 0 to 3, as said below
- qkv_weight: bfloat16 [1536, 2304], replicated, may hold values from -0.15625 to 0.15625
- query_bias: float32 [768], replicated, may hold values from -3 to 3
- value_bias: float32 [768], replicated, may hold values from -3 to 3
- logit_scale: float32 [12], replicated, may hold values from 1 to 2.5
- pair_bias: float32 [12, 72, 72], replicated, may hold values from -3 to 3
- proj_weight: bfloat16 [1536, 768], replicated, may hold values from -0.21875 to 0.21875
- norm_gain: float32 [1536], replicated, may hold values from 0.25 to 1.75
Outputs:
- input_grad: bfloat16 [96, 384, 1536], P('lat', 'lon')
- qkv_weight_grad: float32 [1536, 2304], P(('lon', 'lat'))
- proj_weight_grad: float32 [1536, 768], P(('lon', 'lat'))
- gain_grad: float32 [1536], replicated
- query_bias_grad: float32 [768], replicated
- value_bias_grad: float32 [768], replicated
- scale_grad: float32 [12], replicated
- pair_grad: float32 [12, 72, 72], replicated
Inputs may be any that keep to these rules, and one draw needn't show every extreme that they name: `region_ids`: within each window of 6 x 12 cells of the shifted grid, a boundary row and a boundary column split the cells into at most four rectangular classes: 2 for rows at or below the boundary row plus 1 for columns at or right of the boundary column; the window's last cell is always class 3.
All inputs are finite; a program needn't handle non-finite values.
Results may differ from a plain program's by a relative error of at most 0.015.
Values may be sent and summed in bfloat16 or wider, within the bound.
No kernel may reach another device: no remote copies, remote signals or barrier semaphores. Data moves between devices by JAX's collectives and lax.ppermute only.
A program may use at most 128 MiB of HBM per device.

v0:
```python
import functools

import jax
import jax.numpy as jnp
import numpy as np
from jax import lax
from jax.experimental import pallas as pl
from jax.experimental.pallas import tpu as pltpu
from jax.sharding import Mesh
from jax.sharding import PartitionSpec as P

HEADS = 12
HEAD_DIM = 64
WIN_H = 6
WIN_W = 12
SHIFT_H = 3
SHIFT_W = 6
WIN = 72
C = 1536
HC = 768
HALF = 384
CELLS = 288
WINDOWS = 4
COSINE_EPS = 1e-06
NORM_EPS = 1e-05

F32 = jnp.float32
BF16 = jnp.bfloat16
LON = ("yh", "x", "z")
LAT = ("yl", "c")
Y = ("yh", "yl")
ORDERS = (("x", "y", "z"), ("y", "z", "x"), ("z", "x", "y"))
AXES = {"x": ("x",), "y": Y, "z": ("z",)}
KEEP = np.array([[[0, 3], [1, 2], [1, 2], [0, 3]], [[0, 1], [0, 1], [2, 3], [2, 3]]], np.int32)
SEND = np.array([[[1, 2], [0, 3], [0, 3], [1, 2]], [[2, 3], [2, 3], [0, 1], [0, 1]]], np.int32)
FIRST = np.concatenate([KEEP, SEND], -1)
SECOND = np.array([[[0, 1], [0, 1], [1, 0], [1, 0]], [[0, 1], [1, 0], [0, 1], [1, 0]]], np.int32)
BLOCK = (24, 512)
EXTRA = 2
NT = (((1,), (1,)), ((), ()))
TN = (((0,), (0,)), ((), ()))
NN = (((1,), (0,)), ((), ()))
VMEM = pl.BlockSpec(memory_space=pltpu.VMEM)
HBM = pl.BlockSpec(memory_space=pltpu.HBM)
SMEM = pl.BlockSpec(memory_space=pltpu.SMEM)


def dot(left, right, dims=NN):
    return lax.dot_general(left, right, dims, preferred_element_type=F32)


def cost(outs, operands, flops):
    moved = sum(int(np.prod(o.shape)) * o.dtype.itemsize for o in (*outs, *operands))
    return pl.CostEstimate(flops=flops, bytes_accessed=moved, transcendentals=0)


def call(body, outs, operands, scalars=1, scratch=(), flops=0, vmem=16, far=(), name=None):
    specs = [SMEM] * scalars + [VMEM] * (len(operands) - scalars)
    for i in far:
        specs[i] = HBM
    return pl.pallas_call(
        body,
        out_shape=list(outs),
        in_specs=specs,
        out_specs=[VMEM] * len(outs),
        scratch_shapes=list(scratch),
        compiler_params=pltpu.CompilerParams(vmem_limit_bytes=vmem * 2**20),
        cost_estimate=cost(outs, operands, flops),
        name=name,
    )(*operands)


def grid_call(body, grid, scalars, ins, outs, scratch=(), flops=0, vmem=16, name=None):
    operands = [array for array, _, _ in ins]
    results = [result for result, _, _ in outs]
    spec = pltpu.PrefetchScalarGridSpec(
        num_scalar_prefetch=len(scalars),
        grid=grid,
        in_specs=[pl.BlockSpec(block, at) for _, block, at in ins],
        out_specs=[pl.BlockSpec(block, at) for _, block, at in outs],
        scratch_shapes=list(scratch),
    )
    return pl.pallas_call(
        body,
        grid_spec=spec,
        out_shape=results,
        compiler_params=pltpu.CompilerParams(vmem_limit_bytes=vmem * 2**20),
        cost_estimate=cost(results, operands, flops),
        name=name,
    )(*scalars, *operands)


def shape(dims, dtype):
    return jax.ShapeDtypeStruct(dims, dtype)


def head_sum(value):
    rows = lax.broadcasted_iota(jnp.int32, (128, 128), 0) // HEAD_DIM
    cols = lax.broadcasted_iota(jnp.int32, (128, 128), 1) // HEAD_DIM
    ones = (rows == cols).astype(F32).astype(BF16)
    high = value.astype(BF16)
    low = (value - high.astype(F32)).astype(BF16)
    return dot(high, ones) + dot(low, ones)


def low_half(rows):
    return lax.broadcasted_iota(jnp.int32, (rows, 128), 1) < HEAD_DIM


def stacked(value):
    mask = low_half(WIN)
    return jnp.concatenate([jnp.where(mask, value, 0.0), jnp.where(mask, 0.0, value)], 0).astype(BF16)


def unstacked(value):
    return jnp.where(low_half(WIN), value[:WIN], value[WIN:])


def normalized(rows):
    inv = lax.rsqrt(head_sum(rows * rows) + COSINE_EPS)
    return rows * inv, inv


def penalties(region_row, region_col):
    out = []
    for w in range(WINDOWS):
        same = region_row[w : w + 1, :] == region_col[w * WIN : (w + 1) * WIN, :]
        one = jnp.where(same, 0.0, -100.0).astype(F32)
        out.append(jnp.concatenate([one, one], 0))
    return out


def two_heads(scale_ref, head):
    top = lax.broadcasted_iota(jnp.int32, (2 * WIN, 1), 0) < WIN
    return jnp.where(top, scale_ref[head], scale_ref[head + 1])


def softmax_of(scores):
    exp_scores = [jnp.exp(one) for one in scores]
    sums = [jnp.sum(one, -1, keepdims=True) for one in exp_scores]
    return [one / total for one, total in zip(exp_scores, sums)]


SPANS = [slice(n * WIN, (n + 1) * WIN) for n in range(WINDOWS)]


def window_rows(own, lon, lat, both, grid, rows):
    for j in range(12):
        column, low = (own[j + SHIFT_W], lat) if j < SHIFT_W else (lon[j - SHIFT_W], both)
        at = j % SHIFT_W * SHIFT_H
        column = jnp.concatenate(
            [column.astype(F32)[SHIFT_H:], low[...].astype(F32)[at : at + SHIFT_H]], 0
        )
        for t in range(12):
            grid[t, j * 24 : (j + 1) * 24, :] = column[:, t * 128 : (t + 1) * 128]
    for r in range(24):
        for t in range(12):
            rows[r * 12 : (r + 1) * 12, t * 128 : (t + 1) * 128] = grid[t, pl.ds(r, 12, stride=24), :]


def forward_body(
    scale, own, lon, lat, both, w, bias, pair_bias, row, col, x, projected, attended, grid, rows, wide, sems
):
    copies = []
    for g in range(3):
        for j in range(3):
            at = pl.ds(j * HC + g * 256, 256)
            copies.append(pltpu.make_async_copy(w.at[:, at], wide.at[:, at], sems.at[3 * g + j]))
            copies[-1].start()
    window_rows(own, lon, lat, both, grid, rows)
    x[...] = rows[...].astype(BF16)
    pens = penalties(row[...], col[...])
    for g in range(3):
        for j in range(3):
            lo = j * HC + g * 256
            copies[3 * g + j].wait()
            projected[:, lo : lo + 256] = dot(x[...], wide[:, lo : lo + 256]) + bias[:, lo : lo + 256]
        for half in range(2):
            lo = g * 256 + half * 128
            head = lo // HEAD_DIM
            factor = two_heads(scale, head)
            q = normalized(projected[:, lo : lo + 128])[0]
            k = normalized(projected[:, HC + lo : HC + lo + 128])[0]
            v = projected[:, 2 * HC + lo : 2 * HC + lo + 128]
            pb = pair_bias[head * WIN : (head + 2) * WIN, :]
            cosines = [dot(stacked(q[at]), k[at].astype(BF16), NT) for at in SPANS]
            attention = softmax_of([c * factor + pb + pen for c, pen in zip(cosines, pens)])
            outs = [dot(a.astype(BF16), v[at].astype(BF16)) for a, at in zip(attention, SPANS)]
            attended[:, lo : lo + 128] = jnp.concatenate([unstacked(o) for o in outs], 0).astype(BF16)


def norm_part(attended, rows, pw, gain, mixed_low, attended_grad, gain_part, mixed_all):
    for n in range(6):
        at = slice(n * 256, (n + 1) * 256)
        mixed_all[:, at] = dot(attended[...], pw[at, :], NT)
    total = jnp.zeros((1, C), F32)
    for r in range(6):
        at = slice(r * 48, (r + 1) * 48)
        mixed = mixed_all[at, :]
        center = mixed - jnp.mean(mixed, -1, keepdims=True)
        inv_std = lax.rsqrt(jnp.mean(center * center, -1, keepdims=True) + NORM_EPS)
        normed = center * inv_std
        up = rows[at, :]
        total = total + jnp.sum(up * normed, 0, keepdims=True)
        scaled = up * gain[...]
        grad = inv_std * (
            scaled
            - jnp.mean(scaled, -1, keepdims=True)
            - normed * jnp.mean(scaled * normed, -1, keepdims=True)
        )
        mixed_low[at, :] = grad.astype(BF16)
    gain_part[...] = total
    for n in range(3):
        at = slice(n * 256, (n + 1) * 256)
        attended_grad[:, at] = dot(mixed_low[...], pw[:, at]).astype(BF16).astype(F32)


def attention_pair(scale, head, q, k, v, da, pb, pens, gains):
    factor = two_heads(scale, head)
    q, q_inv = normalized(q)
    k, k_inv = normalized(k)
    qs = [stacked(q[at]) for at in SPANS]
    das = [stacked(da[at]) for at in SPANS]
    kb = [k[at].astype(BF16) for at in SPANS]
    vb = [v[at].astype(BF16) for at in SPANS]
    cosines = [dot(a, b, NT) for a, b in zip(qs, kb)]
    prob_grads = [dot(a, b, NT) for a, b in zip(das, vb)]
    attention = softmax_of([c * factor + pb + pen for c, pen in zip(cosines, pens)])
    v_grad = jnp.concatenate([dot(a.astype(BF16), b, TN) for a, b in zip(attention, das)], 0)
    means = [jnp.sum(a * p, -1, keepdims=True) for a, p in zip(attention, prob_grads)]
    score_grads = [a * (p - m) for a, p, m in zip(attention, prob_grads, means)]
    cosine_grads = [(s * factor).astype(BF16) for s in score_grads]
    gq = jnp.concatenate([unstacked(dot(c, b)) for c, b in zip(cosine_grads, kb)], 0)
    gk = jnp.concatenate([dot(c, b, TN) for c, b in zip(cosine_grads, qs)], 0)
    pair = (score_grads[0] + score_grads[1]) + (score_grads[2] + score_grads[3])
    scaled = sum(s * c for s, c in zip(score_grads, cosines))
    lane = lax.broadcasted_iota(jnp.int32, (1, 128), 1)
    scale_line = jnp.zeros((1, 128), F32)
    for i in range(2):
        one = jnp.sum(jnp.sum(scaled[i * WIN : (i + 1) * WIN], 0, keepdims=True), 1, keepdims=True)
        scale_line = scale_line + jnp.where(lane == i, one * scale[head + i], 0.0)
    q_grad = q_inv * (gq - q * head_sum(q * gq))
    k_grad = k_inv * (gk - k * head_sum(k * gk))
    lines = jnp.concatenate(
        [
            jnp.sum(q_grad, 0, keepdims=True),
            jnp.sum(v_grad, 0, keepdims=True),
            scale_line,
            gains[:, :128],
            gains[:, 128:],
            jnp.zeros((11, 128), F32),
        ],
        0,
    )
    return (q_grad, k_grad, v_grad), pair, lines


def store_pair(grads, small, at, parts, pair, lines):
    for i, part in enumerate(parts):
        grads[:, at * HALF + i * 128 : at * HALF + (i + 1) * 128] = part.astype(BF16)
    rows = slice(at * 48, (at + 1) * 48)
    for g in range(3):
        small[rows, g * 128 : g * 128 + WIN] = pair[g * 48 : (g + 1) * 48]
    small[at * 48 : at * 48 + 16, 384:] = lines


def attention_body(
    side, scale, q_ref, k_ref, v_ref, da_ref, pair_bias, row, col, gain_part, grads, small
):
    pens = penalties(row[...], col[...])
    head = side[0] * 6 + 2 * pl.program_id(0)
    small[...] = jnp.zeros_like(small)
    store_pair(
        grads,
        small,
        0,
        *attention_pair(
            scale, head, q_ref[...], k_ref[...], v_ref[...], da_ref[...], pair_bias[...], pens, gain_part[...]
        ),
    )


def backward_body(
    side,
    scale,
    attended,
    own,
    lon,
    lat,
    both,
    pw,
    gain,
    projected,
    pair_bias,
    row,
    col,
    mixed_low,
    attended_grad,
    gain_part,
    grads,
    small,
    grid,
    rows,
    mixed_all,
):
    window_rows(own, lon, lat, both, grid, rows)
    norm_part(attended, rows, pw, gain, mixed_low, attended_grad, gain_part, mixed_all)
    pens = penalties(row[...], col[...])
    small[...] = jnp.zeros_like(small)
    for hp in range(3):
        def lanes(base):
            return pl.ds(pl.multiple_of(base + side[0] * HALF + hp * 128, 128), 128)

        head = side[0] * 6 + 2 * hp
        gains = gain_part[:, pl.ds(pl.multiple_of(side[0] * HC + hp * 256, 128), 256)]
        store_pair(
            grads,
            small,
            hp,
            *attention_pair(
                scale,
                head,
                projected[:, lanes(0)],
                projected[:, lanes(HC)],
                projected[:, lanes(2 * HC)],
                attended_grad[:, lanes(0)],
                pair_bias[pl.ds(pl.multiple_of(head * WIN, 8), 2 * WIN), :],
                pens,
                gains,
            ),
        )


def write_coded(value, lines, outs, base):
    high = lines.astype(BF16)
    low = (lines - high.astype(F32)).astype(BF16)
    for i, tail in enumerate((high, low)):
        block = jnp.concatenate([value[i][:, :384].astype(BF16), tail], 1)
        for out in outs:
            out[base + i] = block


def add_coded(keep, recv, outs, source, base):
    value = [keep[source + i].astype(F32) + recv[source + i].astype(F32) for i in range(EXTRA)]
    write_coded(value, value[0][:, 384:] + value[1][:, 384:], outs, base)


def row_of(place):
    y = place["y"]
    return 24 * ((y // 2) * 32 + place["x"] * 8 + place["z"] * 2 + y % 2)


def weight_body(order, x0, x1, p0, p1, m0, m1, a0, a1, s0, s1, *rest):
    outs, (left, grads, total) = rest[:6], rest[6:]
    left[:CELLS, :] = x0[...]
    left[CELLS:, :] = x1[...]
    grads[:CELLS, :] = p0[...]
    grads[CELLS:, :] = p1[...]
    for m in range(4):
        at = slice(m * 384, (m + 1) * 384)
        part = dot(left[:, at], grads[...], TN)
        for j in range(3):
            total[at, j * 512 : j * 512 + HALF] = part[:, j * HALF : (j + 1) * HALF]
    left[:CELLS, :] = m0[...]
    left[CELLS:, :] = m1[...]
    grads[:CELLS, :HALF] = a0[...]
    grads[CELLS:, :HALF] = a1[...]
    for m in range(4):
        at = slice(m * 384, (m + 1) * 384)
        part = dot(left[:, at], grads[:, :HALF], TN)
        for j in range(3):
            total[at, j * 512 + HALF : (j + 1) * 512] = part[:, j * 128 : (j + 1) * 128]
    for j in range(3):
        cols = slice(j * 512, (j + 1) * 512)
        for i in range(4):
            out = outs[2 * j + i // 2]
            for second in range(4):
                for third in range(4):
                    places = (order[4 * j + i], second, third)
                    start = row_of(dict(zip(ORDERS[j], places)))
                    rows = pl.ds(pl.multiple_of(start, 8), 24)
                    out[i % 2 * 16 + second * 4 + third] = total[rows, cols].astype(BF16)
        at = slice(j * 48, (j + 1) * 48)
        value = s0[at, :] + s1[at, :]
        write_coded([value[:24], value[24:]], value[:24, 384:], outs[2 * j : 2 * j + 2], 32)


def halve_body(count, size, order, *refs):
    ins, outs = refs[:6], refs[6:]
    for j in range(3):
        keep, recv = ins[2 * j : 2 * j + 2]
        for i in range(2 * count):
            out = outs[2 * j + i // count]
            for b in range(size):
                at = order[2 * count * j + i] * size + b
                out[i % count * size + b] = (keep[at].astype(F32) + recv[at].astype(F32)).astype(BF16)
        add_coded(keep, recv, outs[2 * j : 2 * j + 2], 2 * count * size, count * size)


def total_body(*refs):
    ins, out = refs[:6], refs[6]
    for j in range(3):
        keep, recv = ins[2 * j : 2 * j + 2]
        out[3 * j] = (keep[0].astype(F32) + recv[0].astype(F32)).astype(BF16)
        add_coded(keep, recv, [out], 1, 3 * j + 1)


def finish_body(core, own, other, qkv, proj, pair, gain, qb, vb, scale):
    which = core[0]
    for side in range(2):
        for j in range(3):
            def block(i):
                return jnp.where(which == side, own[3 * j + i].astype(F32), other[3 * j + i].astype(F32))

            rows = block(0)
            rows = jnp.where(which == 0, rows[:12], rows[12:])
            at = side * HALF + j * 128
            for t in range(3):
                qkv[:, t * HC + at : t * HC + at + 128] = rows[:, t * 128 : (t + 1) * 128]
            proj[:, at : at + 128] = rows[:, HALF:]
            top, bottom = block(1), block(2)
            for g in range(3):
                start = (side * 3 + j) * 144 + g * 48
                pair[start : start + 24, :] = top[:, g * 128 : g * 128 + WIN]
                pair[start + 24 : start + 48, :] = bottom[:, g * 128 : g * 128 + WIN]
            lines = top[:, 384:] + bottom[:, 384:]
            qb[:, at : at + 128] = lines[0:1]
            vb[:, at : at + 128] = lines[1:2]
            scale[side * 3 + j : side * 3 + j + 1, :] = lines[2:3]
            gain[:, side * HC + j * 256 : side * HC + j * 256 + 128] = lines[3:4]
            gain[:, side * HC + j * 256 + 128 : side * HC + j * 256 + 256] = lines[4:5]


def branch_body(side, w, own, theirs, branch, low, grads, rows):
    which = side[0]

    @pl.when(pl.program_id(0) == 0)
    def _():
        for pair in range(3):
            for j in range(3):
                at = j * HC + pair * 128
                cols = slice(pair * HALF + j * 128, pair * HALF + (j + 1) * 128)
                grads[:, pl.ds(pl.multiple_of(at + which * HALF, 128), 128)] = own[:, cols]
                grads[:, pl.ds(pl.multiple_of(at + (1 - which) * HALF, 128), 128)] = theirs[:, cols]

    product = dot(grads[...], w[...], NT)
    for i in range(2):
        rows[i] = product[:, i * 128 : (i + 1) * 128]
    lows = []
    for j in range(12):
        column = jnp.concatenate([rows[i, pl.ds(j, 24, stride=12), :] for i in range(2)], 1)
        branch[j] = column.astype(BF16)
        lows.append(column[24 - SHIFT_H :])
    low[...] = jnp.concatenate(lows, 0).astype(BF16)


def down_body(grid, low, go, stay):
    for j in range(12):
        came = low[...].astype(F32)[j * SHIFT_H : (j + 1) * SHIFT_H]
        column = jnp.concatenate([came, grid[j].astype(F32)[: 24 - SHIFT_H]], 0).astype(BF16)
        if j < SHIFT_W:
            stay[j] = column
        else:
            go[j - SHIFT_W] = column


def permuted(value, axes, target):
    sizes = [lax.axis_size(a) for a in axes]
    pairs = []
    for source in range(int(np.prod(sizes))):
        place = np.unravel_index(source, sizes)
        to = target(*[int(v) for v in place])
        pairs.append((source, int(np.ravel_multi_index(to, sizes))))
    return lax.ppermute(value, axes, pairs)


def lon_step(value, steps):
    return permuted(value, LON, lambda *at: np.unravel_index((np.ravel_multi_index(at, (2, 4, 4)) + steps) % 32, (2, 4, 4)))


def lat_step(value, steps):
    return permuted(value, LAT, lambda *at: np.unravel_index((np.ravel_multi_index(at, (2, 2)) + steps) % 4, (2, 2)))


def both_step(value, steps):
    def target(yh, x, z, yl, c):
        lon = (np.ravel_multi_index((yh, x, z), (2, 4, 4)) + steps) % 32
        lat = (yl * 2 + c + steps) % 4
        return (*np.unravel_index(lon, (2, 4, 4)), lat // 2, lat % 2)

    return permuted(value, LON + LAT, target)


def core_swap(value):
    return permuted(value, ("c",), lambda c: (1 - c,))


def ring_swap(value, axis, step):
    def partner(place, c):
        return place ^ 1 if (step == 0) == (c == 0) else 3 - place

    if axis == "y":
        def target(yh, yl, c):
            to = partner(yh * 2 + yl, c)
            return (to // 2, to % 2, c)
    else:
        def target(place, c):
            return (partner(place, c), c)

    return permuted(value, AXES[axis] + ("c",), target)


def messages(grid):
    return [
        grid[:SHIFT_W],
        grid[SHIFT_W:, :SHIFT_H].reshape(-1, C),
        grid[:SHIFT_W, :SHIFT_H].reshape(-1, C),
    ]


def moved(lon, lat, both):
    return [lon_step(lon, -1), lat_step(lat, -1), both_step(both, -1)]


def shards(
    features,
    upstream,
    region_ids,
    qkv_weight,
    query_bias,
    value_bias,
    logit_scale,
    pair_bias,
    proj_weight,
    norm_gain,
):
    core = lax.axis_index("c")
    place = {"x": lax.axis_index("x"), "z": lax.axis_index("z"), "y": lax.axis_index("yh") * 2 + lax.axis_index("yl")}
    mine = core.astype(jnp.int32).reshape(1)
    theirs = 1 - mine
    scale = jnp.exp(logit_scale)
    bias = jnp.concatenate([query_bias, jnp.zeros_like(query_bias), value_bias]).reshape(1, -1)
    pair_rows = pair_bias.reshape(HEADS * WIN, WIN)
    region_row = region_ids.reshape(WINDOWS, WIN)
    region_col = region_ids.reshape(-1, 1)
    gain = norm_gain.reshape(1, C)

    features = features.transpose(1, 0, 2)
    upstream = upstream.transpose(1, 0, 2)
    came = moved(*messages(features))
    going, came[1] = lax.optimization_barrier((messages(upstream), came[1]))
    came_late = moved(*going)
    x, projected, attended = call(
        forward_body,
        [shape((CELLS, C), BF16), shape((CELLS, 3 * HC), F32), shape((CELLS, HC), BF16)],
        [scale, features, *came, qkv_weight, bias, pair_rows, region_row, region_col],
        scratch=[
            pltpu.VMEM((12, CELLS, 128), F32),
            pltpu.VMEM((CELLS, C), F32),
            pltpu.VMEM((C, 3 * HC), BF16),
            pltpu.SemaphoreType.DMA((9,)),
        ],
        flops=2 * CELLS * C * 3 * HC,
        vmem=24,
        far=(5,),
        name="forward",
    )
    x_other = core_swap(x)
    mixed_low, attended_grad, gain_part, grads_theirs, small_theirs = call(
        backward_body,
        [
            shape((CELLS, C), BF16),
            shape((CELLS, HC), F32),
            shape((1, C), F32),
            shape((CELLS, 3 * HALF), BF16),
            shape((144, 512), F32),
        ],
        [
            theirs,
            scale,
            attended,
            upstream,
            *came_late,
            proj_weight,
            gain,
            projected,
            pair_rows,
            region_row,
            region_col,
        ],
        scalars=2,
        scratch=[pltpu.VMEM((12, CELLS, 128), F32)] + [pltpu.VMEM((CELLS, C), F32)] * 2,
        flops=4 * CELLS * C * HC + 2 * CELLS * WIN * 128 * 18,
        vmem=24,
        name="backward",
    )
    mixed_other = core_swap(mixed_low)
    attended_theirs = lax.dynamic_slice(attended, (0, theirs[0] * HALF), (CELLS, HALF))
    attended_mine = lax.dynamic_slice(attended, (0, mine[0] * HALF), (CELLS, HALF))
    attended_other = core_swap(attended_theirs)

    def attention(side):
        def cols(base):
            return lambda i, side, scale: (0, base + side[0] * 3 + i)

        whole = lambda i, side, scale: (0, 0)
        block = (CELLS, 128)
        return grid_call(
            attention_body,
            (3,),
            [side, scale],
            [
                (projected, block, cols(0)),
                (projected, block, cols(6)),
                (projected, block, cols(12)),
                (attended_grad, block, cols(0)),
                (pair_rows, (2 * WIN, WIN), lambda i, side, scale: (side[0] * 3 + i, 0)),
                (region_row, (WINDOWS, WIN), whole),
                (region_col, (CELLS, 1), whole),
                (gain_part, (1, 256), cols(0)),
            ],
            [
                (shape((CELLS, 3 * HALF), BF16), (CELLS, HALF), lambda i, side, scale: (0, i)),
                (shape((144, 512), F32), (48, 512), lambda i, side, scale: (i, 0)),
            ],
            flops=2 * CELLS * WIN * 128 * 6 * 3,
            name="attention",
        )

    def tables(values, step):
        return jnp.concatenate([jnp.asarray(values)[core, place[names[step]]] for names in ORDERS])

    grads_other = core_swap(grads_theirs)
    small_other = core_swap(small_theirs)
    grads_mine, small_mine = attention(mine)

    parts = call(
        weight_body,
        [shape((32 + EXTRA,) + BLOCK, BF16)] * 6,
        [
            tables(FIRST, 0),
            x,
            x_other,
            grads_mine,
            grads_other,
            mixed_low,
            mixed_other,
            attended_mine,
            attended_other,
            small_mine,
            small_other,
        ],
        scratch=[
            pltpu.VMEM((2 * CELLS, C), BF16),
            pltpu.VMEM((2 * CELLS, 3 * HALF), BF16),
            pltpu.VMEM((C, C), F32),
        ],
        flops=4 * CELLS * C * C,
        vmem=28,
        name="weights",
    )
    side, parts = lax.optimization_barrier((mine, parts))
    whole = lambda i, side: (0, 0)
    branch, low = grid_call(
        branch_body,
        (6,),
        [side],
        [
            (qkv_weight, (256, 3 * HC), lambda i, side: (i, 0)),
            (grads_mine, (CELLS, 3 * HALF), whole),
            (grads_theirs, (CELLS, 3 * HALF), whole),
        ],
        [
            (shape((12, 24, C), BF16), (12, 24, 256), lambda i, side: (0, 0, i)),
            (shape((36, C), BF16), (36, 256), lambda i, side: (0, i)),
        ],
        scratch=[pltpu.VMEM((CELLS, 3 * HC), BF16), pltpu.VMEM((2, CELLS, 128), F32)],
        flops=2 * CELLS * C * 3 * HC,
        name="branch",
    )
    go, stay = call(
        down_body,
        [shape((SHIFT_W, 24, C), BF16)] * 2,
        [branch, lat_step(low, 1)],
        scalars=0,
        name="down",
    )
    back = jnp.concatenate([lon_step(go, 1), stay], 0)
    input_grad = (upstream.astype(F32) + back.astype(F32)).astype(BF16)
    for step in range(6):
        terms = []
        for j, names in enumerate(ORDERS):
            terms += [parts[2 * j], ring_swap(parts[2 * j + 1], names[step // 2], step % 2)]
        if step == 5:
            break
        left = 32 >> step
        if step % 2 == 0:
            body = functools.partial(halve_body, 1, left // 2)
            order = tables(SECOND, step // 2)
        else:
            body = functools.partial(halve_body, 2, left // 4)
            order = tables(FIRST, step // 2 + 1)
        if step == 0:
            order, low = lax.optimization_barrier((order, low))
        if step == 1:
            order, stay = lax.optimization_barrier((order, stay))
        parts = call(body, [shape((left // 2 + EXTRA,) + BLOCK, BF16)] * 6, [order, *terms], name="halve")
    terms, input_grad = lax.optimization_barrier((terms, input_grad))
    (sums,) = call(total_body, [shape((9,) + BLOCK, BF16)], terms, scalars=0, name="total")
    sums_other = core_swap(sums)
    qkv_weight_grad, proj_weight_grad, pair_grad, gain_grad, query_bias_grad, value_bias_grad, scale_grad = call(
        finish_body,
        [
            shape((12, 3 * HC), F32),
            shape((12, HC), F32),
            shape((HEADS * WIN, WIN), F32),
            shape((1, C), F32),
            shape((1, HC), F32),
            shape((1, HC), F32),
            shape((6, 128), F32),
        ],
        [mine, sums, sums_other],
        name="finish",
    )
    pair_grad = pair_grad.reshape(HEADS, WIN, WIN)
    gain_grad = gain_grad.reshape(C)
    query_bias_grad = query_bias_grad.reshape(HC)
    value_bias_grad = value_bias_grad.reshape(HC)
    scale_grad = scale_grad[:, :2].reshape(HEADS)

    return (
        input_grad.transpose(1, 0, 2),
        qkv_weight_grad,
        proj_weight_grad,
        gain_grad,
        query_bias_grad,
        value_bias_grad,
        scale_grad,
        pair_grad,
    )


def solution(mesh):
    fine = Mesh(mesh.devices.reshape(2, 4, 4, 2, 2), ("yh", "x", "z", "yl", "c"))
    every = LON + LAT
    return jax.shard_map(
        shards,
        mesh=fine,
        in_specs=(P(LAT, LON, None), P(LAT, LON, None), P(LAT, LON)) + (P(),) * 7,
        out_specs=(P(LAT, LON, None), P(every, None), P(every, None)) + (P(),) * 5,
        check_vma=False,
    )
```

profile of v0, /device:TPU:1, one launch (start us, length us, event | category | flops | bytes accessed | tf_op | source)
XLA Modules:
  0.0 159.9 jit_solution(3166486314779841401)
XLA Ops:
  0.7 1.1 fusion.6
  1.8 1.5 collective-permute-start.1
  3.3 1.0 slice.28
  4.3 8.7 %collective-permute-start = (bf16[6,24,1536]{2,1,0:T(8,128)(2,1)S(1)}, bf16[6,24,1536]{2,1,0:T(8,128)(2,1)S(1)}, u32[]{:S(2)}, u32[]{:S(2)}) collective-permute-start(bf16[6,24,1536]{2,1,0:T(8,128)(2,1)S(1)} %slice.28), channel_id=1, source_target_pairs={{0,124},{4,0},{8,4},{12,8},{16,12},{20,16},{24,20},{28,24},{32,28}... | collective-permute-start | bytes 1327112 | tf_op jit(solution)/shard_map/ppermute | solution.py:474
  13.1 1.0 fusion.7
  14.1 1.8 %slice.29 = bf16[6,24,1536]{2,1,0:T(8,128)(2,1)} slice(bf16[12,24,1536]{2,1,0:T(8,128)(2,1)} %bitcast.24), slice={[0:6], [0:24], [0:1536]} | slice | bytes 884736 | tf_op jit(solution)/shard_map/slice | solution.py:515
  17.4 1.1 collective-permute-start.2
  20.2 12.8 %collective-permute-done.2.both = bf16[18,1536]{1,0:T(8,128)(2,1)S(1)} collective-permute-done((bf16[18,1536]{1,0:T(8,128)(2,1)S(1)}, bf16[18,1536]{1,0:T(8,128)(2,1)S(1)}, u32[]{:S(2)}, u32[]{:S(2)}) %collective-permute-start.2) | collective-permute-done | bytes 55328 | tf_op jit(solution)/shard_map/ppermute | solution.py:474
  34.3 3.0 %copy-done = bf16[1536,2304]{1,0:T(8,128)(2,1)S(1)} copy-done((bf16[1536,2304]{1,0:T(8,128)(2,1)S(1)}, bf16[1536,2304]{1,0:T(8,128)(2,1)}, u32[]{:S(2)}) %copy-start) | copy-done | bytes 7077912
  37.4 1.0 copy-done.2
  38.4 1.2 copy-done.5
  39.5 0.9 copy-done.7
  40.4 1.0 copy-done.14
  41.5 0.9 copy-done.16
  42.3 0.9 copy-done.18
  43.2 10.3 %forward.1 = (bf16[288,1536]{1,0:T(8,128)(2,1)}, f32[288,2304]{1,0:T(8,128)S(1)}, bf16[288,768]{1,0:T(8,128)(2,1)S(1)}) custom-call(f32[12]{0:T(128)S(1)} %exp.3.scale, bf16[12,24,1536]{2,1,0:T(8,128)(2,1)S(1)} %bitcast.31, bf16[6,24,1536]{2,1,0:T(8,128)(2,1)S(1)} %copy-done.14, bf16[18,1536]{1,0:T(8,128)(2,1)S(1)} %copy-done.16, ...), custom_call_target="tpu_custom_call" | custom-call | flops 2038431744 | bytes 12757296 | tf_op jit(solution)/shard_map/forward/pallas_call | solution.py:61
  53.5 2.6 %collective-permute-start.3 = (bf16[288,1536]{1,0:T(8,128)(2,1)}, bf16[288,1536]{1,0:T(8,128)(2,1)}, u32[]{:S(2)}, u32[]{:S(2)}) collective-permute-start(bf16[288,1536]{1,0:T(8,128)(2,1)} %get-tuple-element.86.x0), channel_id=1, source_target_pairs={{0,1},{1,0},{2,3},{3,2},{4,5},{5,4},{6,7},{7,6},{8,9},{9,8},{10,11... | collective-permute-start | bytes 2654216 | tf_op jit(solution)/shard_map/ppermute | solution.py:474
  56.2 8.3 %backward.1 = (bf16[288,1536]{1,0:T(8,128)(2,1)}, f32[288,768]{1,0:T(8,128)S(1)}, f32[1,1536]{1,0:T(1,128)S(1)}, bf16[288,1152]{1,0:T(8,128)(2,1)}, f32[144,512]{1,0:T(8,128)S(1)}) custom-call(s32[1]{0:T(128)S(6)} %sub.3.side, f32[12]{0:T(128)S(1)} %exp.3.scale, bf16[288,768]{1,0:T(8,128)(2,1)S(1)} %get-tuple-element.88.attended, ...), custom_call_target="tpu_custom_call" | custom-call | flops 1454505984 | bytes 9884980 | tf_op jit(solution)/shard_map/backward/pallas_call | solution.py:61
  64.6 0.9 copy-done.11
  66.7 1.1 constant_dynamic-slice_fusion
  69.3 1.0 copy-done.4
  70.3 0.9 copy-done.9
  71.2 1.2 copy-done.12
  72.4 4.5 %attention.1 = (bf16[288,1152]{1,0:T(8,128)(2,1)S(1)}, f32[144,512]{1,0:T(8,128)S(1)}) custom-call(s32[1]{0:T(128)} %bitcast.6.side.core, f32[12]{0:T(128)S(1)} %exp.3.scale, f32[288,2304]{1,0:T(8,128)S(1)} %get-tuple-element.87.projected.q_ref.k_ref.v_ref, f32[288,2304]{1,0:T(8,128)S(1)} %get-tuple-element.87.projected.q_ref.k_ref.v_ref, ...), custom_call_target="tpu_custom_call" | custom-call | flops 95551488 | bytes 10063104 | tf_op jit(solution)/shard_map/attention/pallas_call | solution.py:83
  76.9 7.2 %weights.1 = (bf16[34,24,512]{2,1,0:T(8,128)(2,1)S(1)}, bf16[34,24,512]{2,1,0:T(8,128)(2,1)S(1)}, bf16[34,24,512]{2,1,0:T(8,128)(2,1)S(1)}, bf16[34,24,512]{2,1,...) custom-call(s32[12]{0:T(128)S(1)} %get-tuple-element.177.order, ...), custom_call_target="tpu_custom_call" | custom-call | flops 2717908992 | bytes 10911792 | tf_op jit(solution)/shard_map/weights/pallas_call | solution.py:61
  84.9 7.3 %collective-permute-start.14 = (bf16[34,24,512]{2,1,0:T(8,128)(2,1)S(1)}, bf16[34,24,512]{2,1,0:T(8,128)(2,1)S(1)}, u32[]{:S(2)}, u32[]{:S(2)}) collective-permute-start(bf16[34,24,512]{2,1,0:T(8,128)(2,1)S(1)} %get-tuple-element.116), channel_id=1, source_target_pairs={{0,4},{1,13},{4,0},{5,9},{8,12},{9,5},{12,8},{13,1},{2,6},{3,15},{... | collective-permute-start | bytes 2506760 | tf_op jit(solution)/shard_map/ppermute | solution.py:474
  93.2 4.9 %branch.1 = (bf16[12,24,1536]{2,1,0:T(8,128)(2,1)S(1)}, bf16[36,1536]{1,0:T(8,128)(2,1)S(1)}) custom-call(s32[1]{0:T(128)} %bitcast.6.side.core, bf16[1536,2304]{1,0:T(8,128)(2,1)S(1)} %bitcast.22, bf16[288,1152]{1,0:T(8,128)(2,1)S(1)} %get-tuple-element.94.p0.own, bf16[288,1152]{1,0:T(8,128)(2,1)} %get-tuple-element.95.theirs), custom_call_target="tpu_custom_call" | custom-call | flops 2038431744 | bytes 9400320 | tf_op jit(solution)/shard_map/branch/pallas_call | solution.py:83
  98.1 4.0 %collective-permute-done.14.refs_5_ = bf16[34,24,512]{2,1,0:T(8,128)(2,1)S(1)} collective-permute-done((bf16[34,24,512]{2,1,0:T(8,128)(2,1)S(1)}, bf16[34,24,512]{2,1,0:T(8,128)(2,1)S(1)}, u32[]{:S(2)}, u32[]{:S(2)}) %collective-permute-start.14) | collective-permute-done | bytes 835616 | tf_op jit(solution)/shard_map/ppermute | solution.py:474
  102.2 1.1 halve.5
  103.6 4.9 %collective-permute-start.11 = (bf16[36,1536]{1,0:T(8,128)(2,1)S(1)}, bf16[36,1536]{1,0:T(8,128)(2,1)S(1)}, u32[]{:S(2)}, u32[]{:S(2)}) collective-permute-start(bf16[36,1536]{1,0:T(8,128)(2,1)S(1)} %get-tuple-element.107), channel_id=1, source_target_pairs={{0,1},{1,2},{2,3},{3,0},{4,5},{5,6},{6,7},{7,4},{8,9},{9,10},{10,1... | collective-permute-start | bytes 331784 | tf_op jit(solution)/shard_map/ppermute | solution.py:474
  108.4 1.9 %collective-permute-done.11.low = bf16[36,1536]{1,0:T(8,128)(2,1)S(1)} collective-permute-done((bf16[36,1536]{1,0:T(8,128)(2,1)S(1)}, bf16[36,1536]{1,0:T(8,128)(2,1)S(1)}, u32[]{:S(2)}, u32[]{:S(2)}) %collective-permute-start.11) | collective-permute-done | bytes 110624 | tf_op jit(solution)/shard_map/ppermute | solution.py:474
  111.0 0.9 halve.6
  111.9 0.8 collective-permute-start.18
  112.7 2.7 %collective-permute-start.19 = (bf16[10,24,512]{2,1,0:T(8,128)(2,1)S(1)}, bf16[10,24,512]{2,1,0:T(8,128)(2,1)S(1)}, u32[]{:S(2)}, u32[]{:S(2)}) collective-permute-start(bf16[10,24,512]{2,1,0:T(8,128)(2,1)S(1)} %get-tuple-element.126), channel_id=1, source_target_pairs={{0,4},{1,13},{4,0},{5,9},{8,12},{9,5},{12,8},{13,1},{2,6},{3,15},{... | collective-permute-start | bytes 737288 | tf_op jit(solution)/shard_map/ppermute | solution.py:474
  115.5 2.8 %collective-permute-done.18.refs_1_ = bf16[10,24,512]{2,1,0:T(8,128)(2,1)S(1)} collective-permute-done((bf16[10,24,512]{2,1,0:T(8,128)(2,1)S(1)}, bf16[10,24,512]{2,1,0:T(8,128)(2,1)S(1)}, u32[]{:S(2)}, u32[]{:S(2)}) %collective-permute-start.18) | collective-permute-done | bytes 245792 | tf_op jit(solution)/shard_map/ppermute | solution.py:474
  119.0 2.7 %collective-permute-done.20.refs_5_ = bf16[10,24,512]{2,1,0:T(8,128)(2,1)S(1)} collective-permute-done((bf16[10,24,512]{2,1,0:T(8,128)(2,1)S(1)}, bf16[10,24,512]{2,1,0:T(8,128)(2,1)S(1)}, u32[]{:S(2)}, u32[]{:S(2)}) %collective-permute-start.20) | collective-permute-done | bytes 245792 | tf_op jit(solution)/shard_map/ppermute | solution.py:474
  123.6 3.1 %collective-permute-done.21.refs_1_ = bf16[6,24,512]{2,1,0:T(8,128)(2,1)S(1)} collective-permute-done((bf16[6,24,512]{2,1,0:T(8,128)(2,1)S(1)}, bf16[6,24,512]{2,1,0:T(8,128)(2,1)S(1)}, u32[]{:S(2)}, u32[]{:S(2)}) %collective-permute-start.21) | collective-permute-done | bytes 147488 | tf_op jit(solution)/shard_map/ppermute | solution.py:474
  126.7 1.2 collective-permute-done.22.refs_3_
  128.5 6.7 %collective-permute-start.24 = (bf16[4,24,512]{2,1,0:T(8,128)(2,1)S(1)}, bf16[4,24,512]{2,1,0:T(8,128)(2,1)S(1)}, u32[]{:S(2)}, u32[]{:S(2)}) collective-permute-start(bf16[4,24,512]{2,1,0:T(8,128)(2,1)S(1)} %get-tuple-element.136), channel_id=1, source_target_pairs={{0,4},{1,13},{4,0},{5,9},{8,12},{9,5},{12,8},{13,1},{2,6},{3,15},{... | collective-permute-start | bytes 294920 | tf_op jit(solution)/shard_map/ppermute | solution.py:474
  135.2 0.9 collective-permute-start.25
  136.9 1.2 collective-permute-done.24.refs_1_
  138.1 1.8 %collective-permute-done.25.refs_3_ = bf16[4,24,512]{2,1,0:T(8,128)(2,1)S(1)} collective-permute-done((bf16[4,24,512]{2,1,0:T(8,128)(2,1)S(1)}, bf16[4,24,512]{2,1,0:T(8,128)(2,1)S(1)}, u32[]{:S(2)}, u32[]{:S(2)}) %collective-permute-start.25) | collective-permute-done | bytes 98336 | tf_op jit(solution)/shard_map/ppermute | solution.py:474
  139.9 1.2 collective-permute-done.26.refs_5_
  142.4 1.1 add_convert_fusion
  143.5 1.5 collective-permute-done.27.refs_1_
  145.3 10.2 %collective-permute-start.31 = (bf16[9,24,512]{2,1,0:T(8,128)(2,1)S(1)}, bf16[9,24,512]{2,1,0:T(8,128)(2,1)S(1)}, u32[]{:S(2)}, u32[]{:S(2)}) collective-permute-start(bf16[9,24,512]{2,1,0:T(8,128)(2,1)S(1)} %total.1.own), channel_id=1, source_target_pairs={{0,1},{1,0},{2,3},{3,2},{4,5},{5,4},{6,7},{7,6},{8,9},{9,8},{10,11... | collective-permute-start | bytes 663560 | tf_op jit(solution)/shard_map/ppermute | solution.py:474
  155.5 1.1 collective-permute-done.31.other
  156.6 0.9 finish.1
  (110 shorter events, 18.0 us)
Async XLA Ops:
  0.6 17.9 %copy-start.22 = (f32[768]{0:T(1024)S(1)}, f32[768]{0:T(1024)}, u32[]{:S(2)}) copy-start(f32[768]{0:T(1024)} %param.17) | copy-start | bytes 9220
  0.6 17.9 %copy-start.23 = (f32[768]{0:T(1024)S(1)}, f32[768]{0:T(1024)}, u32[]{:S(2)}) copy-start(f32[768]{0:T(1024)} %param.16) | copy-start | bytes 9220
  0.7 17.9 %copy-start.21 = (s32[24,12]{0,1:T(8,128)S(1)}, s32[24,12]{0,1:T(8,128)}, u32[]{:S(2)}) copy-start(s32[24,12]{0,1:T(8,128)} %param.14) | copy-start | bytes 3460
  0.7 18.8 %copy-start.24 = (f32[12]{0:T(128)S(1)}, f32[12]{0:T(128)}, u32[]{:S(2)}) copy-start(f32[12]{0:T(128)} %param.18) | copy-start | bytes 148
  0.7 18.8 %copy-start.20 = (f32[1536]{0:T(1024)S(1)}, f32[1536]{0:T(1024)}, u32[]{:S(2)}) copy-start(f32[1536]{0:T(1024)} %param.21) | copy-start | bytes 18436
  1.8 15.5 %collective-permute-start.1 = (bf16[18,1536]{1,0:T(8,128)(2,1)S(1)}, bf16[18,1536]{1,0:T(8,128)(2,1)S(1)}, u32[]{:S(2)}, u32[]{:S(2)}) collective-permute-start(bf16[18,1536]{1,0:T(8,128)(2,1)S(1)} %reshape.66), channel_id=1, source_target_pairs={{0,3},{1,0},{2,1},{3,2},{4,7},{5,4},{6,5},{7,6},{8,11},{9,8},{10,9... | collective-permute-start | bytes 165896 | tf_op jit(solution)/shard_map/ppermute | solution.py:474
  4.3 29.2 %collective-permute-start = (bf16[6,24,1536]{2,1,0:T(8,128)(2,1)S(1)}, bf16[6,24,1536]{2,1,0:T(8,128)(2,1)S(1)}, u32[]{:S(2)}, u32[]{:S(2)}) collective-permute-start(bf16[6,24,1536]{2,1,0:T(8,128)(2,1)S(1)} %slice.28), channel_id=1, source_target_pairs={{0,124},{4,0},{8,4},{12,8},{16,12},{20,16},{24,20},{28,24},{32,28}... | collective-permute-start | bytes 1327112 | tf_op jit(solution)/shard_map/ppermute | solution.py:474
  17.3 16.3 %copy-start.15 = (bf16[18,1536]{1,0:T(8,128)(2,1)}, bf16[18,1536]{1,0:T(8,128)(2,1)S(1)}, u32[]{:S(2)}) copy-start(bf16[18,1536]{1,0:T(8,128)(2,1)S(1)} %collective-permute-done.1.lat) | copy-start | bytes 165892
  17.3 38.9 %collective-permute-start.4 = (bf16[6,24,1536]{2,1,0:T(8,128)(2,1)}, bf16[6,24,1536]{2,1,0:T(8,128)(2,1)}, u32[]{:S(2)}, u32[]{:S(2)}) collective-permute-start(bf16[6,24,1536]{2,1,0:T(8,128)(2,1)} %slice.29), channel_id=1, source_target_pairs={{0,124},{4,0},{8,4},{12,8},{16,12},{20,16},{24,20},{28,24},{32,28}... | collective-permute-start | bytes 1327112 | tf_op jit(solution)/shard_map/ppermute | solution.py:474
  17.4 15.5 %collective-permute-start.2 = (bf16[18,1536]{1,0:T(8,128)(2,1)S(1)}, bf16[18,1536]{1,0:T(8,128)(2,1)S(1)}, u32[]{:S(2)}, u32[]{:S(2)}) collective-permute-start(bf16[18,1536]{1,0:T(8,128)(2,1)S(1)} %reshape.67), channel_id=1, source_target_pairs={{0,127},{1,124},{2,125},{3,126},{4,3},{5,0},{6,1},{7,2},{8,7},{9,4... | collective-permute-start | bytes 165896 | tf_op jit(solution)/shard_map/ppermute | solution.py:474
  19.5 36.7 %collective-permute-start.5 = (bf16[18,1536]{1,0:T(8,128)(2,1)}, bf16[18,1536]{1,0:T(8,128)(2,1)S(1)}, u32[]{:S(2)}, u32[]{:S(2)}) collective-permute-start(bf16[18,1536]{1,0:T(8,128)(2,1)} %reshape.64), channel_id=1, source_target_pairs={{0,3},{1,0},{2,1},{3,2},{4,7},{5,4},{6,5},{7,6},{8,11},{9,8},{10,9... | collective-permute-start | bytes 165896 | tf_op jit(solution)/shard_map/ppermute | solution.py:474
  19.9 36.3 %collective-permute-start.6 = (bf16[18,1536]{1,0:T(8,128)(2,1)}, bf16[18,1536]{1,0:T(8,128)(2,1)S(1)}, u32[]{:S(2)}, u32[]{:S(2)}) collective-permute-start(bf16[18,1536]{1,0:T(8,128)(2,1)} %reshape.65), channel_id=1, source_target_pairs={{0,127},{1,124},{2,125},{3,126},{4,3},{5,0},{6,1},{7,2},{8,7},{9,4... | collective-permute-start | bytes 165896 | tf_op jit(solution)/shard_map/ppermute | solution.py:474
  34.3 3.0 %copy-start = (bf16[1536,2304]{1,0:T(8,128)(2,1)S(1)}, bf16[1536,2304]{1,0:T(8,128)(2,1)}, u32[]{:S(2)}) copy-start(bf16[1536,2304]{1,0:T(8,128)(2,1)} %w.3) | copy-start | bytes 21233668
  38.4 1.2 copy-start.5
  43.2 13.0 %copy-start.1 = (bf16[24,12,1536]{2,0,1:T(8,128)(2,1)S(1)}, bf16[24,12,1536]{2,0,1:T(8,128)(2,1)}, u32[]{:S(2)}) copy-start(bf16[24,12,1536]{2,0,1:T(8,128)(2,1)} %param.13) | copy-start | bytes 2654212
  43.2 13.0 %copy-start.3 = (f32[12,72,72]{2,1,0:T(8,128)S(1)}, f32[12,72,72]{2,1,0:T(8,128)}, u32[]{:S(2)}) copy-start(f32[12,72,72]{2,1,0:T(8,128)} %param.19) | copy-start | bytes 746500
  43.2 13.0 %copy-start.6 = (bf16[1536,768]{1,0:T(8,128)(2,1)S(1)}, bf16[1536,768]{1,0:T(8,128)(2,1)}, u32[]{:S(2)}) copy-start(bf16[1536,768]{1,0:T(8,128)(2,1)} %pw.1) | copy-start | bytes 7077892
  43.2 13.0 %copy-start.8 = (s32[288,1]{1,0:T(8,128)S(1)}, s32[288,1]{1,0:T(8,128)}, u32[]{:S(2)}) copy-start(s32[288,1]{1,0:T(8,128)} %reshape.78.col) | copy-start | bytes 3460
  53.5 11.1 %copy-start.10 = (bf16[288,768]{1,0:T(8,128)(2,1)}, bf16[288,768]{1,0:T(8,128)(2,1)S(1)}, u32[]{:S(2)}) copy-start(bf16[288,768]{1,0:T(8,128)(2,1)S(1)} %get-tuple-element.88.attended) | copy-start | bytes 1327108
  53.5 23.3 %collective-permute-start.3 = (bf16[288,1536]{1,0:T(8,128)(2,1)}, bf16[288,1536]{1,0:T(8,128)(2,1)}, u32[]{:S(2)}, u32[]{:S(2)}) collective-permute-start(bf16[288,1536]{1,0:T(8,128)(2,1)} %get-tuple-element.86.x0), channel_id=1, source_target_pairs={{0,1},{1,0},{2,3},{3,2},{4,5},{5,4},{6,7},{7,6},{8,9},{9,8},{10,11... | collective-permute-start | bytes 2654216 | tf_op jit(solution)/shard_map/ppermute | solution.py:474
  66.2 10.7 %collective-permute-start.8 = (bf16[288,1536]{1,0:T(8,128)(2,1)}, bf16[288,1536]{1,0:T(8,128)(2,1)}, u32[]{:S(2)}, u32[]{:S(2)}) collective-permute-start(bf16[288,1536]{1,0:T(8,128)(2,1)} %get-tuple-element.96.m0), channel_id=1, source_target_pairs={{0,1},{1,0},{2,3},{3,2},{4,5},{5,4},{6,7},{7,6},{8,9},{9,8},{10,11... | collective-permute-start | bytes 2654216 | tf_op jit(solution)/shard_map/ppermute | solution.py:474
  66.2 10.6 %collective-permute-start.7 = (bf16[288,1152]{1,0:T(8,128)(2,1)}, bf16[288,1152]{1,0:T(8,128)(2,1)}, u32[]{:S(2)}, u32[]{:S(2)}) collective-permute-start(bf16[288,1152]{1,0:T(8,128)(2,1)} %get-tuple-element.95.theirs), channel_id=1, source_target_pairs={{0,1},{1,0},{2,3},{3,2},{4,5},{5,4},{6,7},{7,6},{8,9},{9,8},{10,11... | collective-permute-start | bytes 1990664 | tf_op jit(solution)/shard_map/ppermute | solution.py:474
  66.7 10.1 %collective-permute-start.10 = (f32[144,512]{1,0:T(8,128)}, f32[144,512]{1,0:T(8,128)S(1)}, u32[]{:S(2)}, u32[]{:S(2)}) collective-permute-start(f32[144,512]{1,0:T(8,128)} %copy-done.19), channel_id=1, source_target_pairs={{0,1},{1,0},{2,3},{3,2},{4,5},{5,4},{6,7},{7,6},{8,9},{9,8},{10,11... | collective-permute-start | bytes 884744 | tf_op jit(solution)/shard_map/ppermute | solution.py:474
  67.8 9.0 %collective-permute-start.9 = (bf16[288,384]{1,0:T(8,128)(2,1)S(1)}, bf16[288,384]{1,0:T(8,128)(2,1)S(1)}, u32[]{:S(2)}, u32[]{:S(2)}) collective-permute-start(bf16[288,384]{1,0:T(8,128)(2,1)S(1)} %get-tuple-element.166), channel_id=1, source_target_pairs={{0,1},{1,0},{2,3},{3,2},{4,5},{5,4},{6,7},{7,6},{8,9},{9,8},{10,11... | collective-permute-start | bytes 663560 | tf_op jit(solution)/shard_map/ppermute | solution.py:474
  71.2 1.2 copy-start.12
  72.4 20.8 %slice-start = ((s8[7077888]{0:T(1024)(128)(4,1)}), s8[4194304]{0:T(1024)(128)(4,1)S(1)}, s32[]{:S(2)}) async-start(s8[7077888]{0:T(1024)(128)(4,1)} %bitcast.21), calls=%async_computation | async-start | bytes 8388608
  76.9 16.3 %slice-start.1 = ((s8[7077888]{0:T(1024)(128)(4,1)}), s8[2883584]{0:T(1024)(128)(4,1)S(1)}, s32[]{:S(2)}) async-start(s8[7077888]{0:T(1024)(128)(4,1)} %bitcast.21), calls=%async_computation.1 | async-start | bytes 5767168
  84.2 14.0 %collective-permute-start.12 = (bf16[34,24,512]{2,1,0:T(8,128)(2,1)S(1)}, bf16[34,24,512]{2,1,0:T(8,128)(2,1)S(1)}, u32[]{:S(2)}, u32[]{:S(2)}) collective-permute-start(bf16[34,24,512]{2,1,0:T(8,128)(2,1)S(1)} %get-tuple-element.112), channel_id=1, source_target_pairs={{0,16},{1,49},{16,0},{17,33},{32,48},{33,17},{48,32},{49,1},{2,18}... | collective-permute-start | bytes 2506760 | tf_op jit(solution)/shard_map/ppermute | solution.py:474
  84.5 13.7 %collective-permute-start.13 = (bf16[34,24,512]{2,1,0:T(8,128)(2,1)S(1)}, bf16[34,24,512]{2,1,0:T(8,128)(2,1)S(1)}, u32[]{:S(2)}, u32[]{:S(2)}) collective-permute-start(bf16[34,24,512]{2,1,0:T(8,128)(2,1)S(1)} %get-tuple-element.114), channel_id=1, source_target_pairs={{0,2},{1,67},{2,0},{3,65},{64,66},{65,3},{66,64},{67,1},{4,6},{5,7... | collective-permute-start | bytes 2506760 | tf_op jit(solution)/shard_map/ppermute | solution.py:474
  84.9 17.2 %collective-permute-start.14 = (bf16[34,24,512]{2,1,0:T(8,128)(2,1)S(1)}, bf16[34,24,512]{2,1,0:T(8,128)(2,1)S(1)}, u32[]{:S(2)}, u32[]{:S(2)}) collective-permute-start(bf16[34,24,512]{2,1,0:T(8,128)(2,1)S(1)} %get-tuple-element.116), channel_id=1, source_target_pairs={{0,4},{1,13},{4,0},{5,9},{8,12},{9,5},{12,8},{13,1},{2,6},{3,15},{... | collective-permute-start | bytes 2506760 | tf_op jit(solution)/shard_map/ppermute | solution.py:474
  103.3 7.5 %collective-permute-start.15 = (bf16[18,24,512]{2,1,0:T(8,128)(2,1)S(1)}, bf16[18,24,512]{2,1,0:T(8,128)(2,1)S(1)}, u32[]{:S(2)}, u32[]{:S(2)}) collective-permute-start(bf16[18,24,512]{2,1,0:T(8,128)(2,1)S(1)} %get-tuple-element.118), channel_id=1, source_target_pairs={{0,48},{1,17},{16,32},{17,1},{32,16},{33,49},{48,0},{49,33},{2,50}... | collective-permute-start | bytes 1327112 | tf_op jit(solution)/shard_map/ppermute | solution.py:474
  103.4 7.5 %collective-permute-start.16 = (bf16[18,24,512]{2,1,0:T(8,128)(2,1)S(1)}, bf16[18,24,512]{2,1,0:T(8,128)(2,1)S(1)}, u32[]{:S(2)}, u32[]{:S(2)}) collective-permute-start(bf16[18,24,512]{2,1,0:T(8,128)(2,1)S(1)} %get-tuple-element.120), channel_id=1, source_target_pairs={{0,66},{1,3},{2,64},{3,1},{64,2},{65,67},{66,0},{67,65},{4,70},{5,... | collective-permute-start | bytes 1327112 | tf_op jit(solution)/shard_map/ppermute | solution.py:474
  103.5 7.5 %collective-permute-start.17 = (bf16[18,24,512]{2,1,0:T(8,128)(2,1)S(1)}, bf16[18,24,512]{2,1,0:T(8,128)(2,1)S(1)}, u32[]{:S(2)}, u32[]{:S(2)}) collective-permute-start(bf16[18,24,512]{2,1,0:T(8,128)(2,1)S(1)} %get-tuple-element.122), channel_id=1, source_target_pairs={{0,12},{1,5},{4,8},{5,1},{8,4},{9,13},{12,0},{13,9},{2,14},{3,7},{... | collective-permute-start | bytes 1327112 | tf_op jit(solution)/shard_map/ppermute | solution.py:474
  103.6 6.7 %collective-permute-start.11 = (bf16[36,1536]{1,0:T(8,128)(2,1)S(1)}, bf16[36,1536]{1,0:T(8,128)(2,1)S(1)}, u32[]{:S(2)}, u32[]{:S(2)}) collective-permute-start(bf16[36,1536]{1,0:T(8,128)(2,1)S(1)} %get-tuple-element.107), channel_id=1, source_target_pairs={{0,1},{1,2},{2,3},{3,0},{4,5},{5,6},{6,7},{7,4},{8,9},{9,10},{10,1... | collective-permute-start | bytes 331784 | tf_op jit(solution)/shard_map/ppermute | solution.py:474
  111.9 6.3 %collective-permute-start.18 = (bf16[10,24,512]{2,1,0:T(8,128)(2,1)S(1)}, bf16[10,24,512]{2,1,0:T(8,128)(2,1)S(1)}, u32[]{:S(2)}, u32[]{:S(2)}) collective-permute-start(bf16[10,24,512]{2,1,0:T(8,128)(2,1)S(1)} %get-tuple-element.124), channel_id=1, source_target_pairs={{0,2},{1,67},{2,0},{3,65},{64,66},{65,3},{66,64},{67,1},{4,6},{5,7... | collective-permute-start | bytes 737288 | tf_op jit(solution)/shard_map/ppermute | solution.py:474
  112.7 6.3 %collective-permute-start.19 = (bf16[10,24,512]{2,1,0:T(8,128)(2,1)S(1)}, bf16[10,24,512]{2,1,0:T(8,128)(2,1)S(1)}, u32[]{:S(2)}, u32[]{:S(2)}) collective-permute-start(bf16[10,24,512]{2,1,0:T(8,128)(2,1)S(1)} %get-tuple-element.126), channel_id=1, source_target_pairs={{0,4},{1,13},{4,0},{5,9},{8,12},{9,5},{12,8},{13,1},{2,6},{3,15},{... | collective-permute-start | bytes 737288 | tf_op jit(solution)/shard_map/ppermute | solution.py:474
  115.4 6.3 %collective-permute-start.20 = (bf16[10,24,512]{2,1,0:T(8,128)(2,1)S(1)}, bf16[10,24,512]{2,1,0:T(8,128)(2,1)S(1)}, u32[]{:S(2)}, u32[]{:S(2)}) collective-permute-start(bf16[10,24,512]{2,1,0:T(8,128)(2,1)S(1)} %get-tuple-element.128), channel_id=1, source_target_pairs={{0,16},{1,49},{16,0},{17,33},{32,48},{33,17},{48,32},{49,1},{2,18}... | collective-permute-start | bytes 737288 | tf_op jit(solution)/shard_map/ppermute | solution.py:474
  115.5 26.9 %collective-permute-start.30 = (bf16[6,24,1536]{2,1,0:T(8,128)(2,1)S(1)}, bf16[6,24,1536]{2,1,0:T(8,128)(2,1)S(1)}, u32[]{:S(2)}, u32[]{:S(2)}) collective-permute-start(bf16[6,24,1536]{2,1,0:T(8,128)(2,1)S(1)} %get-tuple-element.147), channel_id=1, source_target_pairs={{0,4},{4,8},{8,12},{12,16},{16,20},{20,24},{24,28},{28,32},{32,36}... | collective-permute-start | bytes 1327112 | tf_op jit(solution)/shard_map/ppermute | solution.py:474
  122.4 4.4 %collective-permute-start.21 = (bf16[6,24,512]{2,1,0:T(8,128)(2,1)S(1)}, bf16[6,24,512]{2,1,0:T(8,128)(2,1)S(1)}, u32[]{:S(2)}, u32[]{:S(2)}) collective-permute-start(bf16[6,24,512]{2,1,0:T(8,128)(2,1)S(1)} %get-tuple-element.130), channel_id=1, source_target_pairs={{0,66},{1,3},{2,64},{3,1},{64,2},{65,67},{66,0},{67,65},{4,70},{5,... | collective-permute-start | bytes 442376 | tf_op jit(solution)/shard_map/ppermute | solution.py:474
  123.2 4.7 %collective-permute-start.22 = (bf16[6,24,512]{2,1,0:T(8,128)(2,1)S(1)}, bf16[6,24,512]{2,1,0:T(8,128)(2,1)S(1)}, u32[]{:S(2)}, u32[]{:S(2)}) collective-permute-start(bf16[6,24,512]{2,1,0:T(8,128)(2,1)S(1)} %get-tuple-element.132), channel_id=1, source_target_pairs={{0,12},{1,5},{4,8},{5,1},{8,4},{9,13},{12,0},{13,9},{2,14},{3,7},{... | collective-permute-start | bytes 442376 | tf_op jit(solution)/shard_map/ppermute | solution.py:474
  123.2 4.7 %collective-permute-start.23 = (bf16[6,24,512]{2,1,0:T(8,128)(2,1)S(1)}, bf16[6,24,512]{2,1,0:T(8,128)(2,1)S(1)}, u32[]{:S(2)}, u32[]{:S(2)}) collective-permute-start(bf16[6,24,512]{2,1,0:T(8,128)(2,1)S(1)} %get-tuple-element.134), channel_id=1, source_target_pairs={{0,48},{1,17},{16,32},{17,1},{32,16},{33,49},{48,0},{49,33},{2,50}... | collective-permute-start | bytes 442376 | tf_op jit(solution)/shard_map/ppermute | solution.py:474
  128.5 9.5 %collective-permute-start.24 = (bf16[4,24,512]{2,1,0:T(8,128)(2,1)S(1)}, bf16[4,24,512]{2,1,0:T(8,128)(2,1)S(1)}, u32[]{:S(2)}, u32[]{:S(2)}) collective-permute-start(bf16[4,24,512]{2,1,0:T(8,128)(2,1)S(1)} %get-tuple-element.136), channel_id=1, source_target_pairs={{0,4},{1,13},{4,0},{5,9},{8,12},{9,5},{12,8},{13,1},{2,6},{3,15},{... | collective-permute-start | bytes 294920 | tf_op jit(solution)/shard_map/ppermute | solution.py:474
  135.2 4.7 %collective-permute-start.25 = (bf16[4,24,512]{2,1,0:T(8,128)(2,1)S(1)}, bf16[4,24,512]{2,1,0:T(8,128)(2,1)S(1)}, u32[]{:S(2)}, u32[]{:S(2)}) collective-permute-start(bf16[4,24,512]{2,1,0:T(8,128)(2,1)S(1)} %get-tuple-element.138), channel_id=1, source_target_pairs={{0,16},{1,49},{16,0},{17,33},{32,48},{33,17},{48,32},{49,1},{2,18}... | collective-permute-start | bytes 294920 | tf_op jit(solution)/shard_map/ppermute | solution.py:474
  136.2 5.0 %collective-permute-start.26 = (bf16[4,24,512]{2,1,0:T(8,128)(2,1)S(1)}, bf16[4,24,512]{2,1,0:T(8,128)(2,1)S(1)}, u32[]{:S(2)}, u32[]{:S(2)}) collective-permute-start(bf16[4,24,512]{2,1,0:T(8,128)(2,1)S(1)} %get-tuple-element.140), channel_id=1, source_target_pairs={{0,2},{1,67},{2,0},{3,65},{64,66},{65,3},{66,64},{67,1},{4,6},{5,7... | collective-permute-start | bytes 294920 | tf_op jit(solution)/shard_map/ppermute | solution.py:474
  141.8 3.3 %collective-permute-start.27 = (bf16[3,24,512]{2,1,0:T(8,128)(2,1)S(1)}, bf16[3,24,512]{2,1,0:T(8,128)(2,1)S(1)}, u32[]{:S(2)}, u32[]{:S(2)}) collective-permute-start(bf16[3,24,512]{2,1,0:T(8,128)(2,1)S(1)} %get-tuple-element.142), channel_id=1, source_target_pairs={{0,12},{1,5},{4,8},{5,1},{8,4},{9,13},{12,0},{13,9},{2,14},{3,7},{... | collective-permute-start | bytes 221192 | tf_op jit(solution)/shard_map/ppermute | solution.py:474
  141.9 3.3 %collective-permute-start.28 = (bf16[3,24,512]{2,1,0:T(8,128)(2,1)S(1)}, bf16[3,24,512]{2,1,0:T(8,128)(2,1)S(1)}, u32[]{:S(2)}, u32[]{:S(2)}) collective-permute-start(bf16[3,24,512]{2,1,0:T(8,128)(2,1)S(1)} %get-tuple-element.144), channel_id=1, source_target_pairs={{0,48},{1,17},{16,32},{17,1},{32,16},{33,49},{48,0},{49,33},{2,50}... | collective-permute-start | bytes 221192 | tf_op jit(solution)/shard_map/ppermute | solution.py:474
  142.0 3.3 %collective-permute-start.29 = (bf16[3,24,512]{2,1,0:T(8,128)(2,1)S(1)}, bf16[3,24,512]{2,1,0:T(8,128)(2,1)S(1)}, u32[]{:S(2)}, u32[]{:S(2)}) collective-permute-start(bf16[3,24,512]{2,1,0:T(8,128)(2,1)S(1)} %get-tuple-element.146), channel_id=1, source_target_pairs={{0,66},{1,3},{2,64},{3,1},{64,2},{65,67},{66,0},{67,65},{4,70},{5,... | collective-permute-start | bytes 221192 | tf_op jit(solution)/shard_map/ppermute | solution.py:474
  145.3 11.3 %collective-permute-start.31 = (bf16[9,24,512]{2,1,0:T(8,128)(2,1)S(1)}, bf16[9,24,512]{2,1,0:T(8,128)(2,1)S(1)}, u32[]{:S(2)}, u32[]{:S(2)}) collective-permute-start(bf16[9,24,512]{2,1,0:T(8,128)(2,1)S(1)} %total.1.own), channel_id=1, source_target_pairs={{0,1},{1,0},{2,3},{3,2},{4,5},{5,4},{6,7},{7,6},{8,9},{9,8},{10,11... | collective-permute-start | bytes 663560 | tf_op jit(solution)/shard_map/ppermute | solution.py:474
  (11 other events, 9.7 us)
where the time goes:
time: 161 us; the launch traced here: 160 us
  starting transfers between devices  53 us (33%)
  Pallas kernels  40.4 us (25%)
  waiting for transfers between devices  36.7 us (23%)
  local copies, waits for them, and re-layouts  25.7 us (16%)
  other arithmetic  3.12 us (2%)
    ppermute x32, starting transfers between devices, permuted(): return lax.ppermute(value, axes, pairs)  53 us
    ppermute x32, waiting for transfers between devices, permuted(): return lax.ppermute(value, axes, pairs)  36.7 us
    pallas_call x11, Pallas kernels, call(): pl.pallas_call(body, out_shape=list(outs), in_specs=specs, out_specs=[VME...  31 us
    unnamed x55, local copies, waits for them, and re-layouts  15.1 us
    pallas_call x2, Pallas kernels, grid_call(): pl.pallas_call(body, grid_spec=spec, out_shape=results, compiler_params=p...  9.42 us
  transfers between devices with their start and end apart: 32, of which 18 were waited for; matrix products, arithmetic and copies ran while one was open for 6% of the time, Pallas kernels for 19%

commit v1 on v0

--- a/solution.py
+++ b/solution.py
@@ -42,6 +42,7 @@
 NN = (((1,), (0,)), ((), ()))
 VMEM = pl.BlockSpec(memory_space=pltpu.VMEM)
 HBM = pl.BlockSpec(memory_space=pltpu.HBM)
+ANY = pl.BlockSpec(memory_space=pl.ANY)
 SMEM = pl.BlockSpec(memory_space=pltpu.SMEM)
 
 
@@ -54,10 +55,12 @@
     return pl.CostEstimate(flops=flops, bytes_accessed=moved, transcendentals=0)
 
 
-def call(body, outs, operands, scalars=1, scratch=(), flops=0, vmem=16, far=(), name=None):
+def call(body, outs, operands, scalars=1, scratch=(), flops=0, vmem=50, far=(), near=(), name=None):
     specs = [SMEM] * scalars + [VMEM] * (len(operands) - scalars)
     for i in far:
         specs[i] = HBM
+    for i in near:
+        specs[i] = ANY
     return pl.pallas_call(
         body,
         out_shape=list(outs),
@@ -70,7 +73,7 @@
     )(*operands)
 
 
-def grid_call(body, grid, scalars, ins, outs, scratch=(), flops=0, vmem=16, name=None):
+def grid_call(body, grid, scalars, ins, outs, scratch=(), flops=0, vmem=50, name=None):
     operands = [array for array, _, _ in ins]
     results = [result for result, _, _ in outs]
     spec = pltpu.PrefetchScalarGridSpec(
@@ -144,13 +147,23 @@
 SPANS = [slice(n * WIN, (n + 1) * WIN) for n in range(WINDOWS)]
 
 
-def window_rows(own, lon, lat, both, grid, rows):
+HALF_ROWS = 12
+
+
+def f32_rows(ref, start, count):
+    return ref[...].astype(F32)[start : start + count]
+
+
+def window_rows(own, east, west, low, grid, rows):
     for j in range(12):
-        column, low = (own[j + SHIFT_W], lat) if j < SHIFT_W else (lon[j - SHIFT_W], both)
-        at = j % SHIFT_W * SHIFT_H
-        column = jnp.concatenate(
-            [column.astype(F32)[SHIFT_H:], low[...].astype(F32)[at : at + SHIFT_H]], 0
-        )
+        i = j % SHIFT_W
+        if j < SHIFT_W:
+            upper = own[SHIFT_W + i].astype(F32)[SHIFT_H : SHIFT_H + HALF_ROWS]
+            lower = [f32_rows(west, i * HALF_ROWS, HALF_ROWS)]
+        else:
+            upper = f32_rows(east, i * HALF_ROWS, HALF_ROWS)
+            lower = [own[i].astype(F32)[SHIFT_H + HALF_ROWS :], f32_rows(low, i * SHIFT_H, SHIFT_H)]
+        column = jnp.concatenate([upper] + lower, 0)
         for t in range(12):
             grid[t, j * 24 : (j + 1) * 24, :] = column[:, t * 128 : (t + 1) * 128]
     for r in range(24):
@@ -158,8 +171,22 @@
             rows[r * 12 : (r + 1) * 12, t * 128 : (t + 1) * 128] = grid[t, pl.ds(r, 12, stride=24), :]
 
 
+def to_east_body(own, low, out):
+    out[...] = jnp.concatenate(
+        [
+            piece
+            for i in range(SHIFT_W)
+            for piece in (
+                own[i].astype(F32)[SHIFT_H + HALF_ROWS :],
+                f32_rows(low, (SHIFT_W + i) * SHIFT_H, SHIFT_H),
+            )
+        ],
+        0,
+    ).astype(BF16)
+
+
 def forward_body(
-    scale, own, lon, lat, both, w, bias, pair_bias, row, col, x, projected, attended, grid, rows, wide, sems
+    scale, own, east, west, low, w, bias, pair_bias, row, col, x, projected, attended, grid, rows, wide, sems
 ):
     copies = []
     for g in range(3):
@@ -167,7 +194,7 @@
             at = pl.ds(j * HC + g * 256, 256)
             copies.append(pltpu.make_async_copy(w.at[:, at], wide.at[:, at], sems.at[3 * g + j]))
             copies[-1].start()
-    window_rows(own, lon, lat, both, grid, rows)
+    window_rows(own, east, west, low, grid, rows)
     x[...] = rows[...].astype(BF16)
     pens = penalties(row[...], col[...])
     for g in range(3):
@@ -285,9 +312,9 @@
     scale,
     attended,
     own,
-    lon,
-    lat,
-    both,
+    east,
+    west,
+    low,
     pw,
     gain,
     projected,
@@ -302,15 +329,25 @@
     grid,
     rows,
     mixed_all,
+    weight,
+    heads,
+    sems,
 ):
-    window_rows(own, lon, lat, both, grid, rows)
-    norm_part(attended, rows, pw, gain, mixed_low, attended_grad, gain_part, mixed_all)
+    copies = [pltpu.make_async_copy(pw, weight, sems.at[0])]
+    for j in range(3):
+        at = pl.ds(pl.multiple_of(j * HC + side[0] * HALF, 128), HALF)
+        copies.append(pltpu.make_async_copy(projected.at[:, at], heads.at[j], sems.at[1 + j]))
+    for copy in copies:
+        copy.start()
+    window_rows(own, east, west, low, grid, rows)
+    copies[0].wait()
+    norm_part(attended, rows, weight, gain, mixed_low, attended_grad, gain_part, mixed_all)
     pens = penalties(row[...], col[...])
     small[...] = jnp.zeros_like(small)
+    for copy in copies[1:]:
+        copy.wait()
     for hp in range(3):
-        def lanes(base):
-            return pl.ds(pl.multiple_of(base + side[0] * HALF + hp * 128, 128), 128)
-
+        cols = slice(hp * 128, (hp + 1) * 128)
         head = side[0] * 6 + 2 * hp
         gains = gain_part[:, pl.ds(pl.multiple_of(side[0] * HC + hp * 256, 128), 256)]
         store_pair(
@@ -320,10 +357,10 @@
             *attention_pair(
                 scale,
                 head,
-                projected[:, lanes(0)],
-                projected[:, lanes(HC)],
-                projected[:, lanes(2 * HC)],
-                attended_grad[:, lanes(0)],
+                heads[0, :, cols],
+                heads[1, :, cols],
+                heads[2, :, cols],
+                attended_grad[:, pl.ds(pl.multiple_of(side[0] * HALF + hp * 128, 128), 128)],
                 pair_bias[pl.ds(pl.multiple_of(head * WIN, 8), 2 * WIN), :],
                 pens,
                 gains,
@@ -351,23 +388,27 @@
 
 
 def weight_body(order, x0, x1, p0, p1, m0, m1, a0, a1, s0, s1, *rest):
-    outs, (left, grads, total) = rest[:6], rest[6:]
-    left[:CELLS, :] = x0[...]
-    left[CELLS:, :] = x1[...]
-    grads[:CELLS, :] = p0[...]
-    grads[CELLS:, :] = p1[...]
+    outs, (left, grads, mixed, heads, total, sems) = rest[:6], rest[6:]
+    pairs = ((x0, x1, left), (p0, p1, grads), (m0, m1, mixed), (a0, a1, heads))
+    copies = []
+    for i, (own, other, joined) in enumerate(pairs):
+        for k, source in enumerate((own, other)):
+            copies.append(
+                pltpu.make_async_copy(source, joined.at[k * CELLS : (k + 1) * CELLS], sems.at[2 * i + k])
+            )
+            copies[-1].start()
+    for copy in copies[:4]:
+        copy.wait()
     for m in range(4):
         at = slice(m * 384, (m + 1) * 384)
         part = dot(left[:, at], grads[...], TN)
         for j in range(3):
             total[at, j * 512 : j * 512 + HALF] = part[:, j * HALF : (j + 1) * HALF]
-    left[:CELLS, :] = m0[...]
-    left[CELLS:, :] = m1[...]
-    grads[:CELLS, :HALF] = a0[...]
-    grads[CELLS:, :HALF] = a1[...]
+    for copy in copies[4:]:
+        copy.wait()
     for m in range(4):
         at = slice(m * 384, (m + 1) * 384)
-        part = dot(left[:, at], grads[:, :HALF], TN)
+        part = dot(mixed[:, at], heads[...], TN)
         for j in range(3):
             total[at, j * 512 + HALF : (j + 1) * 512] = part[:, j * 128 : (j + 1) * 128]
     for j in range(3):
@@ -424,14 +465,14 @@
                 pair[start : start + 24, :] = top[:, g * 128 : g * 128 + WIN]
                 pair[start + 24 : start + 48, :] = bottom[:, g * 128 : g * 128 + WIN]
             lines = top[:, 384:] + bottom[:, 384:]
-            qb[:, at : at + 128] = lines[0:1]
-            vb[:, at : at + 128] = lines[1:2]
+            qb[at : at + 128] = lines[0]
+            vb[at : at + 128] = lines[1]
             scale[side * 3 + j : side * 3 + j + 1, :] = lines[2:3]
-            gain[:, side * HC + j * 256 : side * HC + j * 256 + 128] = lines[3:4]
-            gain[:, side * HC + j * 256 + 128 : side * HC + j * 256 + 256] = lines[4:5]
-
-
-def branch_body(side, w, own, theirs, branch, low, grads, rows):
+            gain[side * HC + j * 256 : side * HC + j * 256 + 128] = lines[3]
+            gain[side * HC + j * 256 + 128 : side * HC + j * 256 + 256] = lines[4]
+
+
+def branch_body(side, w, own, theirs, to_east, to_west, stay_low, stay_high, grads, rows):
     which = side[0]
 
     @pl.when(pl.program_id(0) == 0)
@@ -446,22 +487,43 @@
     product = dot(grads[...], w[...], NT)
     for i in range(2):
         rows[i] = product[:, i * 128 : (i + 1) * 128]
-    lows = []
+    columns = [
+        jnp.concatenate([rows[i, pl.ds(j, 24, stride=12), :] for i in range(2)], 1) for j in range(12)
+    ]
+    for out, cols, start in (
+        (stay_low, columns[:SHIFT_W], 0),
+        (to_east, columns[SHIFT_W:], 0),
+        (to_west, columns[:SHIFT_W], HALF_ROWS),
+        (stay_high, columns[SHIFT_W:], HALF_ROWS),
+    ):
+        out[...] = jnp.concatenate([one[start : start + HALF_ROWS] for one in cols], 0).astype(BF16)
+
+
+def last_rows_body(stay_high, from_east, out):
+    start = HALF_ROWS - SHIFT_H
+    out[...] = jnp.concatenate(
+        [
+            f32_rows(half, i * HALF_ROWS + start, SHIFT_H)
+            for half in (stay_high, from_east)
+            for i in range(SHIFT_W)
+        ],
+        0,
+    ).astype(BF16)
+
+
+def merge_body(upstream, stay_low, stay_high, from_west, from_east, low, out):
     for j in range(12):
-        column = jnp.concatenate([rows[i, pl.ds(j, 24, stride=12), :] for i in range(2)], 1)
-        branch[j] = column.astype(BF16)
-        lows.append(column[24 - SHIFT_H :])
-    low[...] = jnp.concatenate(lows, 0).astype(BF16)
-
-
-def down_body(grid, low, go, stay):
-    for j in range(12):
-        came = low[...].astype(F32)[j * SHIFT_H : (j + 1) * SHIFT_H]
-        column = jnp.concatenate([came, grid[j].astype(F32)[: 24 - SHIFT_H]], 0).astype(BF16)
-        if j < SHIFT_W:
-            stay[j] = column
-        else:
-            go[j - SHIFT_W] = column
+        i = j % SHIFT_W
+        upper, lower = (from_west, stay_high) if j < SHIFT_W else (stay_low, from_east)
+        back = jnp.concatenate(
+            [
+                f32_rows(low, j * SHIFT_H, SHIFT_H),
+                f32_rows(upper, i * HALF_ROWS, HALF_ROWS),
+                f32_rows(lower, i * HALF_ROWS, HALF_ROWS - SHIFT_H),
+            ],
+            0,
+        )
+        out[j] = (upstream[j].astype(F32) + back).astype(BF16)
 
 
 def permuted(value, axes, target):
@@ -482,15 +544,6 @@
     return permuted(value, LAT, lambda *at: np.unravel_index((np.ravel_multi_index(at, (2, 2)) + steps) % 4, (2, 2)))
 
 
-def both_step(value, steps):
-    def target(yh, x, z, yl, c):
-        lon = (np.ravel_multi_index((yh, x, z), (2, 4, 4)) + steps) % 32
-        lat = (yl * 2 + c + steps) % 4
-        return (*np.unravel_index(lon, (2, 4, 4)), lat // 2, lat % 2)
-
-    return permuted(value, LON + LAT, target)
-
-
 def core_swap(value):
     return permuted(value, ("c",), lambda c: (1 - c,))
 
@@ -510,16 +563,18 @@
     return permuted(value, AXES[axis] + ("c",), target)
 
 
-def messages(grid):
-    return [
-        grid[:SHIFT_W],
-        grid[SHIFT_W:, :SHIFT_H].reshape(-1, C),
-        grid[:SHIFT_W, :SHIFT_H].reshape(-1, C),
-    ]
-
-
-def moved(lon, lat, both):
-    return [lon_step(lon, -1), lat_step(lat, -1), both_step(both, -1)]
+def first_messages(grid):
+    upper = grid[:SHIFT_W, SHIFT_H : SHIFT_H + HALF_ROWS]
+    return grid[:, :SHIFT_H].reshape(-1, C), upper.reshape(-1, C)
+
+
+def halo(grid, low, upper):
+    low = lat_step(low, -1)
+    east = lon_step(upper, -1)
+    (lower,) = call(
+        to_east_body, [shape((72, C), BF16)], [grid[SHIFT_W:], low], scalars=0, name="to_east"
+    )
+    return east, lon_step(lower, 1), low
 
 
 def shards(
@@ -541,15 +596,18 @@
     scale = jnp.exp(logit_scale)
     bias = jnp.concatenate([query_bias, jnp.zeros_like(query_bias), value_bias]).reshape(1, -1)
     pair_rows = pair_bias.reshape(HEADS * WIN, WIN)
+    lower_ids = lon_step(region_ids[HALF_ROWS:], 1)
+    region_ids = jnp.concatenate([region_ids[:HALF_ROWS], lower_ids], 0)
     region_row = region_ids.reshape(WINDOWS, WIN)
     region_col = region_ids.reshape(-1, 1)
     gain = norm_gain.reshape(1, C)
 
     features = features.transpose(1, 0, 2)
     upstream = upstream.transpose(1, 0, 2)
-    came = moved(*messages(features))
-    going, came[1] = lax.optimization_barrier((messages(upstream), came[1]))
-    came_late = moved(*going)
+    came = halo(features, *first_messages(features))
+    late, low = lax.optimization_barrier((first_messages(upstream), came[2]))
+    came = (*came[:2], low)
+    came_late = halo(upstream, *late)
     x, projected, attended = call(
         forward_body,
         [shape((CELLS, C), BF16), shape((CELLS, 3 * HC), F32), shape((CELLS, HC), BF16)],
@@ -561,7 +619,6 @@
             pltpu.SemaphoreType.DMA((9,)),
         ],
         flops=2 * CELLS * C * 3 * HC,
-        vmem=24,
         far=(5,),
         name="forward",
     )
@@ -589,9 +646,17 @@
             region_col,
         ],
         scalars=2,
-        scratch=[pltpu.VMEM((12, CELLS, 128), F32)] + [pltpu.VMEM((CELLS, C), F32)] * 2,
+        scratch=[
+            pltpu.VMEM((12, CELLS, 128), F32),
+            pltpu.VMEM((CELLS, C), F32),
+            pltpu.VMEM((CELLS, C), F32),
+            pltpu.VMEM((C, HC), BF16),
+            pltpu.VMEM((3, CELLS, HALF), F32),
+            pltpu.SemaphoreType.DMA((4,)),
+        ],
+        far=(7,),
+        near=(9,),
         flops=4 * CELLS * C * HC + 2 * CELLS * WIN * 128 * 18,
-        vmem=24,
         name="backward",
     )
     mixed_other = core_swap(mixed_low)
@@ -653,15 +718,18 @@
         scratch=[
             pltpu.VMEM((2 * CELLS, C), BF16),
             pltpu.VMEM((2 * CELLS, 3 * HALF), BF16),
+            pltpu.VMEM((2 * CELLS, C), BF16),
+            pltpu.VMEM((2 * CELLS, HALF), BF16),
             pltpu.VMEM((C, C), F32),
-        ],
+            pltpu.SemaphoreType.DMA((8,)),
+        ],
+        near=tuple(range(1, 9)),
         flops=4 * CELLS * C * C,
-        vmem=28,
         name="weights",
     )
     side, parts = lax.optimization_barrier((mine, parts))
     whole = lambda i, side: (0, 0)
-    branch, low = grid_call(
+    to_east, to_west, stay_low, stay_high = grid_call(
         branch_body,
         (6,),
         [side],
@@ -670,23 +738,23 @@
             (grads_mine, (CELLS, 3 * HALF), whole),
             (grads_theirs, (CELLS, 3 * HALF), whole),
         ],
-        [
-            (shape((12, 24, C), BF16), (12, 24, 256), lambda i, side: (0, 0, i)),
-            (shape((36, C), BF16), (36, 256), lambda i, side: (0, i)),
-        ],
+        [(shape((72, C), BF16), (72, 256), lambda i, side: (0, i))] * 4,
         scratch=[pltpu.VMEM((CELLS, 3 * HC), BF16), pltpu.VMEM((2, CELLS, 128), F32)],
         flops=2 * CELLS * C * 3 * HC,
         name="branch",
     )
-    go, stay = call(
-        down_body,
-        [shape((SHIFT_W, 24, C), BF16)] * 2,
-        [branch, lat_step(low, 1)],
+    from_west = lon_step(to_east, 1)
+    from_east = lon_step(to_west, -1)
+    (last,) = call(
+        last_rows_body, [shape((36, C), BF16)], [stay_high, from_east], scalars=0, name="last_rows"
+    )
+    (input_grad,) = call(
+        merge_body,
+        [shape((12, 24, C), BF16)],
+        [upstream, stay_low, stay_high, from_west, from_east, lat_step(last, 1)],
         scalars=0,
-        name="down",
-    )
-    back = jnp.concatenate([lon_step(go, 1), stay], 0)
-    input_grad = (upstream.astype(F32) + back.astype(F32)).astype(BF16)
+        name="merge",
+    )
     for step in range(6):
         terms = []
         for j, names in enumerate(ORDERS):
@@ -701,9 +769,9 @@
             body = functools.partial(halve_body, 2, left // 4)
             order = tables(FIRST, step // 2 + 1)
         if step == 0:
-            order, low = lax.optimization_barrier((order, low))
+            order, stay_low = lax.optimization_barrier((order, stay_low))
         if step == 1:
-            order, stay = lax.optimization_barrier((order, stay))
+            order, last = lax.optimization_barrier((order, last))
         parts = call(body, [shape((left // 2 + EXTRA,) + BLOCK, BF16)] * 6, [order, *terms], name="halve")
     terms, input_grad = lax.optimization_barrier((terms, input_grad))
     (sums,) = call(total_body, [shape((9,) + BLOCK, BF16)], terms, scalars=0, name="total")
@@ -714,18 +782,15 @@
             shape((12, 3 * HC), F32),
             shape((12, HC), F32),
             shape((HEADS * WIN, WIN), F32),
-            shape((1, C), F32),
-            shape((1, HC), F32),
-            shape((1, HC), F32),
+            shape((C,), F32),
+            shape((HC,), F32),
+            shape((HC,), F32),
             shape((6, 128), F32),
         ],
         [mine, sums, sums_other],
         name="finish",
     )
     pair_grad = pair_grad.reshape(HEADS, WIN, WIN)
-    gain_grad = gain_grad.reshape(C)
-    query_bias_grad = query_bias_grad.reshape(HC)
-    value_bias_grad = value_bias_grad.reshape(HC)
     scale_grad = scale_grad[:, :2].reshape(HEADS)
 
     return (

time: 161 us -> 152 us (0.944)
  waiting for transfers between devices: 36.7 us -> 27.2 us
  Pallas kernels: 40.4 us -> 49.9 us
  local copies, waits for them, and re-layouts: 25.7 us -> 17.9 us
  other arithmetic: 3.12 us -> 0.24 us
  starting transfers between devices: 53 us -> 54.7 us
    unnamed x55 -> x30, local copies, waits for them, and re-layouts: 15.1 us -> 4.5 us
    ppermute x32 -> x34, waiting for transfers between devices: 36.7 us -> 27.2 us  [permuted(): return lax.ppermute(value, axes, pairs)]
    pallas_call x11 -> x14, Pallas kernels: 31 us -> 37.8 us  [call(): pl.pallas_call(body, out_shape=list(outs), in_specs=specs, out_specs=[VME...]
    reshape x4, local copies, waits for them, and re-layouts: 1.46 us -> 4.2 us  [first_messages(): return (grid[:, :SHIFT_H].reshape(-1, C), upper.reshape(-1, C))]
    pallas_call x2, Pallas kernels: 9.42 us -> 12.1 us  [grid_call(): pl.pallas_call(body, grid_spec=spec, out_shape=results, compiler_params=p...]
    pallas_call x3 -> x0, other arithmetic: 1.83 us -> none  [call(): pl.pallas_call(body, out_shape=list(outs), in_specs=specs, out_specs=[VME...]
    ppermute x32 -> x34, starting transfers between devices: 53 us -> 54.7 us  [permuted(): return lax.ppermute(value, axes, pairs)]
    slice x4 -> x7, local copies, waits for them, and re-layouts: 4.94 us -> 6.64 us  [the longest x2 2.9 us: first_messages(): upper = grid[:SHIFT_W, SHIFT_H:SHIFT_H + HALF_ROWS]]
  transfers between devices with their start and end apart: 32 -> 34, of which waited for: 18 -> 14; matrix products, arithmetic and copies ran while one was open for 6% -> 7% of each run, Pallas kernels for 19% -> 24%
where the time goes in v1:
time: 152 us; the launch traced here: 151 us
  starting transfers between devices  54.7 us (36%)
  Pallas kernels  49.9 us (33%)
  waiting for transfers between devices  27.2 us (18%)
  local copies, waits for them, and re-layouts  17.9 us (12%)
    ppermute x34, starting transfers between devices, permuted(): return lax.ppermute(value, axes, pairs)  54.7 us
    pallas_call x14, Pallas kernels, call(): pl.pallas_call(body, out_shape=list(outs), in_specs=specs, out_specs=[VME...  37.8 us
    ppermute x34, waiting for transfers between devices, permuted(): return lax.ppermute(value, axes, pairs)  27.2 us
    pallas_call x2, Pallas kernels, grid_call(): pl.pallas_call(body, grid_spec=spec, out_shape=results, compiler_params=p...  12.1 us
    unnamed x30, local copies, waits for them, and re-layouts  4.5 us
    reshape x4, local copies, waits for them, and re-layouts, first_messages(): return (grid[:, :SHIFT_H].reshape(-1, C), upper.reshape(-1, C))  4.2 us
  transfers between devices with their start and end apart: 34, of which 14 were waited for; matrix products, arithmetic and copies ran while one was open for 7% of the time, Pallas kernels for 24%

profile of v1, /device:TPU:1, one launch (start us, length us, event | category | flops | bytes accessed | tf_op | source)
XLA Modules:
  0.0 151.0 jit_solution(15073443385838802455)
XLA Ops:
  0.7 1.1 slice.38
  2.5 1.4 collective-permute-start.1
  4.0 0.8 fusion.6
  4.8 1.8 %collective-permute-start.3 = (s32[12,12]{0,1:T(8,128)S(1)}, s32[12,12]{0,1:T(8,128)S(1)}, u32[]{:S(2)}, u32[]{:S(2)}) collective-permute-start(s32[12,12]{0,1:T(8,128)S(1)} %get-tuple-element.163), channel_id=1, source_target_pairs={{0,4},{4,8},{8,12},{12,16},{16,20},{20,24},{24,28},{28,32},{32,36}... | collective-permute-start | bytes 1736 | tf_op jit(solution)/shard_map/ppermute | solution.py:536
  6.6 1.1 slice.36
  8.4 7.0 %collective-permute-start = (bf16[72,1536]{1,0:T(8,128)(2,1)}, bf16[72,1536]{1,0:T(8,128)(2,1)S(1)}, u32[]{:S(2)}, u32[]{:S(2)}) collective-permute-start(bf16[72,1536]{1,0:T(8,128)(2,1)} %reshape.55), channel_id=1, source_target_pairs={{0,124},{4,0},{8,4},{12,8},{16,12},{20,16},{24,20},{28,24},{32,28}... | collective-permute-start | bytes 663560 | tf_op jit(solution)/shard_map/ppermute | solution.py:536
  15.4 1.7 %slice.39 = bf16[12,3,1536]{2,1,0:T(4,128)(2,1)} slice(bf16[12,24,1536]{2,1,0:T(8,128)(2,1)} %bitcast.20), slice={[0:12], [0:3], [0:1536]} | slice | bytes 221184 | tf_op jit(solution)/shard_map/slice | solution.py:568
  17.1 1.8 %slice.40 = bf16[6,12,1536]{2,1,0:T(8,128)(2,1)} slice(bf16[12,24,1536]{2,1,0:T(8,128)(2,1)} %bitcast.21), slice={[0:6], [3:15], [0:1536]} | slice | bytes 442368 | tf_op jit(solution)/shard_map/slice | solution.py:567
  19.0 1.0 reshape.57
  20.0 1.7 %reshape.58 = bf16[72,1536]{1,0:T(8,128)(2,1)} reshape(bf16[6,12,1536]{2,1,0:T(8,128)(2,1)} %slice.40) | data formatting | bytes 442368 | tf_op jit(solution)/shard_map/reshape | solution.py:568
  21.8 1.0 collective-permute-start.6
  23.0 7.2 %collective-permute-start.5 = (bf16[72,1536]{1,0:T(8,128)(2,1)}, bf16[72,1536]{1,0:T(8,128)(2,1)S(1)}, u32[]{:S(2)}, u32[]{:S(2)}) collective-permute-start(bf16[72,1536]{1,0:T(8,128)(2,1)} %reshape.58), channel_id=1, source_target_pairs={{0,124},{4,0},{8,4},{12,8},{16,12},{20,16},{24,20},{28,24},{32,28}... | collective-permute-start | bytes 663560 | tf_op jit(solution)/shard_map/ppermute | solution.py:536
  30.8 4.9 %collective-permute-done.2.west = bf16[72,1536]{1,0:T(8,128)(2,1)S(1)} collective-permute-done((bf16[72,1536]{1,0:T(8,128)(2,1)S(1)}, bf16[72,1536]{1,0:T(8,128)(2,1)S(1)}, u32[]{:S(2)}, u32[]{:S(2)}) %collective-permute-start.2) | collective-permute-done | bytes 221216 | tf_op jit(solution)/shard_map/ppermute | solution.py:536
  36.4 0.9 copy-done.6
  37.3 11.0 %forward.1 = (bf16[288,1536]{1,0:T(8,128)(2,1)}, f32[288,2304]{1,0:T(8,128)}, bf16[288,768]{1,0:T(8,128)(2,1)S(1)}) custom-call(f32[12]{0:T(128)S(1)} %exp.3.scale, bf16[12,24,1536]{2,1,0:T(8,128)(2,1)S(1)} %bitcast.31, bf16[72,1536]{1,0:T(8,128)(2,1)S(1)} %collective-permute-done.east, bf16[72,1536]{1,0:T(8,128)(2,1)S(1)} %copy-done.6, ...), custom_call_target="tpu_custom_call" | custom-call | flops 2038431744 | bytes 12757296 | tf_op jit(solution)/shard_map/forward/pallas_call | solution.py:64
  48.3 1.0 collective-permute-start.4
  49.3 9.7 %backward.1 = (bf16[288,1536]{1,0:T(8,128)(2,1)}, f32[288,768]{1,0:T(8,128)}, f32[1,1536]{1,0:T(1,128)S(1)}, bf16[288,1152]{1,0:T(8,128)(2,1)S(1)}, f32[144,512]{1,0:T(8,128)S(1)}) custom-call(s32[1]{0:T(128)S(6)} %sub.3.side, f32[12]{0:T(128)S(1)} %exp.3.scale, bf16[288,768]{1,0:T(8,128)(2,1)S(1)} %get-tuple-element.87.attended, ...), custom_call_target="tpu_custom_call" | custom-call | flops 1454505984 | bytes 9884980 | tf_op jit(solution)/shard_map/backward/pallas_call | solution.py:64
  60.5 0.8 fusion.3
  61.4 1.2 copy-done.4
  62.5 5.4 %attention.1 = (bf16[288,1152]{1,0:T(8,128)(2,1)S(1)}, f32[144,512]{1,0:T(8,128)S(1)}) custom-call(s32[1]{0:T(128)} %bitcast.6.side.core, f32[12]{0:T(128)S(1)} %exp.3.scale, f32[288,2304]{1,0:T(8,128)} %get-tuple-element.86.projected.q_ref.k_ref.v_ref, f32[288,2304]{1,0:T(8,128)} %get-tuple-element.86.projected.q_ref.k_ref.v_ref, ...), custom_call_target="tpu_custom_call" | custom-call | flops 95551488 | bytes 10063104 | tf_op jit(solution)/shard_map/attention/pallas_call | solution.py:86
  68.0 8.5 %weights.1 = (bf16[34,24,512]{2,1,0:T(8,128)(2,1)S(1)}, bf16[34,24,512]{2,1,0:T(8,128)(2,1)S(1)}, bf16[34,24,512]{2,1,0:T(8,128)(2,1)}, bf16[34,24,512]{2,1,0:T(...) custom-call(s32[12]{0:T(128)S(1)} %get-tuple-element.173.order, ...), custom_call_target="tpu_custom_call" | custom-call | flops 2717908992 | bytes 10911792 | tf_op jit(solution)/shard_map/weights/pallas_call | solution.py:64
  76.6 1.2 collective-permute-start.14
  77.8 2.0 %collective-permute-start.15 = (bf16[34,24,512]{2,1,0:T(8,128)(2,1)}, bf16[34,24,512]{2,1,0:T(8,128)(2,1)S(1)}, u32[]{:S(2)}, u32[]{:S(2)}) collective-permute-start(bf16[34,24,512]{2,1,0:T(8,128)(2,1)} %get-tuple-element.114), channel_id=1, source_target_pairs={{0,4},{1,13},{4,0},{5,9},{8,12},{9,5},{12,8},{13,1},{2,6},{3,15},{... | collective-permute-start | bytes 2506760 | tf_op jit(solution)/shard_map/ppermute | solution.py:536
  79.8 0.8 fusion
  80.7 6.6 %branch.1 = (bf16[72,1536]{1,0:T(8,128)(2,1)S(1)}, bf16[72,1536]{1,0:T(8,128)(2,1)S(1)}, bf16[72,1536]{1,0:T(8,128)(2,1)S(1)}, bf16[72,1536]{1,0:T(8,128)(2,1)S(1)}) custom-call(s32[1]{0:T(128)} %bitcast.6.side.core, bf16[1536,2304]{1,0:T(8,128)(2,1)} %w.3, bf16[288,1152]{1,0:T(8,128)(2,1)S(1)} %get-tuple-element.92.p0.own, ...), custom_call_target="tpu_custom_call" | custom-call | flops 2038431744 | bytes 9289728 | tf_op jit(solution)/shard_map/branch/pallas_call | solution.py:86
  87.3 1.9 %collective-permute-done.13.refs_1_ = bf16[34,24,512]{2,1,0:T(8,128)(2,1)S(1)} collective-permute-done((bf16[34,24,512]{2,1,0:T(8,128)(2,1)S(1)}, bf16[34,24,512]{2,1,0:T(8,128)(2,1)S(1)}, u32[]{:S(2)}, u32[]{:S(2)}) %collective-permute-start.13) | collective-permute-done | bytes 835616 | tf_op jit(solution)/shard_map/ppermute | solution.py:536
  89.5 1.1 collective-permute-done.15.refs_5_
  90.6 0.9 copy-done.9
  91.5 2.8 %halve.5 = (bf16[18,24,512]{2,1,0:T(8,128)(2,1)S(1)}, bf16[18,24,512]{2,1,0:T(8,128)(2,1)S(1)}, bf16[18,24,512]{2,1,0:T(8,128)(2,1)S(1)}, bf16[18,24,512]{2,1,0:...) custom-call(s32[6]{0:T(128)S(1)} %get-tuple-element.108.order, ...), custom_call_target="tpu_custom_call" | custom-call | bytes 7667736 | tf_op jit(solution)/shard_map/halve/pallas_call | solution.py:64
  94.8 4.4 %collective-permute-start.12 = (bf16[72,1536]{1,0:T(8,128)(2,1)S(1)}, bf16[72,1536]{1,0:T(8,128)(2,1)S(1)}, u32[]{:S(2)}, u32[]{:S(2)}) collective-permute-start(bf16[72,1536]{1,0:T(8,128)(2,1)S(1)} %get-tuple-element.105), channel_id=1, source_target_pairs={{0,124},{4,0},{8,4},{12,8},{16,12},{20,16},{24,20},{28,24},{32,28}... | collective-permute-start | bytes 663560 | tf_op jit(solution)/shard_map/ppermute | solution.py:536
  99.2 7.5 %collective-permute-done.12.from_east = bf16[72,1536]{1,0:T(8,128)(2,1)S(1)} collective-permute-done((bf16[72,1536]{1,0:T(8,128)(2,1)S(1)}, bf16[72,1536]{1,0:T(8,128)(2,1)S(1)}, u32[]{:S(2)}, u32[]{:S(2)}) %collective-permute-start.12) | collective-permute-done | bytes 221216 | tf_op jit(solution)/shard_map/ppermute | solution.py:536
  107.6 1.4 halve.6
  109.0 1.6 %collective-permute-start.19 = (bf16[10,24,512]{2,1,0:T(8,128)(2,1)S(1)}, bf16[10,24,512]{2,1,0:T(8,128)(2,1)S(1)}, u32[]{:S(2)}, u32[]{:S(2)}) collective-permute-start(bf16[10,24,512]{2,1,0:T(8,128)(2,1)S(1)} %get-tuple-element.122), channel_id=1, source_target_pairs={{0,2},{1,67},{2,0},{3,65},{64,66},{65,3},{66,64},{67,1},{4,6},{5,7... | collective-permute-start | bytes 737288 | tf_op jit(solution)/shard_map/ppermute | solution.py:536
  110.5 2.1 %collective-permute-start.20 = (bf16[10,24,512]{2,1,0:T(8,128)(2,1)S(1)}, bf16[10,24,512]{2,1,0:T(8,128)(2,1)S(1)}, u32[]{:S(2)}, u32[]{:S(2)}) collective-permute-start(bf16[10,24,512]{2,1,0:T(8,128)(2,1)S(1)} %get-tuple-element.124), channel_id=1, source_target_pairs={{0,4},{1,13},{4,0},{5,9},{8,12},{9,5},{12,8},{13,1},{2,6},{3,15},{... | collective-permute-start | bytes 737288 | tf_op jit(solution)/shard_map/ppermute | solution.py:536
  113.2 2.1 %collective-permute-done.19.refs_1_ = bf16[10,24,512]{2,1,0:T(8,128)(2,1)S(1)} collective-permute-done((bf16[10,24,512]{2,1,0:T(8,128)(2,1)S(1)}, bf16[10,24,512]{2,1,0:T(8,128)(2,1)S(1)}, u32[]{:S(2)}, u32[]{:S(2)}) %collective-permute-start.19) | collective-permute-done | bytes 245792 | tf_op jit(solution)/shard_map/ppermute | solution.py:536
  115.3 1.5 collective-permute-done.20.refs_3_
  116.8 2.1 %collective-permute-done.21.refs_5_ = bf16[10,24,512]{2,1,0:T(8,128)(2,1)S(1)} collective-permute-done((bf16[10,24,512]{2,1,0:T(8,128)(2,1)S(1)}, bf16[10,24,512]{2,1,0:T(8,128)(2,1)S(1)}, u32[]{:S(2)}, u32[]{:S(2)}) %collective-permute-start.21) | collective-permute-done | bytes 245792 | tf_op jit(solution)/shard_map/ppermute | solution.py:536
  119.9 1.4 collective-permute-start.31
  121.3 2.7 %collective-permute-done.22.refs_1_ = bf16[6,24,512]{2,1,0:T(8,128)(2,1)S(1)} collective-permute-done((bf16[6,24,512]{2,1,0:T(8,128)(2,1)S(1)}, bf16[6,24,512]{2,1,0:T(8,128)(2,1)S(1)}, u32[]{:S(2)}, u32[]{:S(2)}) %collective-permute-start.22) | collective-permute-done | bytes 147488 | tf_op jit(solution)/shard_map/ppermute | solution.py:536
  125.6 2.9 %collective-permute-start.26 = (bf16[4,24,512]{2,1,0:T(8,128)(2,1)S(1)}, bf16[4,24,512]{2,1,0:T(8,128)(2,1)S(1)}, u32[]{:S(2)}, u32[]{:S(2)}) collective-permute-start(bf16[4,24,512]{2,1,0:T(8,128)(2,1)S(1)} %get-tuple-element.136), channel_id=1, source_target_pairs={{0,16},{1,49},{16,0},{17,33},{32,48},{33,17},{48,32},{49,1},{2,18}... | collective-permute-start | bytes 294920 | tf_op jit(solution)/shard_map/ppermute | solution.py:536
  128.5 0.8 collective-permute-start.27
  129.3 7.5 %collective-permute-start.32 = (bf16[36,1536]{1,0:T(8,128)(2,1)S(1)}, bf16[36,1536]{1,0:T(8,128)(2,1)S(1)}, u32[]{:S(2)}, u32[]{:S(2)}) collective-permute-start(bf16[36,1536]{1,0:T(8,128)(2,1)S(1)} %last_rows.1), channel_id=1, source_target_pairs={{0,1},{1,2},{2,3},{3,0},{4,5},{5,6},{6,7},{7,4},{8,9},{9,10},{10,1... | collective-permute-start | bytes 331784 | tf_op jit(solution)/shard_map/ppermute | solution.py:536
  137.4 1.7 %collective-permute-start.28 = (bf16[3,24,512]{2,1,0:T(8,128)(2,1)S(1)}, bf16[3,24,512]{2,1,0:T(8,128)(2,1)S(1)}, u32[]{:S(2)}, u32[]{:S(2)}) collective-permute-start(bf16[3,24,512]{2,1,0:T(8,128)(2,1)S(1)} %get-tuple-element.140), channel_id=1, source_target_pairs={{0,12},{1,5},{4,8},{5,1},{8,4},{9,13},{12,0},{13,9},{2,14},{3,7},{... | collective-permute-start | bytes 221192 | tf_op jit(solution)/shard_map/ppermute | solution.py:536
  139.1 1.3 merge.1
  140.8 1.5 collective-permute-done.29.refs_3_
  142.4 6.0 %collective-permute-start.33 = (bf16[9,24,512]{2,1,0:T(8,128)(2,1)S(1)}, bf16[9,24,512]{2,1,0:T(8,128)(2,1)S(1)}, u32[]{:S(2)}, u32[]{:S(2)}) collective-permute-start(bf16[9,24,512]{2,1,0:T(8,128)(2,1)S(1)} %total.1.own), channel_id=1, source_target_pairs={{0,1},{1,0},{2,3},{3,2},{4,5},{5,4},{6,7},{7,6},{8,9},{9,8},{10,11... | collective-permute-start | bytes 663560 | tf_op jit(solution)/shard_map/ppermute | solution.py:536
  148.4 1.1 collective-permute-done.33.other
  149.5 0.9 finish.1
  (92 shorter events, 11.2 us)
Async XLA Ops:
  0.6 18.3 %copy-start.3 = (bf16[24,12,1536]{2,0,1:T(8,128)(2,1)S(1)}, bf16[24,12,1536]{2,0,1:T(8,128)(2,1)}, u32[]{:S(2)}) copy-start(bf16[24,12,1536]{2,0,1:T(8,128)(2,1)} %param.12) | copy-start | bytes 2654212
  0.6 18.3 %copy-start = (bf16[24,12,1536]{2,0,1:T(8,128)(2,1)S(1)}, bf16[24,12,1536]{2,0,1:T(8,128)(2,1)}, u32[]{:S(2)}) copy-start(bf16[24,12,1536]{2,0,1:T(8,128)(2,1)} %param.13) | copy-start | bytes 2654212
  0.7 18.4 %copy-start.14 = (f32[12]{0:T(128)S(1)}, f32[12]{0:T(128)}, u32[]{:S(2)}) copy-start(f32[12]{0:T(128)} %param.18) | copy-start | bytes 148
  2.5 19.2 %collective-permute-start.1 = (bf16[36,1536]{1,0:T(8,128)(2,1)}, bf16[36,1536]{1,0:T(8,128)(2,1)S(1)}, u32[]{:S(2)}, u32[]{:S(2)}) collective-permute-start(bf16[36,1536]{1,0:T(8,128)(2,1)} %reshape.56), channel_id=1, source_target_pairs={{0,3},{1,0},{2,1},{3,2},{4,7},{5,4},{6,5},{7,6},{8,11},{9,8},{10,9... | collective-permute-start | bytes 331784 | tf_op jit(solution)/shard_map/ppermute | solution.py:536
  4.8 18.1 %copy-start.12 = (f32[768]{0:T(1024)S(1)}, f32[768]{0:T(1024)}, u32[]{:S(2)}) copy-start(f32[768]{0:T(1024)} %param.17) | copy-start | bytes 9220
  4.8 18.1 %copy-start.13 = (f32[768]{0:T(1024)S(1)}, f32[768]{0:T(1024)}, u32[]{:S(2)}) copy-start(f32[768]{0:T(1024)} %param.16) | copy-start | bytes 9220
  4.8 18.2 %copy-start.11 = (f32[1536]{0:T(1024)S(1)}, f32[1536]{0:T(1024)}, u32[]{:S(2)}) copy-start(f32[1536]{0:T(1024)} %param.21) | copy-start | bytes 18436
  4.8 25.6 %collective-permute-start.3 = (s32[12,12]{0,1:T(8,128)S(1)}, s32[12,12]{0,1:T(8,128)S(1)}, u32[]{:S(2)}, u32[]{:S(2)}) collective-permute-start(s32[12,12]{0,1:T(8,128)S(1)} %get-tuple-element.163), channel_id=1, source_target_pairs={{0,4},{4,8},{8,12},{12,16},{16,20},{20,24},{24,28},{28,32},{32,36}... | collective-permute-start | bytes 1736 | tf_op jit(solution)/shard_map/ppermute | solution.py:536
  8.4 22.4 %collective-permute-start = (bf16[72,1536]{1,0:T(8,128)(2,1)}, bf16[72,1536]{1,0:T(8,128)(2,1)S(1)}, u32[]{:S(2)}, u32[]{:S(2)}) collective-permute-start(bf16[72,1536]{1,0:T(8,128)(2,1)} %reshape.55), channel_id=1, source_target_pairs={{0,124},{4,0},{8,4},{12,8},{16,12},{20,16},{24,20},{28,24},{32,28}... | collective-permute-start | bytes 663560 | tf_op jit(solution)/shard_map/ppermute | solution.py:536
  15.4 21.0 %copy-start.2 = (f32[12,72,72]{2,1,0:T(8,128)S(1)}, f32[12,72,72]{2,1,0:T(8,128)}, u32[]{:S(2)}) copy-start(f32[12,72,72]{2,1,0:T(8,128)} %param.19) | copy-start | bytes 746500
  21.8 8.5 %collective-permute-start.6 = (bf16[36,1536]{1,0:T(8,128)(2,1)S(1)}, bf16[36,1536]{1,0:T(8,128)(2,1)S(1)}, u32[]{:S(2)}, u32[]{:S(2)}) collective-permute-start(bf16[36,1536]{1,0:T(8,128)(2,1)S(1)} %reshape.57), channel_id=1, source_target_pairs={{0,3},{1,0},{2,1},{3,2},{4,7},{5,4},{6,5},{7,6},{8,11},{9,8},{10,9... | collective-permute-start | bytes 331784 | tf_op jit(solution)/shard_map/ppermute | solution.py:536
  22.9 12.9 %collective-permute-start.2 = (bf16[72,1536]{1,0:T(8,128)(2,1)S(1)}, bf16[72,1536]{1,0:T(8,128)(2,1)S(1)}, u32[]{:S(2)}, u32[]{:S(2)}) collective-permute-start(bf16[72,1536]{1,0:T(8,128)(2,1)S(1)} %to_east.2), channel_id=1, source_target_pairs={{0,4},{4,8},{8,12},{12,16},{16,20},{20,24},{24,28},{28,32},{32,36}... | collective-permute-start | bytes 663560 | tf_op jit(solution)/shard_map/ppermute | solution.py:536
  23.0 26.3 %collective-permute-start.5 = (bf16[72,1536]{1,0:T(8,128)(2,1)}, bf16[72,1536]{1,0:T(8,128)(2,1)S(1)}, u32[]{:S(2)}, u32[]{:S(2)}) collective-permute-start(bf16[72,1536]{1,0:T(8,128)(2,1)} %reshape.58), channel_id=1, source_target_pairs={{0,124},{4,0},{8,4},{12,8},{16,12},{20,16},{24,20},{28,24},{32,28}... | collective-permute-start | bytes 663560 | tf_op jit(solution)/shard_map/ppermute | solution.py:536
  30.3 19.0 %collective-permute-start.7 = (bf16[72,1536]{1,0:T(8,128)(2,1)S(1)}, bf16[72,1536]{1,0:T(8,128)(2,1)S(1)}, u32[]{:S(2)}, u32[]{:S(2)}) collective-permute-start(bf16[72,1536]{1,0:T(8,128)(2,1)S(1)} %to_east.3), channel_id=1, source_target_pairs={{0,4},{4,8},{8,12},{12,16},{16,20},{20,24},{24,28},{28,32},{32,36}... | collective-permute-start | bytes 663560 | tf_op jit(solution)/shard_map/ppermute | solution.py:536
  36.4 0.9 copy-start.6
  48.3 19.7 %collective-permute-start.4 = (bf16[288,1536]{1,0:T(8,128)(2,1)}, bf16[288,1536]{1,0:T(8,128)(2,1)}, u32[]{:S(2)}, u32[]{:S(2)}) collective-permute-start(bf16[288,1536]{1,0:T(8,128)(2,1)} %get-tuple-element.85.x0), channel_id=1, source_target_pairs={{0,1},{1,0},{2,3},{3,2},{4,5},{5,4},{6,7},{7,6},{8,9},{9,8},{10,11... | collective-permute-start | bytes 2654216 | tf_op jit(solution)/shard_map/ppermute | solution.py:536
  59.0 9.0 %collective-permute-start.9 = (bf16[288,1536]{1,0:T(8,128)(2,1)}, bf16[288,1536]{1,0:T(8,128)(2,1)}, u32[]{:S(2)}, u32[]{:S(2)}) collective-permute-start(bf16[288,1536]{1,0:T(8,128)(2,1)} %get-tuple-element.94.m0), channel_id=1, source_target_pairs={{0,1},{1,0},{2,3},{3,2},{4,5},{5,4},{6,7},{7,6},{8,9},{9,8},{10,11... | collective-permute-start | bytes 2654216 | tf_op jit(solution)/shard_map/ppermute | solution.py:536
  59.1 8.9 %collective-permute-start.8 = (bf16[288,1152]{1,0:T(8,128)(2,1)S(1)}, bf16[288,1152]{1,0:T(8,128)(2,1)S(1)}, u32[]{:S(2)}, u32[]{:S(2)}) collective-permute-start(bf16[288,1152]{1,0:T(8,128)(2,1)S(1)} %get-tuple-element.93.theirs), channel_id=1, source_target_pairs={{0,1},{1,0},{2,3},{3,2},{4,5},{5,4},{6,7},{7,6},{8,9},{9,8},{10,11... | collective-permute-start | bytes 1990664 | tf_op jit(solution)/shard_map/ppermute | solution.py:536
  59.6 8.4 %collective-permute-start.11 = (f32[144,512]{1,0:T(8,128)S(1)}, f32[144,512]{1,0:T(8,128)S(1)}, u32[]{:S(2)}, u32[]{:S(2)}) collective-permute-start(f32[144,512]{1,0:T(8,128)S(1)} %get-tuple-element.96), channel_id=1, source_target_pairs={{0,1},{1,0},{2,3},{3,2},{4,5},{5,4},{6,7},{7,6},{8,9},{9,8},{10,11... | collective-permute-start | bytes 884744 | tf_op jit(solution)/shard_map/ppermute | solution.py:536
  59.7 8.2 %collective-permute-start.10 = (bf16[288,384]{1,0:T(8,128)(2,1)S(1)}, bf16[288,384]{1,0:T(8,128)(2,1)S(1)}, u32[]{:S(2)}, u32[]{:S(2)}) collective-permute-start(bf16[288,384]{1,0:T(8,128)(2,1)S(1)} %get-tuple-element.160), channel_id=1, source_target_pairs={{0,1},{1,0},{2,3},{3,2},{4,5},{5,4},{6,7},{7,6},{8,9},{9,8},{10,11... | collective-permute-start | bytes 663560 | tf_op jit(solution)/shard_map/ppermute | solution.py:536
  61.3 1.2 copy-start.4
  76.5 12.7 %collective-permute-start.13 = (bf16[34,24,512]{2,1,0:T(8,128)(2,1)S(1)}, bf16[34,24,512]{2,1,0:T(8,128)(2,1)S(1)}, u32[]{:S(2)}, u32[]{:S(2)}) collective-permute-start(bf16[34,24,512]{2,1,0:T(8,128)(2,1)S(1)} %get-tuple-element.110), channel_id=1, source_target_pairs={{0,16},{1,49},{16,0},{17,33},{32,48},{33,17},{48,32},{49,1},{2,18}... | collective-permute-start | bytes 2506760 | tf_op jit(solution)/shard_map/ppermute | solution.py:536
  76.6 12.9 %collective-permute-start.14 = (bf16[34,24,512]{2,1,0:T(8,128)(2,1)}, bf16[34,24,512]{2,1,0:T(8,128)(2,1)S(1)}, u32[]{:S(2)}, u32[]{:S(2)}) collective-permute-start(bf16[34,24,512]{2,1,0:T(8,128)(2,1)} %get-tuple-element.112), channel_id=1, source_target_pairs={{0,2},{1,67},{2,0},{3,65},{64,66},{65,3},{66,64},{67,1},{4,6},{5,7... | collective-permute-start | bytes 2506760 | tf_op jit(solution)/shard_map/ppermute | solution.py:536
  77.8 12.8 %collective-permute-start.15 = (bf16[34,24,512]{2,1,0:T(8,128)(2,1)}, bf16[34,24,512]{2,1,0:T(8,128)(2,1)S(1)}, u32[]{:S(2)}, u32[]{:S(2)}) collective-permute-start(bf16[34,24,512]{2,1,0:T(8,128)(2,1)} %get-tuple-element.114), channel_id=1, source_target_pairs={{0,4},{1,13},{4,0},{5,9},{8,12},{9,5},{12,8},{13,1},{2,6},{3,15},{... | collective-permute-start | bytes 2506760 | tf_op jit(solution)/shard_map/ppermute | solution.py:536
  89.2 1.4 copy-start.7
  89.5 1.1 copy-start.8
  90.6 0.9 copy-start.9
  94.2 12.5 %collective-permute-start.16 = (bf16[18,24,512]{2,1,0:T(8,128)(2,1)S(1)}, bf16[18,24,512]{2,1,0:T(8,128)(2,1)S(1)}, u32[]{:S(2)}, u32[]{:S(2)}) collective-permute-start(bf16[18,24,512]{2,1,0:T(8,128)(2,1)S(1)} %get-tuple-element.116), channel_id=1, source_target_pairs={{0,48},{1,17},{16,32},{17,1},{32,16},{33,49},{48,0},{49,33},{2,50}... | collective-permute-start | bytes 1327112 | tf_op jit(solution)/shard_map/ppermute | solution.py:536
  94.3 12.4 %collective-permute-start.17 = (bf16[18,24,512]{2,1,0:T(8,128)(2,1)S(1)}, bf16[18,24,512]{2,1,0:T(8,128)(2,1)S(1)}, u32[]{:S(2)}, u32[]{:S(2)}) collective-permute-start(bf16[18,24,512]{2,1,0:T(8,128)(2,1)S(1)} %get-tuple-element.118), channel_id=1, source_target_pairs={{0,66},{1,3},{2,64},{3,1},{64,2},{65,67},{66,0},{67,65},{4,70},{5,... | collective-permute-start | bytes 1327112 | tf_op jit(solution)/shard_map/ppermute | solution.py:536
  94.8 12.0 %collective-permute-start.18 = (bf16[18,24,512]{2,1,0:T(8,128)(2,1)S(1)}, bf16[18,24,512]{2,1,0:T(8,128)(2,1)S(1)}, u32[]{:S(2)}, u32[]{:S(2)}) collective-permute-start(bf16[18,24,512]{2,1,0:T(8,128)(2,1)S(1)} %get-tuple-element.120), channel_id=1, source_target_pairs={{0,12},{1,5},{4,8},{5,1},{8,4},{9,13},{12,0},{13,9},{2,14},{3,7},{... | collective-permute-start | bytes 1327112 | tf_op jit(solution)/shard_map/ppermute | solution.py:536
  94.8 11.9 %collective-permute-start.12 = (bf16[72,1536]{1,0:T(8,128)(2,1)S(1)}, bf16[72,1536]{1,0:T(8,128)(2,1)S(1)}, u32[]{:S(2)}, u32[]{:S(2)}) collective-permute-start(bf16[72,1536]{1,0:T(8,128)(2,1)S(1)} %get-tuple-element.105), channel_id=1, source_target_pairs={{0,124},{4,0},{8,4},{12,8},{16,12},{20,16},{24,20},{28,24},{32,28}... | collective-permute-start | bytes 663560 | tf_op jit(solution)/shard_map/ppermute | solution.py:536
  106.8 0.8 copy-start.10
  107.5 31.6 %copy-start.1 = (bf16[24,12,1536]{2,0,1:T(8,128)(2,1)S(1)}, bf16[24,12,1536]{2,0,1:T(8,128)(2,1)}, u32[]{:S(2)}) copy-start(bf16[24,12,1536]{2,0,1:T(8,128)(2,1)} %param.13) | copy-start | bytes 2654212
  109.0 6.3 %collective-permute-start.19 = (bf16[10,24,512]{2,1,0:T(8,128)(2,1)S(1)}, bf16[10,24,512]{2,1,0:T(8,128)(2,1)S(1)}, u32[]{:S(2)}, u32[]{:S(2)}) collective-permute-start(bf16[10,24,512]{2,1,0:T(8,128)(2,1)S(1)} %get-tuple-element.122), channel_id=1, source_target_pairs={{0,2},{1,67},{2,0},{3,65},{64,66},{65,3},{66,64},{67,1},{4,6},{5,7... | collective-permute-start | bytes 737288 | tf_op jit(solution)/shard_map/ppermute | solution.py:536
  110.5 6.3 %collective-permute-start.20 = (bf16[10,24,512]{2,1,0:T(8,128)(2,1)S(1)}, bf16[10,24,512]{2,1,0:T(8,128)(2,1)S(1)}, u32[]{:S(2)}, u32[]{:S(2)}) collective-permute-start(bf16[10,24,512]{2,1,0:T(8,128)(2,1)S(1)} %get-tuple-element.124), channel_id=1, source_target_pairs={{0,4},{1,13},{4,0},{5,9},{8,12},{9,5},{12,8},{13,1},{2,6},{3,15},{... | collective-permute-start | bytes 737288 | tf_op jit(solution)/shard_map/ppermute | solution.py:536
  112.7 6.3 %collective-permute-start.21 = (bf16[10,24,512]{2,1,0:T(8,128)(2,1)S(1)}, bf16[10,24,512]{2,1,0:T(8,128)(2,1)S(1)}, u32[]{:S(2)}, u32[]{:S(2)}) collective-permute-start(bf16[10,24,512]{2,1,0:T(8,128)(2,1)S(1)} %get-tuple-element.126), channel_id=1, source_target_pairs={{0,16},{1,49},{16,0},{17,33},{32,48},{33,17},{48,32},{49,1},{2,18}... | collective-permute-start | bytes 737288 | tf_op jit(solution)/shard_map/ppermute | solution.py:536
  119.7 4.4 %collective-permute-start.22 = (bf16[6,24,512]{2,1,0:T(8,128)(2,1)S(1)}, bf16[6,24,512]{2,1,0:T(8,128)(2,1)S(1)}, u32[]{:S(2)}, u32[]{:S(2)}) collective-permute-start(bf16[6,24,512]{2,1,0:T(8,128)(2,1)S(1)} %get-tuple-element.128), channel_id=1, source_target_pairs={{0,66},{1,3},{2,64},{3,1},{64,2},{65,67},{66,0},{67,65},{4,70},{5,... | collective-permute-start | bytes 442376 | tf_op jit(solution)/shard_map/ppermute | solution.py:536
  119.7 4.4 %collective-permute-start.23 = (bf16[6,24,512]{2,1,0:T(8,128)(2,1)S(1)}, bf16[6,24,512]{2,1,0:T(8,128)(2,1)S(1)}, u32[]{:S(2)}, u32[]{:S(2)}) collective-permute-start(bf16[6,24,512]{2,1,0:T(8,128)(2,1)S(1)} %get-tuple-element.130), channel_id=1, source_target_pairs={{0,12},{1,5},{4,8},{5,1},{8,4},{9,13},{12,0},{13,9},{2,14},{3,7},{... | collective-permute-start | bytes 442376 | tf_op jit(solution)/shard_map/ppermute | solution.py:536
  119.8 4.4 %collective-permute-start.24 = (bf16[6,24,512]{2,1,0:T(8,128)(2,1)S(1)}, bf16[6,24,512]{2,1,0:T(8,128)(2,1)S(1)}, u32[]{:S(2)}, u32[]{:S(2)}) collective-permute-start(bf16[6,24,512]{2,1,0:T(8,128)(2,1)S(1)} %get-tuple-element.132), channel_id=1, source_target_pairs={{0,48},{1,17},{16,32},{17,1},{32,16},{33,49},{48,0},{49,33},{2,50}... | collective-permute-start | bytes 442376 | tf_op jit(solution)/shard_map/ppermute | solution.py:536
  119.9 19.2 %collective-permute-start.31 = (bf16[72,1536]{1,0:T(8,128)(2,1)S(1)}, bf16[72,1536]{1,0:T(8,128)(2,1)S(1)}, u32[]{:S(2)}, u32[]{:S(2)}) collective-permute-start(bf16[72,1536]{1,0:T(8,128)(2,1)S(1)} %get-tuple-element.145), channel_id=1, source_target_pairs={{0,4},{4,8},{8,12},{12,16},{16,20},{20,24},{24,28},{28,32},{32,36}... | collective-permute-start | bytes 663560 | tf_op jit(solution)/shard_map/ppermute | solution.py:536
  124.9 11.9 %collective-permute-start.25 = (bf16[4,24,512]{2,1,0:T(8,128)(2,1)S(1)}, bf16[4,24,512]{2,1,0:T(8,128)(2,1)S(1)}, u32[]{:S(2)}, u32[]{:S(2)}) collective-permute-start(bf16[4,24,512]{2,1,0:T(8,128)(2,1)S(1)} %get-tuple-element.134), channel_id=1, source_target_pairs={{0,4},{1,13},{4,0},{5,9},{8,12},{9,5},{12,8},{13,1},{2,6},{3,15},{... | collective-permute-start | bytes 294920 | tf_op jit(solution)/shard_map/ppermute | solution.py:536
  125.6 11.1 %collective-permute-start.26 = (bf16[4,24,512]{2,1,0:T(8,128)(2,1)S(1)}, bf16[4,24,512]{2,1,0:T(8,128)(2,1)S(1)}, u32[]{:S(2)}, u32[]{:S(2)}) collective-permute-start(bf16[4,24,512]{2,1,0:T(8,128)(2,1)S(1)} %get-tuple-element.136), channel_id=1, source_target_pairs={{0,16},{1,49},{16,0},{17,33},{32,48},{33,17},{48,32},{49,1},{2,18}... | collective-permute-start | bytes 294920 | tf_op jit(solution)/shard_map/ppermute | solution.py:536
  128.5 8.2 %collective-permute-start.27 = (bf16[4,24,512]{2,1,0:T(8,128)(2,1)S(1)}, bf16[4,24,512]{2,1,0:T(8,128)(2,1)S(1)}, u32[]{:S(2)}, u32[]{:S(2)}) collective-permute-start(bf16[4,24,512]{2,1,0:T(8,128)(2,1)S(1)} %get-tuple-element.138), channel_id=1, source_target_pairs={{0,2},{1,67},{2,0},{3,65},{64,66},{65,3},{66,64},{67,1},{4,6},{5,7... | collective-permute-start | bytes 294920 | tf_op jit(solution)/shard_map/ppermute | solution.py:536
  129.3 9.8 %collective-permute-start.32 = (bf16[36,1536]{1,0:T(8,128)(2,1)S(1)}, bf16[36,1536]{1,0:T(8,128)(2,1)S(1)}, u32[]{:S(2)}, u32[]{:S(2)}) collective-permute-start(bf16[36,1536]{1,0:T(8,128)(2,1)S(1)} %last_rows.1), channel_id=1, source_target_pairs={{0,1},{1,2},{2,3},{3,0},{4,5},{5,6},{6,7},{7,4},{8,9},{9,10},{10,1... | collective-permute-start | bytes 331784 | tf_op jit(solution)/shard_map/ppermute | solution.py:536
  137.4 3.5 %collective-permute-start.28 = (bf16[3,24,512]{2,1,0:T(8,128)(2,1)S(1)}, bf16[3,24,512]{2,1,0:T(8,128)(2,1)S(1)}, u32[]{:S(2)}, u32[]{:S(2)}) collective-permute-start(bf16[3,24,512]{2,1,0:T(8,128)(2,1)S(1)} %get-tuple-element.140), channel_id=1, source_target_pairs={{0,12},{1,5},{4,8},{5,1},{8,4},{9,13},{12,0},{13,9},{2,14},{3,7},{... | collective-permute-start | bytes 221192 | tf_op jit(solution)/shard_map/ppermute | solution.py:536
  139.1 3.2 %collective-permute-start.29 = (bf16[3,24,512]{2,1,0:T(8,128)(2,1)S(1)}, bf16[3,24,512]{2,1,0:T(8,128)(2,1)S(1)}, u32[]{:S(2)}, u32[]{:S(2)}) collective-permute-start(bf16[3,24,512]{2,1,0:T(8,128)(2,1)S(1)} %get-tuple-element.142), channel_id=1, source_target_pairs={{0,48},{1,17},{16,32},{17,1},{32,16},{33,49},{48,0},{49,33},{2,50}... | collective-permute-start | bytes 221192 | tf_op jit(solution)/shard_map/ppermute | solution.py:536
  139.1 3.2 %collective-permute-start.30 = (bf16[3,24,512]{2,1,0:T(8,128)(2,1)S(1)}, bf16[3,24,512]{2,1,0:T(8,128)(2,1)S(1)}, u32[]{:S(2)}, u32[]{:S(2)}) collective-permute-start(bf16[3,24,512]{2,1,0:T(8,128)(2,1)S(1)} %get-tuple-element.144), channel_id=1, source_target_pairs={{0,66},{1,3},{2,64},{3,1},{64,2},{65,67},{66,0},{67,65},{4,70},{5,... | collective-permute-start | bytes 221192 | tf_op jit(solution)/shard_map/ppermute | solution.py:536
  142.4 7.1 %collective-permute-start.33 = (bf16[9,24,512]{2,1,0:T(8,128)(2,1)S(1)}, bf16[9,24,512]{2,1,0:T(8,128)(2,1)S(1)}, u32[]{:S(2)}, u32[]{:S(2)}) collective-permute-start(bf16[9,24,512]{2,1,0:T(8,128)(2,1)S(1)} %total.1.own), channel_id=1, source_target_pairs={{0,1},{1,0},{2,3},{3,2},{4,5},{5,4},{6,7},{7,6},{8,9},{9,8},{10,11... | collective-permute-start | bytes 663560 | tf_op jit(solution)/shard_map/ppermute | solution.py:536
  (1 other events, 0.7 us)

commit v2 on v1

--- a/solution.py
+++ b/solution.py
@@ -171,13 +171,20 @@
             rows[r * 12 : (r + 1) * 12, t * 128 : (t + 1) * 128] = grid[t, pl.ds(r, 12, stride=24), :]
 
 
+def first_body(own, low, upper):
+    low[...] = jnp.concatenate([own[j].astype(F32)[:SHIFT_H] for j in range(12)], 0).astype(BF16)
+    upper[...] = jnp.concatenate(
+        [own[j].astype(F32)[SHIFT_H : SHIFT_H + HALF_ROWS] for j in range(SHIFT_W)], 0
+    ).astype(BF16)
+
+
 def to_east_body(own, low, out):
     out[...] = jnp.concatenate(
         [
             piece
             for i in range(SHIFT_W)
             for piece in (
-                own[i].astype(F32)[SHIFT_H + HALF_ROWS :],
+                own[SHIFT_W + i].astype(F32)[SHIFT_H + HALF_ROWS :],
                 f32_rows(low, (SHIFT_W + i) * SHIFT_H, SHIFT_H),
             )
         ],
@@ -265,7 +272,7 @@
     scale_line = jnp.zeros((1, 128), F32)
     for i in range(2):
         one = jnp.sum(jnp.sum(scaled[i * WIN : (i + 1) * WIN], 0, keepdims=True), 1, keepdims=True)
-        scale_line = scale_line + jnp.where(lane == i, one * scale[head + i], 0.0)
+        scale_line = scale_line + jnp.where(lane == head + i, one * scale[head + i], 0.0)
     q_grad = q_inv * (gq - q * head_sum(q * gq))
     k_grad = k_inv * (gk - k * head_sum(k * gk))
     lines = jnp.concatenate(
@@ -448,6 +455,7 @@
 
 def finish_body(core, own, other, qkv, proj, pair, gain, qb, vb, scale):
     which = core[0]
+    scales = jnp.zeros((128,), F32)
     for side in range(2):
         for j in range(3):
             def block(i):
@@ -467,9 +475,10 @@
             lines = top[:, 384:] + bottom[:, 384:]
             qb[at : at + 128] = lines[0]
             vb[at : at + 128] = lines[1]
-            scale[side * 3 + j : side * 3 + j + 1, :] = lines[2:3]
+            scales = scales + lines[2]
             gain[side * HC + j * 256 : side * HC + j * 256 + 128] = lines[3]
             gain[side * HC + j * 256 + 128 : side * HC + j * 256 + 256] = lines[4]
+    scale[...] = scales[:HEADS]
 
 
 def branch_body(side, w, own, theirs, to_east, to_west, stay_low, stay_high, grads, rows):
@@ -564,17 +573,19 @@
 
 
 def first_messages(grid):
-    upper = grid[:SHIFT_W, SHIFT_H : SHIFT_H + HALF_ROWS]
-    return grid[:, :SHIFT_H].reshape(-1, C), upper.reshape(-1, C)
-
-
-def halo(grid, low, upper):
+    return call(
+        first_body, [shape((36, C), BF16), shape((72, C), BF16)], [grid], scalars=0, name="first"
+    )
+
+
+def halo(grid):
+    low, upper = first_messages(grid)
     low = lat_step(low, -1)
     east = lon_step(upper, -1)
     (lower,) = call(
-        to_east_body, [shape((72, C), BF16)], [grid[SHIFT_W:], low], scalars=0, name="to_east"
-    )
-    return east, lon_step(lower, 1), low
+        to_east_body, [shape((72, C), BF16)], [grid, low], scalars=0, name="to_east"
+    )
+    return east, low, lower
 
 
 def shards(
@@ -596,18 +607,19 @@
     scale = jnp.exp(logit_scale)
     bias = jnp.concatenate([query_bias, jnp.zeros_like(query_bias), value_bias]).reshape(1, -1)
     pair_rows = pair_bias.reshape(HEADS * WIN, WIN)
+    gain = norm_gain.reshape(1, C)
+
+    features = features.transpose(1, 0, 2)
+    upstream = upstream.transpose(1, 0, 2)
+    east, low, lower = halo(features)
+    late, region_ids, lower = lax.optimization_barrier((upstream, region_ids, lower))
+    came = east, lon_step(lower, 1), low
     lower_ids = lon_step(region_ids[HALF_ROWS:], 1)
     region_ids = jnp.concatenate([region_ids[:HALF_ROWS], lower_ids], 0)
     region_row = region_ids.reshape(WINDOWS, WIN)
     region_col = region_ids.reshape(-1, 1)
-    gain = norm_gain.reshape(1, C)
-
-    features = features.transpose(1, 0, 2)
-    upstream = upstream.transpose(1, 0, 2)
-    came = halo(features, *first_messages(features))
-    late, low = lax.optimization_barrier((first_messages(upstream), came[2]))
-    came = (*came[:2], low)
-    came_late = halo(upstream, *late)
+    east, low, lower = halo(late)
+    came_late = east, lon_step(lower, 1), low
     x, projected, attended = call(
         forward_body,
         [shape((CELLS, C), BF16), shape((CELLS, 3 * HC), F32), shape((CELLS, HC), BF16)],
@@ -770,7 +782,7 @@
             order = tables(FIRST, step // 2 + 1)
         if step == 0:
             order, stay_low = lax.optimization_barrier((order, stay_low))
-        if step == 1:
+        if step == 3:
             order, last = lax.optimization_barrier((order, last))
         parts = call(body, [shape((left // 2 + EXTRA,) + BLOCK, BF16)] * 6, [order, *terms], name="halve")
     terms, input_grad = lax.optimization_barrier((terms, input_grad))
@@ -785,13 +797,12 @@
             shape((C,), F32),
             shape((HC,), F32),
             shape((HC,), F32),
-            shape((6, 128), F32),
+            shape((HEADS,), F32),
         ],
         [mine, sums, sums_other],
         name="finish",
     )
     pair_grad = pair_grad.reshape(HEADS, WIN, WIN)
-    scale_grad = scale_grad[:, :2].reshape(HEADS)
 
     return (
         input_grad.transpose(1, 0, 2),

time: 152 us -> 142 us (0.934)
  local copies, waits for them, and re-layouts: 17.9 us -> 9.56 us
  waiting for transfers between devices: 27.2 us -> 18.9 us
  starting transfers between devices: 54.7 us -> 59.1 us
  Pallas kernels: 49.9 us -> 51.9 us
    ppermute x34, waiting for transfers between devices: 27.2 us -> 18.9 us  [permuted(): return lax.ppermute(value, axes, pairs)]
    slice x6 -> x0, local copies, waits for them, and re-layouts: 5.8 us -> none  [the longest x2 2.9 us: first_messages(): upper = grid[:SHIFT_W, SHIFT_H:SHIFT_H + HALF_ROWS]]
    reshape x5 -> x0, local copies, waits for them, and re-layouts: 4.79 us -> none  [the longest x4 4.2 us: first_messages(): return (grid[:, :SHIFT_H].reshape(-1, C), upper.reshape(-1, C))]
    ppermute x34, starting transfers between devices: 54.7 us -> 59.1 us  [permuted(): return lax.ppermute(value, axes, pairs)]
    unnamed x30 -> x32, local copies, waits for them, and re-layouts: 4.5 us -> 6.9 us
    pallas_call x14 -> x16, Pallas kernels: 37.8 us -> 39.8 us  [call(): pl.pallas_call(body, out_shape=list(outs), in_specs=specs, out_specs=[VME...]
  transfers between devices with their start and end apart: 34 -> 34, of which waited for: 14 -> 14; matrix products, arithmetic and copies ran while one was open for 7% -> 3% of each run, Pallas kernels for 24% -> 26%
where the time goes in v2:
time: 142 us; the launch traced here: 141 us
  starting transfers between devices  59.1 us (42%)
  Pallas kernels  51.9 us (37%)
  waiting for transfers between devices  18.9 us (13%)
  local copies, waits for them, and re-layouts  9.56 us (7%)
    ppermute x34, starting transfers between devices, permuted(): return lax.ppermute(value, axes, pairs)  59.1 us
    pallas_call x16, Pallas kernels, call(): pl.pallas_call(body, out_shape=list(outs), in_specs=specs, out_specs=[VME...  39.8 us
    ppermute x34, waiting for transfers between devices, permuted(): return lax.ppermute(value, axes, pairs)  18.9 us
    pallas_call x2, Pallas kernels, grid_call(): pl.pallas_call(body, grid_spec=spec, out_shape=results, compiler_params=p...  12.1 us
    unnamed x32, local copies, waits for them, and re-layouts  6.9 us
  transfers between devices with their start and end apart: 34, of which 14 were waited for; matrix products, arithmetic and copies ran while one was open for 3% of the time, Pallas kernels for 26%

profile of v2, /device:TPU:1, one launch (start us, length us, event | category | flops | bytes accessed | tf_op | source)
XLA Modules:
  0.0 141.3 jit_solution(3875563660574342401)
XLA Ops:
  0.7 1.2 copy-done.2
  1.9 0.7 first.2
  2.6 1.4 %collective-permute-start.1 = (bf16[36,1536]{1,0:T(8,128)(2,1)S(1)}, bf16[36,1536]{1,0:T(8,128)(2,1)S(1)}, u32[]{:S(2)}, u32[]{:S(2)}) collective-permute-start(bf16[36,1536]{1,0:T(8,128)(2,1)S(1)} %get-tuple-element.89), channel_id=1, source_target_pairs={{0,3},{1,0},{2,1},{3,2},{4,7},{5,4},{6,5},{7,6},{8,11},{9,8},{10,9... | collective-permute-start | bytes 331784 | tf_op jit(solution)/shard_map/ppermute | solution.py:545
  4.1 8.7 %collective-permute-start = (bf16[72,1536]{1,0:T(8,128)(2,1)}, bf16[72,1536]{1,0:T(8,128)(2,1)S(1)}, u32[]{:S(2)}, u32[]{:S(2)}) collective-permute-start(bf16[72,1536]{1,0:T(8,128)(2,1)} %get-tuple-element.88), channel_id=1, source_target_pairs={{0,124},{4,0},{8,4},{12,8},{16,12},{20,16},{24,20},{28,24},{32,28}... | collective-permute-start | bytes 663560 | tf_op jit(solution)/shard_map/ppermute | solution.py:545
  13.4 0.7 pad_maximum_fusion
  14.1 1.2 copy-done.3
  15.5 0.8 first.3
  16.2 1.0 collective-permute-start.6
  17.4 7.5 %collective-permute-start.5 = (bf16[72,1536]{1,0:T(8,128)(2,1)}, bf16[72,1536]{1,0:T(8,128)(2,1)}, u32[]{:S(2)}, u32[]{:S(2)}) collective-permute-start(bf16[72,1536]{1,0:T(8,128)(2,1)} %get-tuple-element.96), channel_id=1, source_target_pairs={{0,124},{4,0},{8,4},{12,8},{16,12},{20,16},{24,20},{28,24},{32,28}... | collective-permute-start | bytes 663560 | tf_op jit(solution)/shard_map/ppermute | solution.py:545
  25.1 2.2 %collective-permute-done.3 = s32[12,12]{0,1:T(8,128)S(1)} collective-permute-done((s32[12,12]{0,1:T(8,128)S(1)}, s32[12,12]{0,1:T(8,128)S(1)}, u32[]{:S(2)}, u32[]{:S(2)}) %collective-permute-start.3) | collective-permute-done | bytes 608 | tf_op jit(solution)/shard_map/ppermute | solution.py:545
  27.7 11.0 %forward.1 = (bf16[288,1536]{1,0:T(8,128)(2,1)}, f32[288,2304]{1,0:T(8,128)}, bf16[288,768]{1,0:T(8,128)(2,1)S(1)}) custom-call(f32[12]{0:T(128)S(1)} %exp.3.scale, bf16[12,24,1536]{2,1,0:T(8,128)(2,1)S(1)} %bitcast.25, bf16[72,1536]{1,0:T(8,128)(2,1)S(1)} %collective-permute-done.east, bf16[72,1536]{1,0:T(8,128)(2,1)S(1)} %collective-permute-done.2.west, ...), custom_call_target="tpu_custom_call" | custom-call | flops 2038431744 | bytes 12757296 | tf_op jit(solution)/shard_map/forward/pallas_call | solution.py:64
  38.6 2.2 %collective-permute-start.4 = (bf16[288,1536]{1,0:T(8,128)(2,1)}, bf16[288,1536]{1,0:T(8,128)(2,1)}, u32[]{:S(2)}, u32[]{:S(2)}) collective-permute-start(bf16[288,1536]{1,0:T(8,128)(2,1)} %get-tuple-element.92.x0), channel_id=1, source_target_pairs={{0,1},{1,0},{2,3},{3,2},{4,5},{5,4},{6,7},{7,6},{8,9},{9,8},{10,11... | collective-permute-start | bytes 2654216 | tf_op jit(solution)/shard_map/ppermute | solution.py:545
  40.8 0.7 copy-done.7
  41.5 0.9 copy-done.8
  42.5 9.9 %backward.1 = (bf16[288,1536]{1,0:T(8,128)(2,1)S(1)}, f32[288,768]{1,0:T(8,128)}, f32[1,1536]{1,0:T(1,128)S(1)}, bf16[288,1152]{1,0:T(8,128)(2,1)S(1)}, f32[144,512]{1,0:T(8,128)S(1)}) custom-call(s32[1]{0:T(128)S(6)} %sub.3.side, f32[12]{0:T(128)S(1)} %exp.3.scale, bf16[288,768]{1,0:T(8,128)(2,1)S(1)} %get-tuple-element.94.attended, ...), custom_call_target="tpu_custom_call" | custom-call | flops 1454505984 | bytes 9884980 | tf_op jit(solution)/shard_map/backward/pallas_call | solution.py:64
  53.1 0.7 collective-permute-start.10
  53.8 0.8 fusion.3
  54.7 1.2 copy-done.6
  55.9 5.4 %attention.1 = (bf16[288,1152]{1,0:T(8,128)(2,1)S(1)}, f32[144,512]{1,0:T(8,128)S(1)}) custom-call(s32[1]{0:T(128)} %bitcast.6.side.core, f32[12]{0:T(128)S(1)} %exp.3.scale, f32[288,2304]{1,0:T(8,128)} %get-tuple-element.93.projected.q_ref.k_ref.v_ref, f32[288,2304]{1,0:T(8,128)} %get-tuple-element.93.projected.q_ref.k_ref.v_ref, ...), custom_call_target="tpu_custom_call" | custom-call | flops 95551488 | bytes 10063104 | tf_op jit(solution)/shard_map/attention/pallas_call | solution.py:86
  61.4 8.7 %weights.1 = (bf16[34,24,512]{2,1,0:T(8,128)(2,1)S(1)}, bf16[34,24,512]{2,1,0:T(8,128)(2,1)S(1)}, bf16[34,24,512]{2,1,0:T(8,128)(2,1)}, bf16[34,24,512]{2,1,0:T(...) custom-call(s32[12]{0:T(128)S(1)} %get-tuple-element.182.order, ...), custom_call_target="tpu_custom_call" | custom-call | flops 2717908992 | bytes 10911792 | tf_op jit(solution)/shard_map/weights/pallas_call | solution.py:64
  70.2 0.8 collective-permute-start.14
  71.0 3.6 %collective-permute-start.15 = (bf16[34,24,512]{2,1,0:T(8,128)(2,1)}, bf16[34,24,512]{2,1,0:T(8,128)(2,1)S(1)}, u32[]{:S(2)}, u32[]{:S(2)}) collective-permute-start(bf16[34,24,512]{2,1,0:T(8,128)(2,1)} %get-tuple-element.122), channel_id=1, source_target_pairs={{0,4},{1,13},{4,0},{5,9},{8,12},{9,5},{12,8},{13,1},{2,6},{3,15},{... | collective-permute-start | bytes 2506760 | tf_op jit(solution)/shard_map/ppermute | solution.py:545
  74.7 0.8 fusion
  75.5 6.6 %branch.1 = (bf16[72,1536]{1,0:T(8,128)(2,1)S(1)}, bf16[72,1536]{1,0:T(8,128)(2,1)S(1)}, bf16[72,1536]{1,0:T(8,128)(2,1)S(1)}, bf16[72,1536]{1,0:T(8,128)(2,1)S(1)}) custom-call(s32[1]{0:T(128)} %bitcast.6.side.core, bf16[1536,2304]{1,0:T(8,128)(2,1)} %w.3, bf16[288,1152]{1,0:T(8,128)(2,1)S(1)} %get-tuple-element.100.p0.own, ...), custom_call_target="tpu_custom_call" | custom-call | flops 2038431744 | bytes 9289728 | tf_op jit(solution)/shard_map/branch/pallas_call | solution.py:86
  83.1 1.7 %collective-permute-done.15.refs_5_ = bf16[34,24,512]{2,1,0:T(8,128)(2,1)S(1)} collective-permute-done((bf16[34,24,512]{2,1,0:T(8,128)(2,1)}, bf16[34,24,512]{2,1,0:T(8,128)(2,1)S(1)}, u32[]{:S(2)}, u32[]{:S(2)}) %collective-permute-start.15) | collective-permute-done | bytes 835616 | tf_op jit(solution)/shard_map/ppermute | solution.py:545
  84.8 0.9 copy-done.12
  85.7 2.8 %halve.5 = (bf16[18,24,512]{2,1,0:T(8,128)(2,1)S(1)}, bf16[18,24,512]{2,1,0:T(8,128)(2,1)S(1)}, bf16[18,24,512]{2,1,0:T(8,128)(2,1)S(1)}, bf16[18,24,512]{2,1,0:...) custom-call(s32[6]{0:T(128)S(1)} %get-tuple-element.116.order, ...), custom_call_target="tpu_custom_call" | custom-call | bytes 7667736 | tf_op jit(solution)/shard_map/halve/pallas_call | solution.py:64
  88.7 7.2 %collective-permute-done.16.refs_1_ = bf16[18,24,512]{2,1,0:T(8,128)(2,1)S(1)} collective-permute-done((bf16[18,24,512]{2,1,0:T(8,128)(2,1)S(1)}, bf16[18,24,512]{2,1,0:T(8,128)(2,1)S(1)}, u32[]{:S(2)}, u32[]{:S(2)}) %collective-permute-start.16) | collective-permute-done | bytes 442400 | tf_op jit(solution)/shard_map/ppermute | solution.py:545
  96.2 0.8 copy-done.13
  96.9 1.4 halve.6
  98.4 1.1 collective-permute-start.19
  99.4 2.6 %collective-permute-start.20 = (bf16[10,24,512]{2,1,0:T(8,128)(2,1)S(1)}, bf16[10,24,512]{2,1,0:T(8,128)(2,1)S(1)}, u32[]{:S(2)}, u32[]{:S(2)}) collective-permute-start(bf16[10,24,512]{2,1,0:T(8,128)(2,1)S(1)} %get-tuple-element.132), channel_id=1, source_target_pairs={{0,4},{1,13},{4,0},{5,9},{8,12},{9,5},{12,8},{13,1},{2,6},{3,15},{... | collective-permute-start | bytes 737288 | tf_op jit(solution)/shard_map/ppermute | solution.py:545
  102.1 4.2 %collective-permute-start.12 = (bf16[72,1536]{1,0:T(8,128)(2,1)S(1)}, bf16[72,1536]{1,0:T(8,128)(2,1)S(1)}, u32[]{:S(2)}, u32[]{:S(2)}) collective-permute-start(bf16[72,1536]{1,0:T(8,128)(2,1)S(1)} %get-tuple-element.113), channel_id=1, source_target_pairs={{0,124},{4,0},{8,4},{12,8},{16,12},{20,16},{24,20},{28,24},{32,28}... | collective-permute-start | bytes 663560 | tf_op jit(solution)/shard_map/ppermute | solution.py:545
  106.4 1.9 %collective-permute-done.21.refs_5_ = bf16[10,24,512]{2,1,0:T(8,128)(2,1)S(1)} collective-permute-done((bf16[10,24,512]{2,1,0:T(8,128)(2,1)S(1)}, bf16[10,24,512]{2,1,0:T(8,128)(2,1)S(1)}, u32[]{:S(2)}, u32[]{:S(2)}) %collective-permute-start.21) | collective-permute-done | bytes 245792 | tf_op jit(solution)/shard_map/ppermute | solution.py:545
  108.3 0.7 halve.7
  109.0 0.8 collective-permute-start.22
  110.3 1.5 %collective-permute-start.31 = (bf16[72,1536]{1,0:T(8,128)(2,1)S(1)}, bf16[72,1536]{1,0:T(8,128)(2,1)S(1)}, u32[]{:S(2)}, u32[]{:S(2)}) collective-permute-start(bf16[72,1536]{1,0:T(8,128)(2,1)S(1)} %get-tuple-element.153), channel_id=1, source_target_pairs={{0,4},{4,8},{8,12},{12,16},{16,20},{20,24},{24,28},{28,32},{32,36}... | collective-permute-start | bytes 663560 | tf_op jit(solution)/shard_map/ppermute | solution.py:545
  111.8 1.2 collective-permute-done.22.refs_1_
  113.1 0.8 collective-permute-done.23.refs_3_
  114.9 3.1 %collective-permute-start.26 = (bf16[4,24,512]{2,1,0:T(8,128)(2,1)S(1)}, bf16[4,24,512]{2,1,0:T(8,128)(2,1)S(1)}, u32[]{:S(2)}, u32[]{:S(2)}) collective-permute-start(bf16[4,24,512]{2,1,0:T(8,128)(2,1)S(1)} %get-tuple-element.144), channel_id=1, source_target_pairs={{0,16},{1,49},{16,0},{17,33},{32,48},{33,17},{48,32},{49,1},{2,18}... | collective-permute-start | bytes 294920 | tf_op jit(solution)/shard_map/ppermute | solution.py:545
  118.0 0.9 collective-permute-start.27
  118.9 5.4 %collective-permute-start.32 = (bf16[36,1536]{1,0:T(8,128)(2,1)S(1)}, bf16[36,1536]{1,0:T(8,128)(2,1)S(1)}, u32[]{:S(2)}, u32[]{:S(2)}) collective-permute-start(bf16[36,1536]{1,0:T(8,128)(2,1)S(1)} %last_rows.1), channel_id=1, source_target_pairs={{0,1},{1,2},{2,3},{3,0},{4,5},{5,6},{6,7},{7,4},{8,9},{9,10},{10,1... | collective-permute-start | bytes 331784 | tf_op jit(solution)/shard_map/ppermute | solution.py:545
  125.0 1.7 %collective-permute-start.28 = (bf16[3,24,512]{2,1,0:T(8,128)(2,1)S(1)}, bf16[3,24,512]{2,1,0:T(8,128)(2,1)S(1)}, u32[]{:S(2)}, u32[]{:S(2)}) collective-permute-start(bf16[3,24,512]{2,1,0:T(8,128)(2,1)S(1)} %get-tuple-element.148), channel_id=1, source_target_pairs={{0,12},{1,5},{4,8},{5,1},{8,4},{9,13},{12,0},{13,9},{2,14},{3,7},{... | collective-permute-start | bytes 221192 | tf_op jit(solution)/shard_map/ppermute | solution.py:545
  127.0 1.3 merge.1
  128.4 1.5 %collective-permute-done.29.refs_3_ = bf16[3,24,512]{2,1,0:T(8,128)(2,1)S(1)} collective-permute-done((bf16[3,24,512]{2,1,0:T(8,128)(2,1)S(1)}, bf16[3,24,512]{2,1,0:T(8,128)(2,1)S(1)}, u32[]{:S(2)}, u32[]{:S(2)}) %collective-permute-start.29) | collective-permute-done | bytes 73760 | tf_op jit(solution)/shard_map/ppermute | solution.py:545
  129.9 9.4 %collective-permute-start.33 = (bf16[9,24,512]{2,1,0:T(8,128)(2,1)S(1)}, bf16[9,24,512]{2,1,0:T(8,128)(2,1)S(1)}, u32[]{:S(2)}, u32[]{:S(2)}) collective-permute-start(bf16[9,24,512]{2,1,0:T(8,128)(2,1)S(1)} %total.1.own), channel_id=1, source_target_pairs={{0,1},{1,0},{2,3},{3,2},{4,5},{5,4},{6,7},{7,6},{8,9},{9,8},{10,11... | collective-permute-start | bytes 663560 | tf_op jit(solution)/shard_map/ppermute | solution.py:545
  139.3 1.1 collective-permute-done.33.other
  140.4 0.9 finish.1
  (85 shorter events, 6.6 us)
Async XLA Ops:
  0.6 14.8 %copy-start = (bf16[24,12,1536]{2,0,1:T(8,128)(2,1)S(1)}, bf16[24,12,1536]{2,0,1:T(8,128)(2,1)}, u32[]{:S(2)}) copy-start(bf16[24,12,1536]{2,0,1:T(8,128)(2,1)} %param.13) | copy-start | bytes 2654212
  0.6 1.2 copy-start.2
  1.9 15.4 %copy-start.14 = (s32[24,12]{0,1:T(8,128)S(1)}, s32[24,12]{0,1:T(8,128)}, u32[]{:S(2)}) copy-start(s32[24,12]{0,1:T(8,128)} %param.14) | copy-start | bytes 3460
  1.9 15.4 %copy-start.15 = (f32[1536]{0:T(1024)S(1)}, f32[1536]{0:T(1024)}, u32[]{:S(2)}) copy-start(f32[1536]{0:T(1024)} %param.21) | copy-start | bytes 18436
  2.6 11.5 %collective-permute-start.1 = (bf16[36,1536]{1,0:T(8,128)(2,1)S(1)}, bf16[36,1536]{1,0:T(8,128)(2,1)S(1)}, u32[]{:S(2)}, u32[]{:S(2)}) collective-permute-start(bf16[36,1536]{1,0:T(8,128)(2,1)S(1)} %get-tuple-element.89), channel_id=1, source_target_pairs={{0,3},{1,0},{2,1},{3,2},{4,7},{5,4},{6,5},{7,6},{8,11},{9,8},{10,9... | collective-permute-start | bytes 331784 | tf_op jit(solution)/shard_map/ppermute | solution.py:545
  4.1 23.6 %collective-permute-start = (bf16[72,1536]{1,0:T(8,128)(2,1)}, bf16[72,1536]{1,0:T(8,128)(2,1)S(1)}, u32[]{:S(2)}, u32[]{:S(2)}) collective-permute-start(bf16[72,1536]{1,0:T(8,128)(2,1)} %get-tuple-element.88), channel_id=1, source_target_pairs={{0,124},{4,0},{8,4},{12,8},{16,12},{20,16},{24,20},{28,24},{32,28}... | collective-permute-start | bytes 663560 | tf_op jit(solution)/shard_map/ppermute | solution.py:545
  14.1 1.2 copy-start.3
  15.3 12.4 %copy-start.4 = (bf16[24,12,1536]{2,0,1:T(8,128)(2,1)S(1)}, bf16[24,12,1536]{2,0,1:T(8,128)(2,1)}, u32[]{:S(2)}) copy-start(bf16[24,12,1536]{2,0,1:T(8,128)(2,1)} %param.12) | copy-start | bytes 2654212
  15.3 12.4 %copy-start.5 = (f32[12,72,72]{2,1,0:T(8,128)S(1)}, f32[12,72,72]{2,1,0:T(8,128)}, u32[]{:S(2)}) copy-start(f32[12,72,72]{2,1,0:T(8,128)} %param.19) | copy-start | bytes 746500
  15.4 12.3 %collective-permute-start.2 = (bf16[72,1536]{1,0:T(8,128)(2,1)S(1)}, bf16[72,1536]{1,0:T(8,128)(2,1)S(1)}, u32[]{:S(2)}, u32[]{:S(2)}) collective-permute-start(bf16[72,1536]{1,0:T(8,128)(2,1)S(1)} %to_east.2), channel_id=1, source_target_pairs={{0,4},{4,8},{8,12},{12,16},{16,20},{20,24},{24,28},{28,32},{32,36}... | collective-permute-start | bytes 663560 | tf_op jit(solution)/shard_map/ppermute | solution.py:545
  16.2 8.7 %collective-permute-start.6 = (bf16[36,1536]{1,0:T(8,128)(2,1)S(1)}, bf16[36,1536]{1,0:T(8,128)(2,1)S(1)}, u32[]{:S(2)}, u32[]{:S(2)}) collective-permute-start(bf16[36,1536]{1,0:T(8,128)(2,1)S(1)} %get-tuple-element.97), channel_id=1, source_target_pairs={{0,3},{1,0},{2,1},{3,2},{4,7},{5,4},{6,5},{7,6},{8,11},{9,8},{10,9... | collective-permute-start | bytes 331784 | tf_op jit(solution)/shard_map/ppermute | solution.py:545
  17.3 10.0 %collective-permute-start.3 = (s32[12,12]{0,1:T(8,128)S(1)}, s32[12,12]{0,1:T(8,128)S(1)}, u32[]{:S(2)}, u32[]{:S(2)}) collective-permute-start(s32[12,12]{0,1:T(8,128)S(1)} %get-tuple-element.171), channel_id=1, source_target_pairs={{0,4},{4,8},{8,12},{12,16},{16,20},{20,24},{24,28},{28,32},{32,36}... | collective-permute-start | bytes 1736 | tf_op jit(solution)/shard_map/ppermute | solution.py:545
  17.4 23.5 %collective-permute-start.5 = (bf16[72,1536]{1,0:T(8,128)(2,1)}, bf16[72,1536]{1,0:T(8,128)(2,1)}, u32[]{:S(2)}, u32[]{:S(2)}) collective-permute-start(bf16[72,1536]{1,0:T(8,128)(2,1)} %get-tuple-element.96), channel_id=1, source_target_pairs={{0,124},{4,0},{8,4},{12,8},{16,12},{20,16},{24,20},{28,24},{32,28}... | collective-permute-start | bytes 663560 | tf_op jit(solution)/shard_map/ppermute | solution.py:545
  25.0 15.8 %collective-permute-start.7 = (bf16[72,1536]{1,0:T(8,128)(2,1)S(1)}, bf16[72,1536]{1,0:T(8,128)(2,1)S(1)}, u32[]{:S(2)}, u32[]{:S(2)}) collective-permute-start(bf16[72,1536]{1,0:T(8,128)(2,1)S(1)} %to_east.3), channel_id=1, source_target_pairs={{0,4},{4,8},{8,12},{12,16},{16,20},{20,24},{24,28},{28,32},{32,36}... | collective-permute-start | bytes 663560 | tf_op jit(solution)/shard_map/ppermute | solution.py:545
  38.6 22.7 %collective-permute-start.4 = (bf16[288,1536]{1,0:T(8,128)(2,1)}, bf16[288,1536]{1,0:T(8,128)(2,1)}, u32[]{:S(2)}, u32[]{:S(2)}) collective-permute-start(bf16[288,1536]{1,0:T(8,128)(2,1)} %get-tuple-element.92.x0), channel_id=1, source_target_pairs={{0,1},{1,0},{2,3},{3,2},{4,5},{5,4},{6,7},{7,6},{8,9},{9,8},{10,11... | collective-permute-start | bytes 2654216 | tf_op jit(solution)/shard_map/ppermute | solution.py:545
  41.5 0.9 copy-start.8
  52.3 9.0 %copy-start.9 = (bf16[288,1536]{1,0:T(8,128)(2,1)}, bf16[288,1536]{1,0:T(8,128)(2,1)S(1)}, u32[]{:S(2)}) copy-start(bf16[288,1536]{1,0:T(8,128)(2,1)S(1)} %get-tuple-element.102.m0) | copy-start | bytes 2654212
  52.4 9.0 %collective-permute-start.9 = (bf16[288,1536]{1,0:T(8,128)(2,1)S(1)}, bf16[288,1536]{1,0:T(8,128)(2,1)}, u32[]{:S(2)}, u32[]{:S(2)}) collective-permute-start(bf16[288,1536]{1,0:T(8,128)(2,1)S(1)} %get-tuple-element.102.m0), channel_id=1, source_target_pairs={{0,1},{1,0},{2,3},{3,2},{4,5},{5,4},{6,7},{7,6},{8,9},{9,8},{10,11... | collective-permute-start | bytes 2654216 | tf_op jit(solution)/shard_map/ppermute | solution.py:545
  52.5 8.9 %collective-permute-start.8 = (bf16[288,1152]{1,0:T(8,128)(2,1)S(1)}, bf16[288,1152]{1,0:T(8,128)(2,1)}, u32[]{:S(2)}, u32[]{:S(2)}) collective-permute-start(bf16[288,1152]{1,0:T(8,128)(2,1)S(1)} %get-tuple-element.101.theirs), channel_id=1, source_target_pairs={{0,1},{1,0},{2,3},{3,2},{4,5},{5,4},{6,7},{7,6},{8,9},{9,8},{10,11... | collective-permute-start | bytes 1990664 | tf_op jit(solution)/shard_map/ppermute | solution.py:545
  52.9 8.4 %collective-permute-start.11 = (f32[144,512]{1,0:T(8,128)S(1)}, f32[144,512]{1,0:T(8,128)S(1)}, u32[]{:S(2)}, u32[]{:S(2)}) collective-permute-start(f32[144,512]{1,0:T(8,128)S(1)} %get-tuple-element.104), channel_id=1, source_target_pairs={{0,1},{1,0},{2,3},{3,2},{4,5},{5,4},{6,7},{7,6},{8,9},{9,8},{10,11... | collective-permute-start | bytes 884744 | tf_op jit(solution)/shard_map/ppermute | solution.py:545
  53.1 8.2 %collective-permute-start.10 = (bf16[288,384]{1,0:T(8,128)(2,1)S(1)}, bf16[288,384]{1,0:T(8,128)(2,1)S(1)}, u32[]{:S(2)}, u32[]{:S(2)}) collective-permute-start(bf16[288,384]{1,0:T(8,128)(2,1)S(1)} %get-tuple-element.168), channel_id=1, source_target_pairs={{0,1},{1,0},{2,3},{3,2},{4,5},{5,4},{6,7},{7,6},{8,9},{9,8},{10,11... | collective-permute-start | bytes 663560 | tf_op jit(solution)/shard_map/ppermute | solution.py:545
  54.7 1.2 copy-start.6
  70.1 12.7 %collective-permute-start.13 = (bf16[34,24,512]{2,1,0:T(8,128)(2,1)S(1)}, bf16[34,24,512]{2,1,0:T(8,128)(2,1)S(1)}, u32[]{:S(2)}, u32[]{:S(2)}) collective-permute-start(bf16[34,24,512]{2,1,0:T(8,128)(2,1)S(1)} %get-tuple-element.118), channel_id=1, source_target_pairs={{0,16},{1,49},{16,0},{17,33},{32,48},{33,17},{48,32},{49,1},{2,18}... | collective-permute-start | bytes 2506760 | tf_op jit(solution)/shard_map/ppermute | solution.py:545
  70.2 12.9 %collective-permute-start.14 = (bf16[34,24,512]{2,1,0:T(8,128)(2,1)}, bf16[34,24,512]{2,1,0:T(8,128)(2,1)S(1)}, u32[]{:S(2)}, u32[]{:S(2)}) collective-permute-start(bf16[34,24,512]{2,1,0:T(8,128)(2,1)} %get-tuple-element.120), channel_id=1, source_target_pairs={{0,2},{1,67},{2,0},{3,65},{64,66},{65,3},{66,64},{67,1},{4,6},{5,7... | collective-permute-start | bytes 2506760 | tf_op jit(solution)/shard_map/ppermute | solution.py:545
  71.0 13.7 %collective-permute-start.15 = (bf16[34,24,512]{2,1,0:T(8,128)(2,1)}, bf16[34,24,512]{2,1,0:T(8,128)(2,1)S(1)}, u32[]{:S(2)}, u32[]{:S(2)}) collective-permute-start(bf16[34,24,512]{2,1,0:T(8,128)(2,1)} %get-tuple-element.122), channel_id=1, source_target_pairs={{0,4},{1,13},{4,0},{5,9},{8,12},{9,5},{12,8},{13,1},{2,6},{3,15},{... | collective-permute-start | bytes 2506760 | tf_op jit(solution)/shard_map/ppermute | solution.py:545
  82.8 2.0 %copy-start.10 = (bf16[34,24,512]{2,1,0:T(8,128)(2,1)}, bf16[34,24,512]{2,1,0:T(8,128)(2,1)S(1)}, u32[]{:S(2)}) copy-start(bf16[34,24,512]{2,1,0:T(8,128)(2,1)S(1)} %collective-permute-done.13.refs_1_) | copy-start | bytes 2506756
  83.1 1.7 %copy-start.11 = (bf16[34,24,512]{2,1,0:T(8,128)(2,1)}, bf16[34,24,512]{2,1,0:T(8,128)(2,1)S(1)}, u32[]{:S(2)}) copy-start(bf16[34,24,512]{2,1,0:T(8,128)(2,1)S(1)} %collective-permute-done.14.refs_3_) | copy-start | bytes 2506756
  84.8 0.9 copy-start.12
  88.5 7.5 %collective-permute-start.16 = (bf16[18,24,512]{2,1,0:T(8,128)(2,1)S(1)}, bf16[18,24,512]{2,1,0:T(8,128)(2,1)S(1)}, u32[]{:S(2)}, u32[]{:S(2)}) collective-permute-start(bf16[18,24,512]{2,1,0:T(8,128)(2,1)S(1)} %get-tuple-element.124), channel_id=1, source_target_pairs={{0,48},{1,17},{16,32},{17,1},{32,16},{33,49},{48,0},{49,33},{2,50}... | collective-permute-start | bytes 1327112 | tf_op jit(solution)/shard_map/ppermute | solution.py:545
  88.5 7.5 %collective-permute-start.17 = (bf16[18,24,512]{2,1,0:T(8,128)(2,1)S(1)}, bf16[18,24,512]{2,1,0:T(8,128)(2,1)S(1)}, u32[]{:S(2)}, u32[]{:S(2)}) collective-permute-start(bf16[18,24,512]{2,1,0:T(8,128)(2,1)S(1)} %get-tuple-element.126), channel_id=1, source_target_pairs={{0,66},{1,3},{2,64},{3,1},{64,2},{65,67},{66,0},{67,65},{4,70},{5,... | collective-permute-start | bytes 1327112 | tf_op jit(solution)/shard_map/ppermute | solution.py:545
  88.6 7.5 %collective-permute-start.18 = (bf16[18,24,512]{2,1,0:T(8,128)(2,1)S(1)}, bf16[18,24,512]{2,1,0:T(8,128)(2,1)S(1)}, u32[]{:S(2)}, u32[]{:S(2)}) collective-permute-start(bf16[18,24,512]{2,1,0:T(8,128)(2,1)S(1)} %get-tuple-element.128), channel_id=1, source_target_pairs={{0,12},{1,5},{4,8},{5,1},{8,4},{9,13},{12,0},{13,9},{2,14},{3,7},{... | collective-permute-start | bytes 1327112 | tf_op jit(solution)/shard_map/ppermute | solution.py:545
  96.9 30.1 %copy-start.1 = (bf16[24,12,1536]{2,0,1:T(8,128)(2,1)S(1)}, bf16[24,12,1536]{2,0,1:T(8,128)(2,1)}, u32[]{:S(2)}) copy-start(bf16[24,12,1536]{2,0,1:T(8,128)(2,1)} %param.13) | copy-start | bytes 2654212
  98.4 8.0 %collective-permute-start.19 = (bf16[10,24,512]{2,1,0:T(8,128)(2,1)S(1)}, bf16[10,24,512]{2,1,0:T(8,128)(2,1)S(1)}, u32[]{:S(2)}, u32[]{:S(2)}) collective-permute-start(bf16[10,24,512]{2,1,0:T(8,128)(2,1)S(1)} %get-tuple-element.130), channel_id=1, source_target_pairs={{0,2},{1,67},{2,0},{3,65},{64,66},{65,3},{66,64},{67,1},{4,6},{5,7... | collective-permute-start | bytes 737288 | tf_op jit(solution)/shard_map/ppermute | solution.py:545
  99.4 7.0 %collective-permute-start.20 = (bf16[10,24,512]{2,1,0:T(8,128)(2,1)S(1)}, bf16[10,24,512]{2,1,0:T(8,128)(2,1)S(1)}, u32[]{:S(2)}, u32[]{:S(2)}) collective-permute-start(bf16[10,24,512]{2,1,0:T(8,128)(2,1)S(1)} %get-tuple-element.132), channel_id=1, source_target_pairs={{0,4},{1,13},{4,0},{5,9},{8,12},{9,5},{12,8},{13,1},{2,6},{3,15},{... | collective-permute-start | bytes 737288 | tf_op jit(solution)/shard_map/ppermute | solution.py:545
  102.0 6.3 %collective-permute-start.21 = (bf16[10,24,512]{2,1,0:T(8,128)(2,1)S(1)}, bf16[10,24,512]{2,1,0:T(8,128)(2,1)S(1)}, u32[]{:S(2)}, u32[]{:S(2)}) collective-permute-start(bf16[10,24,512]{2,1,0:T(8,128)(2,1)S(1)} %get-tuple-element.134), channel_id=1, source_target_pairs={{0,16},{1,49},{16,0},{17,33},{32,48},{33,17},{48,32},{49,1},{2,18}... | collective-permute-start | bytes 737288 | tf_op jit(solution)/shard_map/ppermute | solution.py:545
  102.1 9.6 %collective-permute-start.12 = (bf16[72,1536]{1,0:T(8,128)(2,1)S(1)}, bf16[72,1536]{1,0:T(8,128)(2,1)S(1)}, u32[]{:S(2)}, u32[]{:S(2)}) collective-permute-start(bf16[72,1536]{1,0:T(8,128)(2,1)S(1)} %get-tuple-element.113), channel_id=1, source_target_pairs={{0,124},{4,0},{8,4},{12,8},{16,12},{20,16},{24,20},{28,24},{32,28}... | collective-permute-start | bytes 663560 | tf_op jit(solution)/shard_map/ppermute | solution.py:545
  109.0 4.1 %collective-permute-start.22 = (bf16[6,24,512]{2,1,0:T(8,128)(2,1)S(1)}, bf16[6,24,512]{2,1,0:T(8,128)(2,1)S(1)}, u32[]{:S(2)}, u32[]{:S(2)}) collective-permute-start(bf16[6,24,512]{2,1,0:T(8,128)(2,1)S(1)} %get-tuple-element.136), channel_id=1, source_target_pairs={{0,66},{1,3},{2,64},{3,1},{64,2},{65,67},{66,0},{67,65},{4,70},{5,... | collective-permute-start | bytes 442376 | tf_op jit(solution)/shard_map/ppermute | solution.py:545
  109.8 4.0 %collective-permute-start.23 = (bf16[6,24,512]{2,1,0:T(8,128)(2,1)S(1)}, bf16[6,24,512]{2,1,0:T(8,128)(2,1)S(1)}, u32[]{:S(2)}, u32[]{:S(2)}) collective-permute-start(bf16[6,24,512]{2,1,0:T(8,128)(2,1)S(1)} %get-tuple-element.138), channel_id=1, source_target_pairs={{0,12},{1,5},{4,8},{5,1},{8,4},{9,13},{12,0},{13,9},{2,14},{3,7},{... | collective-permute-start | bytes 442376 | tf_op jit(solution)/shard_map/ppermute | solution.py:545
  109.9 4.1 %collective-permute-start.24 = (bf16[6,24,512]{2,1,0:T(8,128)(2,1)S(1)}, bf16[6,24,512]{2,1,0:T(8,128)(2,1)S(1)}, u32[]{:S(2)}, u32[]{:S(2)}) collective-permute-start(bf16[6,24,512]{2,1,0:T(8,128)(2,1)S(1)} %get-tuple-element.140), channel_id=1, source_target_pairs={{0,48},{1,17},{16,32},{17,1},{32,16},{33,49},{48,0},{49,33},{2,50}... | collective-permute-start | bytes 442376 | tf_op jit(solution)/shard_map/ppermute | solution.py:545
  110.3 16.7 %collective-permute-start.31 = (bf16[72,1536]{1,0:T(8,128)(2,1)S(1)}, bf16[72,1536]{1,0:T(8,128)(2,1)S(1)}, u32[]{:S(2)}, u32[]{:S(2)}) collective-permute-start(bf16[72,1536]{1,0:T(8,128)(2,1)S(1)} %get-tuple-element.153), channel_id=1, source_target_pairs={{0,4},{4,8},{8,12},{12,16},{16,20},{20,24},{24,28},{28,32},{32,36}... | collective-permute-start | bytes 663560 | tf_op jit(solution)/shard_map/ppermute | solution.py:545
  114.6 9.7 %collective-permute-start.25 = (bf16[4,24,512]{2,1,0:T(8,128)(2,1)S(1)}, bf16[4,24,512]{2,1,0:T(8,128)(2,1)S(1)}, u32[]{:S(2)}, u32[]{:S(2)}) collective-permute-start(bf16[4,24,512]{2,1,0:T(8,128)(2,1)S(1)} %get-tuple-element.142), channel_id=1, source_target_pairs={{0,4},{1,13},{4,0},{5,9},{8,12},{9,5},{12,8},{13,1},{2,6},{3,15},{... | collective-permute-start | bytes 294920 | tf_op jit(solution)/shard_map/ppermute | solution.py:545
  114.9 9.4 %collective-permute-start.26 = (bf16[4,24,512]{2,1,0:T(8,128)(2,1)S(1)}, bf16[4,24,512]{2,1,0:T(8,128)(2,1)S(1)}, u32[]{:S(2)}, u32[]{:S(2)}) collective-permute-start(bf16[4,24,512]{2,1,0:T(8,128)(2,1)S(1)} %get-tuple-element.144), channel_id=1, source_target_pairs={{0,16},{1,49},{16,0},{17,33},{32,48},{33,17},{48,32},{49,1},{2,18}... | collective-permute-start | bytes 294920 | tf_op jit(solution)/shard_map/ppermute | solution.py:545
  118.0 6.3 %collective-permute-start.27 = (bf16[4,24,512]{2,1,0:T(8,128)(2,1)S(1)}, bf16[4,24,512]{2,1,0:T(8,128)(2,1)S(1)}, u32[]{:S(2)}, u32[]{:S(2)}) collective-permute-start(bf16[4,24,512]{2,1,0:T(8,128)(2,1)S(1)} %get-tuple-element.146), channel_id=1, source_target_pairs={{0,2},{1,67},{2,0},{3,65},{64,66},{65,3},{66,64},{67,1},{4,6},{5,7... | collective-permute-start | bytes 294920 | tf_op jit(solution)/shard_map/ppermute | solution.py:545
  118.9 8.1 %collective-permute-start.32 = (bf16[36,1536]{1,0:T(8,128)(2,1)S(1)}, bf16[36,1536]{1,0:T(8,128)(2,1)S(1)}, u32[]{:S(2)}, u32[]{:S(2)}) collective-permute-start(bf16[36,1536]{1,0:T(8,128)(2,1)S(1)} %last_rows.1), channel_id=1, source_target_pairs={{0,1},{1,2},{2,3},{3,0},{4,5},{5,6},{6,7},{7,4},{8,9},{9,10},{10,1... | collective-permute-start | bytes 331784 | tf_op jit(solution)/shard_map/ppermute | solution.py:545
  125.0 3.4 %collective-permute-start.28 = (bf16[3,24,512]{2,1,0:T(8,128)(2,1)S(1)}, bf16[3,24,512]{2,1,0:T(8,128)(2,1)S(1)}, u32[]{:S(2)}, u32[]{:S(2)}) collective-permute-start(bf16[3,24,512]{2,1,0:T(8,128)(2,1)S(1)} %get-tuple-element.148), channel_id=1, source_target_pairs={{0,12},{1,5},{4,8},{5,1},{8,4},{9,13},{12,0},{13,9},{2,14},{3,7},{... | collective-permute-start | bytes 221192 | tf_op jit(solution)/shard_map/ppermute | solution.py:545
  126.7 3.2 %collective-permute-start.29 = (bf16[3,24,512]{2,1,0:T(8,128)(2,1)S(1)}, bf16[3,24,512]{2,1,0:T(8,128)(2,1)S(1)}, u32[]{:S(2)}, u32[]{:S(2)}) collective-permute-start(bf16[3,24,512]{2,1,0:T(8,128)(2,1)S(1)} %get-tuple-element.150), channel_id=1, source_target_pairs={{0,48},{1,17},{16,32},{17,1},{32,16},{33,49},{48,0},{49,33},{2,50}... | collective-permute-start | bytes 221192 | tf_op jit(solution)/shard_map/ppermute | solution.py:545
  126.7 3.2 %collective-permute-start.30 = (bf16[3,24,512]{2,1,0:T(8,128)(2,1)S(1)}, bf16[3,24,512]{2,1,0:T(8,128)(2,1)S(1)}, u32[]{:S(2)}, u32[]{:S(2)}) collective-permute-start(bf16[3,24,512]{2,1,0:T(8,128)(2,1)S(1)} %get-tuple-element.152), channel_id=1, source_target_pairs={{0,66},{1,3},{2,64},{3,1},{64,2},{65,67},{66,0},{67,65},{4,70},{5,... | collective-permute-start | bytes 221192 | tf_op jit(solution)/shard_map/ppermute | solution.py:545
  129.9 10.5 %collective-permute-start.33 = (bf16[9,24,512]{2,1,0:T(8,128)(2,1)S(1)}, bf16[9,24,512]{2,1,0:T(8,128)(2,1)S(1)}, u32[]{:S(2)}, u32[]{:S(2)}) collective-permute-start(bf16[9,24,512]{2,1,0:T(8,128)(2,1)S(1)} %total.1.own), channel_id=1, source_target_pairs={{0,1},{1,0},{2,3},{3,2},{4,5},{5,4},{6,7},{7,6},{8,9},{9,8},{10,11... | collective-permute-start | bytes 663560 | tf_op jit(solution)/shard_map/ppermute | solution.py:545
  (2 other events, 1.4 us)

commit v3 on v2

--- a/solution.py
+++ b/solution.py
@@ -31,10 +31,6 @@
 Y = ("yh", "yl")
 ORDERS = (("x", "y", "z"), ("y", "z", "x"), ("z", "x", "y"))
 AXES = {"x": ("x",), "y": Y, "z": ("z",)}
-KEEP = np.array([[[0, 3], [1, 2], [1, 2], [0, 3]], [[0, 1], [0, 1], [2, 3], [2, 3]]], np.int32)
-SEND = np.array([[[1, 2], [0, 3], [0, 3], [1, 2]], [[2, 3], [2, 3], [0, 1], [0, 1]]], np.int32)
-FIRST = np.concatenate([KEEP, SEND], -1)
-SECOND = np.array([[[0, 1], [0, 1], [1, 0], [1, 0]], [[0, 1], [1, 0], [0, 1], [1, 0]]], np.int32)
 BLOCK = (24, 512)
 EXTRA = 2
 NT = (((1,), (1,)), ((), ()))
@@ -135,7 +131,7 @@
 
 def two_heads(scale_ref, head):
     top = lax.broadcasted_iota(jnp.int32, (2 * WIN, 1), 0) < WIN
-    return jnp.where(top, scale_ref[head], scale_ref[head + 1])
+    return jnp.exp(jnp.where(top, scale_ref[head], scale_ref[head + 1]))
 
 
 def softmax_of(scores):
@@ -171,20 +167,26 @@
             rows[r * 12 : (r + 1) * 12, t * 128 : (t + 1) * 128] = grid[t, pl.ds(r, 12, stride=24), :]
 
 
-def first_body(own, low, upper):
-    low[...] = jnp.concatenate([own[j].astype(F32)[:SHIFT_H] for j in range(12)], 0).astype(BF16)
+def first_body(own, low, upper, part, sem):
+    copy = pltpu.make_async_copy(own.at[:, :16], part, sem)
+    copy.start()
+    copy.wait()
+    low[...] = jnp.concatenate([part[j].astype(F32)[:SHIFT_H] for j in range(12)], 0).astype(BF16)
     upper[...] = jnp.concatenate(
-        [own[j].astype(F32)[SHIFT_H : SHIFT_H + HALF_ROWS] for j in range(SHIFT_W)], 0
+        [part[j].astype(F32)[SHIFT_H : SHIFT_H + HALF_ROWS] for j in range(SHIFT_W)], 0
     ).astype(BF16)
 
 
-def to_east_body(own, low, out):
+def to_east_body(own, low, out, part, sem):
+    copy = pltpu.make_async_copy(own.at[SHIFT_W:, 8:], part, sem)
+    copy.start()
+    copy.wait()
     out[...] = jnp.concatenate(
         [
             piece
             for i in range(SHIFT_W)
             for piece in (
-                own[SHIFT_W + i].astype(F32)[SHIFT_H + HALF_ROWS :],
+                part[i].astype(F32)[SHIFT_H + HALF_ROWS - 8 :],
                 f32_rows(low, (SHIFT_W + i) * SHIFT_H, SHIFT_H),
             )
         ],
@@ -193,7 +195,7 @@
 
 
 def forward_body(
-    scale, own, east, west, low, w, bias, pair_bias, row, col, x, projected, attended, grid, rows, wide, sems
+    scale, own, east, west, low, w, query_bias, value_bias, pair_bias, row, col, x, projected, attended, grid, rows, wide, sems
 ):
     copies = []
     for g in range(3):
@@ -208,7 +210,10 @@
         for j in range(3):
             lo = j * HC + g * 256
             copies[3 * g + j].wait()
-            projected[:, lo : lo + 256] = dot(x[...], wide[:, lo : lo + 256]) + bias[:, lo : lo + 256]
+            product = dot(x[...], wide[:, lo : lo + 256])
+            if j != 1:
+                product = product + (query_bias, None, value_bias)[j][:, g * 256 : (g + 1) * 256]
+            projected[:, lo : lo + 256] = product
         for half in range(2):
             lo = g * 256 + half * 128
             head = lo // HEAD_DIM
@@ -272,7 +277,7 @@
     scale_line = jnp.zeros((1, 128), F32)
     for i in range(2):
         one = jnp.sum(jnp.sum(scaled[i * WIN : (i + 1) * WIN], 0, keepdims=True), 1, keepdims=True)
-        scale_line = scale_line + jnp.where(lane == head + i, one * scale[head + i], 0.0)
+        scale_line = scale_line + jnp.where(lane == head + i, one * factor[i * WIN : i * WIN + 1], 0.0)
     q_grad = q_inv * (gq - q * head_sum(q * gq))
     k_grad = k_inv * (gk - k * head_sum(k * gk))
     lines = jnp.concatenate(
@@ -394,7 +399,24 @@
     return 24 * ((y // 2) * 32 + place["x"] * 8 + place["z"] * 2 + y % 2)
 
 
-def weight_body(order, x0, x1, p0, p1, m0, m1, a0, a1, s0, s1, *rest):
+def first_order(core, at):
+    end, left = (at == 0) | (at == 3), at < 2
+    zero = [jnp.where(end, a, b) for a, b in ((0, 1), (3, 2), (1, 0), (2, 3))]
+    one = [jnp.where(left, a, b) for a, b in ((0, 2), (1, 3), (2, 0), (3, 1))]
+    return [jnp.where(core == 0, a, b) for a, b in zip(zero, one)]
+
+
+def second_order(core, at):
+    kept = jnp.where(core == 0, at // 2, at % 2)
+    return [kept, 1 - kept]
+
+
+def order_of(place, j, axis, second):
+    at = place[1 + "xyz".index(ORDERS[j][axis])]
+    return (second_order if second else first_order)(place[0], at)
+
+
+def weight_body(place, x0, x1, p0, p1, m0, m1, a0, a1, s0, s1, *rest):
     outs, (left, grads, mixed, heads, total, sems) = rest[:6], rest[6:]
     pairs = ((x0, x1, left), (p0, p1, grads), (m0, m1, mixed), (a0, a1, heads))
     copies = []
@@ -420,11 +442,12 @@
             total[at, j * 512 + HALF : (j + 1) * 512] = part[:, j * 128 : (j + 1) * 128]
     for j in range(3):
         cols = slice(j * 512, (j + 1) * 512)
+        order = order_of(place, j, 0, False)
         for i in range(4):
             out = outs[2 * j + i // 2]
             for second in range(4):
                 for third in range(4):
-                    places = (order[4 * j + i], second, third)
+                    places = (order[i], second, third)
                     start = row_of(dict(zip(ORDERS[j], places)))
                     rows = pl.ds(pl.multiple_of(start, 8), 24)
                     out[i % 2 * 16 + second * 4 + third] = total[rows, cols].astype(BF16)
@@ -433,14 +456,15 @@
         write_coded([value[:24], value[24:]], value[:24, 384:], outs[2 * j : 2 * j + 2], 32)
 
 
-def halve_body(count, size, order, *refs):
+def halve_body(count, size, axis, place, *refs):
     ins, outs = refs[:6], refs[6:]
     for j in range(3):
         keep, recv = ins[2 * j : 2 * j + 2]
+        order = order_of(place, j, axis, count == 1)
         for i in range(2 * count):
             out = outs[2 * j + i // count]
             for b in range(size):
-                at = order[2 * count * j + i] * size + b
+                at = order[i] * size + b
                 out[i % count * size + b] = (keep[at].astype(F32) + recv[at].astype(F32)).astype(BF16)
         add_coded(keep, recv, outs[2 * j : 2 * j + 2], 2 * count * size, count * size)
 
@@ -574,7 +598,14 @@
 
 def first_messages(grid):
     return call(
-        first_body, [shape((36, C), BF16), shape((72, C), BF16)], [grid], scalars=0, name="first"
+        first_body,
+        [shape((36, C), BF16), shape((72, C), BF16)],
+        [grid],
+        scalars=0,
+        scratch=[pltpu.VMEM((12, 16, C), BF16), pltpu.SemaphoreType.DMA],
+        vmem=60,
+        far=(0,),
+        name="first",
     )
 
 
@@ -583,7 +614,14 @@
     low = lat_step(low, -1)
     east = lon_step(upper, -1)
     (lower,) = call(
-        to_east_body, [shape((72, C), BF16)], [grid, low], scalars=0, name="to_east"
+        to_east_body,
+        [shape((72, C), BF16)],
+        [grid, low],
+        scalars=0,
+        scratch=[pltpu.VMEM((SHIFT_W, 16, C), BF16), pltpu.SemaphoreType.DMA],
+        vmem=60,
+        far=(0,),
+        name="to_east",
     )
     return east, low, lower
 
@@ -601,11 +639,13 @@
     norm_gain,
 ):
     core = lax.axis_index("c")
-    place = {"x": lax.axis_index("x"), "z": lax.axis_index("z"), "y": lax.axis_index("yh") * 2 + lax.axis_index("yl")}
+    place = jnp.stack(
+        [core, lax.axis_index("x"), lax.axis_index("yh") * 2 + lax.axis_index("yl"), lax.axis_index("z")]
+    ).astype(jnp.int32)
     mine = core.astype(jnp.int32).reshape(1)
     theirs = 1 - mine
-    scale = jnp.exp(logit_scale)
-    bias = jnp.concatenate([query_bias, jnp.zeros_like(query_bias), value_bias]).reshape(1, -1)
+    scale = logit_scale
+    query_row, value_row = query_bias.reshape(1, HC), value_bias.reshape(1, HC)
     pair_rows = pair_bias.reshape(HEADS * WIN, WIN)
     gain = norm_gain.reshape(1, C)
 
@@ -623,7 +663,7 @@
     x, projected, attended = call(
         forward_body,
         [shape((CELLS, C), BF16), shape((CELLS, 3 * HC), F32), shape((CELLS, HC), BF16)],
-        [scale, features, *came, qkv_weight, bias, pair_rows, region_row, region_col],
+        [scale, features, *came, qkv_weight, query_row, value_row, pair_rows, region_row, region_col],
         scratch=[
             pltpu.VMEM((12, CELLS, 128), F32),
             pltpu.VMEM((CELLS, C), F32),
@@ -701,11 +741,9 @@
                 (shape((144, 512), F32), (48, 512), lambda i, side, scale: (i, 0)),
             ],
             flops=2 * CELLS * WIN * 128 * 6 * 3,
+            vmem=16,
             name="attention",
         )
-
-    def tables(values, step):
-        return jnp.concatenate([jnp.asarray(values)[core, place[names[step]]] for names in ORDERS])
 
     grads_other = core_swap(grads_theirs)
     small_other = core_swap(small_theirs)
@@ -715,7 +753,7 @@
         weight_body,
         [shape((32 + EXTRA,) + BLOCK, BF16)] * 6,
         [
-            tables(FIRST, 0),
+            place,
             x,
             x_other,
             grads_mine,
@@ -737,9 +775,11 @@
         ],
         near=tuple(range(1, 9)),
         flops=4 * CELLS * C * C,
+        vmem=26,
         name="weights",
     )
     side, parts = lax.optimization_barrier((mine, parts))
+    order = place
     whole = lambda i, side: (0, 0)
     to_east, to_west, stay_low, stay_high = grid_call(
         branch_body,
@@ -753,18 +793,20 @@
         [(shape((72, C), BF16), (72, 256), lambda i, side: (0, i))] * 4,
         scratch=[pltpu.VMEM((CELLS, 3 * HC), BF16), pltpu.VMEM((2, CELLS, 128), F32)],
         flops=2 * CELLS * C * 3 * HC,
+        vmem=16,
         name="branch",
     )
     from_west = lon_step(to_east, 1)
     from_east = lon_step(to_west, -1)
     (last,) = call(
-        last_rows_body, [shape((36, C), BF16)], [stay_high, from_east], scalars=0, name="last_rows"
+        last_rows_body, [shape((36, C), BF16)], [stay_high, from_east], scalars=0, vmem=6, name="last_rows"
     )
     (input_grad,) = call(
         merge_body,
         [shape((12, 24, C), BF16)],
         [upstream, stay_low, stay_high, from_west, from_east, lat_step(last, 1)],
         scalars=0,
+        vmem=10,
         name="merge",
     )
     for step in range(6):
@@ -775,18 +817,16 @@
             break
         left = 32 >> step
         if step % 2 == 0:
-            body = functools.partial(halve_body, 1, left // 2)
-            order = tables(SECOND, step // 2)
+            body = functools.partial(halve_body, 1, left // 2, step // 2)
         else:
-            body = functools.partial(halve_body, 2, left // 4)
-            order = tables(FIRST, step // 2 + 1)
+            body = functools.partial(halve_body, 2, left // 4, step // 2 + 1)
         if step == 0:
             order, stay_low = lax.optimization_barrier((order, stay_low))
         if step == 3:
             order, last = lax.optimization_barrier((order, last))
-        parts = call(body, [shape((left // 2 + EXTRA,) + BLOCK, BF16)] * 6, [order, *terms], name="halve")
+        parts = call(body, [shape((left // 2 + EXTRA,) + BLOCK, BF16)] * 6, [order, *terms], vmem=10, name="halve")
     terms, input_grad = lax.optimization_barrier((terms, input_grad))
-    (sums,) = call(total_body, [shape((9,) + BLOCK, BF16)], terms, scalars=0, name="total")
+    (sums,) = call(total_body, [shape((9,) + BLOCK, BF16)], terms, scalars=0, vmem=6, name="total")
     sums_other = core_swap(sums)
     qkv_weight_grad, proj_weight_grad, pair_grad, gain_grad, query_bias_grad, value_bias_grad, scale_grad = call(
         finish_body,
@@ -800,6 +840,7 @@
             shape((HEADS,), F32),
         ],
         [mine, sums, sums_other],
+        vmem=8,
         name="finish",
     )
     pair_grad = pair_grad.reshape(HEADS, WIN, WIN)

time: 142 us -> 141 us (level)
  Pallas kernels: 51.9 us -> 53.6 us
    pallas_call x16, Pallas kernels: 39.8 us -> 44.2 us  [call(): pl.pallas_call(body, out_shape=list(outs), in_specs=specs, out_specs=[VME...]
    pallas_call x2, Pallas kernels: 12.1 us -> 9.43 us  [grid_call(): pl.pallas_call(body, grid_spec=spec, out_shape=results, compiler_params=p...]
    dynamic_slice x1, local copies, waits for them, and re-layouts: 0.05 us -> 1.77 us  [shards(): lax.dynamic_slice(attended, (0, theirs[0] * HALF), (CELLS, HALF))]
    squeeze x2 -> x0, local copies, waits for them, and re-layouts: 1.59 us -> none  [tables(): jnp.asarray(values)[core, place[names[step]]]]
    unnamed x32 -> x38, local copies, waits for them, and re-layouts: 6.9 us -> 5.76 us
  transfers between devices with their start and end apart: 34 -> 34, of which waited for: 14 -> 10; matrix products, arithmetic and copies ran while one was open for 3% -> 2% of each run, Pallas kernels for 26% -> 29%
where the time goes in v3:
time: 141 us; the launch traced here: 140 us
  starting transfers between devices  59.1 us (42%)
  Pallas kernels  53.6 us (38%)
  waiting for transfers between devices  18 us (13%)
  local copies, waits for them, and re-layouts  8.57 us (6%)
    ppermute x34, starting transfers between devices, permuted(): return lax.ppermute(value, axes, pairs)  59.1 us
    pallas_call x16, Pallas kernels, call(): pl.pallas_call(body, out_shape=list(outs), in_specs=specs, out_specs=[VME...  44.2 us
    ppermute x34, waiting for transfers between devices, permuted(): return lax.ppermute(value, axes, pairs)  18 us
    pallas_call x2, Pallas kernels, grid_call(): pl.pallas_call(body, grid_spec=spec, out_shape=results, compiler_params=p...  9.43 us
    unnamed x38, local copies, waits for them, and re-layouts  5.76 us
  transfers between devices with their start and end apart: 34, of which 10 were waited for; matrix products, arithmetic and copies ran while one was open for 2% of the time, Pallas kernels for 29%

profile of v3, /device:TPU:1, one launch (start us, length us, event | category | flops | bytes accessed | tf_op | source)
XLA Modules:
  0.0 140.5 jit_solution(12135383637547455448)
XLA Ops:
  0.7 2.0 %first.2 = (bf16[36,1536]{1,0:T(8,128)(2,1)}, bf16[72,1536]{1,0:T(8,128)(2,1)}) custom-call(bf16[12,24,1536]{2,1,0:T(8,128)(2,1)} %bitcast.16), custom_call_target="tpu_custom_call" | custom-call | bytes 1216512 | tf_op jit(solution)/shard_map/first/pallas_call | solution.py:60
  2.7 1.5 %collective-permute-start.1 = (bf16[36,1536]{1,0:T(8,128)(2,1)}, bf16[36,1536]{1,0:T(8,128)(2,1)S(1)}, u32[]{:S(2)}, u32[]{:S(2)}) collective-permute-start(bf16[36,1536]{1,0:T(8,128)(2,1)} %get-tuple-element.89), channel_id=1, source_target_pairs={{0,3},{1,0},{2,1},{3,2},{4,7},{5,4},{6,5},{7,6},{8,11},{9,8},{10,9... | collective-permute-start | bytes 331784 | tf_op jit(solution)/shard_map/ppermute | solution.py:569
  4.2 8.7 %collective-permute-start = (bf16[72,1536]{1,0:T(8,128)(2,1)}, bf16[72,1536]{1,0:T(8,128)(2,1)S(1)}, u32[]{:S(2)}, u32[]{:S(2)}) collective-permute-start(bf16[72,1536]{1,0:T(8,128)(2,1)} %get-tuple-element.88), channel_id=1, source_target_pairs={{0,124},{4,0},{8,4},{12,8},{16,12},{20,16},{24,20},{28,24},{32,28}... | collective-permute-start | bytes 663560 | tf_op jit(solution)/shard_map/ppermute | solution.py:569
  12.8 0.7 reshape.40.query_bias
  14.2 2.6 %to_east.2 = bf16[72,1536]{1,0:T(8,128)(2,1)} custom-call(bf16[12,24,1536]{2,1,0:T(8,128)(2,1)} %bitcast.17, bf16[36,1536]{1,0:T(8,128)(2,1)} %copy-done.6), custom_call_target="tpu_custom_call" | custom-call | bytes 1216512 | tf_op jit(solution)/shard_map/to_east/pallas_call | solution.py:60
  16.9 1.9 %first.3 = (bf16[36,1536]{1,0:T(8,128)(2,1)}, bf16[72,1536]{1,0:T(8,128)(2,1)}) custom-call(bf16[12,24,1536]{2,1,0:T(8,128)(2,1)} %bitcast.12), custom_call_target="tpu_custom_call" | custom-call | bytes 1216512 | tf_op jit(solution)/shard_map/first/pallas_call | solution.py:60
  18.8 1.1 collective-permute-start.6
  20.0 7.5 %collective-permute-start.5 = (bf16[72,1536]{1,0:T(8,128)(2,1)}, bf16[72,1536]{1,0:T(8,128)(2,1)S(1)}, u32[]{:S(2)}, u32[]{:S(2)}) collective-permute-start(bf16[72,1536]{1,0:T(8,128)(2,1)} %get-tuple-element.96), channel_id=1, source_target_pairs={{0,124},{4,0},{8,4},{12,8},{16,12},{20,16},{24,20},{28,24},{32,28}... | collective-permute-start | bytes 663560 | tf_op jit(solution)/shard_map/ppermute | solution.py:569
  28.2 2.6 %to_east.3 = bf16[72,1536]{1,0:T(8,128)(2,1)} custom-call(bf16[12,24,1536]{2,1,0:T(8,128)(2,1)} %bitcast.13, bf16[36,1536]{1,0:T(8,128)(2,1)} %copy-done.8), custom_call_target="tpu_custom_call" | custom-call | bytes 1216512 | tf_op jit(solution)/shard_map/to_east/pallas_call | solution.py:60
  31.3 0.9 copy-done.7
  32.2 10.6 %forward.1 = (bf16[288,1536]{1,0:T(8,128)(2,1)}, f32[288,2304]{1,0:T(8,128)}, bf16[288,768]{1,0:T(8,128)(2,1)S(1)}) custom-call(f32[12]{0:T(128)S(1)} %copy-done.12, bf16[12,24,1536]{2,1,0:T(8,128)(2,1)S(1)} %bitcast.18, bf16[72,1536]{1,0:T(8,128)(2,1)S(1)} %collective-permute-done.east, bf16[72,1536]{1,0:T(8,128)(2,1)S(1)} %collective-permute-done.2.west, ...), custom_call_target="tpu_custom_call" | custom-call | flops 2038431744 | bytes 12754224 | tf_op jit(solution)/shard_map/forward/pallas_call | solution.py:60
  42.8 0.7 collective-permute-start.4
  43.5 0.7 copy-done.10
  44.2 0.9 copy-done.11
  45.1 10.2 %backward.1 = (bf16[288,1536]{1,0:T(8,128)(2,1)}, f32[288,768]{1,0:T(8,128)}, f32[1,1536]{1,0:T(1,128)S(1)}, bf16[288,1152]{1,0:T(8,128)(2,1)}, f32[144,512]{1,0:T(8,128)S(1)}) custom-call(s32[1]{0:T(128)S(6)} %sub.3.side, f32[12]{0:T(128)S(1)} %copy-done.12, bf16[288,768]{1,0:T(8,128)(2,1)S(1)} %get-tuple-element.94.attended, ...), custom_call_target="tpu_custom_call" | custom-call | flops 1454505984 | bytes 9884980 | tf_op jit(solution)/shard_map/backward/pallas_call | solution.py:60
  55.3 0.7 copy-done.13
  57.0 1.8 %constant_dynamic-slice_fusion = (bf16[288,384]{1,0:T(8,128)(2,1)}, bf16[288,384]{1,0:T(8,128)(2,1)S(1)}) fusion(bf16[288,768]{1,0:T(8,128)(2,1)} %copy-done.4, s32[]{:T(128)S(6)} %select_n.7, s32[]{:T(128)S(6)} %select_n.6), kind=kLoop, calls=%fused_computation.2 | loop fusion | bytes 884744 | tf_op jit(solution)/shard_map/dynamic_slice | solution.py:715
  58.9 1.2 copy-done.5
  60.1 4.5 %attention.1 = (bf16[288,1152]{1,0:T(8,128)(2,1)S(1)}, f32[144,512]{1,0:T(8,128)S(1)}) custom-call(s32[1]{0:T(128)} %bitcast.side.core, f32[12]{0:T(128)S(1)} %copy-done.12, f32[288,2304]{1,0:T(8,128)S(1)} %copy-done, f32[288,2304]{1,0:T(8,128)S(1)} %copy-done, f32[288,2304]{1,0:T(8,128)S(1)} %copy-done, f32[288,768]{1,0:T(8,128)S(1)} %copy-done.5, ...), custom_call_target="tpu_custom_call" | custom-call | flops 95551488 | bytes 10063104 | tf_op jit(solution)/shard_map/attention/pallas_call | solution.py:82
  64.6 7.9 %weights.1 = (bf16[34,24,512]{2,1,0:T(8,128)(2,1)S(1)}, bf16[34,24,512]{2,1,0:T(8,128)(2,1)S(1)}, bf16[34,24,512]{2,1,0:T(8,128)(2,1)S(1)}, bf16[34,24,512]{2,1,...) custom-call(s32[4]{0:T(128)S(1)} %pad_add_fusion.1.place, ...), custom_call_target="tpu_custom_call" | custom-call | flops 2717908992 | bytes 10911760 | tf_op jit(solution)/shard_map/weights/pallas_call | solution.py:60
  73.0 7.7 %collective-permute-start.15 = (bf16[34,24,512]{2,1,0:T(8,128)(2,1)S(1)}, bf16[34,24,512]{2,1,0:T(8,128)(2,1)S(1)}, u32[]{:S(2)}, u32[]{:S(2)}) collective-permute-start(bf16[34,24,512]{2,1,0:T(8,128)(2,1)S(1)} %get-tuple-element.122), channel_id=1, source_target_pairs={{0,4},{1,13},{4,0},{5,9},{8,12},{9,5},{12,8},{13,1},{2,6},{3,15},{... | collective-permute-start | bytes 2506760 | tf_op jit(solution)/shard_map/ppermute | solution.py:569
  80.8 5.0 %branch.1 = (bf16[72,1536]{1,0:T(8,128)(2,1)S(1)}, bf16[72,1536]{1,0:T(8,128)(2,1)S(1)}, bf16[72,1536]{1,0:T(8,128)(2,1)S(1)}, bf16[72,1536]{1,0:T(8,128)(2,1)S(1)}) custom-call(s32[1]{0:T(128)} %bitcast.side.core, bf16[1536,2304]{1,0:T(8,128)(2,1)S(1)} %bitcast.11, bf16[288,1152]{1,0:T(8,128)(2,1)S(1)} %get-tuple-element.100.p0.own, ...), custom_call_target="tpu_custom_call" | custom-call | flops 2038431744 | bytes 9289728 | tf_op jit(solution)/shard_map/branch/pallas_call | solution.py:82
  85.8 4.9 %collective-permute-done.15.refs_5_ = bf16[34,24,512]{2,1,0:T(8,128)(2,1)S(1)} collective-permute-done((bf16[34,24,512]{2,1,0:T(8,128)(2,1)S(1)}, bf16[34,24,512]{2,1,0:T(8,128)(2,1)S(1)}, u32[]{:S(2)}, u32[]{:S(2)}) %collective-permute-start.15) | collective-permute-done | bytes 835616 | tf_op jit(solution)/shard_map/ppermute | solution.py:569
  90.7 1.2 halve.5
  92.2 7.2 %collective-permute-done.16.refs_1_ = bf16[18,24,512]{2,1,0:T(8,128)(2,1)S(1)} collective-permute-done((bf16[18,24,512]{2,1,0:T(8,128)(2,1)S(1)}, bf16[18,24,512]{2,1,0:T(8,128)(2,1)S(1)}, u32[]{:S(2)}, u32[]{:S(2)}) %collective-permute-start.16) | collective-permute-done | bytes 442400 | tf_op jit(solution)/shard_map/ppermute | solution.py:569
  99.6 0.9 halve.6
  100.5 0.9 collective-permute-start.19
  101.3 2.7 %collective-permute-start.20 = (bf16[10,24,512]{2,1,0:T(8,128)(2,1)S(1)}, bf16[10,24,512]{2,1,0:T(8,128)(2,1)S(1)}, u32[]{:S(2)}, u32[]{:S(2)}) collective-permute-start(bf16[10,24,512]{2,1,0:T(8,128)(2,1)S(1)} %get-tuple-element.132), channel_id=1, source_target_pairs={{0,4},{1,13},{4,0},{5,9},{8,12},{9,5},{12,8},{13,1},{2,6},{3,15},{... | collective-permute-start | bytes 737288 | tf_op jit(solution)/shard_map/ppermute | solution.py:569
  104.1 4.4 %collective-permute-start.12 = (bf16[72,1536]{1,0:T(8,128)(2,1)S(1)}, bf16[72,1536]{1,0:T(8,128)(2,1)S(1)}, u32[]{:S(2)}, u32[]{:S(2)}) collective-permute-start(bf16[72,1536]{1,0:T(8,128)(2,1)S(1)} %get-tuple-element.115), channel_id=1, source_target_pairs={{0,124},{4,0},{8,4},{12,8},{16,12},{20,16},{24,20},{28,24},{32,28}... | collective-permute-start | bytes 663560 | tf_op jit(solution)/shard_map/ppermute | solution.py:569
  108.5 0.9 collective-permute-done.20.refs_3_
  109.4 0.9 collective-permute-done.21.refs_5_
  110.3 0.7 halve.7
  111.0 0.8 collective-permute-start.22
  112.3 1.5 %collective-permute-start.31 = (bf16[72,1536]{1,0:T(8,128)(2,1)S(1)}, bf16[72,1536]{1,0:T(8,128)(2,1)S(1)}, u32[]{:S(2)}, u32[]{:S(2)}) collective-permute-start(bf16[72,1536]{1,0:T(8,128)(2,1)S(1)} %get-tuple-element.153), channel_id=1, source_target_pairs={{0,4},{4,8},{8,12},{12,16},{16,20},{20,24},{24,28},{28,32},{32,36}... | collective-permute-start | bytes 663560 | tf_op jit(solution)/shard_map/ppermute | solution.py:569
  113.8 1.2 collective-permute-done.22.refs_1_
  115.1 0.8 collective-permute-done.23.refs_3_
  115.8 0.6 halve.8
  116.5 2.3 %collective-permute-start.25 = (bf16[4,24,512]{2,1,0:T(8,128)(2,1)S(1)}, bf16[4,24,512]{2,1,0:T(8,128)(2,1)S(1)}, u32[]{:S(2)}, u32[]{:S(2)}) collective-permute-start(bf16[4,24,512]{2,1,0:T(8,128)(2,1)S(1)} %get-tuple-element.142), channel_id=1, source_target_pairs={{0,4},{1,13},{4,0},{5,9},{8,12},{9,5},{12,8},{13,1},{2,6},{3,15},{... | collective-permute-start | bytes 294920 | tf_op jit(solution)/shard_map/ppermute | solution.py:569
  118.8 1.3 collective-permute-start.26
  120.1 0.8 collective-permute-start.27
  121.0 7.3 %collective-permute-start.32 = (bf16[36,1536]{1,0:T(8,128)(2,1)S(1)}, bf16[36,1536]{1,0:T(8,128)(2,1)S(1)}, u32[]{:S(2)}, u32[]{:S(2)}) collective-permute-start(bf16[36,1536]{1,0:T(8,128)(2,1)S(1)} %last_rows.1), channel_id=1, source_target_pairs={{0,1},{1,2},{2,3},{3,0},{4,5},{5,6},{6,7},{7,4},{8,9},{9,10},{10,1... | collective-permute-start | bytes 331784 | tf_op jit(solution)/shard_map/ppermute | solution.py:569
  128.9 1.7 %collective-permute-start.28 = (bf16[3,24,512]{2,1,0:T(8,128)(2,1)S(1)}, bf16[3,24,512]{2,1,0:T(8,128)(2,1)S(1)}, u32[]{:S(2)}, u32[]{:S(2)}) collective-permute-start(bf16[3,24,512]{2,1,0:T(8,128)(2,1)S(1)} %get-tuple-element.148), channel_id=1, source_target_pairs={{0,12},{1,5},{4,8},{5,1},{8,4},{9,13},{12,0},{13,9},{2,14},{3,7},{... | collective-permute-start | bytes 221192 | tf_op jit(solution)/shard_map/ppermute | solution.py:569
  130.6 1.2 collective-permute-start.30
  131.8 1.3 merge.1
  133.2 0.7 collective-permute-done.29.refs_3_
  133.9 4.6 %collective-permute-start.33 = (bf16[9,24,512]{2,1,0:T(8,128)(2,1)S(1)}, bf16[9,24,512]{2,1,0:T(8,128)(2,1)S(1)}, u32[]{:S(2)}, u32[]{:S(2)}) collective-permute-start(bf16[9,24,512]{2,1,0:T(8,128)(2,1)S(1)} %total.1.own), channel_id=1, source_target_pairs={{0,1},{1,0},{2,3},{3,2},{4,5},{5,4},{6,7},{7,6},{8,9},{9,8},{10,11... | collective-permute-start | bytes 663560 | tf_op jit(solution)/shard_map/ppermute | solution.py:569
  138.5 1.1 collective-permute-done.33.other
  139.6 0.9 finish.1
  (87 shorter events, 5.3 us)
Async XLA Ops:
  0.6 30.7 %copy-start.2 = (bf16[24,12,1536]{2,0,1:T(8,128)(2,1)S(1)}, bf16[24,12,1536]{2,0,1:T(8,128)(2,1)}, u32[]{:S(2)}) copy-start(bf16[24,12,1536]{2,0,1:T(8,128)(2,1)} %param.10) | copy-start | bytes 2654212
  0.6 19.2 %copy-start.14 = (s32[24,12]{0,1:T(8,128)S(1)}, s32[24,12]{0,1:T(8,128)}, u32[]{:S(2)}) copy-start(s32[24,12]{0,1:T(8,128)} %param.12) | copy-start | bytes 3460
  0.7 19.3 %copy-start.16 = (f32[768]{0:T(1024)S(1)}, f32[768]{0:T(1024)}, u32[]{:S(2)}) copy-start(f32[768]{0:T(1024)} %param.15) | copy-start | bytes 9220
  0.7 19.3 %copy-start.15 = (f32[1536]{0:T(1024)S(1)}, f32[1536]{0:T(1024)}, u32[]{:S(2)}) copy-start(f32[1536]{0:T(1024)} %param.19) | copy-start | bytes 18436
  0.7 30.6 %copy-start.12 = (f32[12]{0:T(128)S(1)}, f32[12]{0:T(128)}, u32[]{:S(2)}) copy-start(f32[12]{0:T(128)} %scale.5) | copy-start | bytes 148
  0.7 30.6 %copy-start.3 = (f32[12,72,72]{2,1,0:T(8,128)S(1)}, f32[12,72,72]{2,1,0:T(8,128)}, u32[]{:S(2)}) copy-start(f32[12,72,72]{2,1,0:T(8,128)} %param.17) | copy-start | bytes 746500
  2.7 10.8 %collective-permute-start.1 = (bf16[36,1536]{1,0:T(8,128)(2,1)}, bf16[36,1536]{1,0:T(8,128)(2,1)S(1)}, u32[]{:S(2)}, u32[]{:S(2)}) collective-permute-start(bf16[36,1536]{1,0:T(8,128)(2,1)} %get-tuple-element.89), channel_id=1, source_target_pairs={{0,3},{1,0},{2,1},{3,2},{4,7},{5,4},{6,5},{7,6},{8,11},{9,8},{10,9... | collective-permute-start | bytes 331784 | tf_op jit(solution)/shard_map/ppermute | solution.py:569
  4.2 27.1 %collective-permute-start = (bf16[72,1536]{1,0:T(8,128)(2,1)}, bf16[72,1536]{1,0:T(8,128)(2,1)S(1)}, u32[]{:S(2)}, u32[]{:S(2)}) collective-permute-start(bf16[72,1536]{1,0:T(8,128)(2,1)} %get-tuple-element.88), channel_id=1, source_target_pairs={{0,124},{4,0},{8,4},{12,8},{16,12},{20,16},{24,20},{28,24},{32,28}... | collective-permute-start | bytes 663560 | tf_op jit(solution)/shard_map/ppermute | solution.py:569
  16.8 14.5 %collective-permute-start.2 = (bf16[72,1536]{1,0:T(8,128)(2,1)}, bf16[72,1536]{1,0:T(8,128)(2,1)S(1)}, u32[]{:S(2)}, u32[]{:S(2)}) collective-permute-start(bf16[72,1536]{1,0:T(8,128)(2,1)} %to_east.2), channel_id=1, source_target_pairs={{0,4},{4,8},{8,12},{12,16},{16,20},{20,24},{24,28},{28,32},{32,36}... | collective-permute-start | bytes 663560 | tf_op jit(solution)/shard_map/ppermute | solution.py:569
  18.8 8.7 %collective-permute-start.6 = (bf16[36,1536]{1,0:T(8,128)(2,1)}, bf16[36,1536]{1,0:T(8,128)(2,1)S(1)}, u32[]{:S(2)}, u32[]{:S(2)}) collective-permute-start(bf16[36,1536]{1,0:T(8,128)(2,1)} %get-tuple-element.97), channel_id=1, source_target_pairs={{0,3},{1,0},{2,1},{3,2},{4,7},{5,4},{6,5},{7,6},{8,11},{9,8},{10,9... | collective-permute-start | bytes 331784 | tf_op jit(solution)/shard_map/ppermute | solution.py:569
  19.9 11.0 %collective-permute-start.3 = (s32[12,12]{0,1:T(8,128)S(1)}, s32[12,12]{0,1:T(8,128)S(1)}, u32[]{:S(2)}, u32[]{:S(2)}) collective-permute-start(s32[12,12]{0,1:T(8,128)S(1)} %get-tuple-element.171), channel_id=1, source_target_pairs={{0,4},{4,8},{8,12},{12,16},{16,20},{20,24},{24,28},{28,32},{32,36}... | collective-permute-start | bytes 1736 | tf_op jit(solution)/shard_map/ppermute | solution.py:569
  20.0 23.5 %collective-permute-start.5 = (bf16[72,1536]{1,0:T(8,128)(2,1)}, bf16[72,1536]{1,0:T(8,128)(2,1)S(1)}, u32[]{:S(2)}, u32[]{:S(2)}) collective-permute-start(bf16[72,1536]{1,0:T(8,128)(2,1)} %get-tuple-element.96), channel_id=1, source_target_pairs={{0,124},{4,0},{8,4},{12,8},{16,12},{20,16},{24,20},{28,24},{32,28}... | collective-permute-start | bytes 663560 | tf_op jit(solution)/shard_map/ppermute | solution.py:569
  30.8 13.4 %collective-permute-start.7 = (bf16[72,1536]{1,0:T(8,128)(2,1)}, bf16[72,1536]{1,0:T(8,128)(2,1)S(1)}, u32[]{:S(2)}, u32[]{:S(2)}) collective-permute-start(bf16[72,1536]{1,0:T(8,128)(2,1)} %to_east.3), channel_id=1, source_target_pairs={{0,4},{4,8},{8,12},{12,16},{16,20},{20,24},{24,28},{28,32},{32,36}... | collective-permute-start | bytes 663560 | tf_op jit(solution)/shard_map/ppermute | solution.py:569
  32.2 12.0 %copy-start.9 = (bf16[36,1536]{1,0:T(8,128)(2,1)S(1)}, bf16[36,1536]{1,0:T(8,128)(2,1)}, u32[]{:S(2)}) copy-start(bf16[36,1536]{1,0:T(8,128)(2,1)} %copy-done.8) | copy-start | bytes 331780
  42.8 12.5 %copy-start.4 = (bf16[288,768]{1,0:T(8,128)(2,1)}, bf16[288,768]{1,0:T(8,128)(2,1)S(1)}, u32[]{:S(2)}) copy-start(bf16[288,768]{1,0:T(8,128)(2,1)S(1)} %get-tuple-element.94.attended) | copy-start | bytes 1327108
  42.8 21.8 %collective-permute-start.4 = (bf16[288,1536]{1,0:T(8,128)(2,1)}, bf16[288,1536]{1,0:T(8,128)(2,1)}, u32[]{:S(2)}, u32[]{:S(2)}) collective-permute-start(bf16[288,1536]{1,0:T(8,128)(2,1)} %get-tuple-element.92.x0), channel_id=1, source_target_pairs={{0,1},{1,0},{2,3},{3,2},{4,5},{5,4},{6,7},{7,6},{8,9},{9,8},{10,11... | collective-permute-start | bytes 2654216 | tf_op jit(solution)/shard_map/ppermute | solution.py:569
  44.2 0.9 copy-start.11
  45.1 13.8 %copy-start = (f32[288,2304]{1,0:T(8,128)S(1)}, f32[288,2304]{1,0:T(8,128)}, u32[]{:S(2)}) copy-start(f32[288,2304]{1,0:T(8,128)} %get-tuple-element.93.projected.q_ref.k_ref.v_ref) | copy-start | bytes 7962628
  56.0 8.6 %collective-permute-start.9 = (bf16[288,1536]{1,0:T(8,128)(2,1)}, bf16[288,1536]{1,0:T(8,128)(2,1)}, u32[]{:S(2)}, u32[]{:S(2)}) collective-permute-start(bf16[288,1536]{1,0:T(8,128)(2,1)} %get-tuple-element.102.m0), channel_id=1, source_target_pairs={{0,1},{1,0},{2,3},{3,2},{4,5},{5,4},{6,7},{7,6},{8,9},{9,8},{10,11... | collective-permute-start | bytes 2654216 | tf_op jit(solution)/shard_map/ppermute | solution.py:569
  56.5 8.1 %collective-permute-start.8 = (bf16[288,1152]{1,0:T(8,128)(2,1)}, bf16[288,1152]{1,0:T(8,128)(2,1)}, u32[]{:S(2)}, u32[]{:S(2)}) collective-permute-start(bf16[288,1152]{1,0:T(8,128)(2,1)} %get-tuple-element.101.theirs), channel_id=1, source_target_pairs={{0,1},{1,0},{2,3},{3,2},{4,5},{5,4},{6,7},{7,6},{8,9},{9,8},{10,11... | collective-permute-start | bytes 1990664 | tf_op jit(solution)/shard_map/ppermute | solution.py:569
  56.6 8.0 %collective-permute-start.11 = (f32[144,512]{1,0:T(8,128)}, f32[144,512]{1,0:T(8,128)}, u32[]{:S(2)}, u32[]{:S(2)}) collective-permute-start(f32[144,512]{1,0:T(8,128)} %copy-done.13), channel_id=1, source_target_pairs={{0,1},{1,0},{2,3},{3,2},{4,5},{5,4},{6,7},{7,6},{8,9},{9,8},{10,11... | collective-permute-start | bytes 884744 | tf_op jit(solution)/shard_map/ppermute | solution.py:569
  58.8 5.8 %collective-permute-start.10 = (bf16[288,384]{1,0:T(8,128)(2,1)}, bf16[288,384]{1,0:T(8,128)(2,1)}, u32[]{:S(2)}, u32[]{:S(2)}) collective-permute-start(bf16[288,384]{1,0:T(8,128)(2,1)} %get-tuple-element.168), channel_id=1, source_target_pairs={{0,1},{1,0},{2,3},{3,2},{4,5},{5,4},{6,7},{7,6},{8,9},{9,8},{10,11... | collective-permute-start | bytes 663560 | tf_op jit(solution)/shard_map/ppermute | solution.py:569
  58.9 1.2 copy-start.5
  60.1 20.7 %slice-start = ((s8[7077888]{0:T(1024)(128)(4,1)}), s8[4194304]{0:T(1024)(128)(4,1)S(1)}, s32[]{:S(2)}) async-start(s8[7077888]{0:T(1024)(128)(4,1)} %bitcast.10), calls=%async_computation | async-start | bytes 8388608
  64.6 16.2 %slice-start.1 = ((s8[7077888]{0:T(1024)(128)(4,1)}), s8[2883584]{0:T(1024)(128)(4,1)S(1)}, s32[]{:S(2)}) async-start(s8[7077888]{0:T(1024)(128)(4,1)} %bitcast.10), calls=%async_computation.1 | async-start | bytes 5767168
  72.6 13.2 %collective-permute-start.13 = (bf16[34,24,512]{2,1,0:T(8,128)(2,1)S(1)}, bf16[34,24,512]{2,1,0:T(8,128)(2,1)S(1)}, u32[]{:S(2)}, u32[]{:S(2)}) collective-permute-start(bf16[34,24,512]{2,1,0:T(8,128)(2,1)S(1)} %get-tuple-element.118), channel_id=1, source_target_pairs={{0,16},{1,49},{16,0},{17,33},{32,48},{33,17},{48,32},{49,1},{2,18}... | collective-permute-start | bytes 2506760 | tf_op jit(solution)/shard_map/ppermute | solution.py:569
  72.7 13.1 %collective-permute-start.14 = (bf16[34,24,512]{2,1,0:T(8,128)(2,1)S(1)}, bf16[34,24,512]{2,1,0:T(8,128)(2,1)S(1)}, u32[]{:S(2)}, u32[]{:S(2)}) collective-permute-start(bf16[34,24,512]{2,1,0:T(8,128)(2,1)S(1)} %get-tuple-element.120), channel_id=1, source_target_pairs={{0,2},{1,67},{2,0},{3,65},{64,66},{65,3},{66,64},{67,1},{4,6},{5,7... | collective-permute-start | bytes 2506760 | tf_op jit(solution)/shard_map/ppermute | solution.py:569
  73.0 17.7 %collective-permute-start.15 = (bf16[34,24,512]{2,1,0:T(8,128)(2,1)S(1)}, bf16[34,24,512]{2,1,0:T(8,128)(2,1)S(1)}, u32[]{:S(2)}, u32[]{:S(2)}) collective-permute-start(bf16[34,24,512]{2,1,0:T(8,128)(2,1)S(1)} %get-tuple-element.122), channel_id=1, source_target_pairs={{0,4},{1,13},{4,0},{5,9},{8,12},{9,5},{12,8},{13,1},{2,6},{3,15},{... | collective-permute-start | bytes 2506760 | tf_op jit(solution)/shard_map/ppermute | solution.py:569
  91.9 7.5 %collective-permute-start.16 = (bf16[18,24,512]{2,1,0:T(8,128)(2,1)S(1)}, bf16[18,24,512]{2,1,0:T(8,128)(2,1)S(1)}, u32[]{:S(2)}, u32[]{:S(2)}) collective-permute-start(bf16[18,24,512]{2,1,0:T(8,128)(2,1)S(1)} %get-tuple-element.124), channel_id=1, source_target_pairs={{0,48},{1,17},{16,32},{17,1},{32,16},{33,49},{48,0},{49,33},{2,50}... | collective-permute-start | bytes 1327112 | tf_op jit(solution)/shard_map/ppermute | solution.py:569
  92.0 7.5 %collective-permute-start.17 = (bf16[18,24,512]{2,1,0:T(8,128)(2,1)S(1)}, bf16[18,24,512]{2,1,0:T(8,128)(2,1)S(1)}, u32[]{:S(2)}, u32[]{:S(2)}) collective-permute-start(bf16[18,24,512]{2,1,0:T(8,128)(2,1)S(1)} %get-tuple-element.126), channel_id=1, source_target_pairs={{0,66},{1,3},{2,64},{3,1},{64,2},{65,67},{66,0},{67,65},{4,70},{5,... | collective-permute-start | bytes 1327112 | tf_op jit(solution)/shard_map/ppermute | solution.py:569
  92.1 7.5 %collective-permute-start.18 = (bf16[18,24,512]{2,1,0:T(8,128)(2,1)S(1)}, bf16[18,24,512]{2,1,0:T(8,128)(2,1)S(1)}, u32[]{:S(2)}, u32[]{:S(2)}) collective-permute-start(bf16[18,24,512]{2,1,0:T(8,128)(2,1)S(1)} %get-tuple-element.128), channel_id=1, source_target_pairs={{0,12},{1,5},{4,8},{5,1},{8,4},{9,13},{12,0},{13,9},{2,14},{3,7},{... | collective-permute-start | bytes 1327112 | tf_op jit(solution)/shard_map/ppermute | solution.py:569
  99.6 32.2 %copy-start.1 = (bf16[24,12,1536]{2,0,1:T(8,128)(2,1)S(1)}, bf16[24,12,1536]{2,0,1:T(8,128)(2,1)}, u32[]{:S(2)}) copy-start(bf16[24,12,1536]{2,0,1:T(8,128)(2,1)} %param.11) | copy-start | bytes 2654212
  100.5 8.0 %collective-permute-start.19 = (bf16[10,24,512]{2,1,0:T(8,128)(2,1)S(1)}, bf16[10,24,512]{2,1,0:T(8,128)(2,1)S(1)}, u32[]{:S(2)}, u32[]{:S(2)}) collective-permute-start(bf16[10,24,512]{2,1,0:T(8,128)(2,1)S(1)} %get-tuple-element.130), channel_id=1, source_target_pairs={{0,2},{1,67},{2,0},{3,65},{64,66},{65,3},{66,64},{67,1},{4,6},{5,7... | collective-permute-start | bytes 737288 | tf_op jit(solution)/shard_map/ppermute | solution.py:569
  101.3 8.1 %collective-permute-start.20 = (bf16[10,24,512]{2,1,0:T(8,128)(2,1)S(1)}, bf16[10,24,512]{2,1,0:T(8,128)(2,1)S(1)}, u32[]{:S(2)}, u32[]{:S(2)}) collective-permute-start(bf16[10,24,512]{2,1,0:T(8,128)(2,1)S(1)} %get-tuple-element.132), channel_id=1, source_target_pairs={{0,4},{1,13},{4,0},{5,9},{8,12},{9,5},{12,8},{13,1},{2,6},{3,15},{... | collective-permute-start | bytes 737288 | tf_op jit(solution)/shard_map/ppermute | solution.py:569
  104.0 6.3 %collective-permute-start.21 = (bf16[10,24,512]{2,1,0:T(8,128)(2,1)S(1)}, bf16[10,24,512]{2,1,0:T(8,128)(2,1)S(1)}, u32[]{:S(2)}, u32[]{:S(2)}) collective-permute-start(bf16[10,24,512]{2,1,0:T(8,128)(2,1)S(1)} %get-tuple-element.134), channel_id=1, source_target_pairs={{0,16},{1,49},{16,0},{17,33},{32,48},{33,17},{48,32},{49,1},{2,18}... | collective-permute-start | bytes 737288 | tf_op jit(solution)/shard_map/ppermute | solution.py:569
  104.1 9.7 %collective-permute-start.12 = (bf16[72,1536]{1,0:T(8,128)(2,1)S(1)}, bf16[72,1536]{1,0:T(8,128)(2,1)S(1)}, u32[]{:S(2)}, u32[]{:S(2)}) collective-permute-start(bf16[72,1536]{1,0:T(8,128)(2,1)S(1)} %get-tuple-element.115), channel_id=1, source_target_pairs={{0,124},{4,0},{8,4},{12,8},{16,12},{20,16},{24,20},{28,24},{32,28}... | collective-permute-start | bytes 663560 | tf_op jit(solution)/shard_map/ppermute | solution.py:569
  111.0 4.1 %collective-permute-start.22 = (bf16[6,24,512]{2,1,0:T(8,128)(2,1)S(1)}, bf16[6,24,512]{2,1,0:T(8,128)(2,1)S(1)}, u32[]{:S(2)}, u32[]{:S(2)}) collective-permute-start(bf16[6,24,512]{2,1,0:T(8,128)(2,1)S(1)} %get-tuple-element.136), channel_id=1, source_target_pairs={{0,66},{1,3},{2,64},{3,1},{64,2},{65,67},{66,0},{67,65},{4,70},{5,... | collective-permute-start | bytes 442376 | tf_op jit(solution)/shard_map/ppermute | solution.py:569
  111.8 4.0 %collective-permute-start.23 = (bf16[6,24,512]{2,1,0:T(8,128)(2,1)S(1)}, bf16[6,24,512]{2,1,0:T(8,128)(2,1)S(1)}, u32[]{:S(2)}, u32[]{:S(2)}) collective-permute-start(bf16[6,24,512]{2,1,0:T(8,128)(2,1)S(1)} %get-tuple-element.138), channel_id=1, source_target_pairs={{0,12},{1,5},{4,8},{5,1},{8,4},{9,13},{12,0},{13,9},{2,14},{3,7},{... | collective-permute-start | bytes 442376 | tf_op jit(solution)/shard_map/ppermute | solution.py:569
  111.8 4.0 %collective-permute-start.24 = (bf16[6,24,512]{2,1,0:T(8,128)(2,1)S(1)}, bf16[6,24,512]{2,1,0:T(8,128)(2,1)S(1)}, u32[]{:S(2)}, u32[]{:S(2)}) collective-permute-start(bf16[6,24,512]{2,1,0:T(8,128)(2,1)S(1)} %get-tuple-element.140), channel_id=1, source_target_pairs={{0,48},{1,17},{16,32},{17,1},{32,16},{33,49},{48,0},{49,33},{2,50}... | collective-permute-start | bytes 442376 | tf_op jit(solution)/shard_map/ppermute | solution.py:569
  112.3 19.5 %collective-permute-start.31 = (bf16[72,1536]{1,0:T(8,128)(2,1)S(1)}, bf16[72,1536]{1,0:T(8,128)(2,1)S(1)}, u32[]{:S(2)}, u32[]{:S(2)}) collective-permute-start(bf16[72,1536]{1,0:T(8,128)(2,1)S(1)} %get-tuple-element.153), channel_id=1, source_target_pairs={{0,4},{4,8},{8,12},{12,16},{16,20},{20,24},{24,28},{28,32},{32,36}... | collective-permute-start | bytes 663560 | tf_op jit(solution)/shard_map/ppermute | solution.py:569
  116.5 11.8 %collective-permute-start.25 = (bf16[4,24,512]{2,1,0:T(8,128)(2,1)S(1)}, bf16[4,24,512]{2,1,0:T(8,128)(2,1)S(1)}, u32[]{:S(2)}, u32[]{:S(2)}) collective-permute-start(bf16[4,24,512]{2,1,0:T(8,128)(2,1)S(1)} %get-tuple-element.142), channel_id=1, source_target_pairs={{0,4},{1,13},{4,0},{5,9},{8,12},{9,5},{12,8},{13,1},{2,6},{3,15},{... | collective-permute-start | bytes 294920 | tf_op jit(solution)/shard_map/ppermute | solution.py:569
  118.8 9.5 %collective-permute-start.26 = (bf16[4,24,512]{2,1,0:T(8,128)(2,1)S(1)}, bf16[4,24,512]{2,1,0:T(8,128)(2,1)S(1)}, u32[]{:S(2)}, u32[]{:S(2)}) collective-permute-start(bf16[4,24,512]{2,1,0:T(8,128)(2,1)S(1)} %get-tuple-element.144), channel_id=1, source_target_pairs={{0,16},{1,49},{16,0},{17,33},{32,48},{33,17},{48,32},{49,1},{2,18}... | collective-permute-start | bytes 294920 | tf_op jit(solution)/shard_map/ppermute | solution.py:569
  120.1 8.1 %collective-permute-start.27 = (bf16[4,24,512]{2,1,0:T(8,128)(2,1)S(1)}, bf16[4,24,512]{2,1,0:T(8,128)(2,1)S(1)}, u32[]{:S(2)}, u32[]{:S(2)}) collective-permute-start(bf16[4,24,512]{2,1,0:T(8,128)(2,1)S(1)} %get-tuple-element.146), channel_id=1, source_target_pairs={{0,2},{1,67},{2,0},{3,65},{64,66},{65,3},{66,64},{67,1},{4,6},{5,7... | collective-permute-start | bytes 294920 | tf_op jit(solution)/shard_map/ppermute | solution.py:569
  121.0 10.9 %collective-permute-start.32 = (bf16[36,1536]{1,0:T(8,128)(2,1)S(1)}, bf16[36,1536]{1,0:T(8,128)(2,1)S(1)}, u32[]{:S(2)}, u32[]{:S(2)}) collective-permute-start(bf16[36,1536]{1,0:T(8,128)(2,1)S(1)} %last_rows.1), channel_id=1, source_target_pairs={{0,1},{1,2},{2,3},{3,0},{4,5},{5,6},{6,7},{7,4},{8,9},{9,10},{10,1... | collective-permute-start | bytes 331784 | tf_op jit(solution)/shard_map/ppermute | solution.py:569
  128.9 4.2 %collective-permute-start.28 = (bf16[3,24,512]{2,1,0:T(8,128)(2,1)S(1)}, bf16[3,24,512]{2,1,0:T(8,128)(2,1)S(1)}, u32[]{:S(2)}, u32[]{:S(2)}) collective-permute-start(bf16[3,24,512]{2,1,0:T(8,128)(2,1)S(1)} %get-tuple-element.148), channel_id=1, source_target_pairs={{0,12},{1,5},{4,8},{5,1},{8,4},{9,13},{12,0},{13,9},{2,14},{3,7},{... | collective-permute-start | bytes 221192 | tf_op jit(solution)/shard_map/ppermute | solution.py:569
  130.6 3.2 %collective-permute-start.29 = (bf16[3,24,512]{2,1,0:T(8,128)(2,1)S(1)}, bf16[3,24,512]{2,1,0:T(8,128)(2,1)S(1)}, u32[]{:S(2)}, u32[]{:S(2)}) collective-permute-start(bf16[3,24,512]{2,1,0:T(8,128)(2,1)S(1)} %get-tuple-element.150), channel_id=1, source_target_pairs={{0,48},{1,17},{16,32},{17,1},{32,16},{33,49},{48,0},{49,33},{2,50}... | collective-permute-start | bytes 221192 | tf_op jit(solution)/shard_map/ppermute | solution.py:569
  130.6 3.2 %collective-permute-start.30 = (bf16[3,24,512]{2,1,0:T(8,128)(2,1)S(1)}, bf16[3,24,512]{2,1,0:T(8,128)(2,1)S(1)}, u32[]{:S(2)}, u32[]{:S(2)}) collective-permute-start(bf16[3,24,512]{2,1,0:T(8,128)(2,1)S(1)} %get-tuple-element.152), channel_id=1, source_target_pairs={{0,66},{1,3},{2,64},{3,1},{64,2},{65,67},{66,0},{67,65},{4,70},{5,... | collective-permute-start | bytes 221192 | tf_op jit(solution)/shard_map/ppermute | solution.py:569
  133.9 5.7 %collective-permute-start.33 = (bf16[9,24,512]{2,1,0:T(8,128)(2,1)S(1)}, bf16[9,24,512]{2,1,0:T(8,128)(2,1)S(1)}, u32[]{:S(2)}, u32[]{:S(2)}) collective-permute-start(bf16[9,24,512]{2,1,0:T(8,128)(2,1)S(1)} %total.1.own), channel_id=1, source_target_pairs={{0,1},{1,0},{2,3},{3,2},{4,5},{5,4},{6,7},{7,6},{8,9},{9,8},{10,11... | collective-permute-start | bytes 663560 | tf_op jit(solution)/shard_map/ppermute | solution.py:569
  (5 other events, 3.6 us)

commit v4 on v3

--- a/solution.py
+++ b/solution.py
@@ -167,26 +167,20 @@
             rows[r * 12 : (r + 1) * 12, t * 128 : (t + 1) * 128] = grid[t, pl.ds(r, 12, stride=24), :]
 
 
-def first_body(own, low, upper, part, sem):
-    copy = pltpu.make_async_copy(own.at[:, :16], part, sem)
-    copy.start()
-    copy.wait()
-    low[...] = jnp.concatenate([part[j].astype(F32)[:SHIFT_H] for j in range(12)], 0).astype(BF16)
+def first_body(own, low, upper):
+    low[...] = jnp.concatenate([own[j].astype(F32)[:SHIFT_H] for j in range(12)], 0).astype(BF16)
     upper[...] = jnp.concatenate(
-        [part[j].astype(F32)[SHIFT_H : SHIFT_H + HALF_ROWS] for j in range(SHIFT_W)], 0
+        [own[j].astype(F32)[SHIFT_H : SHIFT_H + HALF_ROWS] for j in range(SHIFT_W)], 0
     ).astype(BF16)
 
 
-def to_east_body(own, low, out, part, sem):
-    copy = pltpu.make_async_copy(own.at[SHIFT_W:, 8:], part, sem)
-    copy.start()
-    copy.wait()
+def to_east_body(own, low, out):
     out[...] = jnp.concatenate(
         [
             piece
             for i in range(SHIFT_W)
             for piece in (
-                part[i].astype(F32)[SHIFT_H + HALF_ROWS - 8 :],
+                own[SHIFT_W + i].astype(F32)[SHIFT_H + HALF_ROWS :],
                 f32_rows(low, (SHIFT_W + i) * SHIFT_H, SHIFT_H),
             )
         ],
@@ -334,15 +328,18 @@
     row,
     col,
     mixed_low,
-    attended_grad,
+    grad_other,
     gain_part,
     grads,
     small,
+    attended_near,
+    attended_far,
     grid,
     rows,
     mixed_all,
     weight,
     heads,
+    attended_grad,
     sems,
 ):
     copies = [pltpu.make_async_copy(pw, weight, sems.at[0])]
@@ -355,6 +352,11 @@
     copies[0].wait()
     norm_part(attended, rows, weight, gain, mixed_low, attended_grad, gain_part, mixed_all)
     pens = penalties(row[...], col[...])
+    near = pl.ds(pl.multiple_of((1 - side[0]) * HALF, 128), HALF)
+    far = pl.ds(pl.multiple_of(side[0] * HALF, 128), HALF)
+    grad_other[...] = attended_grad[:, near]
+    attended_near[...] = attended[:, near]
+    attended_far[...] = attended[:, far]
     small[...] = jnp.zeros_like(small)
     for copy in copies[1:]:
         copy.wait()
@@ -598,14 +600,7 @@
 
 def first_messages(grid):
     return call(
-        first_body,
-        [shape((36, C), BF16), shape((72, C), BF16)],
-        [grid],
-        scalars=0,
-        scratch=[pltpu.VMEM((12, 16, C), BF16), pltpu.SemaphoreType.DMA],
-        vmem=60,
-        far=(0,),
-        name="first",
+        first_body, [shape((36, C), BF16), shape((72, C), BF16)], [grid], scalars=0, name="first"
     )
 
 
@@ -614,14 +609,7 @@
     low = lat_step(low, -1)
     east = lon_step(upper, -1)
     (lower,) = call(
-        to_east_body,
-        [shape((72, C), BF16)],
-        [grid, low],
-        scalars=0,
-        scratch=[pltpu.VMEM((SHIFT_W, 16, C), BF16), pltpu.SemaphoreType.DMA],
-        vmem=60,
-        far=(0,),
-        name="to_east",
+        to_east_body, [shape((72, C), BF16)], [grid, low], scalars=0, name="to_east"
     )
     return east, low, lower
 
@@ -675,14 +663,16 @@
         name="forward",
     )
     x_other = core_swap(x)
-    mixed_low, attended_grad, gain_part, grads_theirs, small_theirs = call(
+    mixed_low, attended_grad, gain_part, grads_theirs, small_theirs, attended_mine, attended_theirs = call(
         backward_body,
         [
             shape((CELLS, C), BF16),
-            shape((CELLS, HC), F32),
+            shape((CELLS, HALF), F32),
             shape((1, C), F32),
             shape((CELLS, 3 * HALF), BF16),
             shape((144, 512), F32),
+            shape((CELLS, HALF), BF16),
+            shape((CELLS, HALF), BF16),
         ],
         [
             theirs,
@@ -704,6 +694,7 @@
             pltpu.VMEM((CELLS, C), F32),
             pltpu.VMEM((C, HC), BF16),
             pltpu.VMEM((3, CELLS, HALF), F32),
+            pltpu.VMEM((CELLS, HC), F32),
             pltpu.SemaphoreType.DMA((4,)),
         ],
         far=(7,),
@@ -712,8 +703,6 @@
         name="backward",
     )
     mixed_other = core_swap(mixed_low)
-    attended_theirs = lax.dynamic_slice(attended, (0, theirs[0] * HALF), (CELLS, HALF))
-    attended_mine = lax.dynamic_slice(attended, (0, mine[0] * HALF), (CELLS, HALF))
     attended_other = core_swap(attended_theirs)
 
     def attention(side):
@@ -730,7 +719,7 @@
                 (projected, block, cols(0)),
                 (projected, block, cols(6)),
                 (projected, block, cols(12)),
-                (attended_grad, block, cols(0)),
+                (attended_grad, block, lambda i, side, scale: (0, i)),
                 (pair_rows, (2 * WIN, WIN), lambda i, side, scale: (side[0] * 3 + i, 0)),
                 (region_row, (WINDOWS, WIN), whole),
                 (region_col, (CELLS, 1), whole),
@@ -801,14 +790,7 @@
     (last,) = call(
         last_rows_body, [shape((36, C), BF16)], [stay_high, from_east], scalars=0, vmem=6, name="last_rows"
     )
-    (input_grad,) = call(
-        merge_body,
-        [shape((12, 24, C), BF16)],
-        [upstream, stay_low, stay_high, from_west, from_east, lat_step(last, 1)],
-        scalars=0,
-        vmem=10,
-        name="merge",
-    )
+    low = lat_step(last, 1)
     for step in range(6):
         terms = []
         for j, names in enumerate(ORDERS):
@@ -823,8 +805,20 @@
         if step == 0:
             order, stay_low = lax.optimization_barrier((order, stay_low))
         if step == 3:
+            order, from_west = lax.optimization_barrier((order, from_west))
+        if step == 4:
+            order, low = lax.optimization_barrier((order, low))
+        if step == 2:
             order, last = lax.optimization_barrier((order, last))
         parts = call(body, [shape((left // 2 + EXTRA,) + BLOCK, BF16)] * 6, [order, *terms], vmem=10, name="halve")
+    (input_grad,) = call(
+        merge_body,
+        [shape((12, 24, C), BF16)],
+        [upstream, stay_low, stay_high, from_west, from_east, low],
+        scalars=0,
+        vmem=10,
+        name="merge",
+    )
     terms, input_grad = lax.optimization_barrier((terms, input_grad))
     (sums,) = call(total_body, [shape((9,) + BLOCK, BF16)], terms, scalars=0, vmem=6, name="total")
     sums_other = core_swap(sums)

time: 141 us -> 139 us (0.986)
  Pallas kernels: 53.6 us -> 46.4 us
  waiting for transfers between devices: 18 us -> 22.1 us
    pallas_call x16, Pallas kernels: 44.2 us -> 37 us  [call(): pl.pallas_call(body, out_shape=list(outs), in_specs=specs, out_specs=[VME...]
    ppermute x34, waiting for transfers between devices: 18 us -> 22.1 us  [permuted(): return lax.ppermute(value, axes, pairs)]
    dynamic_slice x1 -> x0, local copies, waits for them, and re-layouts: 1.77 us -> none  [shards(): lax.dynamic_slice(attended, (0, theirs[0] * HALF), (CELLS, HALF))]
    unnamed x38 -> x44, local copies, waits for them, and re-layouts: 5.76 us -> 7.12 us
  transfers between devices with their start and end apart: 34 -> 34, of which waited for: 10 -> 14; matrix products, arithmetic and copies ran while one was open for 2% -> 1% of each run, Pallas kernels for 29% -> 25%
where the time goes in v4:
time: 139 us; the launch traced here: 138 us
  starting transfers between devices  59.8 us (43%)
  Pallas kernels  46.4 us (33%)
  waiting for transfers between devices  22.1 us (16%)
  local copies, waits for them, and re-layouts  8.84 us (6%)
    ppermute x34, starting transfers between devices, permuted(): return lax.ppermute(value, axes, pairs)  59.8 us
    pallas_call x16, Pallas kernels, call(): pl.pallas_call(body, out_shape=list(outs), in_specs=specs, out_specs=[VME...  37 us
    ppermute x34, waiting for transfers between devices, permuted(): return lax.ppermute(value, axes, pairs)  22.1 us
    pallas_call x2, Pallas kernels, grid_call(): pl.pallas_call(body, grid_spec=spec, out_shape=results, compiler_params=p...  9.41 us
    unnamed x44, local copies, waits for them, and re-layouts  7.12 us
  transfers between devices with their start and end apart: 34, of which 14 were waited for; matrix products, arithmetic and copies ran while one was open for 1% of the time, Pallas kernels for 25%

profile of v4, /device:TPU:1, one launch (start us, length us, event | category | flops | bytes accessed | tf_op | source)
XLA Modules:
  0.0 138.3 jit_solution(4610389376295489032)
XLA Ops:
  0.7 1.2 copy-done.3
  1.9 0.7 first.2
  2.6 1.4 %collective-permute-start.1 = (bf16[36,1536]{1,0:T(8,128)(2,1)S(1)}, bf16[36,1536]{1,0:T(8,128)(2,1)S(1)}, u32[]{:S(2)}, u32[]{:S(2)}) collective-permute-start(bf16[36,1536]{1,0:T(8,128)(2,1)S(1)} %get-tuple-element.96), channel_id=1, source_target_pairs={{0,3},{1,0},{2,1},{3,2},{4,7},{5,4},{6,5},{7,6},{8,11},{9,8},{10,9... | collective-permute-start | bytes 331784 | tf_op jit(solution)/shard_map/ppermute | solution.py:571
  4.1 8.7 %collective-permute-start = (bf16[72,1536]{1,0:T(8,128)(2,1)}, bf16[72,1536]{1,0:T(8,128)(2,1)S(1)}, u32[]{:S(2)}, u32[]{:S(2)}) collective-permute-start(bf16[72,1536]{1,0:T(8,128)(2,1)} %get-tuple-element.95), channel_id=1, source_target_pairs={{0,124},{4,0},{8,4},{12,8},{16,12},{20,16},{24,20},{28,24},{32,28}... | collective-permute-start | bytes 663560 | tf_op jit(solution)/shard_map/ppermute | solution.py:571
  12.7 0.7 reshape.38.query_bias
  13.4 1.2 copy-done.4
  14.8 0.8 first.3
  15.5 1.0 collective-permute-start.6
  16.6 0.7 reshape.39.value_bias
  17.3 7.5 %collective-permute-start.5 = (bf16[72,1536]{1,0:T(8,128)(2,1)}, bf16[72,1536]{1,0:T(8,128)(2,1)S(1)}, u32[]{:S(2)}, u32[]{:S(2)}) collective-permute-start(bf16[72,1536]{1,0:T(8,128)(2,1)} %get-tuple-element.103), channel_id=1, source_target_pairs={{0,124},{4,0},{8,4},{12,8},{16,12},{20,16},{24,20},{28,24},{32,28}... | collective-permute-start | bytes 663560 | tf_op jit(solution)/shard_map/ppermute | solution.py:571
  25.0 0.6 copy-done.8
  25.5 1.1 collective-permute-done.3
  27.0 10.6 %forward.1 = (bf16[288,1536]{1,0:T(8,128)(2,1)}, f32[288,2304]{1,0:T(8,128)}, bf16[288,768]{1,0:T(8,128)(2,1)S(1)}) custom-call(f32[12]{0:T(128)S(1)} %copy-done.14, bf16[12,24,1536]{2,1,0:T(8,128)(2,1)S(1)} %bitcast.17, bf16[72,1536]{1,0:T(8,128)(2,1)S(1)} %collective-permute-done.east, bf16[72,1536]{1,0:T(8,128)(2,1)S(1)} %collective-permute-done.2.west, ...), custom_call_target="tpu_custom_call" | custom-call | flops 2038431744 | bytes 12754224 | tf_op jit(solution)/shard_map/forward/pallas_call | solution.py:60
  37.6 2.2 %collective-permute-start.4 = (bf16[288,1536]{1,0:T(8,128)(2,1)}, bf16[288,1536]{1,0:T(8,128)(2,1)}, u32[]{:S(2)}, u32[]{:S(2)}) collective-permute-start(bf16[288,1536]{1,0:T(8,128)(2,1)} %get-tuple-element.99.x0), channel_id=1, source_target_pairs={{0,1},{1,0},{2,3},{3,2},{4,5},{5,4},{6,7},{7,6},{8,9},{9,8},{10,11... | collective-permute-start | bytes 2654216 | tf_op jit(solution)/shard_map/ppermute | solution.py:571
  39.8 0.7 copy-done.12
  40.5 0.9 copy-done.13
  41.4 10.5 %backward.1 = (bf16[288,1536]{1,0:T(8,128)(2,1)}, f32[288,384]{1,0:T(8,128)S(1)}, f32[1,1536]{1,0:T(1,128)S(1)}, bf16[288,1152]{1,0:T(8,128)(2,1)}, f32[144,512]...) custom-call(s32[1]{0:T(128)S(6)} %sub.3.side, f32[12]{0:T(128)S(1)} %copy-done.14, ...), custom_call_target="tpu_custom_call" | custom-call | flops 1454505984 | bytes 9884980 | tf_op jit(solution)/shard_map/backward/pallas_call | solution.py:60
  51.9 0.8 copy-done.10
  52.7 0.7 copy-done.16
  53.4 0.5 collective-permute-start.8
  53.9 0.5 collective-permute-start.10
  54.5 1.0 copy-done.11
  55.5 4.4 %attention.1 = (bf16[288,1152]{1,0:T(8,128)(2,1)S(1)}, f32[144,512]{1,0:T(8,128)S(1)}) custom-call(s32[1]{0:T(128)} %bitcast.side.core, f32[12]{0:T(128)S(1)} %copy-done.14, f32[288,2304]{1,0:T(8,128)S(1)} %copy-done, f32[288,2304]{1,0:T(8,128)S(1)} %copy-done, f32[288,2304]{1,0:T(8,128)S(1)} %copy-done, f32[288,384]{1,0:T(8,128)S(1)} %copy-done.11, ...), custom_call_target="tpu_custom_call" | custom-call | flops 95551488 | bytes 9620736 | tf_op jit(solution)/shard_map/attention/pallas_call | solution.py:82
  60.0 7.9 %weights.1 = (bf16[34,24,512]{2,1,0:T(8,128)(2,1)S(1)}, bf16[34,24,512]{2,1,0:T(8,128)(2,1)S(1)}, bf16[34,24,512]{2,1,0:T(8,128)(2,1)S(1)}, bf16[34,24,512]{2,1,...) custom-call(s32[4]{0:T(128)S(1)} %pad_add_fusion.1.place, ...), custom_call_target="tpu_custom_call" | custom-call | flops 2717908992 | bytes 10911760 | tf_op jit(solution)/shard_map/weights/pallas_call | solution.py:60
  68.1 0.9 collective-permute-start.16
  68.9 4.8 %collective-permute-start.17 = (bf16[34,24,512]{2,1,0:T(8,128)(2,1)S(1)}, bf16[34,24,512]{2,1,0:T(8,128)(2,1)S(1)}, u32[]{:S(2)}, u32[]{:S(2)}) collective-permute-start(bf16[34,24,512]{2,1,0:T(8,128)(2,1)S(1)} %get-tuple-element.134), channel_id=1, source_target_pairs={{0,4},{1,13},{4,0},{5,9},{8,12},{9,5},{12,8},{13,1},{2,6},{3,15},{... | collective-permute-start | bytes 2506760 | tf_op jit(solution)/shard_map/ppermute | solution.py:571
  73.7 5.0 %branch.1 = (bf16[72,1536]{1,0:T(8,128)(2,1)S(1)}, bf16[72,1536]{1,0:T(8,128)(2,1)S(1)}, bf16[72,1536]{1,0:T(8,128)(2,1)S(1)}, bf16[72,1536]{1,0:T(8,128)(2,1)S(1)}) custom-call(s32[1]{0:T(128)} %bitcast.side.core, bf16[1536,2304]{1,0:T(8,128)(2,1)S(1)} %bitcast.10, bf16[288,1152]{1,0:T(8,128)(2,1)S(1)} %get-tuple-element.107.p0.own, ...), custom_call_target="tpu_custom_call" | custom-call | flops 2038431744 | bytes 9289728 | tf_op jit(solution)/shard_map/branch/pallas_call | solution.py:82
  78.7 2.0 %collective-permute-done.15.refs_1_ = bf16[34,24,512]{2,1,0:T(8,128)(2,1)S(1)} collective-permute-done((bf16[34,24,512]{2,1,0:T(8,128)(2,1)S(1)}, bf16[34,24,512]{2,1,0:T(8,128)(2,1)S(1)}, u32[]{:S(2)}, u32[]{:S(2)}) %collective-permute-start.15) | collective-permute-done | bytes 835616 | tf_op jit(solution)/shard_map/ppermute | solution.py:571
  80.7 2.9 %collective-permute-done.17.refs_5_ = bf16[34,24,512]{2,1,0:T(8,128)(2,1)S(1)} collective-permute-done((bf16[34,24,512]{2,1,0:T(8,128)(2,1)S(1)}, bf16[34,24,512]{2,1,0:T(8,128)(2,1)S(1)}, u32[]{:S(2)}, u32[]{:S(2)}) %collective-permute-start.17) | collective-permute-done | bytes 835616 | tf_op jit(solution)/shard_map/ppermute | solution.py:571
  83.6 1.1 halve.5
  85.0 7.2 %collective-permute-done.18.refs_1_ = bf16[18,24,512]{2,1,0:T(8,128)(2,1)S(1)} collective-permute-done((bf16[18,24,512]{2,1,0:T(8,128)(2,1)S(1)}, bf16[18,24,512]{2,1,0:T(8,128)(2,1)S(1)}, u32[]{:S(2)}, u32[]{:S(2)}) %collective-permute-start.18) | collective-permute-done | bytes 442400 | tf_op jit(solution)/shard_map/ppermute | solution.py:571
  92.4 0.9 halve.6
  93.3 0.9 collective-permute-start.21
  94.1 2.7 %collective-permute-start.22 = (bf16[10,24,512]{2,1,0:T(8,128)(2,1)S(1)}, bf16[10,24,512]{2,1,0:T(8,128)(2,1)S(1)}, u32[]{:S(2)}, u32[]{:S(2)}) collective-permute-start(bf16[10,24,512]{2,1,0:T(8,128)(2,1)S(1)} %get-tuple-element.144), channel_id=1, source_target_pairs={{0,4},{1,13},{4,0},{5,9},{8,12},{9,5},{12,8},{13,1},{2,6},{3,15},{... | collective-permute-start | bytes 737288 | tf_op jit(solution)/shard_map/ppermute | solution.py:571
  96.9 4.4 %collective-permute-start.12 = (bf16[72,1536]{1,0:T(8,128)(2,1)S(1)}, bf16[72,1536]{1,0:T(8,128)(2,1)S(1)}, u32[]{:S(2)}, u32[]{:S(2)}) collective-permute-start(bf16[72,1536]{1,0:T(8,128)(2,1)S(1)} %get-tuple-element.124), channel_id=1, source_target_pairs={{0,124},{4,0},{8,4},{12,8},{16,12},{20,16},{24,20},{28,24},{32,28}... | collective-permute-start | bytes 663560 | tf_op jit(solution)/shard_map/ppermute | solution.py:571
  101.3 4.1 %collective-permute-done.12.from_east = bf16[72,1536]{1,0:T(8,128)(2,1)S(1)} collective-permute-done((bf16[72,1536]{1,0:T(8,128)(2,1)S(1)}, bf16[72,1536]{1,0:T(8,128)(2,1)S(1)}, u32[]{:S(2)}, u32[]{:S(2)}) %collective-permute-start.12) | collective-permute-done | bytes 221216 | tf_op jit(solution)/shard_map/ppermute | solution.py:571
  105.6 0.7 halve.7
  106.5 0.6 collective-permute-start.26
  107.0 9.7 %collective-permute-start.14 = (bf16[36,1536]{1,0:T(8,128)(2,1)S(1)}, bf16[36,1536]{1,0:T(8,128)(2,1)S(1)}, u32[]{:S(2)}, u32[]{:S(2)}) collective-permute-start(bf16[36,1536]{1,0:T(8,128)(2,1)S(1)} %last_rows.1), channel_id=1, source_target_pairs={{0,1},{1,2},{2,3},{3,0},{4,5},{5,6},{6,7},{7,4},{8,9},{9,10},{10,1... | collective-permute-start | bytes 331784 | tf_op jit(solution)/shard_map/ppermute | solution.py:571
  116.8 0.7 halve.8
  117.6 2.3 %collective-permute-start.29 = (bf16[4,24,512]{2,1,0:T(8,128)(2,1)S(1)}, bf16[4,24,512]{2,1,0:T(8,128)(2,1)S(1)}, u32[]{:S(2)}, u32[]{:S(2)}) collective-permute-start(bf16[4,24,512]{2,1,0:T(8,128)(2,1)S(1)} %get-tuple-element.158), channel_id=1, source_target_pairs={{0,2},{1,67},{2,0},{3,65},{64,66},{65,3},{66,64},{67,1},{4,6},{5,7... | collective-permute-start | bytes 294920 | tf_op jit(solution)/shard_map/ppermute | solution.py:571
  119.9 2.3 %collective-permute-done.27.refs_1_ = bf16[4,24,512]{2,1,0:T(8,128)(2,1)S(1)} collective-permute-done((bf16[4,24,512]{2,1,0:T(8,128)(2,1)S(1)}, bf16[4,24,512]{2,1,0:T(8,128)(2,1)S(1)}, u32[]{:S(2)}, u32[]{:S(2)}) %collective-permute-start.27) | collective-permute-done | bytes 98336 | tf_op jit(solution)/shard_map/ppermute | solution.py:571
  122.4 0.6 halve.9
  123.4 1.0 collective-permute-start.32
  124.5 1.3 merge.1
  126.7 9.6 %collective-permute-start.33 = (bf16[9,24,512]{2,1,0:T(8,128)(2,1)S(1)}, bf16[9,24,512]{2,1,0:T(8,128)(2,1)S(1)}, u32[]{:S(2)}, u32[]{:S(2)}) collective-permute-start(bf16[9,24,512]{2,1,0:T(8,128)(2,1)S(1)} %total.1.own), channel_id=1, source_target_pairs={{0,1},{1,0},{2,3},{3,2},{4,5},{5,4},{6,7},{7,6},{8,9},{9,8},{10,11... | collective-permute-start | bytes 663560 | tf_op jit(solution)/shard_map/ppermute | solution.py:571
  136.3 1.1 collective-permute-done.33.other
  137.4 0.9 finish.1
  (92 shorter events, 3.6 us)
Async XLA Ops:
  0.6 14.1 %copy-start.1 = (bf16[24,12,1536]{2,0,1:T(8,128)(2,1)S(1)}, bf16[24,12,1536]{2,0,1:T(8,128)(2,1)}, u32[]{:S(2)}) copy-start(bf16[24,12,1536]{2,0,1:T(8,128)(2,1)} %param.11) | copy-start | bytes 2654212
  1.9 14.7 %copy-start.18 = (s32[24,12]{0,1:T(8,128)S(1)}, s32[24,12]{0,1:T(8,128)}, u32[]{:S(2)}) copy-start(s32[24,12]{0,1:T(8,128)} %param.12) | copy-start | bytes 3460
  1.9 15.4 %copy-start.19 = (f32[1536]{0:T(1024)S(1)}, f32[1536]{0:T(1024)}, u32[]{:S(2)}) copy-start(f32[1536]{0:T(1024)} %param.19) | copy-start | bytes 18436
  1.9 25.1 %copy-start.14 = (f32[12]{0:T(128)S(1)}, f32[12]{0:T(128)}, u32[]{:S(2)}) copy-start(f32[12]{0:T(128)} %scale.5) | copy-start | bytes 148
  2.6 10.8 %collective-permute-start.1 = (bf16[36,1536]{1,0:T(8,128)(2,1)S(1)}, bf16[36,1536]{1,0:T(8,128)(2,1)S(1)}, u32[]{:S(2)}, u32[]{:S(2)}) collective-permute-start(bf16[36,1536]{1,0:T(8,128)(2,1)S(1)} %get-tuple-element.96), channel_id=1, source_target_pairs={{0,3},{1,0},{2,1},{3,2},{4,7},{5,4},{6,5},{7,6},{8,11},{9,8},{10,9... | collective-permute-start | bytes 331784 | tf_op jit(solution)/shard_map/ppermute | solution.py:571
  4.1 22.9 %collective-permute-start = (bf16[72,1536]{1,0:T(8,128)(2,1)}, bf16[72,1536]{1,0:T(8,128)(2,1)S(1)}, u32[]{:S(2)}, u32[]{:S(2)}) collective-permute-start(bf16[72,1536]{1,0:T(8,128)(2,1)} %get-tuple-element.95), channel_id=1, source_target_pairs={{0,124},{4,0},{8,4},{12,8},{16,12},{20,16},{24,20},{28,24},{32,28}... | collective-permute-start | bytes 663560 | tf_op jit(solution)/shard_map/ppermute | solution.py:571
  14.6 12.4 %copy-start.5 = (bf16[24,12,1536]{2,0,1:T(8,128)(2,1)S(1)}, bf16[24,12,1536]{2,0,1:T(8,128)(2,1)}, u32[]{:S(2)}) copy-start(bf16[24,12,1536]{2,0,1:T(8,128)(2,1)} %param.10) | copy-start | bytes 2654212
  14.6 12.4 %copy-start.6 = (f32[12,72,72]{2,1,0:T(8,128)S(1)}, f32[12,72,72]{2,1,0:T(8,128)}, u32[]{:S(2)}) copy-start(f32[12,72,72]{2,1,0:T(8,128)} %param.17) | copy-start | bytes 746500
  14.7 12.3 %collective-permute-start.2 = (bf16[72,1536]{1,0:T(8,128)(2,1)S(1)}, bf16[72,1536]{1,0:T(8,128)(2,1)S(1)}, u32[]{:S(2)}, u32[]{:S(2)}) collective-permute-start(bf16[72,1536]{1,0:T(8,128)(2,1)S(1)} %to_east.2), channel_id=1, source_target_pairs={{0,4},{4,8},{8,12},{12,16},{16,20},{20,24},{24,28},{28,32},{32,36}... | collective-permute-start | bytes 663560 | tf_op jit(solution)/shard_map/ppermute | solution.py:571
  15.5 9.3 %collective-permute-start.6 = (bf16[36,1536]{1,0:T(8,128)(2,1)S(1)}, bf16[36,1536]{1,0:T(8,128)(2,1)S(1)}, u32[]{:S(2)}, u32[]{:S(2)}) collective-permute-start(bf16[36,1536]{1,0:T(8,128)(2,1)S(1)} %get-tuple-element.104), channel_id=1, source_target_pairs={{0,3},{1,0},{2,1},{3,2},{4,7},{5,4},{6,5},{7,6},{8,11},{9,8},{10,9... | collective-permute-start | bytes 331784 | tf_op jit(solution)/shard_map/ppermute | solution.py:571
  16.6 10.0 %collective-permute-start.3 = (s32[12,12]{0,1:T(8,128)S(1)}, s32[12,12]{0,1:T(8,128)S(1)}, u32[]{:S(2)}, u32[]{:S(2)}) collective-permute-start(s32[12,12]{0,1:T(8,128)S(1)} %get-tuple-element.183), channel_id=1, source_target_pairs={{0,4},{4,8},{8,12},{12,16},{16,20},{20,24},{24,28},{28,32},{32,36}... | collective-permute-start | bytes 1736 | tf_op jit(solution)/shard_map/ppermute | solution.py:571
  17.3 22.4 %collective-permute-start.5 = (bf16[72,1536]{1,0:T(8,128)(2,1)}, bf16[72,1536]{1,0:T(8,128)(2,1)S(1)}, u32[]{:S(2)}, u32[]{:S(2)}) collective-permute-start(bf16[72,1536]{1,0:T(8,128)(2,1)} %get-tuple-element.103), channel_id=1, source_target_pairs={{0,124},{4,0},{8,4},{12,8},{16,12},{20,16},{24,20},{28,24},{32,28}... | collective-permute-start | bytes 663560 | tf_op jit(solution)/shard_map/ppermute | solution.py:571
  25.5 14.9 %collective-permute-start.7 = (bf16[72,1536]{1,0:T(8,128)(2,1)S(1)}, bf16[72,1536]{1,0:T(8,128)(2,1)S(1)}, u32[]{:S(2)}, u32[]{:S(2)}) collective-permute-start(bf16[72,1536]{1,0:T(8,128)(2,1)S(1)} %to_east.3), channel_id=1, source_target_pairs={{0,4},{4,8},{8,12},{12,16},{16,20},{20,24},{24,28},{28,32},{32,36}... | collective-permute-start | bytes 663560 | tf_op jit(solution)/shard_map/ppermute | solution.py:571
  27.0 13.5 %copy-start.7 = (f32[12,72,72]{2,1,0:T(8,128)S(1)}, f32[12,72,72]{2,1,0:T(8,128)}, u32[]{:S(2)}) copy-start(f32[12,72,72]{2,1,0:T(8,128)} %param.17) | copy-start | bytes 746500
  27.0 13.5 %copy-start.9 = (bf16[36,1536]{1,0:T(8,128)(2,1)S(1)}, bf16[36,1536]{1,0:T(8,128)(2,1)}, u32[]{:S(2)}) copy-start(bf16[36,1536]{1,0:T(8,128)(2,1)} %copy-done.8) | copy-start | bytes 331780
  37.6 22.4 %collective-permute-start.4 = (bf16[288,1536]{1,0:T(8,128)(2,1)}, bf16[288,1536]{1,0:T(8,128)(2,1)}, u32[]{:S(2)}, u32[]{:S(2)}) collective-permute-start(bf16[288,1536]{1,0:T(8,128)(2,1)} %get-tuple-element.99.x0), channel_id=1, source_target_pairs={{0,1},{1,0},{2,3},{3,2},{4,5},{5,4},{6,7},{7,6},{8,9},{9,8},{10,11... | collective-permute-start | bytes 2654216 | tf_op jit(solution)/shard_map/ppermute | solution.py:571
  41.4 13.1 %copy-start = (f32[288,2304]{1,0:T(8,128)S(1)}, f32[288,2304]{1,0:T(8,128)}, u32[]{:S(2)}) copy-start(f32[288,2304]{1,0:T(8,128)} %get-tuple-element.100.projected.q_ref.k_ref.v_ref) | copy-start | bytes 7962628
  53.4 6.6 %collective-permute-start.9 = (bf16[288,1536]{1,0:T(8,128)(2,1)}, bf16[288,1536]{1,0:T(8,128)(2,1)}, u32[]{:S(2)}, u32[]{:S(2)}) collective-permute-start(bf16[288,1536]{1,0:T(8,128)(2,1)} %get-tuple-element.109.m0), channel_id=1, source_target_pairs={{0,1},{1,0},{2,3},{3,2},{4,5},{5,4},{6,7},{7,6},{8,9},{9,8},{10,11... | collective-permute-start | bytes 2654216 | tf_op jit(solution)/shard_map/ppermute | solution.py:571
  53.4 6.6 %collective-permute-start.8 = (bf16[288,1152]{1,0:T(8,128)(2,1)}, bf16[288,1152]{1,0:T(8,128)(2,1)}, u32[]{:S(2)}, u32[]{:S(2)}) collective-permute-start(bf16[288,1152]{1,0:T(8,128)(2,1)} %get-tuple-element.108.theirs), channel_id=1, source_target_pairs={{0,1},{1,0},{2,3},{3,2},{4,5},{5,4},{6,7},{7,6},{8,9},{9,8},{10,11... | collective-permute-start | bytes 1990664 | tf_op jit(solution)/shard_map/ppermute | solution.py:571
  53.9 6.1 %collective-permute-start.11 = (f32[144,512]{1,0:T(8,128)}, f32[144,512]{1,0:T(8,128)}, u32[]{:S(2)}, u32[]{:S(2)}) collective-permute-start(f32[144,512]{1,0:T(8,128)} %get-tuple-element.113), channel_id=1, source_target_pairs={{0,1},{1,0},{2,3},{3,2},{4,5},{5,4},{6,7},{7,6},{8,9},{9,8},{10,11... | collective-permute-start | bytes 884744 | tf_op jit(solution)/shard_map/ppermute | solution.py:571
  53.9 6.1 %collective-permute-start.10 = (bf16[288,384]{1,0:T(8,128)(2,1)}, bf16[288,384]{1,0:T(8,128)(2,1)S(1)}, u32[]{:S(2)}, u32[]{:S(2)}) collective-permute-start(bf16[288,384]{1,0:T(8,128)(2,1)} %get-tuple-element.111), channel_id=1, source_target_pairs={{0,1},{1,0},{2,3},{3,2},{4,5},{5,4},{6,7},{7,6},{8,9},{9,8},{10,11... | collective-permute-start | bytes 663560 | tf_op jit(solution)/shard_map/ppermute | solution.py:571
  55.5 4.5 %copy-start.15 = (bf16[288,1536]{1,0:T(8,128)(2,1)S(1)}, bf16[288,1536]{1,0:T(8,128)(2,1)}, u32[]{:S(2)}) copy-start(bf16[288,1536]{1,0:T(8,128)(2,1)} %get-tuple-element.109.m0) | copy-start | bytes 2654212
  55.5 4.5 %copy-start.17 = (bf16[288,384]{1,0:T(8,128)(2,1)S(1)}, bf16[288,384]{1,0:T(8,128)(2,1)}, u32[]{:S(2)}) copy-start(bf16[288,384]{1,0:T(8,128)(2,1)} %copy-done.16) | copy-start | bytes 663556
  55.5 18.2 %slice-start = ((s8[7077888]{0:T(1024)(128)(4,1)}), s8[4194304]{0:T(1024)(128)(4,1)S(1)}, s32[]{:S(2)}) async-start(s8[7077888]{0:T(1024)(128)(4,1)} %bitcast.9), calls=%async_computation | async-start | bytes 8388608
  60.0 13.7 %slice-start.1 = ((s8[7077888]{0:T(1024)(128)(4,1)}), s8[2883584]{0:T(1024)(128)(4,1)S(1)}, s32[]{:S(2)}) async-start(s8[7077888]{0:T(1024)(128)(4,1)} %bitcast.9), calls=%async_computation.1 | async-start | bytes 5767168
  68.0 12.7 %collective-permute-start.15 = (bf16[34,24,512]{2,1,0:T(8,128)(2,1)S(1)}, bf16[34,24,512]{2,1,0:T(8,128)(2,1)S(1)}, u32[]{:S(2)}, u32[]{:S(2)}) collective-permute-start(bf16[34,24,512]{2,1,0:T(8,128)(2,1)S(1)} %get-tuple-element.130), channel_id=1, source_target_pairs={{0,16},{1,49},{16,0},{17,33},{32,48},{33,17},{48,32},{49,1},{2,18}... | collective-permute-start | bytes 2506760 | tf_op jit(solution)/shard_map/ppermute | solution.py:571
  68.1 12.7 %collective-permute-start.16 = (bf16[34,24,512]{2,1,0:T(8,128)(2,1)S(1)}, bf16[34,24,512]{2,1,0:T(8,128)(2,1)S(1)}, u32[]{:S(2)}, u32[]{:S(2)}) collective-permute-start(bf16[34,24,512]{2,1,0:T(8,128)(2,1)S(1)} %get-tuple-element.132), channel_id=1, source_target_pairs={{0,2},{1,67},{2,0},{3,65},{64,66},{65,3},{66,64},{67,1},{4,6},{5,7... | collective-permute-start | bytes 2506760 | tf_op jit(solution)/shard_map/ppermute | solution.py:571
  68.9 14.7 %collective-permute-start.17 = (bf16[34,24,512]{2,1,0:T(8,128)(2,1)S(1)}, bf16[34,24,512]{2,1,0:T(8,128)(2,1)S(1)}, u32[]{:S(2)}, u32[]{:S(2)}) collective-permute-start(bf16[34,24,512]{2,1,0:T(8,128)(2,1)S(1)} %get-tuple-element.134), channel_id=1, source_target_pairs={{0,4},{1,13},{4,0},{5,9},{8,12},{9,5},{12,8},{13,1},{2,6},{3,15},{... | collective-permute-start | bytes 2506760 | tf_op jit(solution)/shard_map/ppermute | solution.py:571
  84.7 7.5 %collective-permute-start.18 = (bf16[18,24,512]{2,1,0:T(8,128)(2,1)S(1)}, bf16[18,24,512]{2,1,0:T(8,128)(2,1)S(1)}, u32[]{:S(2)}, u32[]{:S(2)}) collective-permute-start(bf16[18,24,512]{2,1,0:T(8,128)(2,1)S(1)} %get-tuple-element.136), channel_id=1, source_target_pairs={{0,48},{1,17},{16,32},{17,1},{32,16},{33,49},{48,0},{49,33},{2,50}... | collective-permute-start | bytes 1327112 | tf_op jit(solution)/shard_map/ppermute | solution.py:571
  84.8 7.5 %collective-permute-start.19 = (bf16[18,24,512]{2,1,0:T(8,128)(2,1)S(1)}, bf16[18,24,512]{2,1,0:T(8,128)(2,1)S(1)}, u32[]{:S(2)}, u32[]{:S(2)}) collective-permute-start(bf16[18,24,512]{2,1,0:T(8,128)(2,1)S(1)} %get-tuple-element.138), channel_id=1, source_target_pairs={{0,66},{1,3},{2,64},{3,1},{64,2},{65,67},{66,0},{67,65},{4,70},{5,... | collective-permute-start | bytes 1327112 | tf_op jit(solution)/shard_map/ppermute | solution.py:571
  84.9 7.5 %collective-permute-start.20 = (bf16[18,24,512]{2,1,0:T(8,128)(2,1)S(1)}, bf16[18,24,512]{2,1,0:T(8,128)(2,1)S(1)}, u32[]{:S(2)}, u32[]{:S(2)}) collective-permute-start(bf16[18,24,512]{2,1,0:T(8,128)(2,1)S(1)} %get-tuple-element.140), channel_id=1, source_target_pairs={{0,12},{1,5},{4,8},{5,1},{8,4},{9,13},{12,0},{13,9},{2,14},{3,7},{... | collective-permute-start | bytes 1327112 | tf_op jit(solution)/shard_map/ppermute | solution.py:571
  92.4 32.1 %copy-start.2 = (bf16[24,12,1536]{2,0,1:T(8,128)(2,1)S(1)}, bf16[24,12,1536]{2,0,1:T(8,128)(2,1)}, u32[]{:S(2)}) copy-start(bf16[24,12,1536]{2,0,1:T(8,128)(2,1)} %param.11) | copy-start | bytes 2654212
  93.3 12.2 %collective-permute-start.21 = (bf16[10,24,512]{2,1,0:T(8,128)(2,1)S(1)}, bf16[10,24,512]{2,1,0:T(8,128)(2,1)S(1)}, u32[]{:S(2)}, u32[]{:S(2)}) collective-permute-start(bf16[10,24,512]{2,1,0:T(8,128)(2,1)S(1)} %get-tuple-element.142), channel_id=1, source_target_pairs={{0,2},{1,67},{2,0},{3,65},{64,66},{65,3},{66,64},{67,1},{4,6},{5,7... | collective-permute-start | bytes 737288 | tf_op jit(solution)/shard_map/ppermute | solution.py:571
  94.1 11.4 %collective-permute-start.22 = (bf16[10,24,512]{2,1,0:T(8,128)(2,1)S(1)}, bf16[10,24,512]{2,1,0:T(8,128)(2,1)S(1)}, u32[]{:S(2)}, u32[]{:S(2)}) collective-permute-start(bf16[10,24,512]{2,1,0:T(8,128)(2,1)S(1)} %get-tuple-element.144), channel_id=1, source_target_pairs={{0,4},{1,13},{4,0},{5,9},{8,12},{9,5},{12,8},{13,1},{2,6},{3,15},{... | collective-permute-start | bytes 737288 | tf_op jit(solution)/shard_map/ppermute | solution.py:571
  96.8 8.7 %collective-permute-start.23 = (bf16[10,24,512]{2,1,0:T(8,128)(2,1)S(1)}, bf16[10,24,512]{2,1,0:T(8,128)(2,1)S(1)}, u32[]{:S(2)}, u32[]{:S(2)}) collective-permute-start(bf16[10,24,512]{2,1,0:T(8,128)(2,1)S(1)} %get-tuple-element.146), channel_id=1, source_target_pairs={{0,16},{1,49},{16,0},{17,33},{32,48},{33,17},{48,32},{49,1},{2,18}... | collective-permute-start | bytes 737288 | tf_op jit(solution)/shard_map/ppermute | solution.py:571
  96.9 8.6 %collective-permute-start.12 = (bf16[72,1536]{1,0:T(8,128)(2,1)S(1)}, bf16[72,1536]{1,0:T(8,128)(2,1)S(1)}, u32[]{:S(2)}, u32[]{:S(2)}) collective-permute-start(bf16[72,1536]{1,0:T(8,128)(2,1)S(1)} %get-tuple-element.124), channel_id=1, source_target_pairs={{0,124},{4,0},{8,4},{12,8},{16,12},{20,16},{24,20},{28,24},{32,28}... | collective-permute-start | bytes 663560 | tf_op jit(solution)/shard_map/ppermute | solution.py:571
  101.3 15.4 %collective-permute-start.13 = (bf16[72,1536]{1,0:T(8,128)(2,1)S(1)}, bf16[72,1536]{1,0:T(8,128)(2,1)S(1)}, u32[]{:S(2)}, u32[]{:S(2)}) collective-permute-start(bf16[72,1536]{1,0:T(8,128)(2,1)S(1)} %get-tuple-element.126), channel_id=1, source_target_pairs={{0,4},{4,8},{8,12},{12,16},{16,20},{20,24},{24,28},{28,32},{32,36}... | collective-permute-start | bytes 663560 | tf_op jit(solution)/shard_map/ppermute | solution.py:571
  106.3 10.5 %collective-permute-start.24 = (bf16[6,24,512]{2,1,0:T(8,128)(2,1)S(1)}, bf16[6,24,512]{2,1,0:T(8,128)(2,1)S(1)}, u32[]{:S(2)}, u32[]{:S(2)}) collective-permute-start(bf16[6,24,512]{2,1,0:T(8,128)(2,1)S(1)} %get-tuple-element.148), channel_id=1, source_target_pairs={{0,66},{1,3},{2,64},{3,1},{64,2},{65,67},{66,0},{67,65},{4,70},{5,... | collective-permute-start | bytes 442376 | tf_op jit(solution)/shard_map/ppermute | solution.py:571
  106.4 10.4 %collective-permute-start.25 = (bf16[6,24,512]{2,1,0:T(8,128)(2,1)S(1)}, bf16[6,24,512]{2,1,0:T(8,128)(2,1)S(1)}, u32[]{:S(2)}, u32[]{:S(2)}) collective-permute-start(bf16[6,24,512]{2,1,0:T(8,128)(2,1)S(1)} %get-tuple-element.150), channel_id=1, source_target_pairs={{0,12},{1,5},{4,8},{5,1},{8,4},{9,13},{12,0},{13,9},{2,14},{3,7},{... | collective-permute-start | bytes 442376 | tf_op jit(solution)/shard_map/ppermute | solution.py:571
  106.5 10.3 %collective-permute-start.26 = (bf16[6,24,512]{2,1,0:T(8,128)(2,1)S(1)}, bf16[6,24,512]{2,1,0:T(8,128)(2,1)S(1)}, u32[]{:S(2)}, u32[]{:S(2)}) collective-permute-start(bf16[6,24,512]{2,1,0:T(8,128)(2,1)S(1)} %get-tuple-element.152), channel_id=1, source_target_pairs={{0,48},{1,17},{16,32},{17,1},{32,16},{33,49},{48,0},{49,33},{2,50}... | collective-permute-start | bytes 442376 | tf_op jit(solution)/shard_map/ppermute | solution.py:571
  107.0 12.8 %collective-permute-start.14 = (bf16[36,1536]{1,0:T(8,128)(2,1)S(1)}, bf16[36,1536]{1,0:T(8,128)(2,1)S(1)}, u32[]{:S(2)}, u32[]{:S(2)}) collective-permute-start(bf16[36,1536]{1,0:T(8,128)(2,1)S(1)} %last_rows.1), channel_id=1, source_target_pairs={{0,1},{1,2},{2,3},{3,0},{4,5},{5,6},{6,7},{7,4},{8,9},{9,10},{10,1... | collective-permute-start | bytes 331784 | tf_op jit(solution)/shard_map/ppermute | solution.py:571
  117.4 4.8 %collective-permute-start.27 = (bf16[4,24,512]{2,1,0:T(8,128)(2,1)S(1)}, bf16[4,24,512]{2,1,0:T(8,128)(2,1)S(1)}, u32[]{:S(2)}, u32[]{:S(2)}) collective-permute-start(bf16[4,24,512]{2,1,0:T(8,128)(2,1)S(1)} %get-tuple-element.154), channel_id=1, source_target_pairs={{0,4},{1,13},{4,0},{5,9},{8,12},{9,5},{12,8},{13,1},{2,6},{3,15},{... | collective-permute-start | bytes 294920 | tf_op jit(solution)/shard_map/ppermute | solution.py:571
  117.5 4.8 %collective-permute-start.28 = (bf16[4,24,512]{2,1,0:T(8,128)(2,1)S(1)}, bf16[4,24,512]{2,1,0:T(8,128)(2,1)S(1)}, u32[]{:S(2)}, u32[]{:S(2)}) collective-permute-start(bf16[4,24,512]{2,1,0:T(8,128)(2,1)S(1)} %get-tuple-element.156), channel_id=1, source_target_pairs={{0,16},{1,49},{16,0},{17,33},{32,48},{33,17},{48,32},{49,1},{2,18}... | collective-permute-start | bytes 294920 | tf_op jit(solution)/shard_map/ppermute | solution.py:571
  117.6 4.8 %collective-permute-start.29 = (bf16[4,24,512]{2,1,0:T(8,128)(2,1)S(1)}, bf16[4,24,512]{2,1,0:T(8,128)(2,1)S(1)}, u32[]{:S(2)}, u32[]{:S(2)}) collective-permute-start(bf16[4,24,512]{2,1,0:T(8,128)(2,1)S(1)} %get-tuple-element.158), channel_id=1, source_target_pairs={{0,2},{1,67},{2,0},{3,65},{64,66},{65,3},{66,64},{67,1},{4,6},{5,7... | collective-permute-start | bytes 294920 | tf_op jit(solution)/shard_map/ppermute | solution.py:571
  123.0 3.3 %collective-permute-start.30 = (bf16[3,24,512]{2,1,0:T(8,128)(2,1)S(1)}, bf16[3,24,512]{2,1,0:T(8,128)(2,1)S(1)}, u32[]{:S(2)}, u32[]{:S(2)}) collective-permute-start(bf16[3,24,512]{2,1,0:T(8,128)(2,1)S(1)} %get-tuple-element.160), channel_id=1, source_target_pairs={{0,12},{1,5},{4,8},{5,1},{8,4},{9,13},{12,0},{13,9},{2,14},{3,7},{... | collective-permute-start | bytes 221192 | tf_op jit(solution)/shard_map/ppermute | solution.py:571
  123.4 3.2 %collective-permute-start.31 = (bf16[3,24,512]{2,1,0:T(8,128)(2,1)S(1)}, bf16[3,24,512]{2,1,0:T(8,128)(2,1)S(1)}, u32[]{:S(2)}, u32[]{:S(2)}) collective-permute-start(bf16[3,24,512]{2,1,0:T(8,128)(2,1)S(1)} %get-tuple-element.162), channel_id=1, source_target_pairs={{0,48},{1,17},{16,32},{17,1},{32,16},{33,49},{48,0},{49,33},{2,50}... | collective-permute-start | bytes 221192 | tf_op jit(solution)/shard_map/ppermute | solution.py:571
  123.4 3.2 %collective-permute-start.32 = (bf16[3,24,512]{2,1,0:T(8,128)(2,1)S(1)}, bf16[3,24,512]{2,1,0:T(8,128)(2,1)S(1)}, u32[]{:S(2)}, u32[]{:S(2)}) collective-permute-start(bf16[3,24,512]{2,1,0:T(8,128)(2,1)S(1)} %get-tuple-element.164), channel_id=1, source_target_pairs={{0,66},{1,3},{2,64},{3,1},{64,2},{65,67},{66,0},{67,65},{4,70},{5,... | collective-permute-start | bytes 221192 | tf_op jit(solution)/shard_map/ppermute | solution.py:571
  126.7 10.7 %collective-permute-start.33 = (bf16[9,24,512]{2,1,0:T(8,128)(2,1)S(1)}, bf16[9,24,512]{2,1,0:T(8,128)(2,1)S(1)}, u32[]{:S(2)}, u32[]{:S(2)}) collective-permute-start(bf16[9,24,512]{2,1,0:T(8,128)(2,1)S(1)} %total.1.own), channel_id=1, source_target_pairs={{0,1},{1,0},{2,3},{3,2},{4,5},{5,4},{6,7},{7,6},{8,9},{9,8},{10,11... | collective-permute-start | bytes 663560 | tf_op jit(solution)/shard_map/ppermute | solution.py:571
  (8 other events, 7.2 us)

commit v5 on v4

--- a/solution.py
+++ b/solution.py
@@ -167,20 +167,24 @@
             rows[r * 12 : (r + 1) * 12, t * 128 : (t + 1) * 128] = grid[t, pl.ds(r, 12, stride=24), :]
 
 
-def first_body(own, low, upper):
+def first_body(own, low, upper, lower):
     low[...] = jnp.concatenate([own[j].astype(F32)[:SHIFT_H] for j in range(12)], 0).astype(BF16)
     upper[...] = jnp.concatenate(
         [own[j].astype(F32)[SHIFT_H : SHIFT_H + HALF_ROWS] for j in range(SHIFT_W)], 0
     ).astype(BF16)
-
-
-def to_east_body(own, low, out):
+    lower[...] = jnp.concatenate(
+        [own[SHIFT_W + i].astype(F32)[SHIFT_H + HALF_ROWS :] for i in range(SHIFT_W)], 0
+    ).astype(BF16)
+
+
+def to_east_body(lower, low, out):
+    count = HALF_ROWS - SHIFT_H
     out[...] = jnp.concatenate(
         [
             piece
             for i in range(SHIFT_W)
             for piece in (
-                own[SHIFT_W + i].astype(F32)[SHIFT_H + HALF_ROWS :],
+                f32_rows(lower, i * count, count),
                 f32_rows(low, (SHIFT_W + i) * SHIFT_H, SHIFT_H),
             )
         ],
@@ -206,7 +210,7 @@
             copies[3 * g + j].wait()
             product = dot(x[...], wide[:, lo : lo + 256])
             if j != 1:
-                product = product + (query_bias, None, value_bias)[j][:, g * 256 : (g + 1) * 256]
+                product = product + (query_bias, None, value_bias)[j][g * 256 : (g + 1) * 256].reshape(1, 256)
             projected[:, lo : lo + 256] = product
         for half in range(2):
             lo = g * 256 + half * 128
@@ -235,7 +239,7 @@
         normed = center * inv_std
         up = rows[at, :]
         total = total + jnp.sum(up * normed, 0, keepdims=True)
-        scaled = up * gain[...]
+        scaled = up * gain[...].reshape(1, C)
         grad = inv_std * (
             scaled
             - jnp.mean(scaled, -1, keepdims=True)
@@ -297,20 +301,33 @@
     small[at * 48 : at * 48 + 16, 384:] = lines
 
 
-def attention_body(
-    side, scale, q_ref, k_ref, v_ref, da_ref, pair_bias, row, col, gain_part, grads, small
-):
+def attention_body(side, scale, projected, da, pair_bias, row, col, gain_part, grads, small, heads, sems):
+    copies = []
+    for hp in range(3):
+        for j in range(4):
+            lane = hp * 128 if j == 3 else pl.multiple_of(j * HC + side[0] * HALF + hp * 128, 128)
+            source = (da if j == 3 else projected).at[:, pl.ds(lane, 128)]
+            copies.append(pltpu.make_async_copy(source, heads.at[hp, j], sems.at[4 * hp + j]))
+            copies[-1].start()
     pens = penalties(row[...], col[...])
-    head = side[0] * 6 + 2 * pl.program_id(0)
     small[...] = jnp.zeros_like(small)
-    store_pair(
-        grads,
-        small,
-        0,
-        *attention_pair(
-            scale, head, q_ref[...], k_ref[...], v_ref[...], da_ref[...], pair_bias[...], pens, gain_part[...]
-        ),
-    )
+    for hp in range(3):
+        for copy in copies[4 * hp : 4 * hp + 4]:
+            copy.wait()
+        head = side[0] * 6 + 2 * hp
+        store_pair(
+            grads,
+            small,
+            hp,
+            *attention_pair(
+                scale,
+                head,
+                *(heads[hp, j] for j in range(4)),
+                pair_bias[pl.ds(pl.multiple_of(head * WIN, 8), 2 * WIN), :],
+                pens,
+                gain_part[:, pl.ds(pl.multiple_of(side[0] * HC + hp * 256, 128), 256)],
+            ),
+        )
 
 
 def backward_body(
@@ -600,17 +617,18 @@
 
 def first_messages(grid):
     return call(
-        first_body, [shape((36, C), BF16), shape((72, C), BF16)], [grid], scalars=0, name="first"
-    )
-
-
-def halo(grid):
-    low, upper = first_messages(grid)
+        first_body,
+        [shape((36, C), BF16), shape((72, C), BF16), shape((54, C), BF16)],
+        [grid],
+        scalars=0,
+        name="first",
+    )
+
+
+def halo(low, upper, lower):
     low = lat_step(low, -1)
     east = lon_step(upper, -1)
-    (lower,) = call(
-        to_east_body, [shape((72, C), BF16)], [grid, low], scalars=0, name="to_east"
-    )
+    (lower,) = call(to_east_body, [shape((72, C), BF16)], [lower, low], scalars=0, name="to_east")
     return east, low, lower
 
 
@@ -633,25 +651,25 @@
     mine = core.astype(jnp.int32).reshape(1)
     theirs = 1 - mine
     scale = logit_scale
-    query_row, value_row = query_bias.reshape(1, HC), value_bias.reshape(1, HC)
     pair_rows = pair_bias.reshape(HEADS * WIN, WIN)
-    gain = norm_gain.reshape(1, C)
+    gain = norm_gain
 
     features = features.transpose(1, 0, 2)
     upstream = upstream.transpose(1, 0, 2)
-    east, low, lower = halo(features)
-    late, region_ids, lower = lax.optimization_barrier((upstream, region_ids, lower))
+    late = first_messages(upstream)
+    east, low, lower = halo(*first_messages(features))
+    late, region_ids, lower = lax.optimization_barrier((late, region_ids, lower))
     came = east, lon_step(lower, 1), low
     lower_ids = lon_step(region_ids[HALF_ROWS:], 1)
     region_ids = jnp.concatenate([region_ids[:HALF_ROWS], lower_ids], 0)
     region_row = region_ids.reshape(WINDOWS, WIN)
     region_col = region_ids.reshape(-1, 1)
-    east, low, lower = halo(late)
+    east, low, lower = halo(*late)
     came_late = east, lon_step(lower, 1), low
     x, projected, attended = call(
         forward_body,
         [shape((CELLS, C), BF16), shape((CELLS, 3 * HC), F32), shape((CELLS, HC), BF16)],
-        [scale, features, *came, qkv_weight, query_row, value_row, pair_rows, region_row, region_col],
+        [scale, features, *came, qkv_weight, query_bias, value_bias, pair_rows, region_row, region_col],
         scratch=[
             pltpu.VMEM((12, CELLS, 128), F32),
             pltpu.VMEM((CELLS, C), F32),
@@ -663,7 +681,7 @@
         name="forward",
     )
     x_other = core_swap(x)
-    mixed_low, attended_grad, gain_part, grads_theirs, small_theirs, attended_mine, attended_theirs = call(
+    mixed_low, grad_mine, gain_part, grads_theirs, small_theirs, attended_mine, attended_theirs = call(
         backward_body,
         [
             shape((CELLS, C), BF16),
@@ -705,38 +723,19 @@
     mixed_other = core_swap(mixed_low)
     attended_other = core_swap(attended_theirs)
 
-    def attention(side):
-        def cols(base):
-            return lambda i, side, scale: (0, base + side[0] * 3 + i)
-
-        whole = lambda i, side, scale: (0, 0)
-        block = (CELLS, 128)
-        return grid_call(
-            attention_body,
-            (3,),
-            [side, scale],
-            [
-                (projected, block, cols(0)),
-                (projected, block, cols(6)),
-                (projected, block, cols(12)),
-                (attended_grad, block, lambda i, side, scale: (0, i)),
-                (pair_rows, (2 * WIN, WIN), lambda i, side, scale: (side[0] * 3 + i, 0)),
-                (region_row, (WINDOWS, WIN), whole),
-                (region_col, (CELLS, 1), whole),
-                (gain_part, (1, 256), cols(0)),
-            ],
-            [
-                (shape((CELLS, 3 * HALF), BF16), (CELLS, HALF), lambda i, side, scale: (0, i)),
-                (shape((144, 512), F32), (48, 512), lambda i, side, scale: (i, 0)),
-            ],
-            flops=2 * CELLS * WIN * 128 * 6 * 3,
-            vmem=16,
-            name="attention",
-        )
-
     grads_other = core_swap(grads_theirs)
     small_other = core_swap(small_theirs)
-    grads_mine, small_mine = attention(mine)
+    grads_mine, small_mine = call(
+        attention_body,
+        [shape((CELLS, 3 * HALF), BF16), shape((144, 512), F32)],
+        [mine, scale, projected, grad_mine, pair_rows, region_row, region_col, gain_part],
+        scalars=2,
+        scratch=[pltpu.VMEM((3, 4, CELLS, 128), F32), pltpu.SemaphoreType.DMA((12,))],
+        flops=2 * CELLS * WIN * 128 * 6 * 3,
+        vmem=16,
+        near=(2, 3),
+        name="attention",
+    )
 
     parts = call(
         weight_body,
@@ -805,10 +804,6 @@
         if step == 0:
             order, stay_low = lax.optimization_barrier((order, stay_low))
         if step == 3:
-            order, from_west = lax.optimization_barrier((order, from_west))
-        if step == 4:
-            order, low = lax.optimization_barrier((order, low))
-        if step == 2:
             order, last = lax.optimization_barrier((order, last))
         parts = call(body, [shape((left // 2 + EXTRA,) + BLOCK, BF16)] * 6, [order, *terms], vmem=10, name="halve")
     (input_grad,) = call(

time: 139 us -> 139 us (level)
  starting transfers between devices: 59.8 us -> 56.2 us
  local copies, waits for them, and re-layouts: 8.84 us -> 11.3 us
  waiting for transfers between devices: 22.1 us -> 24 us
    pallas_call x2 -> x1, Pallas kernels: 9.41 us -> 4.97 us  [grid_call(): pl.pallas_call(body, grid_spec=spec, out_shape=results, compiler_params=p...]
    pallas_call x16 -> x17, Pallas kernels: 37 us -> 40.9 us  [call(): pl.pallas_call(body, out_shape=list(outs), in_specs=specs, out_specs=[VME...]
    ppermute x34, starting transfers between devices: 59.8 us -> 56.2 us  [permuted(): return lax.ppermute(value, axes, pairs)]
    unnamed x44 -> x42, local copies, waits for them, and re-layouts: 7.12 us -> 10.2 us
    ppermute x34, waiting for transfers between devices: 22.1 us -> 24 us  [permuted(): return lax.ppermute(value, axes, pairs)]
  transfers between devices with their start and end apart: 34 -> 34, of which waited for: 14 -> 15; matrix products, arithmetic and copies ran while one was open for 1% -> 1% of each run, Pallas kernels for 25% -> 25%
where the time goes in v5:
time: 139 us; the launch traced here: 138 us
  starting transfers between devices  56.2 us (40%)
  Pallas kernels  45.8 us (33%)
  waiting for transfers between devices  24 us (17%)
  local copies, waits for them, and re-layouts  11.3 us (8%)
    ppermute x34, starting transfers between devices, permuted(): return lax.ppermute(value, axes, pairs)  56.2 us
    pallas_call x17, Pallas kernels, call(): pl.pallas_call(body, out_shape=list(outs), in_specs=specs, out_specs=[VME...  40.9 us
    ppermute x34, waiting for transfers between devices, permuted(): return lax.ppermute(value, axes, pairs)  24 us
    unnamed x42, local copies, waits for them, and re-layouts  10.2 us
    pallas_call x1, Pallas kernels, grid_call(): pl.pallas_call(body, grid_spec=spec, out_shape=results, compiler_params=p...  4.97 us
  transfers between devices with their start and end apart: 34, of which 15 were waited for; matrix products, arithmetic and copies ran while one was open for 1% of the time, Pallas kernels for 25%

profile of v5, /device:TPU:1, one launch (start us, length us, event | category | flops | bytes accessed | tf_op | source)
XLA Modules:
  0.0 138.5 jit_solution(8487095786065537800)
XLA Ops:
  0.7 1.2 copy-done.4
  1.9 0.7 first.2
  2.6 1.4 %collective-permute-start.1 = (bf16[36,1536]{1,0:T(8,128)(2,1)S(1)}, bf16[36,1536]{1,0:T(8,128)(2,1)S(1)}, u32[]{:S(2)}, u32[]{:S(2)}) collective-permute-start(bf16[36,1536]{1,0:T(8,128)(2,1)S(1)} %get-tuple-element.100), channel_id=1, source_target_pairs={{0,3},{1,0},{2,1},{3,2},{4,7},{5,4},{6,5},{7,6},{8,11},{9,8},{10,9... | collective-permute-start | bytes 331784 | tf_op jit(solution)/shard_map/ppermute | solution.py:588
  4.0 8.7 %collective-permute-start = (bf16[72,1536]{1,0:T(8,128)(2,1)}, bf16[72,1536]{1,0:T(8,128)(2,1)S(1)}, u32[]{:S(2)}, u32[]{:S(2)}) collective-permute-start(bf16[72,1536]{1,0:T(8,128)(2,1)} %get-tuple-element.95), channel_id=1, source_target_pairs={{0,124},{4,0},{8,4},{12,8},{16,12},{20,16},{24,20},{28,24},{32,28}... | collective-permute-start | bytes 663560 | tf_op jit(solution)/shard_map/ppermute | solution.py:588
  12.7 1.2 copy-done.1
  14.2 1.1 collective-permute-start.6
  15.2 0.8 fusion
  16.1 7.2 %collective-permute-start.5 = (bf16[72,1536]{1,0:T(8,128)(2,1)S(1)}, bf16[72,1536]{1,0:T(8,128)(2,1)S(1)}, u32[]{:S(2)}, u32[]{:S(2)}) collective-permute-start(bf16[72,1536]{1,0:T(8,128)(2,1)S(1)} %get-tuple-element.106), channel_id=1, source_target_pairs={{0,124},{4,0},{8,4},{12,8},{16,12},{20,16},{24,20},{28,24},{32,28}... | collective-permute-start | bytes 663560 | tf_op jit(solution)/shard_map/ppermute | solution.py:588
  23.4 4.7 %collective-permute-done.3 = s32[12,12]{0,1:T(8,128)S(1)} collective-permute-done((s32[12,12]{0,1:T(8,128)S(1)}, s32[12,12]{0,1:T(8,128)S(1)}, u32[]{:S(2)}, u32[]{:S(2)}) %collective-permute-start.3) | collective-permute-done | bytes 608 | tf_op jit(solution)/shard_map/ppermute | solution.py:588
  28.6 10.6 %forward.1 = (bf16[288,1536]{1,0:T(8,128)(2,1)}, f32[288,2304]{1,0:T(8,128)}, bf16[288,768]{1,0:T(8,128)(2,1)S(1)}) custom-call(f32[12]{0:T(128)S(1)} %copy-done.13, bf16[12,24,1536]{2,1,0:T(8,128)(2,1)S(1)} %bitcast.18, bf16[72,1536]{1,0:T(8,128)(2,1)S(1)} %collective-permute-done.east, bf16[72,1536]{1,0:T(8,128)(2,1)S(1)} %collective-permute-done.2.west, ...), custom_call_target="tpu_custom_call" | custom-call | flops 2038431744 | bytes 12754224 | tf_op jit(solution)/shard_map/forward/pallas_call | solution.py:60
  39.1 1.1 collective-permute-start.4
  41.6 0.9 copy-done.9
  42.5 0.9 copy-done.11
  43.5 10.5 %backward.1 = (bf16[288,1536]{1,0:T(8,128)(2,1)}, f32[288,384]{1,0:T(8,128)S(1)}, f32[1,1536]{1,0:T(1,128)S(1)}, bf16[288,1152]{1,0:T(8,128)(2,1)}, f32[144,512]...) custom-call(s32[1]{0:T(128)S(6)} %sub.3.side, f32[12]{0:T(128)S(1)} %copy-done.13, ...), custom_call_target="tpu_custom_call" | custom-call | flops 1454505984 | bytes 9884980 | tf_op jit(solution)/shard_map/backward/pallas_call | solution.py:60
  54.0 0.8 copy-done.6
  54.7 0.7 copy-done.17
  56.5 1.0 copy-done.7
  57.6 4.5 %attention.1 = (bf16[288,1152]{1,0:T(8,128)(2,1)S(1)}, f32[144,512]{1,0:T(8,128)S(1)}) custom-call(s32[1]{0:T(128)} %bitcast.side.core, f32[12]{0:T(128)S(1)} %copy-done.13, f32[288,2304]{1,0:T(8,128)S(1)} %copy-done, f32[288,384]{1,0:T(8,128)S(1)} %copy-done.7, f32[864,72]{1,0:T(8,128)S(1)} %bitcast.16, s32[4,72]{1,0:T(4,128)S(1)} %reshape.30.row, ...), custom_call_target="tpu_custom_call" | custom-call | flops 95551488 | bytes 4312372 | tf_op jit(solution)/shard_map/attention/pallas_call | solution.py:60
  62.1 1.2 copy-done.16
  63.3 0.9 copy-done.18
  64.2 7.9 %weights.1 = (bf16[34,24,512]{2,1,0:T(8,128)(2,1)S(1)}, bf16[34,24,512]{2,1,0:T(8,128)(2,1)S(1)}, bf16[34,24,512]{2,1,0:T(8,128)(2,1)S(1)}, bf16[34,24,512]{2,1,...) custom-call(s32[4]{0:T(128)S(1)} %pad_add_fusion.1.place, ...), custom_call_target="tpu_custom_call" | custom-call | flops 2717908992 | bytes 10911760 | tf_op jit(solution)/shard_map/weights/pallas_call | solution.py:60
  72.4 3.2 %collective-permute-start.15 = (bf16[34,24,512]{2,1,0:T(8,128)(2,1)S(1)}, bf16[34,24,512]{2,1,0:T(8,128)(2,1)S(1)}, u32[]{:S(2)}, u32[]{:S(2)}) collective-permute-start(bf16[34,24,512]{2,1,0:T(8,128)(2,1)S(1)} %get-tuple-element.135), channel_id=1, source_target_pairs={{0,4},{1,13},{4,0},{5,9},{8,12},{9,5},{12,8},{13,1},{2,6},{3,15},{... | collective-permute-start | bytes 2506760 | tf_op jit(solution)/shard_map/ppermute | solution.py:588
  75.6 5.0 %branch.1 = (bf16[72,1536]{1,0:T(8,128)(2,1)S(1)}, bf16[72,1536]{1,0:T(8,128)(2,1)S(1)}, bf16[72,1536]{1,0:T(8,128)(2,1)S(1)}, bf16[72,1536]{1,0:T(8,128)(2,1)S(1)}) custom-call(s32[1]{0:T(128)} %bitcast.side.core, bf16[1536,2304]{1,0:T(8,128)(2,1)S(1)} %bitcast.10, bf16[288,1152]{1,0:T(8,128)(2,1)S(1)} %get-tuple-element.111.p0.own, ...), custom_call_target="tpu_custom_call" | custom-call | flops 2038431744 | bytes 9289728 | tf_op jit(solution)/shard_map/branch/pallas_call | solution.py:82
  80.6 4.3 %collective-permute-done.13.refs_1_ = bf16[34,24,512]{2,1,0:T(8,128)(2,1)S(1)} collective-permute-done((bf16[34,24,512]{2,1,0:T(8,128)(2,1)S(1)}, bf16[34,24,512]{2,1,0:T(8,128)(2,1)S(1)}, u32[]{:S(2)}, u32[]{:S(2)}) %collective-permute-start.13) | collective-permute-done | bytes 835616 | tf_op jit(solution)/shard_map/ppermute | solution.py:588
  85.5 1.1 halve.5
  86.9 7.2 %collective-permute-done.16.refs_1_ = bf16[18,24,512]{2,1,0:T(8,128)(2,1)S(1)} collective-permute-done((bf16[18,24,512]{2,1,0:T(8,128)(2,1)S(1)}, bf16[18,24,512]{2,1,0:T(8,128)(2,1)S(1)}, u32[]{:S(2)}, u32[]{:S(2)}) %collective-permute-start.16) | collective-permute-done | bytes 442400 | tf_op jit(solution)/shard_map/ppermute | solution.py:588
  94.3 0.9 halve.6
  95.2 2.2 %collective-permute-start.19 = (bf16[10,24,512]{2,1,0:T(8,128)(2,1)S(1)}, bf16[10,24,512]{2,1,0:T(8,128)(2,1)S(1)}, u32[]{:S(2)}, u32[]{:S(2)}) collective-permute-start(bf16[10,24,512]{2,1,0:T(8,128)(2,1)S(1)} %get-tuple-element.143), channel_id=1, source_target_pairs={{0,2},{1,67},{2,0},{3,65},{64,66},{65,3},{66,64},{67,1},{4,6},{5,7... | collective-permute-start | bytes 737288 | tf_op jit(solution)/shard_map/ppermute | solution.py:588
  97.4 1.3 collective-permute-start.20
  98.7 1.2 collective-permute-start.21
  100.0 3.4 %collective-permute-start.12 = (bf16[72,1536]{1,0:T(8,128)(2,1)S(1)}, bf16[72,1536]{1,0:T(8,128)(2,1)S(1)}, u32[]{:S(2)}, u32[]{:S(2)}) collective-permute-start(bf16[72,1536]{1,0:T(8,128)(2,1)S(1)} %get-tuple-element.128), channel_id=1, source_target_pairs={{0,124},{4,0},{8,4},{12,8},{16,12},{20,16},{24,20},{28,24},{32,28}... | collective-permute-start | bytes 663560 | tf_op jit(solution)/shard_map/ppermute | solution.py:588
  103.6 1.3 collective-permute-done.21.refs_5_
  105.0 0.7 halve.7
  105.7 1.1 collective-permute-start.22
  107.3 1.5 %collective-permute-start.31 = (bf16[72,1536]{1,0:T(8,128)(2,1)S(1)}, bf16[72,1536]{1,0:T(8,128)(2,1)S(1)}, u32[]{:S(2)}, u32[]{:S(2)}) collective-permute-start(bf16[72,1536]{1,0:T(8,128)(2,1)S(1)} %get-tuple-element.167), channel_id=1, source_target_pairs={{0,4},{4,8},{8,12},{12,16},{16,20},{20,24},{24,28},{28,32},{32,36}... | collective-permute-start | bytes 663560 | tf_op jit(solution)/shard_map/ppermute | solution.py:588
  108.8 1.2 collective-permute-done.22.refs_1_
  110.1 0.8 collective-permute-done.23.refs_3_
  111.8 1.4 %collective-permute-start.25 = (bf16[4,24,512]{2,1,0:T(8,128)(2,1)S(1)}, bf16[4,24,512]{2,1,0:T(8,128)(2,1)S(1)}, u32[]{:S(2)}, u32[]{:S(2)}) collective-permute-start(bf16[4,24,512]{2,1,0:T(8,128)(2,1)S(1)} %get-tuple-element.155), channel_id=1, source_target_pairs={{0,4},{1,13},{4,0},{5,9},{8,12},{9,5},{12,8},{13,1},{2,6},{3,15},{... | collective-permute-start | bytes 294920 | tf_op jit(solution)/shard_map/ppermute | solution.py:588
  113.2 2.6 %collective-permute-start.26 = (bf16[4,24,512]{2,1,0:T(8,128)(2,1)S(1)}, bf16[4,24,512]{2,1,0:T(8,128)(2,1)S(1)}, u32[]{:S(2)}, u32[]{:S(2)}) collective-permute-start(bf16[4,24,512]{2,1,0:T(8,128)(2,1)S(1)} %get-tuple-element.157), channel_id=1, source_target_pairs={{0,16},{1,49},{16,0},{17,33},{32,48},{33,17},{48,32},{49,1},{2,18}... | collective-permute-start | bytes 294920 | tf_op jit(solution)/shard_map/ppermute | solution.py:588
  115.8 0.7 collective-permute-start.27
  116.5 5.4 %collective-permute-start.32 = (bf16[36,1536]{1,0:T(8,128)(2,1)S(1)}, bf16[36,1536]{1,0:T(8,128)(2,1)S(1)}, u32[]{:S(2)}, u32[]{:S(2)}) collective-permute-start(bf16[36,1536]{1,0:T(8,128)(2,1)S(1)} %last_rows.1), channel_id=1, source_target_pairs={{0,1},{1,2},{2,3},{3,0},{4,5},{5,6},{6,7},{7,4},{8,9},{9,10},{10,1... | collective-permute-start | bytes 331784 | tf_op jit(solution)/shard_map/ppermute | solution.py:588
  122.5 1.6 %collective-permute-start.28 = (bf16[3,24,512]{2,1,0:T(8,128)(2,1)S(1)}, bf16[3,24,512]{2,1,0:T(8,128)(2,1)S(1)}, u32[]{:S(2)}, u32[]{:S(2)}) collective-permute-start(bf16[3,24,512]{2,1,0:T(8,128)(2,1)S(1)} %get-tuple-element.161), channel_id=1, source_target_pairs={{0,12},{1,5},{4,8},{5,1},{8,4},{9,13},{12,0},{13,9},{2,14},{3,7},{... | collective-permute-start | bytes 221192 | tf_op jit(solution)/shard_map/ppermute | solution.py:588
  124.2 1.7 %collective-permute-start.29 = (bf16[3,24,512]{2,1,0:T(8,128)(2,1)S(1)}, bf16[3,24,512]{2,1,0:T(8,128)(2,1)S(1)}, u32[]{:S(2)}, u32[]{:S(2)}) collective-permute-start(bf16[3,24,512]{2,1,0:T(8,128)(2,1)S(1)} %get-tuple-element.163), channel_id=1, source_target_pairs={{0,48},{1,17},{16,32},{17,1},{32,16},{33,49},{48,0},{49,33},{2,50}... | collective-permute-start | bytes 221192 | tf_op jit(solution)/shard_map/ppermute | solution.py:588
  126.0 1.3 merge.1
  127.7 1.5 %collective-permute-done.30.refs_5_ = bf16[3,24,512]{2,1,0:T(8,128)(2,1)S(1)} collective-permute-done((bf16[3,24,512]{2,1,0:T(8,128)(2,1)S(1)}, bf16[3,24,512]{2,1,0:T(8,128)(2,1)S(1)}, u32[]{:S(2)}, u32[]{:S(2)}) %collective-permute-start.30) | collective-permute-done | bytes 73760 | tf_op jit(solution)/shard_map/ppermute | solution.py:588
  129.2 7.3 %collective-permute-start.33 = (bf16[9,24,512]{2,1,0:T(8,128)(2,1)S(1)}, bf16[9,24,512]{2,1,0:T(8,128)(2,1)S(1)}, u32[]{:S(2)}, u32[]{:S(2)}) collective-permute-start(bf16[9,24,512]{2,1,0:T(8,128)(2,1)S(1)} %total.1.own), channel_id=1, source_target_pairs={{0,1},{1,0},{2,3},{3,2},{4,5},{5,4},{6,7},{7,6},{8,9},{9,8},{10,11... | collective-permute-start | bytes 663560 | tf_op jit(solution)/shard_map/ppermute | solution.py:588
  136.5 1.1 collective-permute-done.33.other
  137.6 0.9 finish.1
  (87 shorter events, 7.5 us)
Async XLA Ops:
  0.6 27.9 %copy-start.3 = (f32[12,72,72]{2,1,0:T(8,128)S(1)}, f32[12,72,72]{2,1,0:T(8,128)}, u32[]{:S(2)}) copy-start(f32[12,72,72]{2,1,0:T(8,128)} %param.17) | copy-start | bytes 746500
  0.6 1.2 copy-start.4
  1.9 26.6 %copy-start.13 = (f32[12]{0:T(128)S(1)}, f32[12]{0:T(128)}, u32[]{:S(2)}) copy-start(f32[12]{0:T(128)} %scale.5) | copy-start | bytes 148
  1.9 26.6 %copy-start.14 = (f32[768]{0:T(1024)S(1)}, f32[768]{0:T(1024)}, u32[]{:S(2)}) copy-start(f32[768]{0:T(1024)} %query_bias.1) | copy-start | bytes 9220
  1.9 26.7 %copy-start.15 = (f32[768]{0:T(1024)S(1)}, f32[768]{0:T(1024)}, u32[]{:S(2)}) copy-start(f32[768]{0:T(1024)} %value_bias.1) | copy-start | bytes 9220
  2.6 11.4 %collective-permute-start.1 = (bf16[36,1536]{1,0:T(8,128)(2,1)S(1)}, bf16[36,1536]{1,0:T(8,128)(2,1)S(1)}, u32[]{:S(2)}, u32[]{:S(2)}) collective-permute-start(bf16[36,1536]{1,0:T(8,128)(2,1)S(1)} %get-tuple-element.100), channel_id=1, source_target_pairs={{0,3},{1,0},{2,1},{3,2},{4,7},{5,4},{6,5},{7,6},{8,11},{9,8},{10,9... | collective-permute-start | bytes 331784 | tf_op jit(solution)/shard_map/ppermute | solution.py:588
  4.0 24.4 %collective-permute-start = (bf16[72,1536]{1,0:T(8,128)(2,1)}, bf16[72,1536]{1,0:T(8,128)(2,1)S(1)}, u32[]{:S(2)}, u32[]{:S(2)}) collective-permute-start(bf16[72,1536]{1,0:T(8,128)(2,1)} %get-tuple-element.95), channel_id=1, source_target_pairs={{0,124},{4,0},{8,4},{12,8},{16,12},{20,16},{24,20},{28,24},{32,28}... | collective-permute-start | bytes 663560 | tf_op jit(solution)/shard_map/ppermute | solution.py:588
  12.7 1.2 copy-start.1
  13.9 14.7 %copy-start.5 = (bf16[24,12,1536]{2,0,1:T(8,128)(2,1)S(1)}, bf16[24,12,1536]{2,0,1:T(8,128)(2,1)}, u32[]{:S(2)}) copy-start(bf16[24,12,1536]{2,0,1:T(8,128)(2,1)} %param.10) | copy-start | bytes 2654212
  14.2 9.1 %collective-permute-start.6 = (bf16[36,1536]{1,0:T(8,128)(2,1)S(1)}, bf16[36,1536]{1,0:T(8,128)(2,1)S(1)}, u32[]{:S(2)}, u32[]{:S(2)}) collective-permute-start(bf16[36,1536]{1,0:T(8,128)(2,1)S(1)} %get-tuple-element.108), channel_id=1, source_target_pairs={{0,3},{1,0},{2,1},{3,2},{4,7},{5,4},{6,5},{7,6},{8,11},{9,8},{10,9... | collective-permute-start | bytes 331784 | tf_op jit(solution)/shard_map/ppermute | solution.py:588
  15.2 13.3 %collective-permute-start.2 = (bf16[72,1536]{1,0:T(8,128)(2,1)S(1)}, bf16[72,1536]{1,0:T(8,128)(2,1)S(1)}, u32[]{:S(2)}, u32[]{:S(2)}) collective-permute-start(bf16[72,1536]{1,0:T(8,128)(2,1)S(1)} %to_east.2), channel_id=1, source_target_pairs={{0,4},{4,8},{8,12},{12,16},{16,20},{20,24},{24,28},{28,32},{32,36}... | collective-permute-start | bytes 663560 | tf_op jit(solution)/shard_map/ppermute | solution.py:588
  16.1 12.0 %collective-permute-start.3 = (s32[12,12]{0,1:T(8,128)S(1)}, s32[12,12]{0,1:T(8,128)S(1)}, u32[]{:S(2)}, u32[]{:S(2)}) collective-permute-start(s32[12,12]{0,1:T(8,128)S(1)} %get-tuple-element.183), channel_id=1, source_target_pairs={{0,4},{4,8},{8,12},{12,16},{16,20},{20,24},{24,28},{28,32},{32,36}... | collective-permute-start | bytes 1736 | tf_op jit(solution)/shard_map/ppermute | solution.py:588
  16.1 24.2 %collective-permute-start.5 = (bf16[72,1536]{1,0:T(8,128)(2,1)S(1)}, bf16[72,1536]{1,0:T(8,128)(2,1)S(1)}, u32[]{:S(2)}, u32[]{:S(2)}) collective-permute-start(bf16[72,1536]{1,0:T(8,128)(2,1)S(1)} %get-tuple-element.106), channel_id=1, source_target_pairs={{0,124},{4,0},{8,4},{12,8},{16,12},{20,16},{24,20},{28,24},{32,28}... | collective-permute-start | bytes 663560 | tf_op jit(solution)/shard_map/ppermute | solution.py:588
  23.4 17.6 %collective-permute-start.7 = (bf16[72,1536]{1,0:T(8,128)(2,1)S(1)}, bf16[72,1536]{1,0:T(8,128)(2,1)S(1)}, u32[]{:S(2)}, u32[]{:S(2)}) collective-permute-start(bf16[72,1536]{1,0:T(8,128)(2,1)S(1)} %to_east.3), channel_id=1, source_target_pairs={{0,4},{4,8},{8,12},{12,16},{16,20},{20,24},{24,28},{28,32},{32,36}... | collective-permute-start | bytes 663560 | tf_op jit(solution)/shard_map/ppermute | solution.py:588
  28.5 13.1 %copy-start.12 = (f32[1536]{0:T(1024)S(1)}, f32[1536]{0:T(1024)}, u32[]{:S(2)}) copy-start(f32[1536]{0:T(1024)} %gain.1) | copy-start | bytes 18436
  39.1 23.0 %collective-permute-start.4 = (bf16[288,1536]{1,0:T(8,128)(2,1)}, bf16[288,1536]{1,0:T(8,128)(2,1)}, u32[]{:S(2)}, u32[]{:S(2)}) collective-permute-start(bf16[288,1536]{1,0:T(8,128)(2,1)} %get-tuple-element.103.x0), channel_id=1, source_target_pairs={{0,1},{1,0},{2,3},{3,2},{4,5},{5,4},{6,7},{7,6},{8,9},{9,8},{10,11... | collective-permute-start | bytes 2654216 | tf_op jit(solution)/shard_map/ppermute | solution.py:588
  43.5 13.1 %copy-start = (f32[288,2304]{1,0:T(8,128)S(1)}, f32[288,2304]{1,0:T(8,128)}, u32[]{:S(2)}) copy-start(f32[288,2304]{1,0:T(8,128)} %get-tuple-element.104.projected) | copy-start | bytes 7962628
  55.4 6.7 %collective-permute-start.9 = (bf16[288,1536]{1,0:T(8,128)(2,1)}, bf16[288,1536]{1,0:T(8,128)(2,1)}, u32[]{:S(2)}, u32[]{:S(2)}) collective-permute-start(bf16[288,1536]{1,0:T(8,128)(2,1)} %get-tuple-element.113.m0), channel_id=1, source_target_pairs={{0,1},{1,0},{2,3},{3,2},{4,5},{5,4},{6,7},{7,6},{8,9},{9,8},{10,11... | collective-permute-start | bytes 2654216 | tf_op jit(solution)/shard_map/ppermute | solution.py:588
  55.5 6.6 %collective-permute-start.8 = (bf16[288,1152]{1,0:T(8,128)(2,1)}, bf16[288,1152]{1,0:T(8,128)(2,1)}, u32[]{:S(2)}, u32[]{:S(2)}) collective-permute-start(bf16[288,1152]{1,0:T(8,128)(2,1)} %get-tuple-element.112.theirs), channel_id=1, source_target_pairs={{0,1},{1,0},{2,3},{3,2},{4,5},{5,4},{6,7},{7,6},{8,9},{9,8},{10,11... | collective-permute-start | bytes 1990664 | tf_op jit(solution)/shard_map/ppermute | solution.py:588
  56.0 6.1 %collective-permute-start.11 = (f32[144,512]{1,0:T(8,128)}, f32[144,512]{1,0:T(8,128)}, u32[]{:S(2)}, u32[]{:S(2)}) collective-permute-start(f32[144,512]{1,0:T(8,128)} %get-tuple-element.117), channel_id=1, source_target_pairs={{0,1},{1,0},{2,3},{3,2},{4,5},{5,4},{6,7},{7,6},{8,9},{9,8},{10,11... | collective-permute-start | bytes 884744 | tf_op jit(solution)/shard_map/ppermute | solution.py:588
  56.0 6.1 %collective-permute-start.10 = (bf16[288,384]{1,0:T(8,128)(2,1)}, bf16[288,384]{1,0:T(8,128)(2,1)}, u32[]{:S(2)}, u32[]{:S(2)}) collective-permute-start(bf16[288,384]{1,0:T(8,128)(2,1)} %get-tuple-element.115), channel_id=1, source_target_pairs={{0,1},{1,0},{2,3},{3,2},{4,5},{5,4},{6,7},{7,6},{8,9},{9,8},{10,11... | collective-permute-start | bytes 663560 | tf_op jit(solution)/shard_map/ppermute | solution.py:588
  56.5 1.0 copy-start.7
  57.6 18.0 %slice-start = ((s8[7077888]{0:T(1024)(128)(4,1)}), s8[4194304]{0:T(1024)(128)(4,1)S(1)}, s32[]{:S(2)}) async-start(s8[7077888]{0:T(1024)(128)(4,1)} %bitcast.9), calls=%async_computation | async-start | bytes 8388608
  62.1 1.2 copy-start.16
  64.2 11.4 %slice-start.1 = ((s8[7077888]{0:T(1024)(128)(4,1)}), s8[2883584]{0:T(1024)(128)(4,1)S(1)}, s32[]{:S(2)}) async-start(s8[7077888]{0:T(1024)(128)(4,1)} %bitcast.9), calls=%async_computation.1 | async-start | bytes 5767168
  72.2 12.7 %collective-permute-start.13 = (bf16[34,24,512]{2,1,0:T(8,128)(2,1)S(1)}, bf16[34,24,512]{2,1,0:T(8,128)(2,1)S(1)}, u32[]{:S(2)}, u32[]{:S(2)}) collective-permute-start(bf16[34,24,512]{2,1,0:T(8,128)(2,1)S(1)} %get-tuple-element.131), channel_id=1, source_target_pairs={{0,16},{1,49},{16,0},{17,33},{32,48},{33,17},{48,32},{49,1},{2,18}... | collective-permute-start | bytes 2506760 | tf_op jit(solution)/shard_map/ppermute | solution.py:588
  72.3 12.7 %collective-permute-start.14 = (bf16[34,24,512]{2,1,0:T(8,128)(2,1)S(1)}, bf16[34,24,512]{2,1,0:T(8,128)(2,1)S(1)}, u32[]{:S(2)}, u32[]{:S(2)}) collective-permute-start(bf16[34,24,512]{2,1,0:T(8,128)(2,1)S(1)} %get-tuple-element.133), channel_id=1, source_target_pairs={{0,2},{1,67},{2,0},{3,65},{64,66},{65,3},{66,64},{67,1},{4,6},{5,7... | collective-permute-start | bytes 2506760 | tf_op jit(solution)/shard_map/ppermute | solution.py:588
  72.4 13.1 %collective-permute-start.15 = (bf16[34,24,512]{2,1,0:T(8,128)(2,1)S(1)}, bf16[34,24,512]{2,1,0:T(8,128)(2,1)S(1)}, u32[]{:S(2)}, u32[]{:S(2)}) collective-permute-start(bf16[34,24,512]{2,1,0:T(8,128)(2,1)S(1)} %get-tuple-element.135), channel_id=1, source_target_pairs={{0,4},{1,13},{4,0},{5,9},{8,12},{9,5},{12,8},{13,1},{2,6},{3,15},{... | collective-permute-start | bytes 2506760 | tf_op jit(solution)/shard_map/ppermute | solution.py:588
  86.6 7.5 %collective-permute-start.16 = (bf16[18,24,512]{2,1,0:T(8,128)(2,1)S(1)}, bf16[18,24,512]{2,1,0:T(8,128)(2,1)S(1)}, u32[]{:S(2)}, u32[]{:S(2)}) collective-permute-start(bf16[18,24,512]{2,1,0:T(8,128)(2,1)S(1)} %get-tuple-element.137), channel_id=1, source_target_pairs={{0,48},{1,17},{16,32},{17,1},{32,16},{33,49},{48,0},{49,33},{2,50}... | collective-permute-start | bytes 1327112 | tf_op jit(solution)/shard_map/ppermute | solution.py:588
  86.7 7.5 %collective-permute-start.17 = (bf16[18,24,512]{2,1,0:T(8,128)(2,1)S(1)}, bf16[18,24,512]{2,1,0:T(8,128)(2,1)S(1)}, u32[]{:S(2)}, u32[]{:S(2)}) collective-permute-start(bf16[18,24,512]{2,1,0:T(8,128)(2,1)S(1)} %get-tuple-element.139), channel_id=1, source_target_pairs={{0,66},{1,3},{2,64},{3,1},{64,2},{65,67},{66,0},{67,65},{4,70},{5,... | collective-permute-start | bytes 1327112 | tf_op jit(solution)/shard_map/ppermute | solution.py:588
  86.8 7.5 %collective-permute-start.18 = (bf16[18,24,512]{2,1,0:T(8,128)(2,1)S(1)}, bf16[18,24,512]{2,1,0:T(8,128)(2,1)S(1)}, u32[]{:S(2)}, u32[]{:S(2)}) collective-permute-start(bf16[18,24,512]{2,1,0:T(8,128)(2,1)S(1)} %get-tuple-element.141), channel_id=1, source_target_pairs={{0,12},{1,5},{4,8},{5,1},{8,4},{9,13},{12,0},{13,9},{2,14},{3,7},{... | collective-permute-start | bytes 1327112 | tf_op jit(solution)/shard_map/ppermute | solution.py:588
  94.3 31.6 %copy-start.2 = (bf16[24,12,1536]{2,0,1:T(8,128)(2,1)S(1)}, bf16[24,12,1536]{2,0,1:T(8,128)(2,1)}, u32[]{:S(2)}) copy-start(bf16[24,12,1536]{2,0,1:T(8,128)(2,1)} %param.11) | copy-start | bytes 2654212
  95.2 8.2 %collective-permute-start.19 = (bf16[10,24,512]{2,1,0:T(8,128)(2,1)S(1)}, bf16[10,24,512]{2,1,0:T(8,128)(2,1)S(1)}, u32[]{:S(2)}, u32[]{:S(2)}) collective-permute-start(bf16[10,24,512]{2,1,0:T(8,128)(2,1)S(1)} %get-tuple-element.143), channel_id=1, source_target_pairs={{0,2},{1,67},{2,0},{3,65},{64,66},{65,3},{66,64},{67,1},{4,6},{5,7... | collective-permute-start | bytes 737288 | tf_op jit(solution)/shard_map/ppermute | solution.py:588
  97.4 6.3 %collective-permute-start.20 = (bf16[10,24,512]{2,1,0:T(8,128)(2,1)S(1)}, bf16[10,24,512]{2,1,0:T(8,128)(2,1)S(1)}, u32[]{:S(2)}, u32[]{:S(2)}) collective-permute-start(bf16[10,24,512]{2,1,0:T(8,128)(2,1)S(1)} %get-tuple-element.145), channel_id=1, source_target_pairs={{0,4},{1,13},{4,0},{5,9},{8,12},{9,5},{12,8},{13,1},{2,6},{3,15},{... | collective-permute-start | bytes 737288 | tf_op jit(solution)/shard_map/ppermute | solution.py:588
  98.7 6.3 %collective-permute-start.21 = (bf16[10,24,512]{2,1,0:T(8,128)(2,1)S(1)}, bf16[10,24,512]{2,1,0:T(8,128)(2,1)S(1)}, u32[]{:S(2)}, u32[]{:S(2)}) collective-permute-start(bf16[10,24,512]{2,1,0:T(8,128)(2,1)S(1)} %get-tuple-element.147), channel_id=1, source_target_pairs={{0,16},{1,49},{16,0},{17,33},{32,48},{33,17},{48,32},{49,1},{2,18}... | collective-permute-start | bytes 737288 | tf_op jit(solution)/shard_map/ppermute | solution.py:588
  100.0 8.8 %collective-permute-start.12 = (bf16[72,1536]{1,0:T(8,128)(2,1)S(1)}, bf16[72,1536]{1,0:T(8,128)(2,1)S(1)}, u32[]{:S(2)}, u32[]{:S(2)}) collective-permute-start(bf16[72,1536]{1,0:T(8,128)(2,1)S(1)} %get-tuple-element.128), channel_id=1, source_target_pairs={{0,124},{4,0},{8,4},{12,8},{16,12},{20,16},{24,20},{28,24},{32,28}... | collective-permute-start | bytes 663560 | tf_op jit(solution)/shard_map/ppermute | solution.py:588
  105.7 4.3 %collective-permute-start.22 = (bf16[6,24,512]{2,1,0:T(8,128)(2,1)S(1)}, bf16[6,24,512]{2,1,0:T(8,128)(2,1)S(1)}, u32[]{:S(2)}, u32[]{:S(2)}) collective-permute-start(bf16[6,24,512]{2,1,0:T(8,128)(2,1)S(1)} %get-tuple-element.149), channel_id=1, source_target_pairs={{0,66},{1,3},{2,64},{3,1},{64,2},{65,67},{66,0},{67,65},{4,70},{5,... | collective-permute-start | bytes 442376 | tf_op jit(solution)/shard_map/ppermute | solution.py:588
  106.8 4.0 %collective-permute-start.23 = (bf16[6,24,512]{2,1,0:T(8,128)(2,1)S(1)}, bf16[6,24,512]{2,1,0:T(8,128)(2,1)S(1)}, u32[]{:S(2)}, u32[]{:S(2)}) collective-permute-start(bf16[6,24,512]{2,1,0:T(8,128)(2,1)S(1)} %get-tuple-element.151), channel_id=1, source_target_pairs={{0,12},{1,5},{4,8},{5,1},{8,4},{9,13},{12,0},{13,9},{2,14},{3,7},{... | collective-permute-start | bytes 442376 | tf_op jit(solution)/shard_map/ppermute | solution.py:588
  106.8 4.3 %collective-permute-start.24 = (bf16[6,24,512]{2,1,0:T(8,128)(2,1)S(1)}, bf16[6,24,512]{2,1,0:T(8,128)(2,1)S(1)}, u32[]{:S(2)}, u32[]{:S(2)}) collective-permute-start(bf16[6,24,512]{2,1,0:T(8,128)(2,1)S(1)} %get-tuple-element.153), channel_id=1, source_target_pairs={{0,48},{1,17},{16,32},{17,1},{32,16},{33,49},{48,0},{49,33},{2,50}... | collective-permute-start | bytes 442376 | tf_op jit(solution)/shard_map/ppermute | solution.py:588
  107.3 18.6 %collective-permute-start.31 = (bf16[72,1536]{1,0:T(8,128)(2,1)S(1)}, bf16[72,1536]{1,0:T(8,128)(2,1)S(1)}, u32[]{:S(2)}, u32[]{:S(2)}) collective-permute-start(bf16[72,1536]{1,0:T(8,128)(2,1)S(1)} %get-tuple-element.167), channel_id=1, source_target_pairs={{0,4},{4,8},{8,12},{12,16},{16,20},{20,24},{24,28},{28,32},{32,36}... | collective-permute-start | bytes 663560 | tf_op jit(solution)/shard_map/ppermute | solution.py:588
  111.8 10.1 %collective-permute-start.25 = (bf16[4,24,512]{2,1,0:T(8,128)(2,1)S(1)}, bf16[4,24,512]{2,1,0:T(8,128)(2,1)S(1)}, u32[]{:S(2)}, u32[]{:S(2)}) collective-permute-start(bf16[4,24,512]{2,1,0:T(8,128)(2,1)S(1)} %get-tuple-element.155), channel_id=1, source_target_pairs={{0,4},{1,13},{4,0},{5,9},{8,12},{9,5},{12,8},{13,1},{2,6},{3,15},{... | collective-permute-start | bytes 294920 | tf_op jit(solution)/shard_map/ppermute | solution.py:588
  113.2 8.8 %collective-permute-start.26 = (bf16[4,24,512]{2,1,0:T(8,128)(2,1)S(1)}, bf16[4,24,512]{2,1,0:T(8,128)(2,1)S(1)}, u32[]{:S(2)}, u32[]{:S(2)}) collective-permute-start(bf16[4,24,512]{2,1,0:T(8,128)(2,1)S(1)} %get-tuple-element.157), channel_id=1, source_target_pairs={{0,16},{1,49},{16,0},{17,33},{32,48},{33,17},{48,32},{49,1},{2,18}... | collective-permute-start | bytes 294920 | tf_op jit(solution)/shard_map/ppermute | solution.py:588
  115.8 6.1 %collective-permute-start.27 = (bf16[4,24,512]{2,1,0:T(8,128)(2,1)S(1)}, bf16[4,24,512]{2,1,0:T(8,128)(2,1)S(1)}, u32[]{:S(2)}, u32[]{:S(2)}) collective-permute-start(bf16[4,24,512]{2,1,0:T(8,128)(2,1)S(1)} %get-tuple-element.159), channel_id=1, source_target_pairs={{0,2},{1,67},{2,0},{3,65},{64,66},{65,3},{66,64},{67,1},{4,6},{5,7... | collective-permute-start | bytes 294920 | tf_op jit(solution)/shard_map/ppermute | solution.py:588
  116.5 9.5 %collective-permute-start.32 = (bf16[36,1536]{1,0:T(8,128)(2,1)S(1)}, bf16[36,1536]{1,0:T(8,128)(2,1)S(1)}, u32[]{:S(2)}, u32[]{:S(2)}) collective-permute-start(bf16[36,1536]{1,0:T(8,128)(2,1)S(1)} %last_rows.1), channel_id=1, source_target_pairs={{0,1},{1,2},{2,3},{3,0},{4,5},{5,6},{6,7},{7,4},{8,9},{9,10},{10,1... | collective-permute-start | bytes 331784 | tf_op jit(solution)/shard_map/ppermute | solution.py:588
  122.5 4.7 %collective-permute-start.28 = (bf16[3,24,512]{2,1,0:T(8,128)(2,1)S(1)}, bf16[3,24,512]{2,1,0:T(8,128)(2,1)S(1)}, u32[]{:S(2)}, u32[]{:S(2)}) collective-permute-start(bf16[3,24,512]{2,1,0:T(8,128)(2,1)S(1)} %get-tuple-element.161), channel_id=1, source_target_pairs={{0,12},{1,5},{4,8},{5,1},{8,4},{9,13},{12,0},{13,9},{2,14},{3,7},{... | collective-permute-start | bytes 221192 | tf_op jit(solution)/shard_map/ppermute | solution.py:588
  124.2 3.5 %collective-permute-start.29 = (bf16[3,24,512]{2,1,0:T(8,128)(2,1)S(1)}, bf16[3,24,512]{2,1,0:T(8,128)(2,1)S(1)}, u32[]{:S(2)}, u32[]{:S(2)}) collective-permute-start(bf16[3,24,512]{2,1,0:T(8,128)(2,1)S(1)} %get-tuple-element.163), channel_id=1, source_target_pairs={{0,48},{1,17},{16,32},{17,1},{32,16},{33,49},{48,0},{49,33},{2,50}... | collective-permute-start | bytes 221192 | tf_op jit(solution)/shard_map/ppermute | solution.py:588
  125.9 3.2 %collective-permute-start.30 = (bf16[3,24,512]{2,1,0:T(8,128)(2,1)S(1)}, bf16[3,24,512]{2,1,0:T(8,128)(2,1)S(1)}, u32[]{:S(2)}, u32[]{:S(2)}) collective-permute-start(bf16[3,24,512]{2,1,0:T(8,128)(2,1)S(1)} %get-tuple-element.165), channel_id=1, source_target_pairs={{0,66},{1,3},{2,64},{3,1},{64,2},{65,67},{66,0},{67,65},{4,70},{5,... | collective-permute-start | bytes 221192 | tf_op jit(solution)/shard_map/ppermute | solution.py:588
  129.2 8.4 %collective-permute-start.33 = (bf16[9,24,512]{2,1,0:T(8,128)(2,1)S(1)}, bf16[9,24,512]{2,1,0:T(8,128)(2,1)S(1)}, u32[]{:S(2)}, u32[]{:S(2)}) collective-permute-start(bf16[9,24,512]{2,1,0:T(8,128)(2,1)S(1)} %total.1.own), channel_id=1, source_target_pairs={{0,1},{1,0},{2,3},{3,2},{4,5},{5,4},{6,7},{7,6},{8,9},{9,8},{10,11... | collective-permute-start | bytes 663560 | tf_op jit(solution)/shard_map/ppermute | solution.py:588
  (7 other events, 5.6 us)

commit v6 on v4

--- a/solution.py
+++ b/solution.py
@@ -167,20 +167,24 @@
             rows[r * 12 : (r + 1) * 12, t * 128 : (t + 1) * 128] = grid[t, pl.ds(r, 12, stride=24), :]
 
 
-def first_body(own, low, upper):
+def first_body(own, low, upper, lower):
     low[...] = jnp.concatenate([own[j].astype(F32)[:SHIFT_H] for j in range(12)], 0).astype(BF16)
     upper[...] = jnp.concatenate(
         [own[j].astype(F32)[SHIFT_H : SHIFT_H + HALF_ROWS] for j in range(SHIFT_W)], 0
     ).astype(BF16)
-
-
-def to_east_body(own, low, out):
+    lower[...] = jnp.concatenate(
+        [own[SHIFT_W + i].astype(F32)[SHIFT_H + HALF_ROWS :] for i in range(SHIFT_W)], 0
+    ).astype(BF16)
+
+
+def to_east_body(lower, low, out):
+    count = HALF_ROWS - SHIFT_H
     out[...] = jnp.concatenate(
         [
             piece
             for i in range(SHIFT_W)
             for piece in (
-                own[SHIFT_W + i].astype(F32)[SHIFT_H + HALF_ROWS :],
+                f32_rows(lower, i * count, count),
                 f32_rows(low, (SHIFT_W + i) * SHIFT_H, SHIFT_H),
             )
         ],
@@ -206,7 +210,7 @@
             copies[3 * g + j].wait()
             product = dot(x[...], wide[:, lo : lo + 256])
             if j != 1:
-                product = product + (query_bias, None, value_bias)[j][:, g * 256 : (g + 1) * 256]
+                product = product + (query_bias, None, value_bias)[j][g * 256 : (g + 1) * 256].reshape(1, 256)
             projected[:, lo : lo + 256] = product
         for half in range(2):
             lo = g * 256 + half * 128
@@ -235,7 +239,7 @@
         normed = center * inv_std
         up = rows[at, :]
         total = total + jnp.sum(up * normed, 0, keepdims=True)
-        scaled = up * gain[...]
+        scaled = up * gain[...].reshape(1, C)
         grad = inv_std * (
             scaled
             - jnp.mean(scaled, -1, keepdims=True)
@@ -600,17 +604,18 @@
 
 def first_messages(grid):
     return call(
-        first_body, [shape((36, C), BF16), shape((72, C), BF16)], [grid], scalars=0, name="first"
-    )
-
-
-def halo(grid):
-    low, upper = first_messages(grid)
+        first_body,
+        [shape((36, C), BF16), shape((72, C), BF16), shape((54, C), BF16)],
+        [grid],
+        scalars=0,
+        name="first",
+    )
+
+
+def halo(low, upper, lower):
     low = lat_step(low, -1)
     east = lon_step(upper, -1)
-    (lower,) = call(
-        to_east_body, [shape((72, C), BF16)], [grid, low], scalars=0, name="to_east"
-    )
+    (lower,) = call(to_east_body, [shape((72, C), BF16)], [lower, low], scalars=0, name="to_east")
     return east, low, lower
 
 
@@ -633,25 +638,25 @@
     mine = core.astype(jnp.int32).reshape(1)
     theirs = 1 - mine
     scale = logit_scale
-    query_row, value_row = query_bias.reshape(1, HC), value_bias.reshape(1, HC)
     pair_rows = pair_bias.reshape(HEADS * WIN, WIN)
-    gain = norm_gain.reshape(1, C)
+    gain = norm_gain
 
     features = features.transpose(1, 0, 2)
     upstream = upstream.transpose(1, 0, 2)
-    east, low, lower = halo(features)
-    late, region_ids, lower = lax.optimization_barrier((upstream, region_ids, lower))
+    late = first_messages(upstream)
+    east, low, lower = halo(*first_messages(features))
+    late, region_ids, lower = lax.optimization_barrier((late, region_ids, lower))
     came = east, lon_step(lower, 1), low
     lower_ids = lon_step(region_ids[HALF_ROWS:], 1)
     region_ids = jnp.concatenate([region_ids[:HALF_ROWS], lower_ids], 0)
     region_row = region_ids.reshape(WINDOWS, WIN)
     region_col = region_ids.reshape(-1, 1)
-    east, low, lower = halo(late)
+    east, low, lower = halo(*late)
     came_late = east, lon_step(lower, 1), low
     x, projected, attended = call(
         forward_body,
         [shape((CELLS, C), BF16), shape((CELLS, 3 * HC), F32), shape((CELLS, HC), BF16)],
-        [scale, features, *came, qkv_weight, query_row, value_row, pair_rows, region_row, region_col],
+        [scale, features, *came, qkv_weight, query_bias, value_bias, pair_rows, region_row, region_col],
         scratch=[
             pltpu.VMEM((12, CELLS, 128), F32),
             pltpu.VMEM((CELLS, C), F32),
@@ -660,10 +665,11 @@
         ],
         flops=2 * CELLS * C * 3 * HC,
         far=(5,),
+        vmem=60,
         name="forward",
     )
     x_other = core_swap(x)
-    mixed_low, attended_grad, gain_part, grads_theirs, small_theirs, attended_mine, attended_theirs = call(
+    mixed_low, grad_mine, gain_part, grads_theirs, small_theirs, attended_mine, attended_theirs = call(
         backward_body,
         [
             shape((CELLS, C), BF16),
@@ -700,11 +706,14 @@
         far=(7,),
         near=(9,),
         flops=4 * CELLS * C * HC + 2 * CELLS * WIN * 128 * 18,
+        vmem=60,
         name="backward",
     )
     mixed_other = core_swap(mixed_low)
     attended_other = core_swap(attended_theirs)
 
+    grads_other = core_swap(grads_theirs)
+    small_other = core_swap(small_theirs)
     def attention(side):
         def cols(base):
             return lambda i, side, scale: (0, base + side[0] * 3 + i)
@@ -719,7 +728,7 @@
                 (projected, block, cols(0)),
                 (projected, block, cols(6)),
                 (projected, block, cols(12)),
-                (attended_grad, block, lambda i, side, scale: (0, i)),
+                (grad_mine, block, lambda i, side, scale: (0, i)),
                 (pair_rows, (2 * WIN, WIN), lambda i, side, scale: (side[0] * 3 + i, 0)),
                 (region_row, (WINDOWS, WIN), whole),
                 (region_col, (CELLS, 1), whole),
@@ -734,8 +743,6 @@
             name="attention",
         )
 
-    grads_other = core_swap(grads_theirs)
-    small_other = core_swap(small_theirs)
     grads_mine, small_mine = attention(mine)
 
     parts = call(
@@ -805,10 +812,6 @@
         if step == 0:
             order, stay_low = lax.optimization_barrier((order, stay_low))
         if step == 3:
-            order, from_west = lax.optimization_barrier((order, from_west))
-        if step == 4:
-            order, low = lax.optimization_barrier((order, low))
-        if step == 2:
             order, last = lax.optimization_barrier((order, last))
         parts = call(body, [shape((left // 2 + EXTRA,) + BLOCK, BF16)] * 6, [order, *terms], vmem=10, name="halve")
     (input_grad,) = call(

time: 139 us -> 136 us (0.978)
  starting transfers between devices: 59.8 us -> 55.9 us
  waiting for transfers between devices: 22.1 us -> 25.3 us
    ppermute x34, starting transfers between devices: 59.8 us -> 55.9 us  [permuted(): return lax.ppermute(value, axes, pairs)]
    ppermute x34, waiting for transfers between devices: 22.1 us -> 25.3 us  [permuted(): return lax.ppermute(value, axes, pairs)]
    unnamed x44, local copies, waits for them, and re-layouts: 7.12 us -> 5.59 us
  transfers between devices with their start and end apart: 34 -> 34, of which waited for: 14 -> 15; matrix products, arithmetic and copies ran while one was open for 1% -> 2% of each run, Pallas kernels for 25% -> 26%
where the time goes in v6:
time: 136 us
  starting transfers between devices  55.9 us (41%)
  Pallas kernels  45.4 us (33%)
  waiting for transfers between devices  25.3 us (19%)
  local copies, waits for them, and re-layouts  7.94 us (6%)
    ppermute x34, starting transfers between devices, permuted(): return lax.ppermute(value, axes, pairs)  55.9 us
    pallas_call x16, Pallas kernels, call(): pl.pallas_call(body, out_shape=list(outs), in_specs=specs, out_specs=[VME...  37.1 us
    ppermute x34, waiting for transfers between devices, permuted(): return lax.ppermute(value, axes, pairs)  25.3 us
    pallas_call x2, Pallas kernels, grid_call(): pl.pallas_call(body, grid_spec=spec, out_shape=results, compiler_params=p...  8.34 us
    unnamed x44, local copies, waits for them, and re-layouts  5.59 us
  transfers between devices with their start and end apart: 34, of which 15 were waited for; matrix products, arithmetic and copies ran while one was open for 2% of the time, Pallas kernels for 26%

profile of v6, /device:TPU:1, one launch (start us, length us, event | category | flops | bytes accessed | tf_op | source)
XLA Modules:
  0.0 135.7 jit_solution(7718285084529166961)
XLA Ops:
  0.6 1.2 copy-done.4
  2.0 1.5 %collective-permute-start.1 = (bf16[36,1536]{1,0:T(8,128)(2,1)S(1)}, bf16[36,1536]{1,0:T(8,128)(2,1)S(1)}, u32[]{:S(2)}, u32[]{:S(2)}) collective-permute-start(bf16[36,1536]{1,0:T(8,128)(2,1)S(1)} %get-tuple-element.100), channel_id=1, source_target_pairs={{0,3},{1,0},{2,1},{3,2},{4,7},{5,4},{6,5},{7,6},{8,11},{9,8},{10,9... | collective-permute-start | bytes 331784 | tf_op jit(solution)/shard_map/ppermute | solution.py:575
  3.5 8.7 %collective-permute-start = (bf16[72,1536]{1,0:T(8,128)(2,1)S(1)}, bf16[72,1536]{1,0:T(8,128)(2,1)S(1)}, u32[]{:S(2)}, u32[]{:S(2)}) collective-permute-start(bf16[72,1536]{1,0:T(8,128)(2,1)S(1)} %get-tuple-element.95), channel_id=1, source_target_pairs={{0,124},{4,0},{8,4},{12,8},{16,12},{20,16},{24,20},{28,24},{32,28}... | collective-permute-start | bytes 663560 | tf_op jit(solution)/shard_map/ppermute | solution.py:575
  12.1 1.2 copy-done.1
  13.6 1.1 collective-permute-start.6
  14.7 0.8 fusion
  15.5 7.2 %collective-permute-start.5 = (bf16[72,1536]{1,0:T(8,128)(2,1)S(1)}, bf16[72,1536]{1,0:T(8,128)(2,1)S(1)}, u32[]{:S(2)}, u32[]{:S(2)}) collective-permute-start(bf16[72,1536]{1,0:T(8,128)(2,1)S(1)} %get-tuple-element.106), channel_id=1, source_target_pairs={{0,124},{4,0},{8,4},{12,8},{16,12},{20,16},{24,20},{28,24},{32,28}... | collective-permute-start | bytes 663560 | tf_op jit(solution)/shard_map/ppermute | solution.py:575
  22.9 4.7 %collective-permute-done.3 = s32[12,12]{0,1:T(8,128)S(1)} collective-permute-done((s32[12,12]{0,1:T(8,128)S(1)}, s32[12,12]{0,1:T(8,128)S(1)}, u32[]{:S(2)}, u32[]{:S(2)}) %collective-permute-start.3) | collective-permute-done | bytes 608 | tf_op jit(solution)/shard_map/ppermute | solution.py:575
  27.7 0.7 reshape.30.row
  28.4 0.8 reshape.33.col
  29.2 0.6 copy-done.16
  29.9 11.5 %forward.1 = (bf16[288,1536]{1,0:T(8,128)(2,1)}, f32[288,2304]{1,0:T(8,128)}, bf16[288,768]{1,0:T(8,128)(2,1)}) custom-call(f32[12]{0:T(128)} %scale.5, bf16[12,24,1536]{2,1,0:T(8,128)(2,1)} %bitcast.17, bf16[72,1536]{1,0:T(8,128)(2,1)} %copy-done.16, bf16[72,1536]{1,0:T(8,128)(2,1)} %copy-done.17, bf16[36,1536]{1,0:T(8,128)(2,1)} %copy-done.8, ...), custom_call_target="tpu_custom_call" | custom-call | flops 2038431744 | bytes 12754224 | tf_op jit(solution)/shard_map/forward/pallas_call | solution.py:60
  41.4 1.1 collective-permute-start.4
  42.5 0.7 copy-done.19
  43.3 11.2 %backward.1 = (bf16[288,1536]{1,0:T(8,128)(2,1)}, f32[288,384]{1,0:T(8,128)}, f32[1,1536]{1,0:T(1,128)}, bf16[288,1152]{1,0:T(8,128)(2,1)}, f32[144,512]{1,0:T(8...) custom-call(s32[1]{0:T(128)S(6)} %sub.3.side, f32[12]{0:T(128)} %scale.5, ...), custom_call_target="tpu_custom_call" | custom-call | flops 1454505984 | bytes 9884980 | tf_op jit(solution)/shard_map/backward/pallas_call | solution.py:60
  55.7 1.0 copy-done.9
  56.7 0.7 copy-done.11
  57.4 4.4 %attention.1 = (bf16[288,1152]{1,0:T(8,128)(2,1)S(1)}, f32[144,512]{1,0:T(8,128)S(1)}) custom-call(s32[1]{0:T(128)} %bitcast.side.core, f32[12]{0:T(128)S(1)} %copy-done.12, f32[288,2304]{1,0:T(8,128)S(1)} %copy-done, f32[288,2304]{1,0:T(8,128)S(1)} %copy-done, f32[288,2304]{1,0:T(8,128)S(1)} %copy-done, f32[288,384]{1,0:T(8,128)S(1)} %copy-done.9, ...), custom_call_target="tpu_custom_call" | custom-call | flops 95551488 | bytes 9620736 | tf_op jit(solution)/shard_map/attention/pallas_call | solution.py:82
  62.0 7.5 %weights.1 = (bf16[34,24,512]{2,1,0:T(8,128)(2,1)S(1)}, bf16[34,24,512]{2,1,0:T(8,128)(2,1)S(1)}, bf16[34,24,512]{2,1,0:T(8,128)(2,1)S(1)}, bf16[34,24,512]{2,1,...) custom-call(s32[4]{0:T(128)S(1)} %pad_add_fusion.1.place, ...), custom_call_target="tpu_custom_call" | custom-call | flops 2717908992 | bytes 10911760 | tf_op jit(solution)/shard_map/weights/pallas_call | solution.py:60
  69.8 3.1 %collective-permute-start.15 = (bf16[34,24,512]{2,1,0:T(8,128)(2,1)S(1)}, bf16[34,24,512]{2,1,0:T(8,128)(2,1)S(1)}, u32[]{:S(2)}, u32[]{:S(2)}) collective-permute-start(bf16[34,24,512]{2,1,0:T(8,128)(2,1)S(1)} %get-tuple-element.135), channel_id=1, source_target_pairs={{0,4},{1,13},{4,0},{5,9},{8,12},{9,5},{12,8},{13,1},{2,6},{3,15},{... | collective-permute-start | bytes 2506760 | tf_op jit(solution)/shard_map/ppermute | solution.py:575
  73.0 3.9 %branch.1 = (bf16[72,1536]{1,0:T(8,128)(2,1)S(1)}, bf16[72,1536]{1,0:T(8,128)(2,1)S(1)}, bf16[72,1536]{1,0:T(8,128)(2,1)S(1)}, bf16[72,1536]{1,0:T(8,128)(2,1)S(1)}) custom-call(s32[1]{0:T(128)} %bitcast.side.core, bf16[1536,2304]{1,0:T(8,128)(2,1)S(1)} %bitcast.10, bf16[288,1152]{1,0:T(8,128)(2,1)S(1)} %get-tuple-element.111.p0.own, ...), custom_call_target="tpu_custom_call" | custom-call | flops 2038431744 | bytes 9289728 | tf_op jit(solution)/shard_map/branch/pallas_call | solution.py:82
  76.9 5.3 %collective-permute-done.13.refs_1_ = bf16[34,24,512]{2,1,0:T(8,128)(2,1)S(1)} collective-permute-done((bf16[34,24,512]{2,1,0:T(8,128)(2,1)S(1)}, bf16[34,24,512]{2,1,0:T(8,128)(2,1)S(1)}, u32[]{:S(2)}, u32[]{:S(2)}) %collective-permute-start.13) | collective-permute-done | bytes 835616 | tf_op jit(solution)/shard_map/ppermute | solution.py:575
  82.9 1.2 halve.5
  84.3 7.2 %collective-permute-done.16.refs_1_ = bf16[18,24,512]{2,1,0:T(8,128)(2,1)S(1)} collective-permute-done((bf16[18,24,512]{2,1,0:T(8,128)(2,1)S(1)}, bf16[18,24,512]{2,1,0:T(8,128)(2,1)S(1)}, u32[]{:S(2)}, u32[]{:S(2)}) %collective-permute-start.16) | collective-permute-done | bytes 442400 | tf_op jit(solution)/shard_map/ppermute | solution.py:575
  91.8 0.9 halve.6
  92.6 2.2 %collective-permute-start.19 = (bf16[10,24,512]{2,1,0:T(8,128)(2,1)S(1)}, bf16[10,24,512]{2,1,0:T(8,128)(2,1)S(1)}, u32[]{:S(2)}, u32[]{:S(2)}) collective-permute-start(bf16[10,24,512]{2,1,0:T(8,128)(2,1)S(1)} %get-tuple-element.143), channel_id=1, source_target_pairs={{0,2},{1,67},{2,0},{3,65},{64,66},{65,3},{66,64},{67,1},{4,6},{5,7... | collective-permute-start | bytes 737288 | tf_op jit(solution)/shard_map/ppermute | solution.py:575
  94.8 1.3 collective-permute-start.20
  96.2 1.2 collective-permute-start.21
  97.4 3.4 %collective-permute-start.12 = (bf16[72,1536]{1,0:T(8,128)(2,1)S(1)}, bf16[72,1536]{1,0:T(8,128)(2,1)S(1)}, u32[]{:S(2)}, u32[]{:S(2)}) collective-permute-start(bf16[72,1536]{1,0:T(8,128)(2,1)S(1)} %get-tuple-element.128), channel_id=1, source_target_pairs={{0,124},{4,0},{8,4},{12,8},{16,12},{20,16},{24,20},{28,24},{32,28}... | collective-permute-start | bytes 663560 | tf_op jit(solution)/shard_map/ppermute | solution.py:575
  101.1 1.3 collective-permute-done.21.refs_5_
  102.4 0.7 halve.7
  103.1 0.8 collective-permute-start.22
  104.5 1.5 %collective-permute-start.31 = (bf16[72,1536]{1,0:T(8,128)(2,1)S(1)}, bf16[72,1536]{1,0:T(8,128)(2,1)S(1)}, u32[]{:S(2)}, u32[]{:S(2)}) collective-permute-start(bf16[72,1536]{1,0:T(8,128)(2,1)S(1)} %get-tuple-element.167), channel_id=1, source_target_pairs={{0,4},{4,8},{8,12},{12,16},{16,20},{20,24},{24,28},{28,32},{32,36}... | collective-permute-start | bytes 663560 | tf_op jit(solution)/shard_map/ppermute | solution.py:575
  106.0 1.2 collective-permute-done.22.refs_1_
  107.2 1.0 collective-permute-done.23.refs_3_
  108.5 0.6 halve.8
  109.2 1.2 collective-permute-start.25
  110.3 2.6 %collective-permute-start.26 = (bf16[4,24,512]{2,1,0:T(8,128)(2,1)S(1)}, bf16[4,24,512]{2,1,0:T(8,128)(2,1)S(1)}, u32[]{:S(2)}, u32[]{:S(2)}) collective-permute-start(bf16[4,24,512]{2,1,0:T(8,128)(2,1)S(1)} %get-tuple-element.157), channel_id=1, source_target_pairs={{0,16},{1,49},{16,0},{17,33},{32,48},{33,17},{48,32},{49,1},{2,18}... | collective-permute-start | bytes 294920 | tf_op jit(solution)/shard_map/ppermute | solution.py:575
  112.9 0.7 collective-permute-start.27
  113.6 5.6 %collective-permute-start.32 = (bf16[36,1536]{1,0:T(8,128)(2,1)S(1)}, bf16[36,1536]{1,0:T(8,128)(2,1)S(1)}, u32[]{:S(2)}, u32[]{:S(2)}) collective-permute-start(bf16[36,1536]{1,0:T(8,128)(2,1)S(1)} %last_rows.1), channel_id=1, source_target_pairs={{0,1},{1,2},{2,3},{3,0},{4,5},{5,6},{6,7},{7,4},{8,9},{9,10},{10,1... | collective-permute-start | bytes 331784 | tf_op jit(solution)/shard_map/ppermute | solution.py:575
  119.3 0.6 halve.9
  119.9 1.6 %collective-permute-start.28 = (bf16[3,24,512]{2,1,0:T(8,128)(2,1)S(1)}, bf16[3,24,512]{2,1,0:T(8,128)(2,1)S(1)}, u32[]{:S(2)}, u32[]{:S(2)}) collective-permute-start(bf16[3,24,512]{2,1,0:T(8,128)(2,1)S(1)} %get-tuple-element.161), channel_id=1, source_target_pairs={{0,12},{1,5},{4,8},{5,1},{8,4},{9,13},{12,0},{13,9},{2,14},{3,7},{... | collective-permute-start | bytes 221192 | tf_op jit(solution)/shard_map/ppermute | solution.py:575
  121.5 1.7 %collective-permute-start.29 = (bf16[3,24,512]{2,1,0:T(8,128)(2,1)S(1)}, bf16[3,24,512]{2,1,0:T(8,128)(2,1)S(1)}, u32[]{:S(2)}, u32[]{:S(2)}) collective-permute-start(bf16[3,24,512]{2,1,0:T(8,128)(2,1)S(1)} %get-tuple-element.163), channel_id=1, source_target_pairs={{0,48},{1,17},{16,32},{17,1},{32,16},{33,49},{48,0},{49,33},{2,50}... | collective-permute-start | bytes 221192 | tf_op jit(solution)/shard_map/ppermute | solution.py:575
  123.3 1.3 merge.1
  125.0 1.5 %collective-permute-done.30.refs_5_ = bf16[3,24,512]{2,1,0:T(8,128)(2,1)S(1)} collective-permute-done((bf16[3,24,512]{2,1,0:T(8,128)(2,1)S(1)}, bf16[3,24,512]{2,1,0:T(8,128)(2,1)S(1)}, u32[]{:S(2)}, u32[]{:S(2)}) %collective-permute-start.30) | collective-permute-done | bytes 73760 | tf_op jit(solution)/shard_map/ppermute | solution.py:575
  126.5 7.1 %collective-permute-start.33 = (bf16[9,24,512]{2,1,0:T(8,128)(2,1)S(1)}, bf16[9,24,512]{2,1,0:T(8,128)(2,1)S(1)}, u32[]{:S(2)}, u32[]{:S(2)}) collective-permute-start(bf16[9,24,512]{2,1,0:T(8,128)(2,1)S(1)} %total.1.own), channel_id=1, source_target_pairs={{0,1},{1,0},{2,3},{3,2},{4,5},{5,4},{6,7},{7,6},{8,9},{9,8},{10,11... | collective-permute-start | bytes 663560 | tf_op jit(solution)/shard_map/ppermute | solution.py:575
  133.6 1.1 collective-permute-done.33.other
  134.7 0.9 finish.1
  (89 shorter events, 5.1 us)
Async XLA Ops:
  2.0 11.5 %collective-permute-start.1 = (bf16[36,1536]{1,0:T(8,128)(2,1)S(1)}, bf16[36,1536]{1,0:T(8,128)(2,1)S(1)}, u32[]{:S(2)}, u32[]{:S(2)}) collective-permute-start(bf16[36,1536]{1,0:T(8,128)(2,1)S(1)} %get-tuple-element.100), channel_id=1, source_target_pairs={{0,3},{1,0},{2,1},{3,2},{4,7},{5,4},{6,5},{7,6},{8,11},{9,8},{10,9... | collective-permute-start | bytes 331784 | tf_op jit(solution)/shard_map/ppermute | solution.py:575
  3.5 25.7 %collective-permute-start = (bf16[72,1536]{1,0:T(8,128)(2,1)S(1)}, bf16[72,1536]{1,0:T(8,128)(2,1)S(1)}, u32[]{:S(2)}, u32[]{:S(2)}) collective-permute-start(bf16[72,1536]{1,0:T(8,128)(2,1)S(1)} %get-tuple-element.95), channel_id=1, source_target_pairs={{0,124},{4,0},{8,4},{12,8},{16,12},{20,16},{24,20},{28,24},{32,28}... | collective-permute-start | bytes 663560 | tf_op jit(solution)/shard_map/ppermute | solution.py:575
  13.5 15.7 %copy-start.8 = (bf16[36,1536]{1,0:T(8,128)(2,1)}, bf16[36,1536]{1,0:T(8,128)(2,1)S(1)}, u32[]{:S(2)}) copy-start(bf16[36,1536]{1,0:T(8,128)(2,1)S(1)} %collective-permute-done.1.low) | copy-start | bytes 331780
  13.6 9.1 %collective-permute-start.6 = (bf16[36,1536]{1,0:T(8,128)(2,1)S(1)}, bf16[36,1536]{1,0:T(8,128)(2,1)S(1)}, u32[]{:S(2)}, u32[]{:S(2)}) collective-permute-start(bf16[36,1536]{1,0:T(8,128)(2,1)S(1)} %get-tuple-element.108), channel_id=1, source_target_pairs={{0,3},{1,0},{2,1},{3,2},{4,7},{5,4},{6,5},{7,6},{8,11},{9,8},{10,9... | collective-permute-start | bytes 331784 | tf_op jit(solution)/shard_map/ppermute | solution.py:575
  14.7 14.5 %collective-permute-start.2 = (bf16[72,1536]{1,0:T(8,128)(2,1)S(1)}, bf16[72,1536]{1,0:T(8,128)(2,1)S(1)}, u32[]{:S(2)}, u32[]{:S(2)}) collective-permute-start(bf16[72,1536]{1,0:T(8,128)(2,1)S(1)} %to_east.2), channel_id=1, source_target_pairs={{0,4},{4,8},{8,12},{12,16},{16,20},{20,24},{24,28},{28,32},{32,36}... | collective-permute-start | bytes 663560 | tf_op jit(solution)/shard_map/ppermute | solution.py:575
  15.5 12.0 %collective-permute-start.3 = (s32[12,12]{0,1:T(8,128)S(1)}, s32[12,12]{0,1:T(8,128)S(1)}, u32[]{:S(2)}, u32[]{:S(2)}) collective-permute-start(s32[12,12]{0,1:T(8,128)S(1)} %get-tuple-element.183), channel_id=1, source_target_pairs={{0,4},{4,8},{8,12},{12,16},{16,20},{20,24},{24,28},{28,32},{32,36}... | collective-permute-start | bytes 1736 | tf_op jit(solution)/shard_map/ppermute | solution.py:575
  15.5 27.0 %collective-permute-start.5 = (bf16[72,1536]{1,0:T(8,128)(2,1)S(1)}, bf16[72,1536]{1,0:T(8,128)(2,1)S(1)}, u32[]{:S(2)}, u32[]{:S(2)}) collective-permute-start(bf16[72,1536]{1,0:T(8,128)(2,1)S(1)} %get-tuple-element.106), channel_id=1, source_target_pairs={{0,124},{4,0},{8,4},{12,8},{16,12},{20,16},{24,20},{28,24},{32,28}... | collective-permute-start | bytes 663560 | tf_op jit(solution)/shard_map/ppermute | solution.py:575
  22.7 18.7 %copy-start.7 = (bf16[36,1536]{1,0:T(8,128)(2,1)}, bf16[36,1536]{1,0:T(8,128)(2,1)S(1)}, u32[]{:S(2)}) copy-start(bf16[36,1536]{1,0:T(8,128)(2,1)S(1)} %collective-permute-done.6.low) | copy-start | bytes 331780
  22.8 19.7 %collective-permute-start.7 = (bf16[72,1536]{1,0:T(8,128)(2,1)S(1)}, bf16[72,1536]{1,0:T(8,128)(2,1)S(1)}, u32[]{:S(2)}, u32[]{:S(2)}) collective-permute-start(bf16[72,1536]{1,0:T(8,128)(2,1)S(1)} %to_east.3), channel_id=1, source_target_pairs={{0,4},{4,8},{8,12},{12,16},{16,20},{20,24},{24,28},{28,32},{32,36}... | collective-permute-start | bytes 663560 | tf_op jit(solution)/shard_map/ppermute | solution.py:575
  41.4 20.5 %collective-permute-start.4 = (bf16[288,1536]{1,0:T(8,128)(2,1)}, bf16[288,1536]{1,0:T(8,128)(2,1)}, u32[]{:S(2)}, u32[]{:S(2)}) collective-permute-start(bf16[288,1536]{1,0:T(8,128)(2,1)} %get-tuple-element.103.x0), channel_id=1, source_target_pairs={{0,1},{1,0},{2,3},{3,2},{4,5},{5,4},{6,7},{7,6},{8,9},{9,8},{10,11... | collective-permute-start | bytes 2654216 | tf_op jit(solution)/shard_map/ppermute | solution.py:575
  43.3 12.4 %copy-start = (f32[288,2304]{1,0:T(8,128)S(1)}, f32[288,2304]{1,0:T(8,128)}, u32[]{:S(2)}) copy-start(f32[288,2304]{1,0:T(8,128)} %get-tuple-element.104.projected.q_ref.k_ref.v_ref) | copy-start | bytes 7962628
  43.3 12.4 %copy-start.3 = (f32[12,72,72]{2,1,0:T(8,128)S(1)}, f32[12,72,72]{2,1,0:T(8,128)}, u32[]{:S(2)}) copy-start(f32[12,72,72]{2,1,0:T(8,128)} %param.17) | copy-start | bytes 746500
  43.3 12.4 %copy-start.5 = (s32[288,1]{1,0:T(8,128)S(1)}, s32[288,1]{1,0:T(8,128)}, u32[]{:S(2)}) copy-start(s32[288,1]{1,0:T(8,128)} %reshape.33.col) | copy-start | bytes 3460
  43.3 12.4 %copy-start.10 = (s32[4,72]{1,0:T(4,128)S(1)}, s32[4,72]{1,0:T(4,128)}, u32[]{:S(2)}) copy-start(s32[4,72]{1,0:T(4,128)} %reshape.30.row) | copy-start | bytes 3460
  43.3 12.4 %copy-start.12 = (f32[12]{0:T(128)S(1)}, f32[12]{0:T(128)}, u32[]{:S(2)}) copy-start(f32[12]{0:T(128)} %scale.5) | copy-start | bytes 148
  54.5 7.4 %collective-permute-start.9 = (bf16[288,1536]{1,0:T(8,128)(2,1)}, bf16[288,1536]{1,0:T(8,128)(2,1)}, u32[]{:S(2)}, u32[]{:S(2)}) collective-permute-start(bf16[288,1536]{1,0:T(8,128)(2,1)} %get-tuple-element.113.m0), channel_id=1, source_target_pairs={{0,1},{1,0},{2,3},{3,2},{4,5},{5,4},{6,7},{7,6},{8,9},{9,8},{10,11... | collective-permute-start | bytes 2654216 | tf_op jit(solution)/shard_map/ppermute | solution.py:575
  54.6 7.3 %collective-permute-start.8 = (bf16[288,1152]{1,0:T(8,128)(2,1)}, bf16[288,1152]{1,0:T(8,128)(2,1)}, u32[]{:S(2)}, u32[]{:S(2)}) collective-permute-start(bf16[288,1152]{1,0:T(8,128)(2,1)} %get-tuple-element.112.theirs), channel_id=1, source_target_pairs={{0,1},{1,0},{2,3},{3,2},{4,5},{5,4},{6,7},{7,6},{8,9},{9,8},{10,11... | collective-permute-start | bytes 1990664 | tf_op jit(solution)/shard_map/ppermute | solution.py:575
  55.1 6.8 %collective-permute-start.11 = (f32[144,512]{1,0:T(8,128)}, f32[144,512]{1,0:T(8,128)S(1)}, u32[]{:S(2)}, u32[]{:S(2)}) collective-permute-start(f32[144,512]{1,0:T(8,128)} %get-tuple-element.117), channel_id=1, source_target_pairs={{0,1},{1,0},{2,3},{3,2},{4,5},{5,4},{6,7},{7,6},{8,9},{9,8},{10,11... | collective-permute-start | bytes 884744 | tf_op jit(solution)/shard_map/ppermute | solution.py:575
  55.2 6.7 %collective-permute-start.10 = (bf16[288,384]{1,0:T(8,128)(2,1)}, bf16[288,384]{1,0:T(8,128)(2,1)}, u32[]{:S(2)}, u32[]{:S(2)}) collective-permute-start(bf16[288,384]{1,0:T(8,128)(2,1)} %get-tuple-element.115), channel_id=1, source_target_pairs={{0,1},{1,0},{2,3},{3,2},{4,5},{5,4},{6,7},{7,6},{8,9},{9,8},{10,11... | collective-permute-start | bytes 663560 | tf_op jit(solution)/shard_map/ppermute | solution.py:575
  57.4 4.5 %copy-start.13 = (bf16[288,1536]{1,0:T(8,128)(2,1)S(1)}, bf16[288,1536]{1,0:T(8,128)(2,1)}, u32[]{:S(2)}) copy-start(bf16[288,1536]{1,0:T(8,128)(2,1)} %get-tuple-element.103.x0) | copy-start | bytes 2654212
  57.4 4.5 %copy-start.14 = (bf16[288,1536]{1,0:T(8,128)(2,1)S(1)}, bf16[288,1536]{1,0:T(8,128)(2,1)}, u32[]{:S(2)}) copy-start(bf16[288,1536]{1,0:T(8,128)(2,1)} %get-tuple-element.113.m0) | copy-start | bytes 2654212
  57.4 4.5 %copy-start.15 = (bf16[288,384]{1,0:T(8,128)(2,1)S(1)}, bf16[288,384]{1,0:T(8,128)(2,1)}, u32[]{:S(2)}) copy-start(bf16[288,384]{1,0:T(8,128)(2,1)} %get-tuple-element.114.a0) | copy-start | bytes 663556
  57.4 15.5 %slice-start = ((s8[7077888]{0:T(1024)(128)(4,1)}), s8[4194304]{0:T(1024)(128)(4,1)S(1)}, s32[]{:S(2)}) async-start(s8[7077888]{0:T(1024)(128)(4,1)} %bitcast.9), calls=%async_computation | async-start | bytes 8388608
  62.0 11.0 %slice-start.1 = ((s8[7077888]{0:T(1024)(128)(4,1)}), s8[2883584]{0:T(1024)(128)(4,1)S(1)}, s32[]{:S(2)}) async-start(s8[7077888]{0:T(1024)(128)(4,1)} %bitcast.9), calls=%async_computation.1 | async-start | bytes 5767168
  62.0 11.0 %copy-start.6 = (bf16[288,1152]{1,0:T(8,128)(2,1)S(1)}, bf16[288,1152]{1,0:T(8,128)(2,1)}, u32[]{:S(2)}) copy-start(bf16[288,1152]{1,0:T(8,128)(2,1)} %get-tuple-element.112.theirs) | copy-start | bytes 1990660
  69.5 12.7 %collective-permute-start.13 = (bf16[34,24,512]{2,1,0:T(8,128)(2,1)S(1)}, bf16[34,24,512]{2,1,0:T(8,128)(2,1)S(1)}, u32[]{:S(2)}, u32[]{:S(2)}) collective-permute-start(bf16[34,24,512]{2,1,0:T(8,128)(2,1)S(1)} %get-tuple-element.131), channel_id=1, source_target_pairs={{0,16},{1,49},{16,0},{17,33},{32,48},{33,17},{48,32},{49,1},{2,18}... | collective-permute-start | bytes 2506760 | tf_op jit(solution)/shard_map/ppermute | solution.py:575
  69.6 12.7 %collective-permute-start.14 = (bf16[34,24,512]{2,1,0:T(8,128)(2,1)S(1)}, bf16[34,24,512]{2,1,0:T(8,128)(2,1)S(1)}, u32[]{:S(2)}, u32[]{:S(2)}) collective-permute-start(bf16[34,24,512]{2,1,0:T(8,128)(2,1)S(1)} %get-tuple-element.133), channel_id=1, source_target_pairs={{0,2},{1,67},{2,0},{3,65},{64,66},{65,3},{66,64},{67,1},{4,6},{5,7... | collective-permute-start | bytes 2506760 | tf_op jit(solution)/shard_map/ppermute | solution.py:575
  69.8 13.0 %collective-permute-start.15 = (bf16[34,24,512]{2,1,0:T(8,128)(2,1)S(1)}, bf16[34,24,512]{2,1,0:T(8,128)(2,1)S(1)}, u32[]{:S(2)}, u32[]{:S(2)}) collective-permute-start(bf16[34,24,512]{2,1,0:T(8,128)(2,1)S(1)} %get-tuple-element.135), channel_id=1, source_target_pairs={{0,4},{1,13},{4,0},{5,9},{8,12},{9,5},{12,8},{13,1},{2,6},{3,15},{... | collective-permute-start | bytes 2506760 | tf_op jit(solution)/shard_map/ppermute | solution.py:575
  84.1 7.5 %collective-permute-start.16 = (bf16[18,24,512]{2,1,0:T(8,128)(2,1)S(1)}, bf16[18,24,512]{2,1,0:T(8,128)(2,1)S(1)}, u32[]{:S(2)}, u32[]{:S(2)}) collective-permute-start(bf16[18,24,512]{2,1,0:T(8,128)(2,1)S(1)} %get-tuple-element.137), channel_id=1, source_target_pairs={{0,48},{1,17},{16,32},{17,1},{32,16},{33,49},{48,0},{49,33},{2,50}... | collective-permute-start | bytes 1327112 | tf_op jit(solution)/shard_map/ppermute | solution.py:575
  84.1 7.5 %collective-permute-start.17 = (bf16[18,24,512]{2,1,0:T(8,128)(2,1)S(1)}, bf16[18,24,512]{2,1,0:T(8,128)(2,1)S(1)}, u32[]{:S(2)}, u32[]{:S(2)}) collective-permute-start(bf16[18,24,512]{2,1,0:T(8,128)(2,1)S(1)} %get-tuple-element.139), channel_id=1, source_target_pairs={{0,66},{1,3},{2,64},{3,1},{64,2},{65,67},{66,0},{67,65},{4,70},{5,... | collective-permute-start | bytes 1327112 | tf_op jit(solution)/shard_map/ppermute | solution.py:575
  84.2 7.5 %collective-permute-start.18 = (bf16[18,24,512]{2,1,0:T(8,128)(2,1)S(1)}, bf16[18,24,512]{2,1,0:T(8,128)(2,1)S(1)}, u32[]{:S(2)}, u32[]{:S(2)}) collective-permute-start(bf16[18,24,512]{2,1,0:T(8,128)(2,1)S(1)} %get-tuple-element.141), channel_id=1, source_target_pairs={{0,12},{1,5},{4,8},{5,1},{8,4},{9,13},{12,0},{13,9},{2,14},{3,7},{... | collective-permute-start | bytes 1327112 | tf_op jit(solution)/shard_map/ppermute | solution.py:575
  91.8 31.5 %copy-start.2 = (bf16[24,12,1536]{2,0,1:T(8,128)(2,1)S(1)}, bf16[24,12,1536]{2,0,1:T(8,128)(2,1)}, u32[]{:S(2)}) copy-start(bf16[24,12,1536]{2,0,1:T(8,128)(2,1)} %param.11) | copy-start | bytes 2654212
  92.6 8.2 %collective-permute-start.19 = (bf16[10,24,512]{2,1,0:T(8,128)(2,1)S(1)}, bf16[10,24,512]{2,1,0:T(8,128)(2,1)S(1)}, u32[]{:S(2)}, u32[]{:S(2)}) collective-permute-start(bf16[10,24,512]{2,1,0:T(8,128)(2,1)S(1)} %get-tuple-element.143), channel_id=1, source_target_pairs={{0,2},{1,67},{2,0},{3,65},{64,66},{65,3},{66,64},{67,1},{4,6},{5,7... | collective-permute-start | bytes 737288 | tf_op jit(solution)/shard_map/ppermute | solution.py:575
  94.8 6.3 %collective-permute-start.20 = (bf16[10,24,512]{2,1,0:T(8,128)(2,1)S(1)}, bf16[10,24,512]{2,1,0:T(8,128)(2,1)S(1)}, u32[]{:S(2)}, u32[]{:S(2)}) collective-permute-start(bf16[10,24,512]{2,1,0:T(8,128)(2,1)S(1)} %get-tuple-element.145), channel_id=1, source_target_pairs={{0,4},{1,13},{4,0},{5,9},{8,12},{9,5},{12,8},{13,1},{2,6},{3,15},{... | collective-permute-start | bytes 737288 | tf_op jit(solution)/shard_map/ppermute | solution.py:575
  96.2 6.3 %collective-permute-start.21 = (bf16[10,24,512]{2,1,0:T(8,128)(2,1)S(1)}, bf16[10,24,512]{2,1,0:T(8,128)(2,1)S(1)}, u32[]{:S(2)}, u32[]{:S(2)}) collective-permute-start(bf16[10,24,512]{2,1,0:T(8,128)(2,1)S(1)} %get-tuple-element.147), channel_id=1, source_target_pairs={{0,16},{1,49},{16,0},{17,33},{32,48},{33,17},{48,32},{49,1},{2,18}... | collective-permute-start | bytes 737288 | tf_op jit(solution)/shard_map/ppermute | solution.py:575
  97.4 8.5 %collective-permute-start.12 = (bf16[72,1536]{1,0:T(8,128)(2,1)S(1)}, bf16[72,1536]{1,0:T(8,128)(2,1)S(1)}, u32[]{:S(2)}, u32[]{:S(2)}) collective-permute-start(bf16[72,1536]{1,0:T(8,128)(2,1)S(1)} %get-tuple-element.128), channel_id=1, source_target_pairs={{0,124},{4,0},{8,4},{12,8},{16,12},{20,16},{24,20},{28,24},{32,28}... | collective-permute-start | bytes 663560 | tf_op jit(solution)/shard_map/ppermute | solution.py:575
  103.1 4.1 %collective-permute-start.22 = (bf16[6,24,512]{2,1,0:T(8,128)(2,1)S(1)}, bf16[6,24,512]{2,1,0:T(8,128)(2,1)S(1)}, u32[]{:S(2)}, u32[]{:S(2)}) collective-permute-start(bf16[6,24,512]{2,1,0:T(8,128)(2,1)S(1)} %get-tuple-element.149), channel_id=1, source_target_pairs={{0,66},{1,3},{2,64},{3,1},{64,2},{65,67},{66,0},{67,65},{4,70},{5,... | collective-permute-start | bytes 442376 | tf_op jit(solution)/shard_map/ppermute | solution.py:575
  104.0 4.3 %collective-permute-start.23 = (bf16[6,24,512]{2,1,0:T(8,128)(2,1)S(1)}, bf16[6,24,512]{2,1,0:T(8,128)(2,1)S(1)}, u32[]{:S(2)}, u32[]{:S(2)}) collective-permute-start(bf16[6,24,512]{2,1,0:T(8,128)(2,1)S(1)} %get-tuple-element.151), channel_id=1, source_target_pairs={{0,12},{1,5},{4,8},{5,1},{8,4},{9,13},{12,0},{13,9},{2,14},{3,7},{... | collective-permute-start | bytes 442376 | tf_op jit(solution)/shard_map/ppermute | solution.py:575
  104.0 4.5 %collective-permute-start.24 = (bf16[6,24,512]{2,1,0:T(8,128)(2,1)S(1)}, bf16[6,24,512]{2,1,0:T(8,128)(2,1)S(1)}, u32[]{:S(2)}, u32[]{:S(2)}) collective-permute-start(bf16[6,24,512]{2,1,0:T(8,128)(2,1)S(1)} %get-tuple-element.153), channel_id=1, source_target_pairs={{0,48},{1,17},{16,32},{17,1},{32,16},{33,49},{48,0},{49,33},{2,50}... | collective-permute-start | bytes 442376 | tf_op jit(solution)/shard_map/ppermute | solution.py:575
  104.5 18.8 %collective-permute-start.31 = (bf16[72,1536]{1,0:T(8,128)(2,1)S(1)}, bf16[72,1536]{1,0:T(8,128)(2,1)S(1)}, u32[]{:S(2)}, u32[]{:S(2)}) collective-permute-start(bf16[72,1536]{1,0:T(8,128)(2,1)S(1)} %get-tuple-element.167), channel_id=1, source_target_pairs={{0,4},{4,8},{8,12},{12,16},{16,20},{20,24},{24,28},{28,32},{32,36}... | collective-permute-start | bytes 663560 | tf_op jit(solution)/shard_map/ppermute | solution.py:575
  109.2 10.1 %collective-permute-start.25 = (bf16[4,24,512]{2,1,0:T(8,128)(2,1)S(1)}, bf16[4,24,512]{2,1,0:T(8,128)(2,1)S(1)}, u32[]{:S(2)}, u32[]{:S(2)}) collective-permute-start(bf16[4,24,512]{2,1,0:T(8,128)(2,1)S(1)} %get-tuple-element.155), channel_id=1, source_target_pairs={{0,4},{1,13},{4,0},{5,9},{8,12},{9,5},{12,8},{13,1},{2,6},{3,15},{... | collective-permute-start | bytes 294920 | tf_op jit(solution)/shard_map/ppermute | solution.py:575
  110.3 8.9 %collective-permute-start.26 = (bf16[4,24,512]{2,1,0:T(8,128)(2,1)S(1)}, bf16[4,24,512]{2,1,0:T(8,128)(2,1)S(1)}, u32[]{:S(2)}, u32[]{:S(2)}) collective-permute-start(bf16[4,24,512]{2,1,0:T(8,128)(2,1)S(1)} %get-tuple-element.157), channel_id=1, source_target_pairs={{0,16},{1,49},{16,0},{17,33},{32,48},{33,17},{48,32},{49,1},{2,18}... | collective-permute-start | bytes 294920 | tf_op jit(solution)/shard_map/ppermute | solution.py:575
  112.9 6.3 %collective-permute-start.27 = (bf16[4,24,512]{2,1,0:T(8,128)(2,1)S(1)}, bf16[4,24,512]{2,1,0:T(8,128)(2,1)S(1)}, u32[]{:S(2)}, u32[]{:S(2)}) collective-permute-start(bf16[4,24,512]{2,1,0:T(8,128)(2,1)S(1)} %get-tuple-element.159), channel_id=1, source_target_pairs={{0,2},{1,67},{2,0},{3,65},{64,66},{65,3},{66,64},{67,1},{4,6},{5,7... | collective-permute-start | bytes 294920 | tf_op jit(solution)/shard_map/ppermute | solution.py:575
  113.6 9.7 %collective-permute-start.32 = (bf16[36,1536]{1,0:T(8,128)(2,1)S(1)}, bf16[36,1536]{1,0:T(8,128)(2,1)S(1)}, u32[]{:S(2)}, u32[]{:S(2)}) collective-permute-start(bf16[36,1536]{1,0:T(8,128)(2,1)S(1)} %last_rows.1), channel_id=1, source_target_pairs={{0,1},{1,2},{2,3},{3,0},{4,5},{5,6},{6,7},{7,4},{8,9},{9,10},{10,1... | collective-permute-start | bytes 331784 | tf_op jit(solution)/shard_map/ppermute | solution.py:575
  119.9 4.7 %collective-permute-start.28 = (bf16[3,24,512]{2,1,0:T(8,128)(2,1)S(1)}, bf16[3,24,512]{2,1,0:T(8,128)(2,1)S(1)}, u32[]{:S(2)}, u32[]{:S(2)}) collective-permute-start(bf16[3,24,512]{2,1,0:T(8,128)(2,1)S(1)} %get-tuple-element.161), channel_id=1, source_target_pairs={{0,12},{1,5},{4,8},{5,1},{8,4},{9,13},{12,0},{13,9},{2,14},{3,7},{... | collective-permute-start | bytes 221192 | tf_op jit(solution)/shard_map/ppermute | solution.py:575
  121.5 3.5 %collective-permute-start.29 = (bf16[3,24,512]{2,1,0:T(8,128)(2,1)S(1)}, bf16[3,24,512]{2,1,0:T(8,128)(2,1)S(1)}, u32[]{:S(2)}, u32[]{:S(2)}) collective-permute-start(bf16[3,24,512]{2,1,0:T(8,128)(2,1)S(1)} %get-tuple-element.163), channel_id=1, source_target_pairs={{0,48},{1,17},{16,32},{17,1},{32,16},{33,49},{48,0},{49,33},{2,50}... | collective-permute-start | bytes 221192 | tf_op jit(solution)/shard_map/ppermute | solution.py:575
  123.3 3.2 %collective-permute-start.30 = (bf16[3,24,512]{2,1,0:T(8,128)(2,1)S(1)}, bf16[3,24,512]{2,1,0:T(8,128)(2,1)S(1)}, u32[]{:S(2)}, u32[]{:S(2)}) collective-permute-start(bf16[3,24,512]{2,1,0:T(8,128)(2,1)S(1)} %get-tuple-element.165), channel_id=1, source_target_pairs={{0,66},{1,3},{2,64},{3,1},{64,2},{65,67},{66,0},{67,65},{4,70},{5,... | collective-permute-start | bytes 221192 | tf_op jit(solution)/shard_map/ppermute | solution.py:575
  126.5 8.2 %collective-permute-start.33 = (bf16[9,24,512]{2,1,0:T(8,128)(2,1)S(1)}, bf16[9,24,512]{2,1,0:T(8,128)(2,1)S(1)}, u32[]{:S(2)}, u32[]{:S(2)}) collective-permute-start(bf16[9,24,512]{2,1,0:T(8,128)(2,1)S(1)} %total.1.own), channel_id=1, source_target_pairs={{0,1},{1,0},{2,3},{3,2},{4,5},{5,4},{6,7},{7,6},{8,9},{9,8},{10,11... | collective-permute-start | bytes 663560 | tf_op jit(solution)/shard_map/ppermute | solution.py:575
  (8 other events, 7.0 us)

commit v7 on v6

--- a/solution.py
+++ b/solution.py
@@ -739,7 +739,7 @@
                 (shape((144, 512), F32), (48, 512), lambda i, side, scale: (i, 0)),
             ],
             flops=2 * CELLS * WIN * 128 * 6 * 3,
-            vmem=16,
+            vmem=60,
             name="attention",
         )
 

time: 136 us -> 141 us (1.037)
  local copies, waits for them, and re-layouts: 7.94 us -> 10.4 us
  Pallas kernels: 45.4 us -> 47.7 us
    pallas_call x2, Pallas kernels: 8.34 us -> 10.8 us  [grid_call(): pl.pallas_call(body, grid_spec=spec, out_shape=results, compiler_params=p...]
    unnamed x44 -> x34, local copies, waits for them, and re-layouts: 5.59 us -> 8.06 us
where the time goes in v7:
time: 141 us; the launch traced here: 140 us
  starting transfers between devices  55.9 us (40%)
  Pallas kernels  47.7 us (34%)
  waiting for transfers between devices  25.3 us (18%)
  local copies, waits for them, and re-layouts  10.4 us (7%)
    ppermute x34, starting transfers between devices, permuted(): return lax.ppermute(value, axes, pairs)  55.9 us
    pallas_call x16, Pallas kernels, call(): pl.pallas_call(body, out_shape=list(outs), in_specs=specs, out_specs=[VME...  36.9 us
    ppermute x34, waiting for transfers between devices, permuted(): return lax.ppermute(value, axes, pairs)  25.3 us
    pallas_call x2, Pallas kernels, grid_call(): pl.pallas_call(body, grid_spec=spec, out_shape=results, compiler_params=p...  10.8 us
    unnamed x34, local copies, waits for them, and re-layouts  8.06 us
  transfers between devices with their start and end apart: 34, of which 15 were waited for; matrix products, arithmetic and copies ran while one was open for 2% of the time, Pallas kernels for 26%

profile of v7, /device:TPU:1, one launch (start us, length us, event | category | flops | bytes accessed | tf_op | source)
XLA Modules:
  0.0 140.4 jit_solution(1401228870336280394)
XLA Ops:
  0.6 1.2 copy-done.2
  2.0 1.5 %collective-permute-start.1 = (bf16[36,1536]{1,0:T(8,128)(2,1)S(1)}, bf16[36,1536]{1,0:T(8,128)(2,1)S(1)}, u32[]{:S(2)}, u32[]{:S(2)}) collective-permute-start(bf16[36,1536]{1,0:T(8,128)(2,1)S(1)} %get-tuple-element.100), channel_id=1, source_target_pairs={{0,3},{1,0},{2,1},{3,2},{4,7},{5,4},{6,5},{7,6},{8,11},{9,8},{10,9... | collective-permute-start | bytes 331784 | tf_op jit(solution)/shard_map/ppermute | solution.py:575
  3.5 8.7 %collective-permute-start = (bf16[72,1536]{1,0:T(8,128)(2,1)S(1)}, bf16[72,1536]{1,0:T(8,128)(2,1)S(1)}, u32[]{:S(2)}, u32[]{:S(2)}) collective-permute-start(bf16[72,1536]{1,0:T(8,128)(2,1)S(1)} %get-tuple-element.95), channel_id=1, source_target_pairs={{0,124},{4,0},{8,4},{12,8},{16,12},{20,16},{24,20},{28,24},{32,28}... | collective-permute-start | bytes 663560 | tf_op jit(solution)/shard_map/ppermute | solution.py:575
  12.1 1.2 copy-done
  13.6 1.1 collective-permute-start.6
  14.7 0.8 fusion
  15.5 7.2 %collective-permute-start.5 = (bf16[72,1536]{1,0:T(8,128)(2,1)S(1)}, bf16[72,1536]{1,0:T(8,128)(2,1)S(1)}, u32[]{:S(2)}, u32[]{:S(2)}) collective-permute-start(bf16[72,1536]{1,0:T(8,128)(2,1)S(1)} %get-tuple-element.106), channel_id=1, source_target_pairs={{0,124},{4,0},{8,4},{12,8},{16,12},{20,16},{24,20},{28,24},{32,28}... | collective-permute-start | bytes 663560 | tf_op jit(solution)/shard_map/ppermute | solution.py:575
  22.9 4.7 %collective-permute-done.3 = s32[12,12]{0,1:T(8,128)S(1)} collective-permute-done((s32[12,12]{0,1:T(8,128)S(1)}, s32[12,12]{0,1:T(8,128)S(1)}, u32[]{:S(2)}, u32[]{:S(2)}) %collective-permute-start.3) | collective-permute-done | bytes 608 | tf_op jit(solution)/shard_map/ppermute | solution.py:575
  27.7 0.7 reshape.30.row
  28.4 0.8 reshape.33.col
  29.2 0.7 copy-done.11
  29.9 11.5 %forward.1 = (bf16[288,1536]{1,0:T(8,128)(2,1)}, f32[288,2304]{1,0:T(8,128)}, bf16[288,768]{1,0:T(8,128)(2,1)}) custom-call(f32[12]{0:T(128)} %scale.5, bf16[12,24,1536]{2,1,0:T(8,128)(2,1)} %bitcast.14, bf16[72,1536]{1,0:T(8,128)(2,1)} %copy-done.11, bf16[72,1536]{1,0:T(8,128)(2,1)} %copy-done.12, bf16[36,1536]{1,0:T(8,128)(2,1)} %copy-done.6, ...), custom_call_target="tpu_custom_call" | custom-call | flops 2038431744 | bytes 12754224 | tf_op jit(solution)/shard_map/forward/pallas_call | solution.py:60
  41.4 1.1 collective-permute-start.4
  42.6 0.7 copy-done.13
  43.4 11.0 %backward.1 = (bf16[288,1536]{1,0:T(8,128)(2,1)}, f32[288,384]{1,0:T(8,128)}, f32[1,1536]{1,0:T(1,128)}, bf16[288,1152]{1,0:T(8,128)(2,1)}, f32[144,512]{1,0:T(8...) custom-call(s32[1]{0:T(128)S(6)} %sub.3.side, f32[12]{0:T(128)} %scale.5, ...), custom_call_target="tpu_custom_call" | custom-call | flops 1454505984 | bytes 9884980 | tf_op jit(solution)/shard_map/backward/pallas_call | solution.py:60
  55.5 6.9 %attention.1 = (bf16[288,1152]{1,0:T(8,128)(2,1)}, f32[144,512]{1,0:T(8,128)}) custom-call(s32[1]{0:T(128)} %bitcast.side.core, f32[12]{0:T(128)} %scale.5, f32[288,2304]{1,0:T(8,128)} %get-tuple-element.104.projected.q_ref.k_ref.v_ref, f32[288,2304]{1,0:T(8,128)} %get-tuple-element.104.projected.q_ref.k_ref.v_ref, ...), custom_call_target="tpu_custom_call" | custom-call | flops 95551488 | bytes 9620736 | tf_op jit(solution)/shard_map/attention/pallas_call | solution.py:82
  62.5 1.1 copy-done.4
  63.6 1.2 copy-done.8
  64.8 1.0 copy-done.9
  65.7 0.9 copy-done.10
  66.7 7.6 %weights.1 = (bf16[34,24,512]{2,1,0:T(8,128)(2,1)S(1)}, bf16[34,24,512]{2,1,0:T(8,128)(2,1)S(1)}, bf16[34,24,512]{2,1,0:T(8,128)(2,1)S(1)}, bf16[34,24,512]{2,1,...) custom-call(s32[4]{0:T(128)S(1)} %pad_add_fusion.1.place, ...), custom_call_target="tpu_custom_call" | custom-call | flops 2717908992 | bytes 10911760 | tf_op jit(solution)/shard_map/weights/pallas_call | solution.py:60
  74.6 3.1 %collective-permute-start.15 = (bf16[34,24,512]{2,1,0:T(8,128)(2,1)S(1)}, bf16[34,24,512]{2,1,0:T(8,128)(2,1)S(1)}, u32[]{:S(2)}, u32[]{:S(2)}) collective-permute-start(bf16[34,24,512]{2,1,0:T(8,128)(2,1)S(1)} %get-tuple-element.135), channel_id=1, source_target_pairs={{0,4},{1,13},{4,0},{5,9},{8,12},{9,5},{12,8},{13,1},{2,6},{3,15},{... | collective-permute-start | bytes 2506760 | tf_op jit(solution)/shard_map/ppermute | solution.py:575
  77.7 3.9 %branch.1 = (bf16[72,1536]{1,0:T(8,128)(2,1)S(1)}, bf16[72,1536]{1,0:T(8,128)(2,1)S(1)}, bf16[72,1536]{1,0:T(8,128)(2,1)S(1)}, bf16[72,1536]{1,0:T(8,128)(2,1)S(1)}) custom-call(s32[1]{0:T(128)} %bitcast.side.core, bf16[1536,2304]{1,0:T(8,128)(2,1)S(1)} %bitcast.10, bf16[288,1152]{1,0:T(8,128)(2,1)S(1)} %copy-done.4, bf16[288,1152]{1,0:T(8,128)(2,1)S(1)} %copy-done.3), custom_call_target="tpu_custom_call" | custom-call | flops 2038431744 | bytes 9289728 | tf_op jit(solution)/shard_map/branch/pallas_call | solution.py:82
  81.6 5.3 %collective-permute-done.13.refs_1_ = bf16[34,24,512]{2,1,0:T(8,128)(2,1)S(1)} collective-permute-done((bf16[34,24,512]{2,1,0:T(8,128)(2,1)S(1)}, bf16[34,24,512]{2,1,0:T(8,128)(2,1)S(1)}, u32[]{:S(2)}, u32[]{:S(2)}) %collective-permute-start.13) | collective-permute-done | bytes 835616 | tf_op jit(solution)/shard_map/ppermute | solution.py:575
  87.6 1.1 halve.5
  89.0 7.2 %collective-permute-done.16.refs_1_ = bf16[18,24,512]{2,1,0:T(8,128)(2,1)S(1)} collective-permute-done((bf16[18,24,512]{2,1,0:T(8,128)(2,1)S(1)}, bf16[18,24,512]{2,1,0:T(8,128)(2,1)S(1)}, u32[]{:S(2)}, u32[]{:S(2)}) %collective-permute-start.16) | collective-permute-done | bytes 442400 | tf_op jit(solution)/shard_map/ppermute | solution.py:575
  96.5 0.9 halve.6
  97.3 2.2 %collective-permute-start.19 = (bf16[10,24,512]{2,1,0:T(8,128)(2,1)S(1)}, bf16[10,24,512]{2,1,0:T(8,128)(2,1)S(1)}, u32[]{:S(2)}, u32[]{:S(2)}) collective-permute-start(bf16[10,24,512]{2,1,0:T(8,128)(2,1)S(1)} %get-tuple-element.143), channel_id=1, source_target_pairs={{0,2},{1,67},{2,0},{3,65},{64,66},{65,3},{66,64},{67,1},{4,6},{5,7... | collective-permute-start | bytes 737288 | tf_op jit(solution)/shard_map/ppermute | solution.py:575
  99.5 1.4 collective-permute-start.20
  100.9 1.2 collective-permute-start.21
  102.1 3.4 %collective-permute-start.12 = (bf16[72,1536]{1,0:T(8,128)(2,1)S(1)}, bf16[72,1536]{1,0:T(8,128)(2,1)S(1)}, u32[]{:S(2)}, u32[]{:S(2)}) collective-permute-start(bf16[72,1536]{1,0:T(8,128)(2,1)S(1)} %get-tuple-element.128), channel_id=1, source_target_pairs={{0,124},{4,0},{8,4},{12,8},{16,12},{20,16},{24,20},{28,24},{32,28}... | collective-permute-start | bytes 663560 | tf_op jit(solution)/shard_map/ppermute | solution.py:575
  105.8 1.4 collective-permute-done.21.refs_5_
  107.1 0.7 halve.7
  107.8 0.8 collective-permute-start.22
  109.1 1.5 %collective-permute-start.31 = (bf16[72,1536]{1,0:T(8,128)(2,1)S(1)}, bf16[72,1536]{1,0:T(8,128)(2,1)S(1)}, u32[]{:S(2)}, u32[]{:S(2)}) collective-permute-start(bf16[72,1536]{1,0:T(8,128)(2,1)S(1)} %get-tuple-element.167), channel_id=1, source_target_pairs={{0,4},{4,8},{8,12},{12,16},{16,20},{20,24},{24,28},{28,32},{32,36}... | collective-permute-start | bytes 663560 | tf_op jit(solution)/shard_map/ppermute | solution.py:575
  110.7 1.2 collective-permute-done.22.refs_1_
  111.9 1.0 collective-permute-done.23.refs_3_
  113.9 1.2 collective-permute-start.25
  115.0 2.6 %collective-permute-start.26 = (bf16[4,24,512]{2,1,0:T(8,128)(2,1)S(1)}, bf16[4,24,512]{2,1,0:T(8,128)(2,1)S(1)}, u32[]{:S(2)}, u32[]{:S(2)}) collective-permute-start(bf16[4,24,512]{2,1,0:T(8,128)(2,1)S(1)} %get-tuple-element.157), channel_id=1, source_target_pairs={{0,16},{1,49},{16,0},{17,33},{32,48},{33,17},{48,32},{49,1},{2,18}... | collective-permute-start | bytes 294920 | tf_op jit(solution)/shard_map/ppermute | solution.py:575
  117.6 0.7 collective-permute-start.27
  118.3 5.6 %collective-permute-start.32 = (bf16[36,1536]{1,0:T(8,128)(2,1)S(1)}, bf16[36,1536]{1,0:T(8,128)(2,1)S(1)}, u32[]{:S(2)}, u32[]{:S(2)}) collective-permute-start(bf16[36,1536]{1,0:T(8,128)(2,1)S(1)} %last_rows.1), channel_id=1, source_target_pairs={{0,1},{1,2},{2,3},{3,0},{4,5},{5,6},{6,7},{7,4},{8,9},{9,10},{10,1... | collective-permute-start | bytes 331784 | tf_op jit(solution)/shard_map/ppermute | solution.py:575
  124.6 1.6 %collective-permute-start.28 = (bf16[3,24,512]{2,1,0:T(8,128)(2,1)S(1)}, bf16[3,24,512]{2,1,0:T(8,128)(2,1)S(1)}, u32[]{:S(2)}, u32[]{:S(2)}) collective-permute-start(bf16[3,24,512]{2,1,0:T(8,128)(2,1)S(1)} %get-tuple-element.161), channel_id=1, source_target_pairs={{0,12},{1,5},{4,8},{5,1},{8,4},{9,13},{12,0},{13,9},{2,14},{3,7},{... | collective-permute-start | bytes 221192 | tf_op jit(solution)/shard_map/ppermute | solution.py:575
  126.2 1.7 %collective-permute-start.29 = (bf16[3,24,512]{2,1,0:T(8,128)(2,1)S(1)}, bf16[3,24,512]{2,1,0:T(8,128)(2,1)S(1)}, u32[]{:S(2)}, u32[]{:S(2)}) collective-permute-start(bf16[3,24,512]{2,1,0:T(8,128)(2,1)S(1)} %get-tuple-element.163), channel_id=1, source_target_pairs={{0,48},{1,17},{16,32},{17,1},{32,16},{33,49},{48,0},{49,33},{2,50}... | collective-permute-start | bytes 221192 | tf_op jit(solution)/shard_map/ppermute | solution.py:575
  128.0 1.3 merge.1
  129.7 1.5 %collective-permute-done.30.refs_5_ = bf16[3,24,512]{2,1,0:T(8,128)(2,1)S(1)} collective-permute-done((bf16[3,24,512]{2,1,0:T(8,128)(2,1)S(1)}, bf16[3,24,512]{2,1,0:T(8,128)(2,1)S(1)}, u32[]{:S(2)}, u32[]{:S(2)}) %collective-permute-start.30) | collective-permute-done | bytes 73760 | tf_op jit(solution)/shard_map/ppermute | solution.py:575
  131.2 7.1 %collective-permute-start.33 = (bf16[9,24,512]{2,1,0:T(8,128)(2,1)S(1)}, bf16[9,24,512]{2,1,0:T(8,128)(2,1)S(1)}, u32[]{:S(2)}, u32[]{:S(2)}) collective-permute-start(bf16[9,24,512]{2,1,0:T(8,128)(2,1)S(1)} %total.1.own), channel_id=1, source_target_pairs={{0,1},{1,0},{2,3},{3,2},{4,5},{5,4},{6,7},{7,6},{8,9},{9,8},{10,11... | collective-permute-start | bytes 663560 | tf_op jit(solution)/shard_map/ppermute | solution.py:575
  138.3 1.1 collective-permute-done.33.other
  139.4 0.9 finish.1
  (79 shorter events, 6.4 us)
Async XLA Ops:
  0.6 1.2 copy-start.2
  2.0 11.5 %collective-permute-start.1 = (bf16[36,1536]{1,0:T(8,128)(2,1)S(1)}, bf16[36,1536]{1,0:T(8,128)(2,1)S(1)}, u32[]{:S(2)}, u32[]{:S(2)}) collective-permute-start(bf16[36,1536]{1,0:T(8,128)(2,1)S(1)} %get-tuple-element.100), channel_id=1, source_target_pairs={{0,3},{1,0},{2,1},{3,2},{4,7},{5,4},{6,5},{7,6},{8,11},{9,8},{10,9... | collective-permute-start | bytes 331784 | tf_op jit(solution)/shard_map/ppermute | solution.py:575
  3.5 25.7 %collective-permute-start = (bf16[72,1536]{1,0:T(8,128)(2,1)S(1)}, bf16[72,1536]{1,0:T(8,128)(2,1)S(1)}, u32[]{:S(2)}, u32[]{:S(2)}) collective-permute-start(bf16[72,1536]{1,0:T(8,128)(2,1)S(1)} %get-tuple-element.95), channel_id=1, source_target_pairs={{0,124},{4,0},{8,4},{12,8},{16,12},{20,16},{24,20},{28,24},{32,28}... | collective-permute-start | bytes 663560 | tf_op jit(solution)/shard_map/ppermute | solution.py:575
  12.1 1.2 copy-start
  13.5 15.7 %copy-start.6 = (bf16[36,1536]{1,0:T(8,128)(2,1)}, bf16[36,1536]{1,0:T(8,128)(2,1)S(1)}, u32[]{:S(2)}) copy-start(bf16[36,1536]{1,0:T(8,128)(2,1)S(1)} %collective-permute-done.1.low) | copy-start | bytes 331780
  13.6 9.1 %collective-permute-start.6 = (bf16[36,1536]{1,0:T(8,128)(2,1)S(1)}, bf16[36,1536]{1,0:T(8,128)(2,1)S(1)}, u32[]{:S(2)}, u32[]{:S(2)}) collective-permute-start(bf16[36,1536]{1,0:T(8,128)(2,1)S(1)} %get-tuple-element.108), channel_id=1, source_target_pairs={{0,3},{1,0},{2,1},{3,2},{4,7},{5,4},{6,5},{7,6},{8,11},{9,8},{10,9... | collective-permute-start | bytes 331784 | tf_op jit(solution)/shard_map/ppermute | solution.py:575
  14.7 14.5 %collective-permute-start.2 = (bf16[72,1536]{1,0:T(8,128)(2,1)S(1)}, bf16[72,1536]{1,0:T(8,128)(2,1)S(1)}, u32[]{:S(2)}, u32[]{:S(2)}) collective-permute-start(bf16[72,1536]{1,0:T(8,128)(2,1)S(1)} %to_east.2), channel_id=1, source_target_pairs={{0,4},{4,8},{8,12},{12,16},{16,20},{20,24},{24,28},{28,32},{32,36}... | collective-permute-start | bytes 663560 | tf_op jit(solution)/shard_map/ppermute | solution.py:575
  15.5 12.0 %collective-permute-start.3 = (s32[12,12]{0,1:T(8,128)S(1)}, s32[12,12]{0,1:T(8,128)S(1)}, u32[]{:S(2)}, u32[]{:S(2)}) collective-permute-start(s32[12,12]{0,1:T(8,128)S(1)} %get-tuple-element.183), channel_id=1, source_target_pairs={{0,4},{4,8},{8,12},{12,16},{16,20},{20,24},{24,28},{28,32},{32,36}... | collective-permute-start | bytes 1736 | tf_op jit(solution)/shard_map/ppermute | solution.py:575
  15.5 27.0 %collective-permute-start.5 = (bf16[72,1536]{1,0:T(8,128)(2,1)S(1)}, bf16[72,1536]{1,0:T(8,128)(2,1)S(1)}, u32[]{:S(2)}, u32[]{:S(2)}) collective-permute-start(bf16[72,1536]{1,0:T(8,128)(2,1)S(1)} %get-tuple-element.106), channel_id=1, source_target_pairs={{0,124},{4,0},{8,4},{12,8},{16,12},{20,16},{24,20},{28,24},{32,28}... | collective-permute-start | bytes 663560 | tf_op jit(solution)/shard_map/ppermute | solution.py:575
  22.7 18.7 %copy-start.5 = (bf16[36,1536]{1,0:T(8,128)(2,1)}, bf16[36,1536]{1,0:T(8,128)(2,1)S(1)}, u32[]{:S(2)}) copy-start(bf16[36,1536]{1,0:T(8,128)(2,1)S(1)} %collective-permute-done.6.low) | copy-start | bytes 331780
  22.8 19.7 %collective-permute-start.7 = (bf16[72,1536]{1,0:T(8,128)(2,1)S(1)}, bf16[72,1536]{1,0:T(8,128)(2,1)S(1)}, u32[]{:S(2)}, u32[]{:S(2)}) collective-permute-start(bf16[72,1536]{1,0:T(8,128)(2,1)S(1)} %to_east.3), channel_id=1, source_target_pairs={{0,4},{4,8},{8,12},{12,16},{16,20},{20,24},{24,28},{28,32},{32,36}... | collective-permute-start | bytes 663560 | tf_op jit(solution)/shard_map/ppermute | solution.py:575
  41.4 21.1 %collective-permute-start.4 = (bf16[288,1536]{1,0:T(8,128)(2,1)}, bf16[288,1536]{1,0:T(8,128)(2,1)}, u32[]{:S(2)}, u32[]{:S(2)}) collective-permute-start(bf16[288,1536]{1,0:T(8,128)(2,1)} %get-tuple-element.103.x0), channel_id=1, source_target_pairs={{0,1},{1,0},{2,3},{3,2},{4,5},{5,4},{6,7},{7,6},{8,9},{9,8},{10,11... | collective-permute-start | bytes 2654216 | tf_op jit(solution)/shard_map/ppermute | solution.py:575
  42.5 0.8 copy-start.14
  54.3 8.2 %collective-permute-start.9 = (bf16[288,1536]{1,0:T(8,128)(2,1)}, bf16[288,1536]{1,0:T(8,128)(2,1)}, u32[]{:S(2)}, u32[]{:S(2)}) collective-permute-start(bf16[288,1536]{1,0:T(8,128)(2,1)} %get-tuple-element.113.m0), channel_id=1, source_target_pairs={{0,1},{1,0},{2,3},{3,2},{4,5},{5,4},{6,7},{7,6},{8,9},{9,8},{10,11... | collective-permute-start | bytes 2654216 | tf_op jit(solution)/shard_map/ppermute | solution.py:575
  54.4 8.0 %collective-permute-start.8 = (bf16[288,1152]{1,0:T(8,128)(2,1)}, bf16[288,1152]{1,0:T(8,128)(2,1)}, u32[]{:S(2)}, u32[]{:S(2)}) collective-permute-start(bf16[288,1152]{1,0:T(8,128)(2,1)} %get-tuple-element.112.theirs), channel_id=1, source_target_pairs={{0,1},{1,0},{2,3},{3,2},{4,5},{5,4},{6,7},{7,6},{8,9},{9,8},{10,11... | collective-permute-start | bytes 1990664 | tf_op jit(solution)/shard_map/ppermute | solution.py:575
  54.9 7.5 %collective-permute-start.11 = (f32[144,512]{1,0:T(8,128)}, f32[144,512]{1,0:T(8,128)S(1)}, u32[]{:S(2)}, u32[]{:S(2)}) collective-permute-start(f32[144,512]{1,0:T(8,128)} %get-tuple-element.117), channel_id=1, source_target_pairs={{0,1},{1,0},{2,3},{3,2},{4,5},{5,4},{6,7},{7,6},{8,9},{9,8},{10,11... | collective-permute-start | bytes 884744 | tf_op jit(solution)/shard_map/ppermute | solution.py:575
  55.0 7.4 %collective-permute-start.10 = (bf16[288,384]{1,0:T(8,128)(2,1)}, bf16[288,384]{1,0:T(8,128)(2,1)}, u32[]{:S(2)}, u32[]{:S(2)}) collective-permute-start(bf16[288,384]{1,0:T(8,128)(2,1)} %get-tuple-element.115), channel_id=1, source_target_pairs={{0,1},{1,0},{2,3},{3,2},{4,5},{5,4},{6,7},{7,6},{8,9},{9,8},{10,11... | collective-permute-start | bytes 663560 | tf_op jit(solution)/shard_map/ppermute | solution.py:575
  55.5 7.0 %copy-start.7 = (bf16[288,1536]{1,0:T(8,128)(2,1)S(1)}, bf16[288,1536]{1,0:T(8,128)(2,1)}, u32[]{:S(2)}) copy-start(bf16[288,1536]{1,0:T(8,128)(2,1)} %get-tuple-element.103.x0) | copy-start | bytes 2654212
  55.5 22.2 %slice-start = ((s8[7077888]{0:T(1024)(128)(4,1)}), s8[2883584]{0:T(1024)(128)(4,1)S(1)}, s32[]{:S(2)}) async-start(s8[7077888]{0:T(1024)(128)(4,1)} %bitcast.9), calls=%async_computation | async-start | bytes 5767168
  62.5 1.1 copy-start.4
  63.6 1.2 copy-start.8
  64.8 1.0 copy-start.9
  65.7 0.9 copy-start.10
  66.7 11.1 %slice-start.1 = ((s8[7077888]{0:T(1024)(128)(4,1)}), s8[4194304]{0:T(1024)(128)(4,1)S(1)}, s32[]{:S(2)}) async-start(s8[7077888]{0:T(1024)(128)(4,1)} %bitcast.9), calls=%async_computation.1 | async-start | bytes 8388608
  66.7 11.1 %copy-start.3 = (bf16[288,1152]{1,0:T(8,128)(2,1)S(1)}, bf16[288,1152]{1,0:T(8,128)(2,1)}, u32[]{:S(2)}) copy-start(bf16[288,1152]{1,0:T(8,128)(2,1)} %get-tuple-element.112.theirs) | copy-start | bytes 1990660
  74.3 12.7 %collective-permute-start.13 = (bf16[34,24,512]{2,1,0:T(8,128)(2,1)S(1)}, bf16[34,24,512]{2,1,0:T(8,128)(2,1)S(1)}, u32[]{:S(2)}, u32[]{:S(2)}) collective-permute-start(bf16[34,24,512]{2,1,0:T(8,128)(2,1)S(1)} %get-tuple-element.131), channel_id=1, source_target_pairs={{0,16},{1,49},{16,0},{17,33},{32,48},{33,17},{48,32},{49,1},{2,18}... | collective-permute-start | bytes 2506760 | tf_op jit(solution)/shard_map/ppermute | solution.py:575
  74.4 12.7 %collective-permute-start.14 = (bf16[34,24,512]{2,1,0:T(8,128)(2,1)S(1)}, bf16[34,24,512]{2,1,0:T(8,128)(2,1)S(1)}, u32[]{:S(2)}, u32[]{:S(2)}) collective-permute-start(bf16[34,24,512]{2,1,0:T(8,128)(2,1)S(1)} %get-tuple-element.133), channel_id=1, source_target_pairs={{0,2},{1,67},{2,0},{3,65},{64,66},{65,3},{66,64},{67,1},{4,6},{5,7... | collective-permute-start | bytes 2506760 | tf_op jit(solution)/shard_map/ppermute | solution.py:575
  74.6 13.0 %collective-permute-start.15 = (bf16[34,24,512]{2,1,0:T(8,128)(2,1)S(1)}, bf16[34,24,512]{2,1,0:T(8,128)(2,1)S(1)}, u32[]{:S(2)}, u32[]{:S(2)}) collective-permute-start(bf16[34,24,512]{2,1,0:T(8,128)(2,1)S(1)} %get-tuple-element.135), channel_id=1, source_target_pairs={{0,4},{1,13},{4,0},{5,9},{8,12},{9,5},{12,8},{13,1},{2,6},{3,15},{... | collective-permute-start | bytes 2506760 | tf_op jit(solution)/shard_map/ppermute | solution.py:575
  88.8 7.5 %collective-permute-start.16 = (bf16[18,24,512]{2,1,0:T(8,128)(2,1)S(1)}, bf16[18,24,512]{2,1,0:T(8,128)(2,1)S(1)}, u32[]{:S(2)}, u32[]{:S(2)}) collective-permute-start(bf16[18,24,512]{2,1,0:T(8,128)(2,1)S(1)} %get-tuple-element.137), channel_id=1, source_target_pairs={{0,48},{1,17},{16,32},{17,1},{32,16},{33,49},{48,0},{49,33},{2,50}... | collective-permute-start | bytes 1327112 | tf_op jit(solution)/shard_map/ppermute | solution.py:575
  88.8 7.5 %collective-permute-start.17 = (bf16[18,24,512]{2,1,0:T(8,128)(2,1)S(1)}, bf16[18,24,512]{2,1,0:T(8,128)(2,1)S(1)}, u32[]{:S(2)}, u32[]{:S(2)}) collective-permute-start(bf16[18,24,512]{2,1,0:T(8,128)(2,1)S(1)} %get-tuple-element.139), channel_id=1, source_target_pairs={{0,66},{1,3},{2,64},{3,1},{64,2},{65,67},{66,0},{67,65},{4,70},{5,... | collective-permute-start | bytes 1327112 | tf_op jit(solution)/shard_map/ppermute | solution.py:575
  88.9 7.5 %collective-permute-start.18 = (bf16[18,24,512]{2,1,0:T(8,128)(2,1)S(1)}, bf16[18,24,512]{2,1,0:T(8,128)(2,1)S(1)}, u32[]{:S(2)}, u32[]{:S(2)}) collective-permute-start(bf16[18,24,512]{2,1,0:T(8,128)(2,1)S(1)} %get-tuple-element.141), channel_id=1, source_target_pairs={{0,12},{1,5},{4,8},{5,1},{8,4},{9,13},{12,0},{13,9},{2,14},{3,7},{... | collective-permute-start | bytes 1327112 | tf_op jit(solution)/shard_map/ppermute | solution.py:575
  96.5 31.5 %copy-start.1 = (bf16[24,12,1536]{2,0,1:T(8,128)(2,1)S(1)}, bf16[24,12,1536]{2,0,1:T(8,128)(2,1)}, u32[]{:S(2)}) copy-start(bf16[24,12,1536]{2,0,1:T(8,128)(2,1)} %param.11) | copy-start | bytes 2654212
  97.3 8.1 %collective-permute-start.19 = (bf16[10,24,512]{2,1,0:T(8,128)(2,1)S(1)}, bf16[10,24,512]{2,1,0:T(8,128)(2,1)S(1)}, u32[]{:S(2)}, u32[]{:S(2)}) collective-permute-start(bf16[10,24,512]{2,1,0:T(8,128)(2,1)S(1)} %get-tuple-element.143), channel_id=1, source_target_pairs={{0,2},{1,67},{2,0},{3,65},{64,66},{65,3},{66,64},{67,1},{4,6},{5,7... | collective-permute-start | bytes 737288 | tf_op jit(solution)/shard_map/ppermute | solution.py:575
  99.5 6.3 %collective-permute-start.20 = (bf16[10,24,512]{2,1,0:T(8,128)(2,1)S(1)}, bf16[10,24,512]{2,1,0:T(8,128)(2,1)S(1)}, u32[]{:S(2)}, u32[]{:S(2)}) collective-permute-start(bf16[10,24,512]{2,1,0:T(8,128)(2,1)S(1)} %get-tuple-element.145), channel_id=1, source_target_pairs={{0,4},{1,13},{4,0},{5,9},{8,12},{9,5},{12,8},{13,1},{2,6},{3,15},{... | collective-permute-start | bytes 737288 | tf_op jit(solution)/shard_map/ppermute | solution.py:575
  100.9 6.3 %collective-permute-start.21 = (bf16[10,24,512]{2,1,0:T(8,128)(2,1)S(1)}, bf16[10,24,512]{2,1,0:T(8,128)(2,1)S(1)}, u32[]{:S(2)}, u32[]{:S(2)}) collective-permute-start(bf16[10,24,512]{2,1,0:T(8,128)(2,1)S(1)} %get-tuple-element.147), channel_id=1, source_target_pairs={{0,16},{1,49},{16,0},{17,33},{32,48},{33,17},{48,32},{49,1},{2,18}... | collective-permute-start | bytes 737288 | tf_op jit(solution)/shard_map/ppermute | solution.py:575
  102.1 8.5 %collective-permute-start.12 = (bf16[72,1536]{1,0:T(8,128)(2,1)S(1)}, bf16[72,1536]{1,0:T(8,128)(2,1)S(1)}, u32[]{:S(2)}, u32[]{:S(2)}) collective-permute-start(bf16[72,1536]{1,0:T(8,128)(2,1)S(1)} %get-tuple-element.128), channel_id=1, source_target_pairs={{0,124},{4,0},{8,4},{12,8},{16,12},{20,16},{24,20},{28,24},{32,28}... | collective-permute-start | bytes 663560 | tf_op jit(solution)/shard_map/ppermute | solution.py:575
  107.8 4.1 %collective-permute-start.22 = (bf16[6,24,512]{2,1,0:T(8,128)(2,1)S(1)}, bf16[6,24,512]{2,1,0:T(8,128)(2,1)S(1)}, u32[]{:S(2)}, u32[]{:S(2)}) collective-permute-start(bf16[6,24,512]{2,1,0:T(8,128)(2,1)S(1)} %get-tuple-element.149), channel_id=1, source_target_pairs={{0,66},{1,3},{2,64},{3,1},{64,2},{65,67},{66,0},{67,65},{4,70},{5,... | collective-permute-start | bytes 442376 | tf_op jit(solution)/shard_map/ppermute | solution.py:575
  108.7 4.3 %collective-permute-start.23 = (bf16[6,24,512]{2,1,0:T(8,128)(2,1)S(1)}, bf16[6,24,512]{2,1,0:T(8,128)(2,1)S(1)}, u32[]{:S(2)}, u32[]{:S(2)}) collective-permute-start(bf16[6,24,512]{2,1,0:T(8,128)(2,1)S(1)} %get-tuple-element.151), channel_id=1, source_target_pairs={{0,12},{1,5},{4,8},{5,1},{8,4},{9,13},{12,0},{13,9},{2,14},{3,7},{... | collective-permute-start | bytes 442376 | tf_op jit(solution)/shard_map/ppermute | solution.py:575
  108.7 4.5 %collective-permute-start.24 = (bf16[6,24,512]{2,1,0:T(8,128)(2,1)S(1)}, bf16[6,24,512]{2,1,0:T(8,128)(2,1)S(1)}, u32[]{:S(2)}, u32[]{:S(2)}) collective-permute-start(bf16[6,24,512]{2,1,0:T(8,128)(2,1)S(1)} %get-tuple-element.153), channel_id=1, source_target_pairs={{0,48},{1,17},{16,32},{17,1},{32,16},{33,49},{48,0},{49,33},{2,50}... | collective-permute-start | bytes 442376 | tf_op jit(solution)/shard_map/ppermute | solution.py:575
  109.1 18.8 %collective-permute-start.31 = (bf16[72,1536]{1,0:T(8,128)(2,1)S(1)}, bf16[72,1536]{1,0:T(8,128)(2,1)S(1)}, u32[]{:S(2)}, u32[]{:S(2)}) collective-permute-start(bf16[72,1536]{1,0:T(8,128)(2,1)S(1)} %get-tuple-element.167), channel_id=1, source_target_pairs={{0,4},{4,8},{8,12},{12,16},{16,20},{20,24},{24,28},{28,32},{32,36}... | collective-permute-start | bytes 663560 | tf_op jit(solution)/shard_map/ppermute | solution.py:575
  113.9 10.1 %collective-permute-start.25 = (bf16[4,24,512]{2,1,0:T(8,128)(2,1)S(1)}, bf16[4,24,512]{2,1,0:T(8,128)(2,1)S(1)}, u32[]{:S(2)}, u32[]{:S(2)}) collective-permute-start(bf16[4,24,512]{2,1,0:T(8,128)(2,1)S(1)} %get-tuple-element.155), channel_id=1, source_target_pairs={{0,4},{1,13},{4,0},{5,9},{8,12},{9,5},{12,8},{13,1},{2,6},{3,15},{... | collective-permute-start | bytes 294920 | tf_op jit(solution)/shard_map/ppermute | solution.py:575
  115.0 8.9 %collective-permute-start.26 = (bf16[4,24,512]{2,1,0:T(8,128)(2,1)S(1)}, bf16[4,24,512]{2,1,0:T(8,128)(2,1)S(1)}, u32[]{:S(2)}, u32[]{:S(2)}) collective-permute-start(bf16[4,24,512]{2,1,0:T(8,128)(2,1)S(1)} %get-tuple-element.157), channel_id=1, source_target_pairs={{0,16},{1,49},{16,0},{17,33},{32,48},{33,17},{48,32},{49,1},{2,18}... | collective-permute-start | bytes 294920 | tf_op jit(solution)/shard_map/ppermute | solution.py:575
  117.6 6.3 %collective-permute-start.27 = (bf16[4,24,512]{2,1,0:T(8,128)(2,1)S(1)}, bf16[4,24,512]{2,1,0:T(8,128)(2,1)S(1)}, u32[]{:S(2)}, u32[]{:S(2)}) collective-permute-start(bf16[4,24,512]{2,1,0:T(8,128)(2,1)S(1)} %get-tuple-element.159), channel_id=1, source_target_pairs={{0,2},{1,67},{2,0},{3,65},{64,66},{65,3},{66,64},{67,1},{4,6},{5,7... | collective-permute-start | bytes 294920 | tf_op jit(solution)/shard_map/ppermute | solution.py:575
  118.3 9.7 %collective-permute-start.32 = (bf16[36,1536]{1,0:T(8,128)(2,1)S(1)}, bf16[36,1536]{1,0:T(8,128)(2,1)S(1)}, u32[]{:S(2)}, u32[]{:S(2)}) collective-permute-start(bf16[36,1536]{1,0:T(8,128)(2,1)S(1)} %last_rows.1), channel_id=1, source_target_pairs={{0,1},{1,2},{2,3},{3,0},{4,5},{5,6},{6,7},{7,4},{8,9},{9,10},{10,1... | collective-permute-start | bytes 331784 | tf_op jit(solution)/shard_map/ppermute | solution.py:575
  124.6 4.7 %collective-permute-start.28 = (bf16[3,24,512]{2,1,0:T(8,128)(2,1)S(1)}, bf16[3,24,512]{2,1,0:T(8,128)(2,1)S(1)}, u32[]{:S(2)}, u32[]{:S(2)}) collective-permute-start(bf16[3,24,512]{2,1,0:T(8,128)(2,1)S(1)} %get-tuple-element.161), channel_id=1, source_target_pairs={{0,12},{1,5},{4,8},{5,1},{8,4},{9,13},{12,0},{13,9},{2,14},{3,7},{... | collective-permute-start | bytes 221192 | tf_op jit(solution)/shard_map/ppermute | solution.py:575
  126.2 3.5 %collective-permute-start.29 = (bf16[3,24,512]{2,1,0:T(8,128)(2,1)S(1)}, bf16[3,24,512]{2,1,0:T(8,128)(2,1)S(1)}, u32[]{:S(2)}, u32[]{:S(2)}) collective-permute-start(bf16[3,24,512]{2,1,0:T(8,128)(2,1)S(1)} %get-tuple-element.163), channel_id=1, source_target_pairs={{0,48},{1,17},{16,32},{17,1},{32,16},{33,49},{48,0},{49,33},{2,50}... | collective-permute-start | bytes 221192 | tf_op jit(solution)/shard_map/ppermute | solution.py:575
  128.0 3.2 %collective-permute-start.30 = (bf16[3,24,512]{2,1,0:T(8,128)(2,1)S(1)}, bf16[3,24,512]{2,1,0:T(8,128)(2,1)S(1)}, u32[]{:S(2)}, u32[]{:S(2)}) collective-permute-start(bf16[3,24,512]{2,1,0:T(8,128)(2,1)S(1)} %get-tuple-element.165), channel_id=1, source_target_pairs={{0,66},{1,3},{2,64},{3,1},{64,2},{65,67},{66,0},{67,65},{4,70},{5,... | collective-permute-start | bytes 221192 | tf_op jit(solution)/shard_map/ppermute | solution.py:575
  131.2 8.2 %collective-permute-start.33 = (bf16[9,24,512]{2,1,0:T(8,128)(2,1)S(1)}, bf16[9,24,512]{2,1,0:T(8,128)(2,1)S(1)}, u32[]{:S(2)}, u32[]{:S(2)}) collective-permute-start(bf16[9,24,512]{2,1,0:T(8,128)(2,1)S(1)} %total.1.own), channel_id=1, source_target_pairs={{0,1},{1,0},{2,3},{3,2},{4,5},{5,4},{6,7},{7,6},{8,9},{9,8},{10,11... | collective-permute-start | bytes 663560 | tf_op jit(solution)/shard_map/ppermute | solution.py:575
  (3 other events, 2.2 us)

commit v8 on v6

--- a/solution.py
+++ b/solution.py
@@ -51,7 +51,7 @@
     return pl.CostEstimate(flops=flops, bytes_accessed=moved, transcendentals=0)
 
 
-def call(body, outs, operands, scalars=1, scratch=(), flops=0, vmem=50, far=(), near=(), name=None):
+def call(body, outs, operands, scalars=1, scratch=(), flops=0, vmem=50, far=(), near=(), sent=(), name=None):
     specs = [SMEM] * scalars + [VMEM] * (len(operands) - scalars)
     for i in far:
         specs[i] = HBM
@@ -61,7 +61,7 @@
         body,
         out_shape=list(outs),
         in_specs=specs,
-        out_specs=[VMEM] * len(outs),
+        out_specs=[ANY if i in sent else VMEM for i in range(len(outs))],
         scratch_shapes=list(scratch),
         compiler_params=pltpu.CompilerParams(vmem_limit_bytes=vmem * 2**20),
         cost_estimate=cost(outs, operands, flops),
@@ -193,7 +193,7 @@
 
 
 def forward_body(
-    scale, own, east, west, low, w, query_bias, value_bias, pair_bias, row, col, x, projected, attended, grid, rows, wide, sems
+    scale, own, east, west, low, w, query_bias, value_bias, pair_bias, row, col, x_out, projected_out, attended, grid, rows, wide, x, projected, sems
 ):
     copies = []
     for g in range(3):
@@ -203,6 +203,8 @@
             copies[-1].start()
     window_rows(own, east, west, low, grid, rows)
     x[...] = rows[...].astype(BF16)
+    sends = [pltpu.make_async_copy(x, x_out, sems.at[9])]
+    sends[0].start()
     pens = penalties(row[...], col[...])
     for g in range(3):
         for j in range(3):
@@ -212,6 +214,11 @@
             if j != 1:
                 product = product + (query_bias, None, value_bias)[j][g * 256 : (g + 1) * 256].reshape(1, 256)
             projected[:, lo : lo + 256] = product
+            at = pl.ds(lo, 256)
+            sends.append(
+                pltpu.make_async_copy(projected.at[:, at], projected_out.at[:, at], sems.at[10 + 3 * g + j])
+            )
+            sends[-1].start()
         for half in range(2):
             lo = g * 256 + half * 128
             head = lo // HEAD_DIM
@@ -224,6 +231,8 @@
             attention = softmax_of([c * factor + pb + pen for c, pen in zip(cosines, pens)])
             outs = [dot(a.astype(BF16), v[at].astype(BF16)) for a, at in zip(attention, SPANS)]
             attended[:, lo : lo + 128] = jnp.concatenate([unstacked(o) for o in outs], 0).astype(BF16)
+    for send in sends:
+        send.wait()
 
 
 def norm_part(attended, rows, pw, gain, mixed_low, attended_grad, gain_part, mixed_all):
@@ -331,7 +340,7 @@
     pair_bias,
     row,
     col,
-    mixed_low,
+    mixed_out,
     grad_other,
     gain_part,
     grads,
@@ -344,6 +353,7 @@
     weight,
     heads,
     attended_grad,
+    mixed_low,
     sems,
 ):
     copies = [pltpu.make_async_copy(pw, weight, sems.at[0])]
@@ -356,6 +366,8 @@
     copies[0].wait()
     norm_part(attended, rows, weight, gain, mixed_low, attended_grad, gain_part, mixed_all)
     pens = penalties(row[...], col[...])
+    send = pltpu.make_async_copy(mixed_low, mixed_out, sems.at[4])
+    send.start()
     near = pl.ds(pl.multiple_of((1 - side[0]) * HALF, 128), HALF)
     far = pl.ds(pl.multiple_of(side[0] * HALF, 128), HALF)
     grad_other[...] = attended_grad[:, near]
@@ -384,6 +396,7 @@
                 gains,
             ),
         )
+    send.wait()
 
 
 def write_coded(value, lines, outs, base):
@@ -661,11 +674,14 @@
             pltpu.VMEM((12, CELLS, 128), F32),
             pltpu.VMEM((CELLS, C), F32),
             pltpu.VMEM((C, 3 * HC), BF16),
-            pltpu.SemaphoreType.DMA((9,)),
+            pltpu.VMEM((CELLS, C), BF16),
+            pltpu.VMEM((CELLS, 3 * HC), F32),
+            pltpu.SemaphoreType.DMA((19,)),
         ],
         flops=2 * CELLS * C * 3 * HC,
         far=(5,),
         vmem=60,
+        sent=(0, 1),
         name="forward",
     )
     x_other = core_swap(x)
@@ -701,12 +717,14 @@
             pltpu.VMEM((C, HC), BF16),
             pltpu.VMEM((3, CELLS, HALF), F32),
             pltpu.VMEM((CELLS, HC), F32),
-            pltpu.SemaphoreType.DMA((4,)),
+            pltpu.VMEM((CELLS, C), BF16),
+            pltpu.SemaphoreType.DMA((5,)),
         ],
         far=(7,),
         near=(9,),
         flops=4 * CELLS * C * HC + 2 * CELLS * WIN * 128 * 18,
         vmem=60,
+        sent=(0,),
         name="backward",
     )
     mixed_other = core_swap(mixed_low)

time: 136 us -> 136 us (level)
  no operation moved by 1% of the time
where the time goes in v8:
time: 136 us
  starting transfers between devices  55.9 us (41%)
  Pallas kernels  45.4 us (33%)
  waiting for transfers between devices  25.3 us (19%)
  local copies, waits for them, and re-layouts  7.94 us (6%)
    ppermute x34, starting transfers between devices, permuted(): return lax.ppermute(value, axes, pairs)  55.9 us
    pallas_call x16, Pallas kernels, call(): pl.pallas_call(body, out_shape=list(outs), in_specs=specs, out_specs=[ANY...  37.1 us
    ppermute x34, waiting for transfers between devices, permuted(): return lax.ppermute(value, axes, pairs)  25.3 us
    pallas_call x2, Pallas kernels, grid_call(): pl.pallas_call(body, grid_spec=spec, out_shape=results, compiler_params=p...  8.34 us
    unnamed x44, local copies, waits for them, and re-layouts  5.59 us
  transfers between devices with their start and end apart: 34, of which 15 were waited for; matrix products, arithmetic and copies ran while one was open for 2% of the time, Pallas kernels for 26%

profile of v8, /device:TPU:1, one launch (start us, length us, event | category | flops | bytes accessed | tf_op | source)
XLA Modules:
  0.0 135.7 jit_solution(10628955074373555158)
XLA Ops:
  0.6 1.2 copy-done.4
  2.0 1.5 %collective-permute-start.1 = (bf16[36,1536]{1,0:T(8,128)(2,1)S(1)}, bf16[36,1536]{1,0:T(8,128)(2,1)S(1)}, u32[]{:S(2)}, u32[]{:S(2)}) collective-permute-start(bf16[36,1536]{1,0:T(8,128)(2,1)S(1)} %get-tuple-element.100), channel_id=1, source_target_pairs={{0,3},{1,0},{2,1},{3,2},{4,7},{5,4},{6,5},{7,6},{8,11},{9,8},{10,9... | collective-permute-start | bytes 331784 | tf_op jit(solution)/shard_map/ppermute | solution.py:588
  3.5 8.7 %collective-permute-start = (bf16[72,1536]{1,0:T(8,128)(2,1)S(1)}, bf16[72,1536]{1,0:T(8,128)(2,1)S(1)}, u32[]{:S(2)}, u32[]{:S(2)}) collective-permute-start(bf16[72,1536]{1,0:T(8,128)(2,1)S(1)} %get-tuple-element.95), channel_id=1, source_target_pairs={{0,124},{4,0},{8,4},{12,8},{16,12},{20,16},{24,20},{28,24},{32,28}... | collective-permute-start | bytes 663560 | tf_op jit(solution)/shard_map/ppermute | solution.py:588
  12.1 1.2 copy-done.1
  13.6 1.1 collective-permute-start.6
  14.7 0.8 fusion
  15.5 7.2 %collective-permute-start.5 = (bf16[72,1536]{1,0:T(8,128)(2,1)S(1)}, bf16[72,1536]{1,0:T(8,128)(2,1)S(1)}, u32[]{:S(2)}, u32[]{:S(2)}) collective-permute-start(bf16[72,1536]{1,0:T(8,128)(2,1)S(1)} %get-tuple-element.106), channel_id=1, source_target_pairs={{0,124},{4,0},{8,4},{12,8},{16,12},{20,16},{24,20},{28,24},{32,28}... | collective-permute-start | bytes 663560 | tf_op jit(solution)/shard_map/ppermute | solution.py:588
  22.9 4.7 %collective-permute-done.3 = s32[12,12]{0,1:T(8,128)S(1)} collective-permute-done((s32[12,12]{0,1:T(8,128)S(1)}, s32[12,12]{0,1:T(8,128)S(1)}, u32[]{:S(2)}, u32[]{:S(2)}) %collective-permute-start.3) | collective-permute-done | bytes 608 | tf_op jit(solution)/shard_map/ppermute | solution.py:588
  27.7 0.7 reshape.30.row
  28.4 0.8 reshape.33.col
  29.2 0.6 copy-done.16
  29.9 11.4 %forward.1 = (bf16[288,1536]{1,0:T(8,128)(2,1)}, f32[288,2304]{1,0:T(8,128)}, bf16[288,768]{1,0:T(8,128)(2,1)}) custom-call(f32[12]{0:T(128)} %scale.5, bf16[12,24,1536]{2,1,0:T(8,128)(2,1)} %bitcast.17, bf16[72,1536]{1,0:T(8,128)(2,1)} %copy-done.16, bf16[72,1536]{1,0:T(8,128)(2,1)} %copy-done.17, bf16[36,1536]{1,0:T(8,128)(2,1)} %copy-done.8, ...), custom_call_target="tpu_custom_call" | custom-call | flops 2038431744 | bytes 12754224 | tf_op jit(solution)/shard_map/forward/pallas_call | solution.py:60
  41.4 1.1 collective-permute-start.4
  42.5 0.7 copy-done.19
  43.3 11.2 %backward.1 = (bf16[288,1536]{1,0:T(8,128)(2,1)}, f32[288,384]{1,0:T(8,128)}, f32[1,1536]{1,0:T(1,128)}, bf16[288,1152]{1,0:T(8,128)(2,1)}, f32[144,512]{1,0:T(8...) custom-call(s32[1]{0:T(128)S(6)} %sub.3.side, f32[12]{0:T(128)} %scale.5, ...), custom_call_target="tpu_custom_call" | custom-call | flops 1454505984 | bytes 9884980 | tf_op jit(solution)/shard_map/backward/pallas_call | solution.py:60
  55.7 1.0 copy-done.9
  56.7 0.7 copy-done.11
  57.4 4.4 %attention.1 = (bf16[288,1152]{1,0:T(8,128)(2,1)S(1)}, f32[144,512]{1,0:T(8,128)S(1)}) custom-call(s32[1]{0:T(128)} %bitcast.side.core, f32[12]{0:T(128)S(1)} %copy-done.12, f32[288,2304]{1,0:T(8,128)S(1)} %copy-done, f32[288,2304]{1,0:T(8,128)S(1)} %copy-done, f32[288,2304]{1,0:T(8,128)S(1)} %copy-done, f32[288,384]{1,0:T(8,128)S(1)} %copy-done.9, ...), custom_call_target="tpu_custom_call" | custom-call | flops 95551488 | bytes 9620736 | tf_op jit(solution)/shard_map/attention/pallas_call | solution.py:82
  62.0 7.5 %weights.1 = (bf16[34,24,512]{2,1,0:T(8,128)(2,1)S(1)}, bf16[34,24,512]{2,1,0:T(8,128)(2,1)S(1)}, bf16[34,24,512]{2,1,0:T(8,128)(2,1)S(1)}, bf16[34,24,512]{2,1,...) custom-call(s32[4]{0:T(128)S(1)} %pad_add_fusion.1.place, ...), custom_call_target="tpu_custom_call" | custom-call | flops 2717908992 | bytes 10911760 | tf_op jit(solution)/shard_map/weights/pallas_call | solution.py:60
  69.8 3.1 %collective-permute-start.15 = (bf16[34,24,512]{2,1,0:T(8,128)(2,1)S(1)}, bf16[34,24,512]{2,1,0:T(8,128)(2,1)S(1)}, u32[]{:S(2)}, u32[]{:S(2)}) collective-permute-start(bf16[34,24,512]{2,1,0:T(8,128)(2,1)S(1)} %get-tuple-element.135), channel_id=1, source_target_pairs={{0,4},{1,13},{4,0},{5,9},{8,12},{9,5},{12,8},{13,1},{2,6},{3,15},{... | collective-permute-start | bytes 2506760 | tf_op jit(solution)/shard_map/ppermute | solution.py:588
  72.9 3.9 %branch.1 = (bf16[72,1536]{1,0:T(8,128)(2,1)S(1)}, bf16[72,1536]{1,0:T(8,128)(2,1)S(1)}, bf16[72,1536]{1,0:T(8,128)(2,1)S(1)}, bf16[72,1536]{1,0:T(8,128)(2,1)S(1)}) custom-call(s32[1]{0:T(128)} %bitcast.side.core, bf16[1536,2304]{1,0:T(8,128)(2,1)S(1)} %bitcast.10, bf16[288,1152]{1,0:T(8,128)(2,1)S(1)} %get-tuple-element.111.p0.own, ...), custom_call_target="tpu_custom_call" | custom-call | flops 2038431744 | bytes 9289728 | tf_op jit(solution)/shard_map/branch/pallas_call | solution.py:82
  76.8 5.3 %collective-permute-done.13.refs_1_ = bf16[34,24,512]{2,1,0:T(8,128)(2,1)S(1)} collective-permute-done((bf16[34,24,512]{2,1,0:T(8,128)(2,1)S(1)}, bf16[34,24,512]{2,1,0:T(8,128)(2,1)S(1)}, u32[]{:S(2)}, u32[]{:S(2)}) %collective-permute-start.13) | collective-permute-done | bytes 835616 | tf_op jit(solution)/shard_map/ppermute | solution.py:588
  82.8 1.2 halve.5
  84.3 7.2 %collective-permute-done.16.refs_1_ = bf16[18,24,512]{2,1,0:T(8,128)(2,1)S(1)} collective-permute-done((bf16[18,24,512]{2,1,0:T(8,128)(2,1)S(1)}, bf16[18,24,512]{2,1,0:T(8,128)(2,1)S(1)}, u32[]{:S(2)}, u32[]{:S(2)}) %collective-permute-start.16) | collective-permute-done | bytes 442400 | tf_op jit(solution)/shard_map/ppermute | solution.py:588
  91.8 0.9 halve.6
  92.6 2.2 %collective-permute-start.19 = (bf16[10,24,512]{2,1,0:T(8,128)(2,1)S(1)}, bf16[10,24,512]{2,1,0:T(8,128)(2,1)S(1)}, u32[]{:S(2)}, u32[]{:S(2)}) collective-permute-start(bf16[10,24,512]{2,1,0:T(8,128)(2,1)S(1)} %get-tuple-element.143), channel_id=1, source_target_pairs={{0,2},{1,67},{2,0},{3,65},{64,66},{65,3},{66,64},{67,1},{4,6},{5,7... | collective-permute-start | bytes 737288 | tf_op jit(solution)/shard_map/ppermute | solution.py:588
  94.8 1.3 collective-permute-start.20
  96.1 1.3 collective-permute-start.21
  97.4 3.4 %collective-permute-start.12 = (bf16[72,1536]{1,0:T(8,128)(2,1)S(1)}, bf16[72,1536]{1,0:T(8,128)(2,1)S(1)}, u32[]{:S(2)}, u32[]{:S(2)}) collective-permute-start(bf16[72,1536]{1,0:T(8,128)(2,1)S(1)} %get-tuple-element.128), channel_id=1, source_target_pairs={{0,124},{4,0},{8,4},{12,8},{16,12},{20,16},{24,20},{28,24},{32,28}... | collective-permute-start | bytes 663560 | tf_op jit(solution)/shard_map/ppermute | solution.py:588
  101.1 1.3 collective-permute-done.21.refs_5_
  102.4 0.7 halve.7
  103.1 0.8 collective-permute-start.22
  104.4 1.5 %collective-permute-start.31 = (bf16[72,1536]{1,0:T(8,128)(2,1)S(1)}, bf16[72,1536]{1,0:T(8,128)(2,1)S(1)}, u32[]{:S(2)}, u32[]{:S(2)}) collective-permute-start(bf16[72,1536]{1,0:T(8,128)(2,1)S(1)} %get-tuple-element.167), channel_id=1, source_target_pairs={{0,4},{4,8},{8,12},{12,16},{16,20},{20,24},{24,28},{28,32},{32,36}... | collective-permute-start | bytes 663560 | tf_op jit(solution)/shard_map/ppermute | solution.py:588
  106.0 1.2 collective-permute-done.22.refs_1_
  107.2 1.0 collective-permute-done.23.refs_3_
  108.5 0.6 halve.8
  109.2 1.2 collective-permute-start.25
  110.3 2.6 %collective-permute-start.26 = (bf16[4,24,512]{2,1,0:T(8,128)(2,1)S(1)}, bf16[4,24,512]{2,1,0:T(8,128)(2,1)S(1)}, u32[]{:S(2)}, u32[]{:S(2)}) collective-permute-start(bf16[4,24,512]{2,1,0:T(8,128)(2,1)S(1)} %get-tuple-element.157), channel_id=1, source_target_pairs={{0,16},{1,49},{16,0},{17,33},{32,48},{33,17},{48,32},{49,1},{2,18}... | collective-permute-start | bytes 294920 | tf_op jit(solution)/shard_map/ppermute | solution.py:588
  112.9 0.7 collective-permute-start.27
  113.6 5.6 %collective-permute-start.32 = (bf16[36,1536]{1,0:T(8,128)(2,1)S(1)}, bf16[36,1536]{1,0:T(8,128)(2,1)S(1)}, u32[]{:S(2)}, u32[]{:S(2)}) collective-permute-start(bf16[36,1536]{1,0:T(8,128)(2,1)S(1)} %last_rows.1), channel_id=1, source_target_pairs={{0,1},{1,2},{2,3},{3,0},{4,5},{5,6},{6,7},{7,4},{8,9},{9,10},{10,1... | collective-permute-start | bytes 331784 | tf_op jit(solution)/shard_map/ppermute | solution.py:588
  119.3 0.6 halve.9
  119.9 1.6 %collective-permute-start.28 = (bf16[3,24,512]{2,1,0:T(8,128)(2,1)S(1)}, bf16[3,24,512]{2,1,0:T(8,128)(2,1)S(1)}, u32[]{:S(2)}, u32[]{:S(2)}) collective-permute-start(bf16[3,24,512]{2,1,0:T(8,128)(2,1)S(1)} %get-tuple-element.161), channel_id=1, source_target_pairs={{0,12},{1,5},{4,8},{5,1},{8,4},{9,13},{12,0},{13,9},{2,14},{3,7},{... | collective-permute-start | bytes 221192 | tf_op jit(solution)/shard_map/ppermute | solution.py:588
  121.5 1.7 %collective-permute-start.29 = (bf16[3,24,512]{2,1,0:T(8,128)(2,1)S(1)}, bf16[3,24,512]{2,1,0:T(8,128)(2,1)S(1)}, u32[]{:S(2)}, u32[]{:S(2)}) collective-permute-start(bf16[3,24,512]{2,1,0:T(8,128)(2,1)S(1)} %get-tuple-element.163), channel_id=1, source_target_pairs={{0,48},{1,17},{16,32},{17,1},{32,16},{33,49},{48,0},{49,33},{2,50}... | collective-permute-start | bytes 221192 | tf_op jit(solution)/shard_map/ppermute | solution.py:588
  123.3 1.3 merge.1
  125.0 1.5 %collective-permute-done.30.refs_5_ = bf16[3,24,512]{2,1,0:T(8,128)(2,1)S(1)} collective-permute-done((bf16[3,24,512]{2,1,0:T(8,128)(2,1)S(1)}, bf16[3,24,512]{2,1,0:T(8,128)(2,1)S(1)}, u32[]{:S(2)}, u32[]{:S(2)}) %collective-permute-start.30) | collective-permute-done | bytes 73760 | tf_op jit(solution)/shard_map/ppermute | solution.py:588
  126.5 7.1 %collective-permute-start.33 = (bf16[9,24,512]{2,1,0:T(8,128)(2,1)S(1)}, bf16[9,24,512]{2,1,0:T(8,128)(2,1)S(1)}, u32[]{:S(2)}, u32[]{:S(2)}) collective-permute-start(bf16[9,24,512]{2,1,0:T(8,128)(2,1)S(1)} %total.1.own), channel_id=1, source_target_pairs={{0,1},{1,0},{2,3},{3,2},{4,5},{5,4},{6,7},{7,6},{8,9},{9,8},{10,11... | collective-permute-start | bytes 663560 | tf_op jit(solution)/shard_map/ppermute | solution.py:588
  133.6 1.1 collective-permute-done.33.other
  134.7 0.9 finish.1
  (89 shorter events, 5.1 us)
Async XLA Ops:
  2.0 11.5 %collective-permute-start.1 = (bf16[36,1536]{1,0:T(8,128)(2,1)S(1)}, bf16[36,1536]{1,0:T(8,128)(2,1)S(1)}, u32[]{:S(2)}, u32[]{:S(2)}) collective-permute-start(bf16[36,1536]{1,0:T(8,128)(2,1)S(1)} %get-tuple-element.100), channel_id=1, source_target_pairs={{0,3},{1,0},{2,1},{3,2},{4,7},{5,4},{6,5},{7,6},{8,11},{9,8},{10,9... | collective-permute-start | bytes 331784 | tf_op jit(solution)/shard_map/ppermute | solution.py:588
  3.5 25.7 %collective-permute-start = (bf16[72,1536]{1,0:T(8,128)(2,1)S(1)}, bf16[72,1536]{1,0:T(8,128)(2,1)S(1)}, u32[]{:S(2)}, u32[]{:S(2)}) collective-permute-start(bf16[72,1536]{1,0:T(8,128)(2,1)S(1)} %get-tuple-element.95), channel_id=1, source_target_pairs={{0,124},{4,0},{8,4},{12,8},{16,12},{20,16},{24,20},{28,24},{32,28}... | collective-permute-start | bytes 663560 | tf_op jit(solution)/shard_map/ppermute | solution.py:588
  13.5 15.7 %copy-start.8 = (bf16[36,1536]{1,0:T(8,128)(2,1)}, bf16[36,1536]{1,0:T(8,128)(2,1)S(1)}, u32[]{:S(2)}) copy-start(bf16[36,1536]{1,0:T(8,128)(2,1)S(1)} %collective-permute-done.1.low) | copy-start | bytes 331780
  13.6 9.1 %collective-permute-start.6 = (bf16[36,1536]{1,0:T(8,128)(2,1)S(1)}, bf16[36,1536]{1,0:T(8,128)(2,1)S(1)}, u32[]{:S(2)}, u32[]{:S(2)}) collective-permute-start(bf16[36,1536]{1,0:T(8,128)(2,1)S(1)} %get-tuple-element.108), channel_id=1, source_target_pairs={{0,3},{1,0},{2,1},{3,2},{4,7},{5,4},{6,5},{7,6},{8,11},{9,8},{10,9... | collective-permute-start | bytes 331784 | tf_op jit(solution)/shard_map/ppermute | solution.py:588
  14.7 14.5 %collective-permute-start.2 = (bf16[72,1536]{1,0:T(8,128)(2,1)S(1)}, bf16[72,1536]{1,0:T(8,128)(2,1)S(1)}, u32[]{:S(2)}, u32[]{:S(2)}) collective-permute-start(bf16[72,1536]{1,0:T(8,128)(2,1)S(1)} %to_east.2), channel_id=1, source_target_pairs={{0,4},{4,8},{8,12},{12,16},{16,20},{20,24},{24,28},{28,32},{32,36}... | collective-permute-start | bytes 663560 | tf_op jit(solution)/shard_map/ppermute | solution.py:588
  15.5 12.0 %collective-permute-start.3 = (s32[12,12]{0,1:T(8,128)S(1)}, s32[12,12]{0,1:T(8,128)S(1)}, u32[]{:S(2)}, u32[]{:S(2)}) collective-permute-start(s32[12,12]{0,1:T(8,128)S(1)} %get-tuple-element.183), channel_id=1, source_target_pairs={{0,4},{4,8},{8,12},{12,16},{16,20},{20,24},{24,28},{28,32},{32,36}... | collective-permute-start | bytes 1736 | tf_op jit(solution)/shard_map/ppermute | solution.py:588
  15.5 27.0 %collective-permute-start.5 = (bf16[72,1536]{1,0:T(8,128)(2,1)S(1)}, bf16[72,1536]{1,0:T(8,128)(2,1)S(1)}, u32[]{:S(2)}, u32[]{:S(2)}) collective-permute-start(bf16[72,1536]{1,0:T(8,128)(2,1)S(1)} %get-tuple-element.106), channel_id=1, source_target_pairs={{0,124},{4,0},{8,4},{12,8},{16,12},{20,16},{24,20},{28,24},{32,28}... | collective-permute-start | bytes 663560 | tf_op jit(solution)/shard_map/ppermute | solution.py:588
  22.7 18.6 %copy-start.7 = (bf16[36,1536]{1,0:T(8,128)(2,1)}, bf16[36,1536]{1,0:T(8,128)(2,1)S(1)}, u32[]{:S(2)}) copy-start(bf16[36,1536]{1,0:T(8,128)(2,1)S(1)} %collective-permute-done.6.low) | copy-start | bytes 331780
  22.8 19.7 %collective-permute-start.7 = (bf16[72,1536]{1,0:T(8,128)(2,1)S(1)}, bf16[72,1536]{1,0:T(8,128)(2,1)S(1)}, u32[]{:S(2)}, u32[]{:S(2)}) collective-permute-start(bf16[72,1536]{1,0:T(8,128)(2,1)S(1)} %to_east.3), channel_id=1, source_target_pairs={{0,4},{4,8},{8,12},{12,16},{16,20},{20,24},{24,28},{28,32},{32,36}... | collective-permute-start | bytes 663560 | tf_op jit(solution)/shard_map/ppermute | solution.py:588
  41.4 20.5 %collective-permute-start.4 = (bf16[288,1536]{1,0:T(8,128)(2,1)}, bf16[288,1536]{1,0:T(8,128)(2,1)}, u32[]{:S(2)}, u32[]{:S(2)}) collective-permute-start(bf16[288,1536]{1,0:T(8,128)(2,1)} %get-tuple-element.103.x0), channel_id=1, source_target_pairs={{0,1},{1,0},{2,3},{3,2},{4,5},{5,4},{6,7},{7,6},{8,9},{9,8},{10,11... | collective-permute-start | bytes 2654216 | tf_op jit(solution)/shard_map/ppermute | solution.py:588
  43.3 12.4 %copy-start = (f32[288,2304]{1,0:T(8,128)S(1)}, f32[288,2304]{1,0:T(8,128)}, u32[]{:S(2)}) copy-start(f32[288,2304]{1,0:T(8,128)} %get-tuple-element.104.projected.q_ref.k_ref.v_ref) | copy-start | bytes 7962628
  43.3 12.4 %copy-start.3 = (f32[12,72,72]{2,1,0:T(8,128)S(1)}, f32[12,72,72]{2,1,0:T(8,128)}, u32[]{:S(2)}) copy-start(f32[12,72,72]{2,1,0:T(8,128)} %param.17) | copy-start | bytes 746500
  43.3 12.4 %copy-start.5 = (s32[288,1]{1,0:T(8,128)S(1)}, s32[288,1]{1,0:T(8,128)}, u32[]{:S(2)}) copy-start(s32[288,1]{1,0:T(8,128)} %reshape.33.col) | copy-start | bytes 3460
  43.3 12.4 %copy-start.10 = (s32[4,72]{1,0:T(4,128)S(1)}, s32[4,72]{1,0:T(4,128)}, u32[]{:S(2)}) copy-start(s32[4,72]{1,0:T(4,128)} %reshape.30.row) | copy-start | bytes 3460
  43.3 12.4 %copy-start.12 = (f32[12]{0:T(128)S(1)}, f32[12]{0:T(128)}, u32[]{:S(2)}) copy-start(f32[12]{0:T(128)} %scale.5) | copy-start | bytes 148
  54.5 7.4 %collective-permute-start.9 = (bf16[288,1536]{1,0:T(8,128)(2,1)}, bf16[288,1536]{1,0:T(8,128)(2,1)}, u32[]{:S(2)}, u32[]{:S(2)}) collective-permute-start(bf16[288,1536]{1,0:T(8,128)(2,1)} %get-tuple-element.113.m0), channel_id=1, source_target_pairs={{0,1},{1,0},{2,3},{3,2},{4,5},{5,4},{6,7},{7,6},{8,9},{9,8},{10,11... | collective-permute-start | bytes 2654216 | tf_op jit(solution)/shard_map/ppermute | solution.py:588
  54.6 7.3 %collective-permute-start.8 = (bf16[288,1152]{1,0:T(8,128)(2,1)}, bf16[288,1152]{1,0:T(8,128)(2,1)}, u32[]{:S(2)}, u32[]{:S(2)}) collective-permute-start(bf16[288,1152]{1,0:T(8,128)(2,1)} %get-tuple-element.112.theirs), channel_id=1, source_target_pairs={{0,1},{1,0},{2,3},{3,2},{4,5},{5,4},{6,7},{7,6},{8,9},{9,8},{10,11... | collective-permute-start | bytes 1990664 | tf_op jit(solution)/shard_map/ppermute | solution.py:588
  55.1 6.8 %collective-permute-start.11 = (f32[144,512]{1,0:T(8,128)}, f32[144,512]{1,0:T(8,128)S(1)}, u32[]{:S(2)}, u32[]{:S(2)}) collective-permute-start(f32[144,512]{1,0:T(8,128)} %get-tuple-element.117), channel_id=1, source_target_pairs={{0,1},{1,0},{2,3},{3,2},{4,5},{5,4},{6,7},{7,6},{8,9},{9,8},{10,11... | collective-permute-start | bytes 884744 | tf_op jit(solution)/shard_map/ppermute | solution.py:588
  55.2 6.7 %collective-permute-start.10 = (bf16[288,384]{1,0:T(8,128)(2,1)}, bf16[288,384]{1,0:T(8,128)(2,1)}, u32[]{:S(2)}, u32[]{:S(2)}) collective-permute-start(bf16[288,384]{1,0:T(8,128)(2,1)} %get-tuple-element.115), channel_id=1, source_target_pairs={{0,1},{1,0},{2,3},{3,2},{4,5},{5,4},{6,7},{7,6},{8,9},{9,8},{10,11... | collective-permute-start | bytes 663560 | tf_op jit(solution)/shard_map/ppermute | solution.py:588
  57.4 4.5 %copy-start.13 = (bf16[288,1536]{1,0:T(8,128)(2,1)S(1)}, bf16[288,1536]{1,0:T(8,128)(2,1)}, u32[]{:S(2)}) copy-start(bf16[288,1536]{1,0:T(8,128)(2,1)} %get-tuple-element.103.x0) | copy-start | bytes 2654212
  57.4 4.5 %copy-start.14 = (bf16[288,1536]{1,0:T(8,128)(2,1)S(1)}, bf16[288,1536]{1,0:T(8,128)(2,1)}, u32[]{:S(2)}) copy-start(bf16[288,1536]{1,0:T(8,128)(2,1)} %get-tuple-element.113.m0) | copy-start | bytes 2654212
  57.4 4.5 %copy-start.15 = (bf16[288,384]{1,0:T(8,128)(2,1)S(1)}, bf16[288,384]{1,0:T(8,128)(2,1)}, u32[]{:S(2)}) copy-start(bf16[288,384]{1,0:T(8,128)(2,1)} %get-tuple-element.114.a0) | copy-start | bytes 663556
  57.4 15.5 %slice-start = ((s8[7077888]{0:T(1024)(128)(4,1)}), s8[4194304]{0:T(1024)(128)(4,1)S(1)}, s32[]{:S(2)}) async-start(s8[7077888]{0:T(1024)(128)(4,1)} %bitcast.9), calls=%async_computation | async-start | bytes 8388608
  61.9 11.0 %slice-start.1 = ((s8[7077888]{0:T(1024)(128)(4,1)}), s8[2883584]{0:T(1024)(128)(4,1)S(1)}, s32[]{:S(2)}) async-start(s8[7077888]{0:T(1024)(128)(4,1)} %bitcast.9), calls=%async_computation.1 | async-start | bytes 5767168
  62.0 11.0 %copy-start.6 = (bf16[288,1152]{1,0:T(8,128)(2,1)S(1)}, bf16[288,1152]{1,0:T(8,128)(2,1)}, u32[]{:S(2)}) copy-start(bf16[288,1152]{1,0:T(8,128)(2,1)} %get-tuple-element.112.theirs) | copy-start | bytes 1990660
  69.5 12.7 %collective-permute-start.13 = (bf16[34,24,512]{2,1,0:T(8,128)(2,1)S(1)}, bf16[34,24,512]{2,1,0:T(8,128)(2,1)S(1)}, u32[]{:S(2)}, u32[]{:S(2)}) collective-permute-start(bf16[34,24,512]{2,1,0:T(8,128)(2,1)S(1)} %get-tuple-element.131), channel_id=1, source_target_pairs={{0,16},{1,49},{16,0},{17,33},{32,48},{33,17},{48,32},{49,1},{2,18}... | collective-permute-start | bytes 2506760 | tf_op jit(solution)/shard_map/ppermute | solution.py:588
  69.6 12.7 %collective-permute-start.14 = (bf16[34,24,512]{2,1,0:T(8,128)(2,1)S(1)}, bf16[34,24,512]{2,1,0:T(8,128)(2,1)S(1)}, u32[]{:S(2)}, u32[]{:S(2)}) collective-permute-start(bf16[34,24,512]{2,1,0:T(8,128)(2,1)S(1)} %get-tuple-element.133), channel_id=1, source_target_pairs={{0,2},{1,67},{2,0},{3,65},{64,66},{65,3},{66,64},{67,1},{4,6},{5,7... | collective-permute-start | bytes 2506760 | tf_op jit(solution)/shard_map/ppermute | solution.py:588
  69.8 13.0 %collective-permute-start.15 = (bf16[34,24,512]{2,1,0:T(8,128)(2,1)S(1)}, bf16[34,24,512]{2,1,0:T(8,128)(2,1)S(1)}, u32[]{:S(2)}, u32[]{:S(2)}) collective-permute-start(bf16[34,24,512]{2,1,0:T(8,128)(2,1)S(1)} %get-tuple-element.135), channel_id=1, source_target_pairs={{0,4},{1,13},{4,0},{5,9},{8,12},{9,5},{12,8},{13,1},{2,6},{3,15},{... | collective-permute-start | bytes 2506760 | tf_op jit(solution)/shard_map/ppermute | solution.py:588
  84.0 7.5 %collective-permute-start.16 = (bf16[18,24,512]{2,1,0:T(8,128)(2,1)S(1)}, bf16[18,24,512]{2,1,0:T(8,128)(2,1)S(1)}, u32[]{:S(2)}, u32[]{:S(2)}) collective-permute-start(bf16[18,24,512]{2,1,0:T(8,128)(2,1)S(1)} %get-tuple-element.137), channel_id=1, source_target_pairs={{0,48},{1,17},{16,32},{17,1},{32,16},{33,49},{48,0},{49,33},{2,50}... | collective-permute-start | bytes 1327112 | tf_op jit(solution)/shard_map/ppermute | solution.py:588
  84.1 7.5 %collective-permute-start.17 = (bf16[18,24,512]{2,1,0:T(8,128)(2,1)S(1)}, bf16[18,24,512]{2,1,0:T(8,128)(2,1)S(1)}, u32[]{:S(2)}, u32[]{:S(2)}) collective-permute-start(bf16[18,24,512]{2,1,0:T(8,128)(2,1)S(1)} %get-tuple-element.139), channel_id=1, source_target_pairs={{0,66},{1,3},{2,64},{3,1},{64,2},{65,67},{66,0},{67,65},{4,70},{5,... | collective-permute-start | bytes 1327112 | tf_op jit(solution)/shard_map/ppermute | solution.py:588
  84.2 7.5 %collective-permute-start.18 = (bf16[18,24,512]{2,1,0:T(8,128)(2,1)S(1)}, bf16[18,24,512]{2,1,0:T(8,128)(2,1)S(1)}, u32[]{:S(2)}, u32[]{:S(2)}) collective-permute-start(bf16[18,24,512]{2,1,0:T(8,128)(2,1)S(1)} %get-tuple-element.141), channel_id=1, source_target_pairs={{0,12},{1,5},{4,8},{5,1},{8,4},{9,13},{12,0},{13,9},{2,14},{3,7},{... | collective-permute-start | bytes 1327112 | tf_op jit(solution)/shard_map/ppermute | solution.py:588
  91.8 31.5 %copy-start.2 = (bf16[24,12,1536]{2,0,1:T(8,128)(2,1)S(1)}, bf16[24,12,1536]{2,0,1:T(8,128)(2,1)}, u32[]{:S(2)}) copy-start(bf16[24,12,1536]{2,0,1:T(8,128)(2,1)} %param.11) | copy-start | bytes 2654212
  92.6 8.2 %collective-permute-start.19 = (bf16[10,24,512]{2,1,0:T(8,128)(2,1)S(1)}, bf16[10,24,512]{2,1,0:T(8,128)(2,1)S(1)}, u32[]{:S(2)}, u32[]{:S(2)}) collective-permute-start(bf16[10,24,512]{2,1,0:T(8,128)(2,1)S(1)} %get-tuple-element.143), channel_id=1, source_target_pairs={{0,2},{1,67},{2,0},{3,65},{64,66},{65,3},{66,64},{67,1},{4,6},{5,7... | collective-permute-start | bytes 737288 | tf_op jit(solution)/shard_map/ppermute | solution.py:588
  94.8 6.3 %collective-permute-start.20 = (bf16[10,24,512]{2,1,0:T(8,128)(2,1)S(1)}, bf16[10,24,512]{2,1,0:T(8,128)(2,1)S(1)}, u32[]{:S(2)}, u32[]{:S(2)}) collective-permute-start(bf16[10,24,512]{2,1,0:T(8,128)(2,1)S(1)} %get-tuple-element.145), channel_id=1, source_target_pairs={{0,4},{1,13},{4,0},{5,9},{8,12},{9,5},{12,8},{13,1},{2,6},{3,15},{... | collective-permute-start | bytes 737288 | tf_op jit(solution)/shard_map/ppermute | solution.py:588
  96.1 6.3 %collective-permute-start.21 = (bf16[10,24,512]{2,1,0:T(8,128)(2,1)S(1)}, bf16[10,24,512]{2,1,0:T(8,128)(2,1)S(1)}, u32[]{:S(2)}, u32[]{:S(2)}) collective-permute-start(bf16[10,24,512]{2,1,0:T(8,128)(2,1)S(1)} %get-tuple-element.147), channel_id=1, source_target_pairs={{0,16},{1,49},{16,0},{17,33},{32,48},{33,17},{48,32},{49,1},{2,18}... | collective-permute-start | bytes 737288 | tf_op jit(solution)/shard_map/ppermute | solution.py:588
  97.4 8.5 %collective-permute-start.12 = (bf16[72,1536]{1,0:T(8,128)(2,1)S(1)}, bf16[72,1536]{1,0:T(8,128)(2,1)S(1)}, u32[]{:S(2)}, u32[]{:S(2)}) collective-permute-start(bf16[72,1536]{1,0:T(8,128)(2,1)S(1)} %get-tuple-element.128), channel_id=1, source_target_pairs={{0,124},{4,0},{8,4},{12,8},{16,12},{20,16},{24,20},{28,24},{32,28}... | collective-permute-start | bytes 663560 | tf_op jit(solution)/shard_map/ppermute | solution.py:588
  103.1 4.1 %collective-permute-start.22 = (bf16[6,24,512]{2,1,0:T(8,128)(2,1)S(1)}, bf16[6,24,512]{2,1,0:T(8,128)(2,1)S(1)}, u32[]{:S(2)}, u32[]{:S(2)}) collective-permute-start(bf16[6,24,512]{2,1,0:T(8,128)(2,1)S(1)} %get-tuple-element.149), channel_id=1, source_target_pairs={{0,66},{1,3},{2,64},{3,1},{64,2},{65,67},{66,0},{67,65},{4,70},{5,... | collective-permute-start | bytes 442376 | tf_op jit(solution)/shard_map/ppermute | solution.py:588
  104.0 4.3 %collective-permute-start.23 = (bf16[6,24,512]{2,1,0:T(8,128)(2,1)S(1)}, bf16[6,24,512]{2,1,0:T(8,128)(2,1)S(1)}, u32[]{:S(2)}, u32[]{:S(2)}) collective-permute-start(bf16[6,24,512]{2,1,0:T(8,128)(2,1)S(1)} %get-tuple-element.151), channel_id=1, source_target_pairs={{0,12},{1,5},{4,8},{5,1},{8,4},{9,13},{12,0},{13,9},{2,14},{3,7},{... | collective-permute-start | bytes 442376 | tf_op jit(solution)/shard_map/ppermute | solution.py:588
  104.0 4.5 %collective-permute-start.24 = (bf16[6,24,512]{2,1,0:T(8,128)(2,1)S(1)}, bf16[6,24,512]{2,1,0:T(8,128)(2,1)S(1)}, u32[]{:S(2)}, u32[]{:S(2)}) collective-permute-start(bf16[6,24,512]{2,1,0:T(8,128)(2,1)S(1)} %get-tuple-element.153), channel_id=1, source_target_pairs={{0,48},{1,17},{16,32},{17,1},{32,16},{33,49},{48,0},{49,33},{2,50}... | collective-permute-start | bytes 442376 | tf_op jit(solution)/shard_map/ppermute | solution.py:588
  104.4 18.8 %collective-permute-start.31 = (bf16[72,1536]{1,0:T(8,128)(2,1)S(1)}, bf16[72,1536]{1,0:T(8,128)(2,1)S(1)}, u32[]{:S(2)}, u32[]{:S(2)}) collective-permute-start(bf16[72,1536]{1,0:T(8,128)(2,1)S(1)} %get-tuple-element.167), channel_id=1, source_target_pairs={{0,4},{4,8},{8,12},{12,16},{16,20},{20,24},{24,28},{28,32},{32,36}... | collective-permute-start | bytes 663560 | tf_op jit(solution)/shard_map/ppermute | solution.py:588
  109.2 10.1 %collective-permute-start.25 = (bf16[4,24,512]{2,1,0:T(8,128)(2,1)S(1)}, bf16[4,24,512]{2,1,0:T(8,128)(2,1)S(1)}, u32[]{:S(2)}, u32[]{:S(2)}) collective-permute-start(bf16[4,24,512]{2,1,0:T(8,128)(2,1)S(1)} %get-tuple-element.155), channel_id=1, source_target_pairs={{0,4},{1,13},{4,0},{5,9},{8,12},{9,5},{12,8},{13,1},{2,6},{3,15},{... | collective-permute-start | bytes 294920 | tf_op jit(solution)/shard_map/ppermute | solution.py:588
  110.3 8.9 %collective-permute-start.26 = (bf16[4,24,512]{2,1,0:T(8,128)(2,1)S(1)}, bf16[4,24,512]{2,1,0:T(8,128)(2,1)S(1)}, u32[]{:S(2)}, u32[]{:S(2)}) collective-permute-start(bf16[4,24,512]{2,1,0:T(8,128)(2,1)S(1)} %get-tuple-element.157), channel_id=1, source_target_pairs={{0,16},{1,49},{16,0},{17,33},{32,48},{33,17},{48,32},{49,1},{2,18}... | collective-permute-start | bytes 294920 | tf_op jit(solution)/shard_map/ppermute | solution.py:588
  112.9 6.3 %collective-permute-start.27 = (bf16[4,24,512]{2,1,0:T(8,128)(2,1)S(1)}, bf16[4,24,512]{2,1,0:T(8,128)(2,1)S(1)}, u32[]{:S(2)}, u32[]{:S(2)}) collective-permute-start(bf16[4,24,512]{2,1,0:T(8,128)(2,1)S(1)} %get-tuple-element.159), channel_id=1, source_target_pairs={{0,2},{1,67},{2,0},{3,65},{64,66},{65,3},{66,64},{67,1},{4,6},{5,7... | collective-permute-start | bytes 294920 | tf_op jit(solution)/shard_map/ppermute | solution.py:588
  113.6 9.7 %collective-permute-start.32 = (bf16[36,1536]{1,0:T(8,128)(2,1)S(1)}, bf16[36,1536]{1,0:T(8,128)(2,1)S(1)}, u32[]{:S(2)}, u32[]{:S(2)}) collective-permute-start(bf16[36,1536]{1,0:T(8,128)(2,1)S(1)} %last_rows.1), channel_id=1, source_target_pairs={{0,1},{1,2},{2,3},{3,0},{4,5},{5,6},{6,7},{7,4},{8,9},{9,10},{10,1... | collective-permute-start | bytes 331784 | tf_op jit(solution)/shard_map/ppermute | solution.py:588
  119.9 4.7 %collective-permute-start.28 = (bf16[3,24,512]{2,1,0:T(8,128)(2,1)S(1)}, bf16[3,24,512]{2,1,0:T(8,128)(2,1)S(1)}, u32[]{:S(2)}, u32[]{:S(2)}) collective-permute-start(bf16[3,24,512]{2,1,0:T(8,128)(2,1)S(1)} %get-tuple-element.161), channel_id=1, source_target_pairs={{0,12},{1,5},{4,8},{5,1},{8,4},{9,13},{12,0},{13,9},{2,14},{3,7},{... | collective-permute-start | bytes 221192 | tf_op jit(solution)/shard_map/ppermute | solution.py:588
  121.5 3.5 %collective-permute-start.29 = (bf16[3,24,512]{2,1,0:T(8,128)(2,1)S(1)}, bf16[3,24,512]{2,1,0:T(8,128)(2,1)S(1)}, u32[]{:S(2)}, u32[]{:S(2)}) collective-permute-start(bf16[3,24,512]{2,1,0:T(8,128)(2,1)S(1)} %get-tuple-element.163), channel_id=1, source_target_pairs={{0,48},{1,17},{16,32},{17,1},{32,16},{33,49},{48,0},{49,33},{2,50}... | collective-permute-start | bytes 221192 | tf_op jit(solution)/shard_map/ppermute | solution.py:588
  123.3 3.2 %collective-permute-start.30 = (bf16[3,24,512]{2,1,0:T(8,128)(2,1)S(1)}, bf16[3,24,512]{2,1,0:T(8,128)(2,1)S(1)}, u32[]{:S(2)}, u32[]{:S(2)}) collective-permute-start(bf16[3,24,512]{2,1,0:T(8,128)(2,1)S(1)} %get-tuple-element.165), channel_id=1, source_target_pairs={{0,66},{1,3},{2,64},{3,1},{64,2},{65,67},{66,0},{67,65},{4,70},{5,... | collective-permute-start | bytes 221192 | tf_op jit(solution)/shard_map/ppermute | solution.py:588
  126.5 8.2 %collective-permute-start.33 = (bf16[9,24,512]{2,1,0:T(8,128)(2,1)S(1)}, bf16[9,24,512]{2,1,0:T(8,128)(2,1)S(1)}, u32[]{:S(2)}, u32[]{:S(2)}) collective-permute-start(bf16[9,24,512]{2,1,0:T(8,128)(2,1)S(1)} %total.1.own), channel_id=1, source_target_pairs={{0,1},{1,0},{2,3},{3,2},{4,5},{5,4},{6,7},{7,6},{8,9},{9,8},{10,11... | collective-permute-start | bytes 663560 | tf_op jit(solution)/shard_map/ppermute | solution.py:588
  (8 other events, 7.0 us)
